TPU v7x, 32 devices: a whole 2x2x4 slice. The times are simulated.
32 devices in a mesh: tm: 4 (over y, core), height: 2 (over x), width: 4 (over z).
Axes of the slice: x: 2, y: 2, z: 4, core: 2. Of those that a mesh axis runs over, the one named last changes fastest.
Arguments:
- latents: bfloat16 [16, 16, 32, 512], P('tm', 'height', 'width'), may hold values from -6 to 6
- spatial_taps: float32 [3, 3, 512], replicated, may hold values from -2 to 2
- kernel_taps: bfloat16 [16, 512], replicated, may hold values from -0.4 to 0.4
- skip_gain: float32 [512], replicated, may hold values from 0.5 to 1.5
- gate_weight: bfloat16 [512, 512], replicated, may hold values from -0.25 to 0.25
- value_weight: bfloat16 [512, 512], replicated, may hold values from -0.25 to 0.25
- out_weight: bfloat16 [512, 512], replicated, may hold values from -0.25 to 0.25
Outputs:
- mixed_out: bfloat16 [16, 16, 32, 512], P('tm', 'height', 'width')
All inputs are finite; a program needn't handle non-finite values.
Results may differ from a plain program's by a relative error of at most 0.0064.
Values may be sent and summed in bfloat16 or wider, within the bound.
No kernel may reach another device: no remote copies, remote signals or barrier semaphores. Data moves between devices by JAX's collectives and lax.ppermute only.
A program may use at most 64 MiB of HBM per device.

v0:
```python
import jax
import jax.numpy as jnp
from jax import lax
from jax.sharding import PartitionSpec as P


def with_halo(cells, sides, width):
    for axis, dim in sides:
        count = lax.axis_size(axis)
        ends = count - 1
        head = lax.slice_in_dim(cells, 0, width, axis=dim)
        tail = lax.slice_in_dim(cells, cells.shape[dim] - width, cells.shape[dim], axis=dim)
        cells = jnp.concatenate(
            [
                lax.ppermute(tail, axis, [(i, (i + 1) % count) for i in range(ends)]),
                cells,
                lax.ppermute(head, axis, [((i + 1) % count, i) for i in range(ends)]),
            ],
            axis=dim,
        )
    return cells


def spatial_mix(padded, spatial_taps):
    rows = padded.shape[1] - 2
    cols = padded.shape[2] - 2
    total = jnp.zeros((padded.shape[0], rows, cols, padded.shape[3]), jnp.float32)
    for first in range(3):
        for second in range(3):
            window = padded[:, first : first + rows, second : second + cols, :].astype(jnp.float32)
            total = total + window * spatial_taps[first, second]
    return total.astype(jnp.bfloat16)


def body(latents, spatial_taps, kernel_taps, skip_gain, gate_weight, value_weight, out_weight):
    frames_dev, rows, cols, chans = latents.shape
    clip_len = kernel_taps.shape[0]
    padded = with_halo(latents, (("height", 1), ("width", 2)), 1)
    spatial = spatial_mix(padded, spatial_taps)
    share = chans // lax.axis_size("tm")
    first = lax.axis_index("tm") * share
    local_taps = lax.dynamic_slice_in_dim(kernel_taps, first, share, 1)
    local_skip = lax.dynamic_slice_in_dim(skip_gain, first, share, 0)
    lag = (
        jnp.arange(clip_len, dtype=jnp.int32)[:, None]
        - jnp.arange(clip_len, dtype=jnp.int32)[None, :]
    )
    index = jnp.clip(lag, 0, clip_len - 1)
    picked = jnp.take(local_taps.T, index, axis=1)
    toeplitz = jnp.where(lag[None, :, :] >= 0, picked, jnp.zeros_like(picked))
    block = lax.all_to_all(spatial, "tm", split_axis=3, concat_axis=0, tiled=True)
    flat = block.reshape(clip_len, -1, share)
    causal = jnp.einsum("cts,sxc->txc", toeplitz, flat, preferred_element_type=jnp.float32)
    result = (causal + local_skip * flat.astype(jnp.float32)).astype(jnp.bfloat16)
    mixed = lax.all_to_all(
        result.reshape(block.shape), "tm", split_axis=0, concat_axis=3, tiled=True
    )
    flat_in = latents.reshape(-1, chans)
    flat_mixed = mixed.reshape(-1, chans)
    gate = jax.nn.silu(jnp.dot(flat_in, gate_weight, preferred_element_type=jnp.float32))
    value = jnp.dot(flat_mixed, value_weight, preferred_element_type=jnp.float32)
    hidden = (value * gate).astype(jnp.bfloat16)
    result = jnp.dot(hidden, out_weight, preferred_element_type=jnp.float32).astype(jnp.bfloat16)
    return result.reshape(latents.shape)


def solution(mesh):
    in_specs = (P("tm", "height", "width", None), P(), P(), P(), P(), P(), P())
    out_specs = P("tm", "height", "width", None)
    return jax.shard_map(body, mesh=mesh, in_specs=in_specs, out_specs=out_specs, check_vma=False)
```

profile of v0, /device:TPU:0, one launch (start us, length us, event | category | flops | bytes accessed | tf_op | source)
XLA Modules:
  0.0 69.9 jit_solution(17143788152735138402)
XLA Ops:
  0.0 0.0 copy-start
  0.0 0.8 %fusion.29 = (bf16[4,1,8,512]{3,2,1,0:T(8,128)(2,1)S(1)}, bf16[4,1,8,512]{3,2,1,0:T(8,128)(2,1)S(1)}) fusion(bf16[4,8,8,512]{3,2,1,0:T(8,128)(2,1)} %param.7), kind=kLoop, calls=%fused_computation.54 | loop fusion | bytes 131072 | tf_op jit(solution)/shard_map/slice | solution.py:11
  0.8 4.8 %collective-permute-start = (bf16[4,1,8,512]{3,2,1,0:T(8,128)(2,1)S(1)}, bf16[4,1,8,512]{3,2,1,0:T(8,128)(2,1)S(1)}, u32[]{:S(2)}, u32[]{:S(2)}) collective-permute-start(bf16[4,1,8,512]{3,2,1,0:T(8,128)(2,1)S(1)} %get-tuple-element.8), channel_id=1, source_target_pairs={{0,4},{1,5},{2,6},{3,7},{8,12},{9,13},{10,14},{11,15},{16,20},{17,... | collective-permute-start | bytes 98312 | tf_op jit(solution)/shard_map/ppermute | solution.py:15
  5.7 1.3 %collective-permute-start.1 = (bf16[4,1,8,512]{3,2,1,0:T(8,128)(2,1)S(1)}, bf16[4,1,8,512]{3,2,1,0:T(8,128)(2,1)S(1)}, u32[]{:S(2)}, u32[]{:S(2)}) collective-permute-start(bf16[4,1,8,512]{3,2,1,0:T(8,128)(2,1)S(1)} %get-tuple-element.7), channel_id=1, source_target_pairs={{4,0},{5,1},{6,2},{7,3},{12,8},{13,9},{14,10},{15,11},{20,16},{21,... | collective-permute-start | bytes 98312 | tf_op jit(solution)/shard_map/ppermute | solution.py:17
  7.0 0.9 %fusion.30 = (f32[1,1,512]{2,1,0:T(1,128)S(1)}, f32[1,1,512]{2,1,0:T(1,128)S(1)}, f32[1,1,512]{2,1,0:T(1,128)S(1)}, f32[1,1,512]{2,1,0:T(1,128)S(1)}, f32[1,1,51...) fusion(f32[3,3,512]{2,1,0:T(4,128)} %param.8), kind=kLoop, calls=%fused_computation.55 | loop fusion | bytes 36864 | tf_op jit(solution)/shard_map/slice | solution.py:31
  7.9 0.1 reshape.90
  8.0 0.0 collective-permute-done
  8.0 1.0 %constant_dynamic-update-slice_fusion.1 = bf16[4,10,8,512]{3,2,1,0:T(8,128)(2,1)S(1)} fusion(bf16[4,10,8,512]{3,2,1,0:T(8,128)(2,1)S(1)} %constant_dynamic-update-slice_fusion.2, bf16[4,8,8,512]{3,2,1,0:T(8,128)(2,1)} %param.7), kind=kLoop, calls=%fused_computation.46 | loop fusion | bytes 524288
  8.9 2.5 %collective-permute-done.1 = bf16[4,1,8,512]{3,2,1,0:T(8,128)(2,1)S(1)} collective-permute-done((bf16[4,1,8,512]{3,2,1,0:T(8,128)(2,1)S(1)}, bf16[4,1,8,512]{3,2,1,0:T(8,128)(2,1)S(1)}, u32[]{:S(2)}, u32[]{:S(2)}) %collective-permute-start.1) | collective-permute-done | bytes 32800 | tf_op jit(solution)/shard_map/ppermute | solution.py:17
  11.5 0.1 fusion.28
  11.6 3.5 %collective-permute-start.2 = (bf16[4,10,1,512]{3,0,2,1:T(4,128)(2,1)S(1)}, bf16[4,10,1,512]{3,0,2,1:T(4,128)(2,1)S(1)}, u32[]{:S(2)}, u32[]{:S(2)}) collective-permute-start(bf16[4,10,1,512]{3,0,2,1:T(4,128)(2,1)S(1)} %copy.106), channel_id=1, source_target_pairs={{0,1},{1,2},{2,3},{4,5},{5,6},{6,7},{8,9},{9,10},{10,11},{12,13},{... | collective-permute-start | bytes 122888 | tf_op jit(solution)/shard_map/ppermute | solution.py:15
  15.2 1.3 %collective-permute-start.3 = (bf16[4,10,1,512]{3,0,2,1:T(4,128)(2,1)S(1)}, bf16[4,10,1,512]{3,0,2,1:T(4,128)(2,1)S(1)}, u32[]{:S(2)}, u32[]{:S(2)}) collective-permute-start(bf16[4,10,1,512]{3,0,2,1:T(4,128)(2,1)S(1)} %copy.107), channel_id=1, source_target_pairs={{1,0},{2,1},{3,2},{5,4},{6,5},{7,6},{9,8},{10,9},{11,10},{13,12},{... | collective-permute-start | bytes 122888 | tf_op jit(solution)/shard_map/ppermute | solution.py:17
  16.5 0.3 collective-permute-done.2
  16.8 0.1 copy.96
  16.9 4.2 %collective-permute-done.3 = bf16[4,10,1,512]{3,0,2,1:T(4,128)(2,1)S(1)} collective-permute-done((bf16[4,10,1,512]{3,0,2,1:T(4,128)(2,1)S(1)}, bf16[4,10,1,512]{3,0,2,1:T(4,128)(2,1)S(1)}, u32[]{:S(2)}, u32[]{:S(2)}) %collective-permute-start.3) | collective-permute-done | bytes 40992 | tf_op jit(solution)/shard_map/ppermute | solution.py:17
  21.1 0.1 copy.98
  21.1 2.2 %add_convert_fusion = bf16[4,8,8,512]{3,2,1,0:T(8,128)(2,1)S(1)} fusion(bf16[4,8,8,512]{3,2,1,0:T(8,128)(2,1)} %param.7, bf16[4,10,8,512]{3,2,1,0:T(8,128)(2,1)S(1)} %constant_dynamic-update-slice_fusion, bf16[4,10,1,512]{3,2,1,0:T(2,128)(2,1)S(1)} %copy.98, bf16[4,10,1,512]{3,2,1,0:T(2,128)(2,1)S(1)} %copy.96, ...), kind=kLoop, calls=%fused_computation.23 | loop fusion | flops 6684672 | bytes 1017856 | tf_op jit(solution)/shard_map/convert_element_type | solution.py:32
  23.3 6.4 %copy.99 = bf16[4,8,8,512]{2,1,0,3:T(8,128)(2,1)} copy(bf16[4,8,8,512]{3,2,1,0:T(8,128)(2,1)S(1)} %add_convert_fusion) | data formatting | bytes 524288 | tf_op jit(solution)/shard_map/convert_element_type | solution.py:32
  29.7 6.4 %reshape.97 = bf16[4,2,16384]{2,1,0:T(2,128)(2,1)} reshape(bf16[512,4,8,8]{3,2,1,0:T(8,128)(2,1)} %bitcast.43) | data formatting | bytes 524288
  36.1 3.4 %all-to-all-start = ((bf16[4,2,16384]{2,1,0:T(2,128)(2,1)}), bf16[4,2,16384]{2,1,0:T(2,128)(2,1)S(1)}, u32[]{:S(2)}, u32[]{:S(2)}) async-start(bf16[4,2,16384]{2,1,0:T(2,128)(2,1)} %reshape.97), calls=%async_computation | async-start | bytes 524288 | tf_op jit(solution)/shard_map/all_to_all | solution.py:51
  39.5 0.7 dynamic-slice_bitcast_fusion
  40.2 0.9 %gather_fusion = bf16[256,128]{1,0:T(8,128)(2,1)S(1)} fusion(bf16[128,16]{0,1:T(8,128)(2,1)S(1)} %dynamic-slice_bitcast_fusion, s32[1024]{0:T(1024)S(1)} %pad_clamp_fusion), kind=kCustom, calls=%fused_computation | custom fusion | bytes 132096 | tf_op jit(solution)/shard_map/jit(_take)/gather | solution.py:49
  41.0 0.4 copy.102
  41.5 0.8 %dynamic_slice.7 = f32[128]{0:T(128)S(1)} dynamic-slice(f32[512]{0:T(512)} %param.10, s32[]{:T(128)S(6)} %select_n.29), dynamic_slice_sizes={128} | dynamic-slice | bytes 1028 | tf_op jit(solution)/shard_map/dynamic_slice | solution.py:43
  42.3 3.2 %all-to-all-done = bf16[4,2,16384]{2,1,0:T(2,128)(2,1)S(1)} async-done(((bf16[4,2,16384]{2,1,0:T(2,128)(2,1)}), bf16[4,2,16384]{2,1,0:T(2,128)(2,1)S(1)}, u32[]{:S(2)}, u32[]{:S(2)}) %all-to-all-start) | async-done | bytes 262176 | tf_op jit(solution)/shard_map/all_to_all | solution.py:51
  45.5 5.9 %reshape.98 = bf16[512,4,8,8]{3,2,1,0:T(8,128)(2,1)} reshape(bf16[4,2,16384]{2,1,0:T(2,128)(2,1)S(1)} %all-to-all-done) | data formatting | bytes 524288
  51.4 4.4 %copy.100 = bf16[4,8,8,512]{3,2,1,0:T(8,128)(2,1)S(1)} copy(bf16[4,8,8,512]{2,1,0,3:T(8,128)(2,1)} %bitcast.44) | data formatting | bytes 524288 | tf_op jit(solution)/shard_map/all_to_all | solution.py:51
  55.8 0.0 copy-start.1
  55.8 0.1 copy.101
  55.9 0.4 copy.103
  56.4 0.4 fusion.2
  56.8 0.5 copy.104
  57.3 0.8 %fusion.13 = bf16[16,8,8,128]{3,2,1,0:T(8,128)(2,1)} fusion(bf16[16,64,128]{2,1,0:T(8,128)(2,1)S(1)} %bitcast.48, f32[128,64,16]{0,1,2:T(8,128)S(1)} %copy.104, f32[128]{0:T(128)S(1)} %dynamic_slice.7), kind=kLoop, calls=%fused_computation.26 | loop fusion | flops 524288 | bytes 1049088 | tf_op jit(solution)/shard_map/reshape | solution.py:56
  58.1 3.4 %all-to-all-start.1 = ((bf16[16,8,8,128]{3,2,1,0:T(8,128)(2,1)}), bf16[16,8,8,128]{3,2,1,0:T(8,128)(2,1)S(1)}, u32[]{:S(2)}, u32[]{:S(2)}) async-start(bf16[16,8,8,128]{3,2,1,0:T(8,128)(2,1)} %fusion.13), calls=%async_computation.1 | async-start | bytes 524288 | tf_op jit(solution)/shard_map/all_to_all | solution.py:55
  61.5 0.0 copy-done
  61.5 0.0 copy-done.1
  61.5 0.3 fusion.31
  61.8 5.7 %all-to-all-done.1 = bf16[16,8,8,128]{3,2,1,0:T(8,128)(2,1)S(1)} async-done(((bf16[16,8,8,128]{3,2,1,0:T(8,128)(2,1)}), bf16[16,8,8,128]{3,2,1,0:T(8,128)(2,1)S(1)}, u32[]{:S(2)}, u32[]{:S(2)}) %all-to-all-start.1) | async-done | bytes 262176 | tf_op jit(solution)/shard_map/all_to_all | solution.py:55
  67.5 2.4 %convolution_convert_fusion = bf16[256,512]{1,0:T(8,128)(2,1)} fusion(bf16[512,512]{1,0:T(8,128)(2,1)} %param.13, bf16[256,512]{1,0:T(8,128)(2,1)S(1)} %bitcast.51, bf16[512,512]{1,0:T(8,128)(2,1)} %param.12, f32[256,512]{1,0:T(8,128)S(1)} %fusion.31), kind=kOutput, calls=%fused_computation.3 | convolution fusion | flops 269352960 | bytes 2097152 | tf_op jit(solution)/shard_map/dot_general | solution.py:63
  (8 shorter events, 0.1 us)
Async XLA Ops:
  0.0 61.5 %copy-start = (bf16[512,512]{1,0:T(8,128)(2,1)S(1)}, bf16[512,512]{1,0:T(8,128)(2,1)}, u32[]{:S(2)}) copy-start(bf16[512,512]{1,0:T(8,128)(2,1)} %param.11) | copy-start | bytes 1572868
  0.8 7.1 %collective-permute-start = (bf16[4,1,8,512]{3,2,1,0:T(8,128)(2,1)S(1)}, bf16[4,1,8,512]{3,2,1,0:T(8,128)(2,1)S(1)}, u32[]{:S(2)}, u32[]{:S(2)}) collective-permute-start(bf16[4,1,8,512]{3,2,1,0:T(8,128)(2,1)S(1)} %get-tuple-element.8), channel_id=1, source_target_pairs={{0,4},{1,5},{2,6},{3,7},{8,12},{9,13},{10,14},{11,15},{16,20},{17,... | collective-permute-start | bytes 98312 | tf_op jit(solution)/shard_map/ppermute | solution.py:15
  5.7 5.8 %collective-permute-start.1 = (bf16[4,1,8,512]{3,2,1,0:T(8,128)(2,1)S(1)}, bf16[4,1,8,512]{3,2,1,0:T(8,128)(2,1)S(1)}, u32[]{:S(2)}, u32[]{:S(2)}) collective-permute-start(bf16[4,1,8,512]{3,2,1,0:T(8,128)(2,1)S(1)} %get-tuple-element.7), channel_id=1, source_target_pairs={{4,0},{5,1},{6,2},{7,3},{12,8},{13,9},{14,10},{15,11},{20,16},{21,... | collective-permute-start | bytes 98312 | tf_op jit(solution)/shard_map/ppermute | solution.py:17
  11.6 5.1 %collective-permute-start.2 = (bf16[4,10,1,512]{3,0,2,1:T(4,128)(2,1)S(1)}, bf16[4,10,1,512]{3,0,2,1:T(4,128)(2,1)S(1)}, u32[]{:S(2)}, u32[]{:S(2)}) collective-permute-start(bf16[4,10,1,512]{3,0,2,1:T(4,128)(2,1)S(1)} %copy.106), channel_id=1, source_target_pairs={{0,1},{1,2},{2,3},{4,5},{5,6},{6,7},{8,9},{9,10},{10,11},{12,13},{... | collective-permute-start | bytes 122888 | tf_op jit(solution)/shard_map/ppermute | solution.py:15
  15.2 5.9 %collective-permute-start.3 = (bf16[4,10,1,512]{3,0,2,1:T(4,128)(2,1)S(1)}, bf16[4,10,1,512]{3,0,2,1:T(4,128)(2,1)S(1)}, u32[]{:S(2)}, u32[]{:S(2)}) collective-permute-start(bf16[4,10,1,512]{3,0,2,1:T(4,128)(2,1)S(1)} %copy.107), channel_id=1, source_target_pairs={{1,0},{2,1},{3,2},{5,4},{6,5},{7,6},{9,8},{10,9},{11,10},{13,12},{... | collective-permute-start | bytes 122888 | tf_op jit(solution)/shard_map/ppermute | solution.py:17
  36.1 9.4 %all-to-all-start = ((bf16[4,2,16384]{2,1,0:T(2,128)(2,1)}), bf16[4,2,16384]{2,1,0:T(2,128)(2,1)S(1)}, u32[]{:S(2)}, u32[]{:S(2)}) async-start(bf16[4,2,16384]{2,1,0:T(2,128)(2,1)} %reshape.97), calls=%async_computation | async-start | bytes 524288 | tf_op jit(solution)/shard_map/all_to_all | solution.py:51
  55.8 5.6 %copy-start.1 = (bf16[4,8,8,512]{3,2,1,0:T(8,128)(2,1)S(1)}, bf16[4,8,8,512]{3,2,1,0:T(8,128)(2,1)}, u32[]{:S(2)}) copy-start(bf16[4,8,8,512]{3,2,1,0:T(8,128)(2,1)} %param.7) | copy-start | bytes 786436
  58.1 9.4 %all-to-all-start.1 = ((bf16[16,8,8,128]{3,2,1,0:T(8,128)(2,1)}), bf16[16,8,8,128]{3,2,1,0:T(8,128)(2,1)S(1)}, u32[]{:S(2)}, u32[]{:S(2)}) async-start(bf16[16,8,8,128]{3,2,1,0:T(8,128)(2,1)} %fusion.13), calls=%async_computation.1 | async-start | bytes 524288 | tf_op jit(solution)/shard_map/all_to_all | solution.py:55
where the time goes:
time: 70.6 us; the launch traced here: 69.9 us
  local copies, waits for them, and re-layouts  29.9 us (42%)
  starting transfers between devices  17.7 us (25%)
  waiting for transfers between devices  16 us (23%)
  matrix products  3.16 us (4%)
  other arithmetic  3.01 us (4%)
    unnamed x10, local copies, waits for them, and re-layouts  13.4 us
    ppermute x2, starting transfers between devices, with_halo(): lax.ppermute(tail, axis, [(i, (i + 1) % count) for i in range(ends)])  8.31 us
    ppermute x2, waiting for transfers between devices, with_halo(): lax.ppermute(head, axis, [((i + 1) % count, i) for i in range(ends)])  6.75 us
    convert_element_type x1, local copies, waits for them, and re-layouts, spatial_mix(): return total.astype(jnp.bfloat16)  6.37 us
    all_to_all x1, waiting for transfers between devices, body(): lax.all_to_all(result.reshape(block.shape), 'tm', split_axis=0, concat_ax...  5.68 us
    all_to_all x2, local copies, waits for them, and re-layouts, body(): lax.all_to_all(spatial, 'tm', split_axis=3, concat_axis=0, tiled=True)  4.46 us
    all_to_all x1, starting transfers between devices, body(): lax.all_to_all(spatial, 'tm', split_axis=3, concat_axis=0, tiled=True)  3.41 us
    all_to_all x1, starting transfers between devices, body(): lax.all_to_all(result.reshape(block.shape), 'tm', split_axis=0, concat_ax...  3.41 us
  transfers between devices with their start and end apart: 6, of which 5 were waited for; matrix products, arithmetic and copies ran while one was open for 7% of the time, Pallas kernels for 0%

commit v1 on v0

v1 whole, which is shorter than its diff:
```python
import functools

import jax
import jax.numpy as jnp
from jax import lax
from jax.experimental import pallas as pl
from jax.experimental.pallas import tpu as pltpu
from jax.sharding import PartitionSpec as P

LANES = 128
VMEM = pl.BlockSpec(memory_space=pltpu.VMEM)
SMEM = pl.BlockSpec(memory_space=pltpu.SMEM)
PARAMS = pltpu.CompilerParams(vmem_limit_bytes=16 * 1024 * 1024)


def gate_kernel(x_ref, w_ref, gate_ref):
    v = jnp.dot(x_ref[...], w_ref[...], preferred_element_type=jnp.float32)
    gate_ref[...] = v / (1.0 + jnp.exp(-v))


def mix_kernel(frames, cols, me_ref, clip_ref, taps_ref, skip_ref, u_ref, left_ref, right_ref, table, held):
    me = me_ref[0]
    lags, chans = taps_ref.shape
    sites = u_ref.shape[0] // frames
    taps = taps_ref[...].astype(jnp.float32)
    table[0:lags] = jnp.zeros((lags, cols, chans), jnp.float32)
    for lag in range(lags):
        tap = taps[lag : lag + 1] + (skip_ref[...] if lag == 0 else 0.0)
        table[lags + lag] = jnp.broadcast_to(tap, (cols, chans))
    for lane in range(0, chans, LANES):
        span = slice(lane, lane + LANES)

        def step(block, totals):
            totals = list(totals)
            for s in range(frames):
                start = pl.multiple_of((block * frames + s) * sites, sites)
                x = clip_ref[pl.ds(start, sites), span].astype(jnp.float32).reshape(sites // cols, cols, LANES)
                for t in range(frames):
                    tap = table[lags + (me - block) * frames + t - s, :, span]
                    totals[t] = totals[t] + tap * x
            return tuple(totals)

        zero = jnp.zeros((sites // cols, cols, LANES), jnp.float32)
        totals = lax.fori_loop(0, me + 1, step, (zero,) * frames)
        for t in range(frames):
            held[t * sites : (t + 1) * sites, :] = totals[t].reshape(sites, LANES)
        u_ref[:, span] = held[...].astype(jnp.bfloat16)
        lines = frames * sites // cols
        left_ref[:, span] = held[pl.ds(0, lines, stride=cols), :].astype(jnp.bfloat16)
        right_ref[:, span] = held[pl.ds(cols - 1, lines, stride=cols), :].astype(jnp.bfloat16)


def finish_kernel(
    frames, rows, cols, at_ref, u_ref, left_ref, right_ref, above_ref, below_ref, taps_ref, gate_ref, wv_ref, wo_ref,
    out_ref, mixed,
):
    first = at_ref[0].astype(jnp.float32)
    last = at_ref[1].astype(jnp.float32)
    chans = u_ref.shape[1]
    place = lax.broadcasted_iota(jnp.int32, (cols, LANES), 0)
    for lane in range(0, chans, LANES):
        span = slice(lane, lane + LANES)
        taps = [[taps_ref[3 * a + b : 3 * a + b + 1, span] for b in range(3)] for a in range(3)]
        left = left_ref[:, span].astype(jnp.float32)
        right = right_ref[:, span].astype(jnp.float32)
        above = above_ref[:, span].astype(jnp.float32) * first
        below = below_ref[:, span].astype(jnp.float32) * last
        corner = frames * cols
        for t in range(frames):
            tile = u_ref[t * rows * cols : (t + 1) * rows * cols, span].astype(jnp.float32)
            lines = [above[t * cols : (t + 1) * cols]]
            lefts = [above[corner + t : corner + t + 1]]
            rights = [above[corner + frames + t : corner + frames + t + 1]]
            for r in range(rows):
                lines.append(tile[r * cols : (r + 1) * cols])
                lefts.append(left[t * rows + r : t * rows + r + 1])
                rights.append(right[t * rows + r : t * rows + r + 1])
            lines.append(below[t * cols : (t + 1) * cols])
            lefts.append(below[corner + t : corner + t + 1])
            rights.append(below[corner + frames + t : corner + frames + t + 1])
            totals = [None] * rows
            for r in range(rows + 2):
                before = jnp.where(place == 0, lefts[r], pltpu.roll(lines[r], 1, 0))
                after = jnp.where(place == cols - 1, rights[r], pltpu.roll(lines[r], cols - 1, 0))
                for a in range(3):
                    to = r - a
                    if 0 <= to < rows:
                        term = before * taps[a][0] + lines[r] * taps[a][1] + after * taps[a][2]
                        totals[to] = term if totals[to] is None else totals[to] + term
            mixed[t * rows * cols : (t + 1) * rows * cols, span] = jnp.concatenate(totals, axis=0).astype(jnp.bfloat16)
    value = jnp.dot(mixed[...], wv_ref[...], preferred_element_type=jnp.float32)
    hidden = (value * gate_ref[...]).astype(jnp.bfloat16)
    out_ref[...] = jnp.dot(hidden, wo_ref[...], preferred_element_type=jnp.float32).astype(jnp.bfloat16)


def body(latents, spatial_taps, kernel_taps, skip_gain, gate_weight, value_weight, out_weight):
    frames, rows, cols, chans = latents.shape
    lags = kernel_taps.shape[0]
    n_h, n_w = lax.axis_size("height"), lax.axis_size("width")
    sites = rows * cols
    lines = frames * rows
    bf16, f32 = jnp.bfloat16, jnp.float32
    x = latents.reshape(frames * sites, chans)

    clip = lax.all_gather(x, "tm", axis=0, tiled=True)
    gate = pl.pallas_call(
        gate_kernel,
        out_shape=jax.ShapeDtypeStruct(x.shape, f32),
        in_specs=[VMEM] * 2,
        out_specs=VMEM,
        compiler_params=PARAMS,
        cost_estimate=pl.CostEstimate(flops=2 * x.size * chans, bytes_accessed=2 * x.size * 4, transcendentals=x.size),
        name="gate",
    )(x, gate_weight)
    me = lax.axis_index("tm").astype(jnp.int32).reshape(1)
    u, left, right = pl.pallas_call(
        functools.partial(mix_kernel, frames, cols),
        out_shape=(
            jax.ShapeDtypeStruct(x.shape, bf16),
            jax.ShapeDtypeStruct((lines, chans), bf16),
            jax.ShapeDtypeStruct((lines, chans), bf16),
        ),
        in_specs=[SMEM, VMEM, VMEM, VMEM],
        out_specs=(VMEM, VMEM, VMEM),
        scratch_shapes=[pltpu.VMEM((2 * lags, cols, chans), f32), pltpu.VMEM((frames * sites, LANES), f32)],
        compiler_params=PARAMS,
        name="mix",
    )(me, clip, kernel_taps, skip_gain.reshape(1, chans))

    from_left = lax.ppermute(right, "width", [(i, i + 1) for i in range(n_w - 1)])
    from_right = lax.ppermute(left, "width", [(i + 1, i) for i in range(n_w - 1)])

    def border(row):
        pick = slice(row, row + 1)
        line = u.reshape(frames, rows, cols, chans)[:, row].reshape(frames * cols, chans)
        lhs = from_left.reshape(frames, rows, chans)[:, row]
        rhs = from_right.reshape(frames, rows, chans)[:, row]
        fill = jnp.zeros((-(frames * cols + 2 * frames) % 16, chans), bf16)
        return jnp.concatenate([line, lhs, rhs, fill], axis=0)

    h = lax.axis_index("height")
    top, bottom = border(0), border(rows - 1)
    if n_h == 2:
        above = below = lax.ppermute(jnp.where(h == 0, bottom, top), "height", [(0, 1), (1, 0)])
    else:
        above = lax.ppermute(bottom, "height", [(i, i + 1) for i in range(n_h - 1)])
        below = lax.ppermute(top, "height", [(i + 1, i) for i in range(n_h - 1)])
    at = jnp.stack([h > 0, h < n_h - 1]).astype(jnp.int32)

    out = pl.pallas_call(
        functools.partial(finish_kernel, frames, rows, cols),
        out_shape=jax.ShapeDtypeStruct(x.shape, bf16),
        in_specs=[SMEM] + [VMEM] * 9,
        out_specs=VMEM,
        scratch_shapes=[pltpu.VMEM(x.shape, bf16)],
        compiler_params=PARAMS,
        name="finish",
    )(at, u, from_left, from_right, above, below, spatial_taps.reshape(9, chans), gate, value_weight, out_weight)
    return out.reshape(latents.shape)


def solution(mesh):
    in_specs = (P("tm", "height", "width", None), P(), P(), P(), P(), P(), P())
    out_specs = P("tm", "height", "width", None)
    return jax.shard_map(body, mesh=mesh, in_specs=in_specs, out_specs=out_specs, check_vma=False)
```

time: 70.6 us -> 52.8 us (0.75)
  local copies, waits for them, and re-layouts: 29.9 us -> 1.4 us
  between operations: 0.19 us -> 13.5 us
  waiting for transfers between devices: 16 us -> 28.3 us
  starting transfers between devices: 17.7 us -> 6.35 us
  matrix products: 3.16 us -> 0 us
  Pallas kernels: 0 us -> 2.88 us
  other arithmetic: 3.01 us -> 0.16 us
    all_gather x0 -> x1, waiting for transfers between devices: none -> 21 us  [body(): clip = lax.all_gather(x, 'tm', axis=0, tiled=True)]
    unnamed x10 -> x16, local copies, waits for them, and re-layouts: 13.4 us -> 1.26 us
    all_to_all x2 -> x0, waiting for transfers between devices: 8.92 us -> none  [the longest x1 5.68 us: body(): lax.all_to_all(result.reshape(block.shape), 'tm', split_axis=0, concat_ax...]
    all_to_all x2 -> x0, starting transfers between devices: 6.81 us -> none  [the longest x1 3.41 us: body(): lax.all_to_all(spatial, 'tm', split_axis=3, concat_axis=0, tiled=True)]
    convert_element_type x1 -> x0, local copies, waits for them, and re-layouts: 6.37 us -> none  [spatial_mix(): return total.astype(jnp.bfloat16)]
    ppermute x4 -> x3, starting transfers between devices: 10.9 us -> 6.35 us  [the longest x1 3.52 us: body(): lax.ppermute(right, 'width', [(i, i + 1) for i in range(n_w - 1)])]
    all_to_all x3 -> x0, local copies, waits for them, and re-layouts: 4.5 us -> none  [the longest x2 4.46 us: body(): lax.all_to_all(spatial, 'tm', split_axis=3, concat_axis=0, tiled=True)]
    dot_general x3 -> x0, matrix products: 3.16 us -> none  [the longest x1 2.43 us: body(): jnp.dot(hidden, out_weight, preferred_element_type=jnp.float32)]
  transfers between devices with their start and end apart: 6 -> 4, of which waited for: 5 -> 4; matrix products, arithmetic and copies ran while one was open for 7% -> 0% of each run, Pallas kernels for 0% -> 1%
where the time goes in v1:
time: 52.8 us; the launch traced here: 52.6 us
  waiting for transfers between devices  28.3 us (54%)
  between operations  13.5 us (26%)
  starting transfers between devices  6.35 us (12%)
  Pallas kernels  2.88 us (5%)
  local copies, waits for them, and re-layouts  1.4 us (3%)
    all_gather x1, waiting for transfers between devices, body(): clip = lax.all_gather(x, 'tm', axis=0, tiled=True)  21 us
    ppermute x1, waiting for transfers between devices, body(): lax.ppermute(left, 'width', [(i + 1, i) for i in range(n_w - 1)])  4.21 us
    ppermute x1, starting transfers between devices, body(): lax.ppermute(right, 'width', [(i, i + 1) for i in range(n_w - 1)])  3.52 us
    pallas_call x1, Pallas kernels, body(): pl.pallas_call(functools.partial(finish_kernel, frames, rows, cols), out_...  2.14 us
    ppermute x1, waiting for transfers between devices, body(): lax.ppermute(jnp.where(h == 0, bottom, top), 'height', [(0, 1), (1, 0)])  2.1 us
    ppermute x1, starting transfers between devices, body(): lax.ppermute(jnp.where(h == 0, bottom, top), 'height', [(0, 1), (1, 0)])  1.53 us
    ppermute x1, starting transfers between devices, body(): lax.ppermute(left, 'width', [(i + 1, i) for i in range(n_w - 1)])  1.29 us
    unnamed x16, local copies, waits for them, and re-layouts  1.26 us
  transfers between devices with their start and end apart: 4, of which 4 were waited for; matrix products, arithmetic and copies ran while one was open for 0% of the time, Pallas kernels for 1%

profile of v1, /device:TPU:0, one launch (start us, length us, event | category | flops | bytes accessed | tf_op | source)
XLA Modules:
  0.0 52.6 jit_solution(2606345988370685411)
XLA Ops:
  6.5 0.0 all-gather.2.cloned.1.call-start
  6.5 0.7 %all-gather.2.cloned.1.call-update = ((bf16[256,512]{1,0:T(8,128)(2,1)}), bf16[1024,512]{1,0:T(8,128)(2,1)}) async-update(((), (), s32[]{:S(2)}) %all-gather.2.cloned.1.call-start, bf16[256,512]{1,0:T(8,128)(2,1)} %bitcast.25) | async-update | bytes 1572888
  7.3 0.0 copy-start.5
  7.3 0.1 pad.7.clone
  7.4 0.0 copy-start.6
  7.4 21.0 %all-gather.2.cloned.1.call-done.clip_ref = bf16[1024,512]{1,0:T(8,128)(2,1)} async-done(((bf16[256,512]{1,0:T(8,128)(2,1)}), bf16[1024,512]{1,0:T(8,128)(2,1)}) %all-gather.2.cloned.1.call-update) | async-done | bytes 1048592 | tf_op jit(solution)/shard_map/all_gather | solution.py:105
  28.4 0.0 copy-done.5
  28.4 0.0 copy-done.6
  28.4 0.0 copy-start.1
  28.4 1.2 %copy-done.1 = bf16[1024,512]{1,0:T(8,128)(2,1)S(1)} copy-done((bf16[1024,512]{1,0:T(8,128)(2,1)S(1)}, bf16[1024,512]{1,0:T(8,128)(2,1)}, u32[]{:S(2)}) %copy-start.1) | copy-done | bytes 1048600
  29.6 0.0 copy-start.4
  29.6 0.4 mix.1
  30.0 0.0 copy-start
  30.0 3.5 %collective-permute-start = (bf16[32,512]{1,0:T(8,128)(2,1)S(1)}, bf16[32,512]{1,0:T(8,128)(2,1)S(1)}, u32[]{:S(2)}, u32[]{:S(2)}) collective-permute-start(bf16[32,512]{1,0:T(8,128)(2,1)S(1)} %get-tuple-element.9), channel_id=1, source_target_pairs={{0,1},{1,2},{2,3},{4,5},{5,6},{6,7},{8,9},{9,10},{10,11},{12,13},{... | collective-permute-start | bytes 98312 | tf_op jit(solution)/shard_map/ppermute | solution.py:130
  33.5 1.3 %collective-permute-start.1 = (bf16[32,512]{1,0:T(8,128)(2,1)S(1)}, bf16[32,512]{1,0:T(8,128)(2,1)S(1)}, u32[]{:S(2)}, u32[]{:S(2)}) collective-permute-start(bf16[32,512]{1,0:T(8,128)(2,1)S(1)} %get-tuple-element.10), channel_id=1, source_target_pairs={{1,0},{2,1},{3,2},{5,4},{6,5},{7,6},{9,8},{10,9},{11,10},{13,12},{... | collective-permute-start | bytes 98312 | tf_op jit(solution)/shard_map/ppermute | solution.py:131
  34.8 0.3 collective-permute-done.left_ref
  35.1 4.2 %collective-permute-done.1.right_ref = bf16[32,512]{1,0:T(8,128)(2,1)S(1)} collective-permute-done((bf16[32,512]{1,0:T(8,128)(2,1)S(1)}, bf16[32,512]{1,0:T(8,128)(2,1)S(1)}, u32[]{:S(2)}, u32[]{:S(2)}) %collective-permute-start.1) | collective-permute-done | bytes 32800 | tf_op jit(solution)/shard_map/ppermute | solution.py:131
  39.4 0.0 copy-start.7
  39.4 0.1 maximum_select_fusion
  39.5 1.5 %collective-permute-start.2 = (bf16[48,512]{1,0:T(8,128)(2,1)S(1)}, bf16[48,512]{1,0:T(8,128)(2,1)S(1)}, u32[]{:S(2)}, u32[]{:S(2)}) collective-permute-start(bf16[48,512]{1,0:T(8,128)(2,1)S(1)} %maximum_select_fusion), channel_id=1, source_target_pairs={{0,4},{4,0},{1,5},{5,1},{2,6},{6,2},{3,7},{7,3},{8,12},{12,8},{9,1... | collective-permute-start | bytes 147464 | tf_op jit(solution)/shard_map/ppermute | solution.py:144
  41.0 0.1 add_convert_fusion.at_ref
  41.1 0.0 copy-done.7
  41.1 0.0 copy-done.4
  41.1 0.0 copy-done
  41.1 0.0 copy-start.2
  41.1 0.0 copy-start.3
  41.1 0.4 gate.1.gate_ref
  41.5 2.1 %collective-permute-done.2.above_ref.below_ref = bf16[48,512]{1,0:T(8,128)(2,1)S(1)} collective-permute-done((bf16[48,512]{1,0:T(8,128)(2,1)S(1)}, bf16[48,512]{1,0:T(8,128)(2,1)S(1)}, u32[]{:S(2)}, u32[]{:S(2)}) %collective-permute-start.2) | collective-permute-done | bytes 49184 | tf_op jit(solution)/shard_map/ppermute | solution.py:144
  43.6 0.0 copy-done.2
  43.6 0.0 copy-done.3
  43.6 2.1 %finish.1 = bf16[256,512]{1,0:T(8,128)(2,1)} custom-call(s32[2]{0:T(128)S(1)} %add_convert_fusion.at_ref, bf16[256,512]{1,0:T(8,128)(2,1)S(1)} %get-tuple-element.8.u_ref, bf16[32,512]{1,0:T(8,128)(2,1)S(1)} %collective-permute-done.left_ref, bf16[32,512]{1,0:T(8,128)(2,1)S(1)} %collective-permute-done.1.right_ref, ...), custom_call_target="tpu_custom_call" | custom-call | tf_op jit(solution)/shard_map/finish/pallas_call | solution.py:150
  (7 shorter events, 0.1 us)
Async XLA Ops:
  6.5 21.8 %all-gather.2.cloned.1.call-start = ((), (), s32[]{:S(2)}) async-start(), calls=%async_computation | async-start | bytes 1310720 | tf_op jit(solution)/shard_map/all_gather | solution.py:105
  7.3 21.1 %copy-start.5 = (bf16[16,512]{1,0:T(8,128)(2,1)S(1)}, bf16[16,512]{1,0:T(8,128)(2,1)}, u32[]{:S(2)}) copy-start(bf16[16,512]{1,0:T(8,128)(2,1)} %taps_ref.1) | copy-start | bytes 49156
  7.4 21.0 %copy-start.6 = (f32[512]{0:T(512)S(1)}, f32[512]{0:T(512)}, u32[]{:S(2)}) copy-start(f32[512]{0:T(512)} %param.10) | copy-start | bytes 6148
  28.4 1.2 %copy-start.1 = (bf16[1024,512]{1,0:T(8,128)(2,1)S(1)}, bf16[1024,512]{1,0:T(8,128)(2,1)}, u32[]{:S(2)}) copy-start(bf16[1024,512]{1,0:T(8,128)(2,1)} %all-gather.2.cloned.1.call-done.clip_ref) | copy-start | bytes 3145732
  29.6 11.5 %copy-start.4 = (bf16[512,512]{1,0:T(8,128)(2,1)S(1)}, bf16[512,512]{1,0:T(8,128)(2,1)}, u32[]{:S(2)}) copy-start(bf16[512,512]{1,0:T(8,128)(2,1)} %w_ref.1) | copy-start | bytes 1572868
  30.0 11.1 %copy-start = (bf16[4,8,8,512]{3,2,1,0:T(8,128)(2,1)S(1)}, bf16[4,8,8,512]{3,2,1,0:T(8,128)(2,1)}, u32[]{:S(2)}) copy-start(bf16[4,8,8,512]{3,2,1,0:T(8,128)(2,1)} %param.7) | copy-start | bytes 786436
  30.0 5.1 %collective-permute-start = (bf16[32,512]{1,0:T(8,128)(2,1)S(1)}, bf16[32,512]{1,0:T(8,128)(2,1)S(1)}, u32[]{:S(2)}, u32[]{:S(2)}) collective-permute-start(bf16[32,512]{1,0:T(8,128)(2,1)S(1)} %get-tuple-element.9), channel_id=1, source_target_pairs={{0,1},{1,2},{2,3},{4,5},{5,6},{6,7},{8,9},{9,10},{10,11},{12,13},{... | collective-permute-start | bytes 98312 | tf_op jit(solution)/shard_map/ppermute | solution.py:130
  33.5 5.8 %collective-permute-start.1 = (bf16[32,512]{1,0:T(8,128)(2,1)S(1)}, bf16[32,512]{1,0:T(8,128)(2,1)S(1)}, u32[]{:S(2)}, u32[]{:S(2)}) collective-permute-start(bf16[32,512]{1,0:T(8,128)(2,1)S(1)} %get-tuple-element.10), channel_id=1, source_target_pairs={{1,0},{2,1},{3,2},{5,4},{6,5},{7,6},{9,8},{10,9},{11,10},{13,12},{... | collective-permute-start | bytes 98312 | tf_op jit(solution)/shard_map/ppermute | solution.py:131
  39.4 1.7 %copy-start.7 = (f32[3,3,512]{2,1,0:T(4,128)S(1)}, f32[3,3,512]{2,1,0:T(4,128)}, u32[]{:S(2)}) copy-start(f32[3,3,512]{2,1,0:T(4,128)} %param.8) | copy-start | bytes 55300
  39.5 4.2 %collective-permute-start.2 = (bf16[48,512]{1,0:T(8,128)(2,1)S(1)}, bf16[48,512]{1,0:T(8,128)(2,1)S(1)}, u32[]{:S(2)}, u32[]{:S(2)}) collective-permute-start(bf16[48,512]{1,0:T(8,128)(2,1)S(1)} %maximum_select_fusion), channel_id=1, source_target_pairs={{0,4},{4,0},{1,5},{5,1},{2,6},{6,2},{3,7},{7,3},{8,12},{12,8},{9,1... | collective-permute-start | bytes 147464 | tf_op jit(solution)/shard_map/ppermute | solution.py:144
  41.1 2.5 %copy-start.2 = (bf16[512,512]{1,0:T(8,128)(2,1)S(1)}, bf16[512,512]{1,0:T(8,128)(2,1)}, u32[]{:S(2)}) copy-start(bf16[512,512]{1,0:T(8,128)(2,1)} %wv_ref.1) | copy-start | bytes 1572868
  41.1 2.5 %copy-start.3 = (bf16[512,512]{1,0:T(8,128)(2,1)S(1)}, bf16[512,512]{1,0:T(8,128)(2,1)}, u32[]{:S(2)}) copy-start(bf16[512,512]{1,0:T(8,128)(2,1)} %wo_ref.1) | copy-start | bytes 1572868
Sparse Core Ops, SparseCore 0:
  8.9 19.4 all-gather.1

commit v2 on v0

v2 whole, which is shorter than its diff:
```python
import functools

import jax
import jax.numpy as jnp
from jax import lax
from jax.experimental import pallas as pl
from jax.experimental.pallas import tpu as pltpu
from jax.sharding import PartitionSpec as P

LANES = 128
F32, BF16 = jnp.float32, jnp.bfloat16
VMEM = pl.BlockSpec(memory_space=pltpu.VMEM)


def call(kernel, name, outs, scratch, operands, flops=0, exps=0):
    moved = sum(a.size * a.dtype.itemsize for a in operands) + sum(a.size * a.dtype.itemsize for a in outs)
    return pl.pallas_call(
        kernel,
        out_shape=tuple(outs),
        in_specs=[VMEM] * len(operands),
        out_specs=(VMEM,) * len(outs),
        scratch_shapes=scratch,
        compiler_params=pltpu.CompilerParams(vmem_limit_bytes=24 * 1024 * 1024),
        cost_estimate=pl.CostEstimate(flops=flops, bytes_accessed=moved, transcendentals=exps),
        name=name,
    )(*operands)


def swaps(axis):
    n = lax.axis_size(axis)
    rounds = []
    for first in range(2 if n > 2 else 1):
        to = list(range(n))
        for i in range(first, n - 1, 2):
            to[i], to[i + 1] = i + 1, i
        rounds.append(list(enumerate(to)))
    return rounds


def position(axis):
    i, n = lax.axis_index(axis), lax.axis_size(axis)
    return lax.rem(i, 2) == 1, i > 0, i < n - 1


def received(axis, arrived):
    odd, lower, upper = position(axis)
    even_low, even_high = arrived[-1], arrived[0]
    low = jnp.where(odd, arrived[0], even_low)
    high = jnp.where(odd, arrived[-1], even_high)
    zero = jnp.zeros_like(low)
    return jnp.where(lower, low, zero), jnp.where(upper, high, zero)


def gate_kernel(x_ref, w_ref, gate_ref):
    v = jnp.dot(x_ref[...], w_ref[...], preferred_element_type=F32)
    gate_ref[...] = v / (1.0 + jnp.exp(-v))


def mix_kernel(frames, rows, cols, own_ref, partner_ref, taps_ref, skip_ref, fields_ref, lines_ref, *refs):
    *sides, table, held = refs
    lags, chans = taps_ref.shape
    block = rows * cols * frames
    pad = 2 * frames
    shift = jnp.where(lax.rem(lax.axis_index("tm"), 2) == 1, frames, -frames)
    odd, _, _ = position("width")
    taps = taps_ref[...].astype(F32)
    table[0:pad] = jnp.zeros((pad, cols, chans), F32)
    for lag in range(lags):
        tap = taps[lag : lag + 1] + (skip_ref[...] if lag == 0 else 0.0)
        table[pad + lag] = jnp.broadcast_to(tap, (cols, chans))
    sites = rows * cols
    for lane in range(0, chans, LANES):
        span = slice(lane, lane + LANES)
        for d in range(fields_ref.shape[0] // block):
            totals = [jnp.zeros((rows, cols, LANES), F32)] * frames
            for source, offset in ((own_ref, 0), (partner_ref, shift)):
                for s in range(frames):
                    x = source[s * sites : (s + 1) * sites, span].astype(F32).reshape(rows, cols, LANES)
                    for t in range(frames):
                        if source is own_ref and d == 0 and t < s:
                            continue
                        totals[t] = totals[t] + table[pad + 2 * d * frames + offset + t - s, :, span] * x
            for t in range(frames):
                held[t * sites : (t + 1) * sites, :] = totals[t].reshape(sites, LANES)
            fields_ref[d * block : (d + 1) * block, span] = held[...]
            first = held[pl.ds(0, frames * rows, stride=cols), :].astype(BF16)
            last = held[pl.ds(cols - 1, frames * rows, stride=cols), :].astype(BF16)
            out = slice(d * frames * rows, (d + 1) * frames * rows)
            sides[0][out, span] = jnp.where(odd, first, last)
            if len(sides) > 1:
                sides[1][out, span] = jnp.where(odd, last, first)
            for k, r in enumerate((0, rows - 1)):
                line = jnp.concatenate([t[r] for t in totals], axis=0).astype(BF16)
                at = (2 * d + k) * frames * cols
                lines_ref[at : at + frames * cols, span] = line


def border_kernel(frames, rows, cols, rounds_w, lines_ref, *refs):
    sides, outs = refs[:rounds_w], refs[rounds_w:]
    odd, _, _ = position("height")
    low, high = received("width", [s[...].astype(F32) for s in sides])
    size = outs[0].shape[0] * frames * rows // low.shape[0]
    fill = jnp.zeros((size - frames * cols - 2 * frames, low.shape[1]), F32)
    for d in range(low.shape[0] // (frames * rows)):
        ends = []
        for k, r in enumerate((0, rows - 1)):
            at = (2 * d + k) * frames * cols
            line = lines_ref[at : at + frames * cols].astype(F32)
            base = d * frames * rows + r
            lefts = [low[base + t * rows : base + t * rows + 1] for t in range(frames)]
            rights = [high[base + t * rows : base + t * rows + 1] for t in range(frames)]
            ends.append(jnp.concatenate([line] + lefts + rights + [fill], axis=0).astype(BF16))
        out = slice(d * size, (d + 1) * size)
        outs[0][out] = jnp.where(odd, ends[0], ends[1])
        if len(outs) > 1:
            outs[1][out] = jnp.where(odd, ends[1], ends[0])


def filter_kernel(frames, rows, cols, rounds_w, fields_ref, taps_ref, *refs):
    sides, ends, (mine_ref, *others) = refs[:rounds_w], refs[rounds_w : -2], refs[-2:]
    chans = fields_ref.shape[1]
    sites = rows * cols
    block = frames * sites
    count = fields_ref.shape[0] // block
    size = ends[0].shape[0] // count
    place = lax.broadcasted_iota(jnp.int32, (cols, LANES), 0)
    for lane in range(0, chans, LANES):
        span = slice(lane, lane + LANES)
        taps = [[taps_ref[3 * a + b : 3 * a + b + 1, span] for b in range(3)] for a in range(3)]
        low, high = received("width", [s[:, span].astype(F32) for s in sides])
        above, below = received("height", [e[:, span].astype(F32) for e in ends])
        for d in range(count):
            for t in range(frames):
                at = d * block + t * sites
                tile = fields_ref[at : at + sites, span]
                lines = [tile[r * cols : (r + 1) * cols] for r in range(rows)]
                side = (d * frames + t) * rows
                lefts = [low[side + r : side + r + 1] for r in range(rows)]
                rights = [high[side + r : side + r + 1] for r in range(rows)]
                for end, where in ((above, 0), (below, rows + 1)):
                    row = d * size + t * cols
                    corner = d * size + frames * cols + t
                    lines.insert(where, end[row : row + cols])
                    lefts.insert(where, end[corner : corner + 1])
                    rights.insert(where, end[corner + frames : corner + frames + 1])
                totals = [None] * rows
                for r in range(rows + 2):
                    before = jnp.where(place == 0, lefts[r], pltpu.roll(lines[r], 1, 0))
                    after = jnp.where(place == cols - 1, rights[r], pltpu.roll(lines[r], cols - 1, 0))
                    for a in range(3):
                        to = r - a
                        if 0 <= to < rows:
                            term = before * taps[a][0] + lines[r] * taps[a][1] + after * taps[a][2]
                            totals[to] = term if totals[to] is None else totals[to] + term
                total = jnp.concatenate(totals, axis=0)
                if d == 0:
                    mine_ref[at : at + sites, span] = total
                else:
                    others[0][at - block : at - block + sites, span] = total.astype(BF16)


def finish_kernel(mine_ref, gate_ref, wv_ref, wo_ref, *refs):
    *arrived, out_ref = refs
    chip = lax.div(lax.axis_index("tm"), 2)
    mixed = mine_ref[...]
    for d, ref in enumerate(arrived, 1):
        mixed = mixed + jnp.where(chip >= d, ref[...].astype(F32), 0.0)
    value = jnp.dot(mixed.astype(BF16), wv_ref[...], preferred_element_type=F32)
    hidden = (value * gate_ref[...]).astype(BF16)
    out_ref[...] = jnp.dot(hidden, wo_ref[...], preferred_element_type=F32).astype(BF16)


def body(latents, spatial_taps, kernel_taps, skip_gain, gate_weight, value_weight, out_weight):
    frames, rows, cols, chans = latents.shape
    lags = kernel_taps.shape[0]
    n_t = lax.axis_size("tm")
    chips = n_t // 2
    sites = rows * cols
    block = frames * sites
    shape = jax.ShapeDtypeStruct
    x = latents.reshape(block, chans)

    partner = lax.ppermute(x, "tm", [(i, i ^ 1) for i in range(n_t)])
    (gate,) = call(gate_kernel, "gate", [shape((block, chans), F32)], [], [x, gate_weight], 2 * block * chans * chans, x.size)

    w_rounds, h_rounds = swaps("width"), swaps("height")
    side = shape((chips * frames * rows, chans), BF16)
    fields, lines, *sides = call(
        functools.partial(mix_kernel, frames, rows, cols),
        "mix",
        [shape((chips * block, chans), F32), shape((chips * 2 * frames * cols, chans), BF16)] + [side] * len(w_rounds),
        [pltpu.VMEM((lags + 2 * frames, cols, chans), F32), pltpu.VMEM((block, LANES), F32)],
        [x, partner, kernel_taps, skip_gain.reshape(1, chans)],
        4 * chips * frames * x.size,
    )
    sides = [lax.ppermute(s, "width", pairs) for s, pairs in zip(sides, w_rounds)]

    size = -(-(frames * cols + 2 * frames) // 16) * 16
    ends = call(
        functools.partial(border_kernel, frames, rows, cols, len(w_rounds)),
        "border",
        [shape((chips * size, chans), BF16)] * len(h_rounds),
        [],
        [lines] + sides,
    )
    ends = [lax.ppermute(e, "height", pairs) for e, pairs in zip(ends, h_rounds)]

    mine, others = call(
        functools.partial(filter_kernel, frames, rows, cols, len(w_rounds)),
        "filter",
        [shape((block, chans), F32), shape(((chips - 1) * block, chans), BF16)],
        [],
        [fields, spatial_taps.reshape(9, chans)] + sides + ends,
        18 * chips * x.size,
    )
    arrived = [
        lax.ppermute(others[(d - 1) * block : d * block], "tm", [(i, (i + 2 * d) % n_t) for i in range(n_t)])
        for d in range(1, chips)
    ]
    (out,) = call(
        finish_kernel,
        "finish",
        [shape((block, chans), BF16)],
        [],
        [mine, gate, value_weight, out_weight] + arrived,
        4 * block * chans * chans,
    )
    return out.reshape(latents.shape)


def solution(mesh):
    in_specs = (P("tm", "height", "width", None), P(), P(), P(), P(), P(), P())
    out_specs = P("tm", "height", "width", None)
    return jax.shard_map(body, mesh=mesh, in_specs=in_specs, out_specs=out_specs, check_vma=False)
```

time: 70.6 us -> 25.5 us (0.36)
  the two profiles are of different devices: /device:TPU:0 before, /device:TPU:22 now
where the time goes in v2:
time: 25.5 us; the launch traced here: 25.3 us
  waiting for transfers between devices  15.5 us (61%)
  starting transfers between devices  4.72 us (19%)
  Pallas kernels  3.29 us (13%)
  local copies, waits for them, and re-layouts  1.75 us (7%)
    ppermute x1, waiting for transfers between devices, body(): lax.ppermute(others[(d - 1) * block:d * block], 'tm', [(i, (i + 2 * d) %...  5.47 us
    ppermute x2, waiting for transfers between devices, body(): lax.ppermute(s, 'width', pairs)  4.23 us
    ppermute x1, waiting for transfers between devices, body(): lax.ppermute(e, 'height', pairs)  4.02 us
    ppermute x2, starting transfers between devices, body(): lax.ppermute(s, 'width', pairs)  3.55 us
    pallas_call x5, Pallas kernels, call(): pl.pallas_call(kernel, out_shape=tuple(outs), in_specs=[VMEM] * len(opera...  3.29 us
    ppermute x1, waiting for transfers between devices, body(): partner = lax.ppermute(x, 'tm', [(i, i ^ 1) for i in range(n_t)])  1.74 us
    unnamed x16, local copies, waits for them, and re-layouts  1.74 us
    ppermute x1, starting transfers between devices, body(): lax.ppermute(e, 'height', pairs)  0.6 us
  transfers between devices with their start and end apart: 5, of which 5 were waited for; matrix products, arithmetic and copies ran while one was open for 0% of the time, Pallas kernels for 1%

profile of v2, /device:TPU:22, one launch (start us, length us, event | category | flops | bytes accessed | tf_op | source)
XLA Modules:
  0.0 25.3 jit_solution(16103897908634982867)
XLA Ops:
  0.0 0.0 copy-start.6
  0.0 0.0 collective-permute-start
  0.0 1.7 %collective-permute-done.partner_ref = bf16[256,512]{1,0:T(8,128)(2,1)S(1)} collective-permute-done((bf16[256,512]{1,0:T(8,128)(2,1)}, bf16[256,512]{1,0:T(8,128)(2,1)S(1)}, u32[]{:S(2)}, u32[]{:S(2)}) %collective-permute-start) | collective-permute-done | bytes 262176 | tf_op jit(solution)/shard_map/ppermute | solution.py:183
  1.7 0.0 copy-done.6
  1.8 0.0 copy-start
  1.8 0.9 %copy-done = bf16[4,8,8,512]{3,2,1,0:T(8,128)(2,1)S(1)} copy-done((bf16[4,8,8,512]{3,2,1,0:T(8,128)(2,1)S(1)}, bf16[4,8,8,512]{3,2,1,0:T(8,128)(2,1)}, u32[]{:S(2)}) %copy-start) | copy-done | bytes 262168
  2.7 0.0 copy-start.5
  2.7 0.7 %copy-done.5 = bf16[16,512]{1,0:T(8,128)(2,1)S(1)} copy-done((bf16[16,512]{1,0:T(8,128)(2,1)S(1)}, bf16[16,512]{1,0:T(8,128)(2,1)}, u32[]{:S(2)}) %copy-start.5) | copy-done | bytes 16408
  3.4 0.7 %mix.1 = (f32[512,512]{1,0:T(8,128)S(1)}, bf16[128,512]{1,0:T(8,128)(2,1)S(1)}, bf16[64,512]{1,0:T(8,128)(2,1)S(1)}, bf16[64,512]{1,0:T(8,128)(2,1)S(1)}) custom-call(bf16[256,512]{1,0:T(8,128)(2,1)S(1)} %bitcast.4, bf16[256,512]{1,0:T(8,128)(2,1)S(1)} %collective-permute-done.partner_ref, bf16[16,512]{1,0:T(8,128)(2,1)S(1)} %copy-done.5, f32[1,512]{1,0:T(1,128)S(1)} %bitcast.6), custom_call_target="tpu_custom_call" | custom-call | flops 4194304 | bytes 1853440 | tf_op jit(solution)/shard_map/mix/pallas_call | solution.py:17
  4.1 1.6 %collective-permute-start.1 = (bf16[64,512]{1,0:T(8,128)(2,1)S(1)}, bf16[64,512]{1,0:T(8,128)(2,1)S(1)}, u32[]{:S(2)}, u32[]{:S(2)}) collective-permute-start(bf16[64,512]{1,0:T(8,128)(2,1)S(1)} %get-tuple-element.12), channel_id=1, source_target_pairs={{0,1},{1,0},{2,3},{3,2},{4,5},{5,4},{6,7},{7,6},{8,9},{9,8},{10,11... | collective-permute-start | bytes 196616 | tf_op jit(solution)/shard_map/ppermute | solution.py:196
  5.8 1.9 %collective-permute-start.2 = (bf16[64,512]{1,0:T(8,128)(2,1)S(1)}, bf16[64,512]{1,0:T(8,128)(2,1)S(1)}, u32[]{:S(2)}, u32[]{:S(2)}) collective-permute-start(bf16[64,512]{1,0:T(8,128)(2,1)S(1)} %get-tuple-element.13), channel_id=1, source_target_pairs={{0,0},{1,2},{2,1},{3,3},{4,4},{5,6},{6,5},{7,7},{8,8},{9,10},{10,9... | collective-permute-start | bytes 196616 | tf_op jit(solution)/shard_map/ppermute | solution.py:196
  7.7 0.8 %collective-permute-done.1.refs_0_ = bf16[64,512]{1,0:T(8,128)(2,1)S(1)} collective-permute-done((bf16[64,512]{1,0:T(8,128)(2,1)S(1)}, bf16[64,512]{1,0:T(8,128)(2,1)S(1)}, u32[]{:S(2)}, u32[]{:S(2)}) %collective-permute-start.1) | collective-permute-done | bytes 65568 | tf_op jit(solution)/shard_map/ppermute | solution.py:196
  8.5 3.5 %collective-permute-done.2.refs_1_ = bf16[64,512]{1,0:T(8,128)(2,1)S(1)} collective-permute-done((bf16[64,512]{1,0:T(8,128)(2,1)S(1)}, bf16[64,512]{1,0:T(8,128)(2,1)S(1)}, u32[]{:S(2)}, u32[]{:S(2)}) %collective-permute-start.2) | collective-permute-done | bytes 65568 | tf_op jit(solution)/shard_map/ppermute | solution.py:196
  11.9 0.0 copy-start.7
  11.9 0.1 border.1
  12.0 0.6 %collective-permute-start.3 = (bf16[96,512]{1,0:T(8,128)(2,1)S(1)}, bf16[96,512]{1,0:T(8,128)(2,1)S(1)}, u32[]{:S(2)}, u32[]{:S(2)}) collective-permute-start(bf16[96,512]{1,0:T(8,128)(2,1)S(1)} %border.1), channel_id=1, source_target_pairs={{0,4},{4,0},{1,5},{5,1},{2,6},{6,2},{3,7},{7,3},{8,12},{12,8},{9,1... | collective-permute-start | bytes 294920 | tf_op jit(solution)/shard_map/ppermute | solution.py:206
  12.6 0.0 copy-done.7
  12.7 4.0 %collective-permute-done.3.refs_2_ = bf16[96,512]{1,0:T(8,128)(2,1)S(1)} collective-permute-done((bf16[96,512]{1,0:T(8,128)(2,1)S(1)}, bf16[96,512]{1,0:T(8,128)(2,1)S(1)}, u32[]{:S(2)}, u32[]{:S(2)}) %collective-permute-start.3) | collective-permute-done | bytes 98336 | tf_op jit(solution)/shard_map/ppermute | solution.py:206
  16.7 0.0 copy-start.1
  16.7 0.0 copy-start.4
  16.7 0.9 %filter.1 = (f32[256,512]{1,0:T(8,128)S(1)}, bf16[256,512]{1,0:T(8,128)(2,1)S(1)}) custom-call(f32[512,512]{1,0:T(8,128)S(1)} %get-tuple-element.11.fields_ref, f32[9,512]{1,0:T(8,128)S(1)} %reshape.14.taps_ref, bf16[64,512]{1,0:T(8,128)(2,1)S(1)} %collective-permute-done.1.refs_0_, bf16[64,512]{1,0:T(8,128)(2,1)S(1)} %collective-permute-done.2.refs_1_, ...), custom_call_target="tpu_custom_call" | custom-call | flops 4718592 | bytes 2082816 | tf_op jit(solution)/shard_map/filter/pallas_call | solution.py:17
  17.6 0.0 copy-start.2
  17.6 0.0 copy-start.3
  17.6 0.6 %collective-permute-start.4 = (bf16[256,512]{1,0:T(8,128)(2,1)S(1)}, bf16[256,512]{1,0:T(8,128)(2,1)S(1)}, u32[]{:S(2)}, u32[]{:S(2)}) collective-permute-start(bf16[256,512]{1,0:T(8,128)(2,1)S(1)} %get-tuple-element.16), channel_id=1, source_target_pairs={{0,16},{8,24},{16,0},{24,8},{1,17},{9,25},{17,1},{25,9},{2,18},{10... | collective-permute-start | bytes 786440 | tf_op jit(solution)/shard_map/ppermute | solution.py:217
  18.2 0.0 copy-done.1
  18.2 0.0 copy-done.4
  18.2 0.4 %gate.1.gate_ref = f32[256,512]{1,0:T(8,128)S(1)} custom-call(bf16[256,512]{1,0:T(8,128)(2,1)S(1)} %bitcast.5, bf16[512,512]{1,0:T(8,128)(2,1)S(1)} %copy-done.4), custom_call_target="tpu_custom_call" | custom-call | flops 134217728 | bytes 1310720 | tf_op jit(solution)/shard_map/gate/pallas_call | solution.py:17
  18.6 5.5 %collective-permute-done.4.refs_0_ = bf16[256,512]{1,0:T(8,128)(2,1)S(1)} collective-permute-done((bf16[256,512]{1,0:T(8,128)(2,1)S(1)}, bf16[256,512]{1,0:T(8,128)(2,1)S(1)}, u32[]{:S(2)}, u32[]{:S(2)}) %collective-permute-start.4) | collective-permute-done | bytes 262176 | tf_op jit(solution)/shard_map/ppermute | solution.py:217
  24.1 0.0 copy-done.2
  24.1 0.0 copy-done.3
  24.1 1.2 %finish.1 = bf16[256,512]{1,0:T(8,128)(2,1)} custom-call(f32[256,512]{1,0:T(8,128)S(1)} %get-tuple-element.15.mine_ref, f32[256,512]{1,0:T(8,128)S(1)} %gate.1.gate_ref, bf16[512,512]{1,0:T(8,128)(2,1)S(1)} %copy-done.2, bf16[512,512]{1,0:T(8,128)(2,1)S(1)} %copy-done.3, bf16[256,512]{1,0:T(8,128)(2,1)S(1)} %collective-permute-done.4.refs_0_), custom_call_target="tpu_custom_call" | custom-call | flops 268435456 | bytes 2621440 | tf_op jit(solution)/shard_map/finish/pallas_call | solution.py:17
  (1 shorter events, 0.0 us)
Async XLA Ops:
  0.0 1.8 %copy-start.6 = (f32[512]{0:T(512)S(1)}, f32[512]{0:T(512)}, u32[]{:S(2)}) copy-start(f32[512]{0:T(512)} %param.10) | copy-start | bytes 6148
  0.0 1.7 %collective-permute-start = (bf16[256,512]{1,0:T(8,128)(2,1)}, bf16[256,512]{1,0:T(8,128)(2,1)S(1)}, u32[]{:S(2)}, u32[]{:S(2)}) collective-permute-start(bf16[256,512]{1,0:T(8,128)(2,1)} %bitcast.3), channel_id=1, source_target_pairs={{0,8},{8,0},{16,24},{24,16},{1,9},{9,1},{17,25},{25,17},{2,10},{10... | collective-permute-start | bytes 786440 | tf_op jit(solution)/shard_map/ppermute | solution.py:183
  1.8 1.0 %copy-start = (bf16[4,8,8,512]{3,2,1,0:T(8,128)(2,1)S(1)}, bf16[4,8,8,512]{3,2,1,0:T(8,128)(2,1)}, u32[]{:S(2)}) copy-start(bf16[4,8,8,512]{3,2,1,0:T(8,128)(2,1)} %param.7) | copy-start | bytes 786436
  2.7 0.7 %copy-start.5 = (bf16[16,512]{1,0:T(8,128)(2,1)S(1)}, bf16[16,512]{1,0:T(8,128)(2,1)}, u32[]{:S(2)}) copy-start(bf16[16,512]{1,0:T(8,128)(2,1)} %taps_ref.1) | copy-start | bytes 49156
  4.1 4.3 %collective-permute-start.1 = (bf16[64,512]{1,0:T(8,128)(2,1)S(1)}, bf16[64,512]{1,0:T(8,128)(2,1)S(1)}, u32[]{:S(2)}, u32[]{:S(2)}) collective-permute-start(bf16[64,512]{1,0:T(8,128)(2,1)S(1)} %get-tuple-element.12), channel_id=1, source_target_pairs={{0,1},{1,0},{2,3},{3,2},{4,5},{5,4},{6,7},{7,6},{8,9},{9,8},{10,11... | collective-permute-start | bytes 196616 | tf_op jit(solution)/shard_map/ppermute | solution.py:196
  5.8 6.1 %collective-permute-start.2 = (bf16[64,512]{1,0:T(8,128)(2,1)S(1)}, bf16[64,512]{1,0:T(8,128)(2,1)S(1)}, u32[]{:S(2)}, u32[]{:S(2)}) collective-permute-start(bf16[64,512]{1,0:T(8,128)(2,1)S(1)} %get-tuple-element.13), channel_id=1, source_target_pairs={{0,0},{1,2},{2,1},{3,3},{4,4},{5,6},{6,5},{7,7},{8,8},{9,10},{10,9... | collective-permute-start | bytes 196616 | tf_op jit(solution)/shard_map/ppermute | solution.py:196
  11.9 0.7 %copy-start.7 = (f32[3,3,512]{2,1,0:T(4,128)S(1)}, f32[3,3,512]{2,1,0:T(4,128)}, u32[]{:S(2)}) copy-start(f32[3,3,512]{2,1,0:T(4,128)} %param.8) | copy-start | bytes 55300
  12.0 4.7 %collective-permute-start.3 = (bf16[96,512]{1,0:T(8,128)(2,1)S(1)}, bf16[96,512]{1,0:T(8,128)(2,1)S(1)}, u32[]{:S(2)}, u32[]{:S(2)}) collective-permute-start(bf16[96,512]{1,0:T(8,128)(2,1)S(1)} %border.1), channel_id=1, source_target_pairs={{0,4},{4,0},{1,5},{5,1},{2,6},{6,2},{3,7},{7,3},{8,12},{12,8},{9,1... | collective-permute-start | bytes 294920 | tf_op jit(solution)/shard_map/ppermute | solution.py:206
  16.7 1.5 %copy-start.1 = (bf16[4,8,8,512]{3,2,1,0:T(8,128)(2,1)S(1)}, bf16[4,8,8,512]{3,2,1,0:T(8,128)(2,1)}, u32[]{:S(2)}) copy-start(bf16[4,8,8,512]{3,2,1,0:T(8,128)(2,1)} %param.7) | copy-start | bytes 786436
  16.7 1.5 %copy-start.4 = (bf16[512,512]{1,0:T(8,128)(2,1)S(1)}, bf16[512,512]{1,0:T(8,128)(2,1)}, u32[]{:S(2)}) copy-start(bf16[512,512]{1,0:T(8,128)(2,1)} %w_ref.1) | copy-start | bytes 1572868
  17.6 6.5 %copy-start.2 = (bf16[512,512]{1,0:T(8,128)(2,1)S(1)}, bf16[512,512]{1,0:T(8,128)(2,1)}, u32[]{:S(2)}) copy-start(bf16[512,512]{1,0:T(8,128)(2,1)} %wv_ref.1) | copy-start | bytes 1572868
  17.6 6.5 %copy-start.3 = (bf16[512,512]{1,0:T(8,128)(2,1)S(1)}, bf16[512,512]{1,0:T(8,128)(2,1)}, u32[]{:S(2)}) copy-start(bf16[512,512]{1,0:T(8,128)(2,1)} %wo_ref.1) | copy-start | bytes 1572868
  17.6 6.4 %collective-permute-start.4 = (bf16[256,512]{1,0:T(8,128)(2,1)S(1)}, bf16[256,512]{1,0:T(8,128)(2,1)S(1)}, u32[]{:S(2)}, u32[]{:S(2)}) collective-permute-start(bf16[256,512]{1,0:T(8,128)(2,1)S(1)} %get-tuple-element.16), channel_id=1, source_target_pairs={{0,16},{8,24},{16,0},{24,8},{1,17},{9,25},{17,1},{25,9},{2,18},{10... | collective-permute-start | bytes 786440 | tf_op jit(solution)/shard_map/ppermute | solution.py:217

commit v3 on v0

v3 whole, which is shorter than its diff:
```python
import functools

import jax
import jax.numpy as jnp
from jax import lax
from jax.experimental import pallas as pl
from jax.experimental.pallas import tpu as pltpu
from jax.sharding import PartitionSpec as P

LANES = 128
F32, BF16 = jnp.float32, jnp.bfloat16
VMEM = pl.BlockSpec(memory_space=pltpu.VMEM)
HBM = pl.BlockSpec(memory_space=pltpu.HBM)


def call(kernel, name, outs, scratch, operands, flops=0, exps=0, far=0):
    operands = [pltpu.with_memory_space_constraint(a, pltpu.HBM) for a in operands[:far]] + list(operands[far:])
    moved = sum(a.size * a.dtype.itemsize for a in operands) + sum(a.size * a.dtype.itemsize for a in outs)
    return pl.pallas_call(
        kernel,
        out_shape=tuple(outs),
        in_specs=[HBM] * far + [VMEM] * (len(operands) - far),
        out_specs=(VMEM,) * len(outs),
        scratch_shapes=scratch,
        compiler_params=pltpu.CompilerParams(vmem_limit_bytes=24 * 1024 * 1024),
        cost_estimate=pl.CostEstimate(flops=flops, bytes_accessed=moved, transcendentals=exps),
        name=name,
    )(*operands)


def swaps(axis):
    n = lax.axis_size(axis)
    rounds = []
    for first in range(2 if n > 2 else 1):
        to = list(range(n))
        for i in range(first, n - 1, 2):
            to[i], to[i + 1] = i + 1, i
        rounds.append(list(enumerate(to)))
    return rounds


def position(axis):
    i, n = lax.axis_index(axis), lax.axis_size(axis)
    return lax.rem(i, 2) == 1, i > 0, i < n - 1


def received(axis, arrived):
    odd, lower, upper = position(axis)
    even_low, even_high = arrived[-1], arrived[0]
    low = jnp.where(odd, arrived[0], even_low)
    high = jnp.where(odd, arrived[-1], even_high)
    zero = jnp.zeros_like(low)
    return jnp.where(lower, low, zero), jnp.where(upper, high, zero)


def early_kernel(frames, rows, cols, *refs):
    far, (gate_ref, fields_ref, table_ref), near, arrived = refs[:4], refs[4:7], refs[7:11], refs[11]
    copies = [pltpu.make_async_copy(a, b, arrived.at[i]) for i, (a, b) in enumerate(zip(far, near))]
    for copy in copies:
        copy.start()
    taps_ref, skip_ref, x_ref, w_ref = near
    lags, chans = taps_ref.shape
    copies[0].wait()
    copies[1].wait()
    pad = 2 * frames
    taps = taps_ref[...].astype(F32)
    table_ref[0:pad] = jnp.zeros((pad, cols, chans), F32)
    for lag in range(lags):
        tap = taps[lag : lag + 1] + (skip_ref[...] if lag == 0 else 0.0)
        table_ref[pad + lag] = jnp.broadcast_to(tap, (cols, chans))
    sites = rows * cols
    block = frames * sites
    copies[2].wait()
    for lane in range(0, chans, LANES):
        span = slice(lane, lane + LANES)
        for d in range(fields_ref.shape[0] // block):
            totals = [None] * frames
            for s in range(frames):
                x = x_ref[s * sites : (s + 1) * sites, span].astype(F32).reshape(rows, cols, LANES)
                for t in range(s if d == 0 else 0, frames):
                    term = table_ref[pad + 2 * d * frames + t - s, :, span] * x
                    totals[t] = term if totals[t] is None else totals[t] + term
            for t in range(frames):
                at = d * block + t * sites
                fields_ref[at : at + sites, span] = totals[t].reshape(sites, LANES)
    copies[3].wait()
    v = jnp.dot(x_ref[...], w_ref[...], preferred_element_type=F32)
    gate_ref[...] = v / (1.0 + jnp.exp(-v))


def mix_kernel(frames, rows, cols, rounds_w, rounds_h, partner_ref, fields_ref, table_ref, mine_ref, *refs):
    *outs, held = refs
    sites = rows * cols
    block = frames * sites
    pad = 2 * frames
    shift = jnp.where(lax.rem(lax.axis_index("tm"), 2) == 1, frames, -frames)
    odd_w, odd_h = position("width")[0], position("height")[0]
    for lane in range(0, mine_ref.shape[1], LANES):
        span = slice(lane, lane + LANES)
        outs_left = list(outs)
        for d in range(fields_ref.shape[0] // block):
            totals = []
            for t in range(frames):
                at = d * block + t * sites
                totals.append(fields_ref[at : at + sites, span].reshape(rows, cols, LANES))
            for s in range(frames):
                x = partner_ref[s * sites : (s + 1) * sites, span].astype(F32).reshape(rows, cols, LANES)
                for t in range(frames):
                    totals[t] = totals[t] + table_ref[pad + 2 * d * frames + shift + t - s, :, span] * x
            for t in range(frames):
                held[t * sites : (t + 1) * sites, :] = totals[t].reshape(sites, LANES)
            first = held[pl.ds(0, frames * rows, stride=cols), :].astype(BF16)
            last = held[pl.ds(cols - 1, frames * rows, stride=cols), :].astype(BF16)
            for k in range(rounds_w):
                outs_left.pop(0)[:, span] = jnp.where(odd_w, last, first) if k else jnp.where(odd_w, first, last)
            if d == 0:
                mine_ref[:, span] = held[...]
                continue
            top = jnp.concatenate([t[0] for t in totals], axis=0).astype(BF16)
            bottom = jnp.concatenate([t[rows - 1] for t in totals], axis=0).astype(BF16)
            lines_ref = outs_left.pop(0)
            for k in range(rounds_h):
                line = jnp.where(odd_h, bottom, top) if k else jnp.where(odd_h, top, bottom)
                lines_ref[k * frames * cols : (k + 1) * frames * cols, span] = line
            outs_left.pop(0)[:, span] = held[...]


def round_kernel(x_ref, out_ref):
    out_ref[...] = x_ref[...].astype(BF16)


def later(d, value):
    return jnp.where(lax.div(lax.axis_index("tm"), 2) >= d, value, jnp.zeros_like(value))


def border_kernel(frames, rows, cols, rounds_w, chips, mine_ref, *refs):
    ins, (low_ref, high_ref, *outs) = refs[: chips * rounds_w + chips - 1], refs[chips * rounds_w + chips - 1 :]
    sites = rows * cols
    odd, _, _ = position("height")
    low = high = None
    lines = []
    for d in range(chips):
        sides, ins = ins[:rounds_w], ins[rounds_w:]
        arrived = received("width", [s[...].astype(F32) for s in sides])
        if d == 0:
            low, high = arrived
        else:
            low, high = low + later(d, arrived[0]), high + later(d, arrived[1])
            lines.append(ins[0])
            ins = ins[1:]
    low_ref[...] = low
    high_ref[...] = high
    size = frames * cols
    fill = jnp.zeros((outs[0].shape[0] - size - 2 * frames, low.shape[1]), F32)
    for k, out in enumerate(outs):
        ends = []
        for r in (0, rows - 1):
            line = [mine_ref[t * sites + r * cols : t * sites + (r + 1) * cols] for t in range(frames)]
            lefts = [low[t * rows + r : t * rows + r + 1] for t in range(frames)]
            rights = [high[t * rows + r : t * rows + r + 1] for t in range(frames)]
            ends.append((jnp.concatenate(line, axis=0), jnp.concatenate(lefts + rights + [fill], axis=0)))
        pick = lambda j: jnp.where(odd, ends[1][j], ends[0][j]) if k else jnp.where(odd, ends[0][j], ends[1][j])
        line = pick(0)
        for d, ref in enumerate(lines, 1):
            line = line + later(d, ref[k * size : (k + 1) * size].astype(F32))
        out[...] = jnp.concatenate([line, pick(1)], axis=0).astype(BF16)


def finish_kernel(frames, rows, cols, rounds_h, mine_ref, low_ref, high_ref, taps_ref, gate_ref, wv_ref, wo_ref, *refs):
    ends, wholes, (out_ref, mixed) = refs[:rounds_h], refs[rounds_h:-2], refs[-2:]
    chans = mine_ref.shape[1]
    sites = rows * cols
    place = lax.broadcasted_iota(jnp.int32, (cols, LANES), 0)
    corner = frames * cols
    for lane in range(0, chans, LANES):
        span = slice(lane, lane + LANES)
        taps = [[taps_ref[3 * a + b : 3 * a + b + 1, span] for b in range(3)] for a in range(3)]
        low, high = low_ref[:, span], high_ref[:, span]
        above, below = received("height", [e[:, span].astype(F32) for e in ends])
        for t in range(frames):
            at = t * sites
            tile = mine_ref[at : at + sites, span]
            for d, ref in enumerate(wholes, 1):
                tile = tile + later(d, ref[at : at + sites, span].astype(F32))
            lines = [tile[r * cols : (r + 1) * cols] for r in range(rows)]
            lefts = [low[t * rows + r : t * rows + r + 1] for r in range(rows)]
            rights = [high[t * rows + r : t * rows + r + 1] for r in range(rows)]
            for end, where in ((above, 0), (below, rows + 1)):
                lines.insert(where, end[t * cols : (t + 1) * cols])
                lefts.insert(where, end[corner + t : corner + t + 1])
                rights.insert(where, end[corner + frames + t : corner + frames + t + 1])
            totals = [None] * rows
            for r in range(rows + 2):
                before = jnp.where(place == 0, lefts[r], pltpu.roll(lines[r], 1, 0))
                after = jnp.where(place == cols - 1, rights[r], pltpu.roll(lines[r], cols - 1, 0))
                for a in range(3):
                    to = r - a
                    if 0 <= to < rows:
                        term = before * taps[a][0] + lines[r] * taps[a][1] + after * taps[a][2]
                        totals[to] = term if totals[to] is None else totals[to] + term
            mixed[at : at + sites, span] = jnp.concatenate(totals, axis=0).astype(BF16)
    value = jnp.dot(mixed[...], wv_ref[...], preferred_element_type=F32)
    hidden = (value * gate_ref[...]).astype(BF16)
    out_ref[...] = jnp.dot(hidden, wo_ref[...], preferred_element_type=F32).astype(BF16)


def body(latents, spatial_taps, kernel_taps, skip_gain, gate_weight, value_weight, out_weight):
    frames, rows, cols, chans = latents.shape
    lags = kernel_taps.shape[0]
    n_t, n_w = lax.axis_size("tm"), lax.axis_size("width")
    chips = n_t // 2
    block = frames * rows * cols
    shape = jax.ShapeDtypeStruct
    x = latents.reshape(block, chans)

    partner = lax.ppermute(x, "tm", [(i, i ^ 1) for i in range(n_t)])
    inputs = [kernel_taps, skip_gain.reshape(1, chans), x, gate_weight]
    gate, fields, table = call(
        functools.partial(early_kernel, frames, rows, cols),
        "early",
        [
            shape((block, chans), F32),
            shape((chips * block, chans), F32),
            shape((lags + 2 * frames, cols, chans), F32),
        ],
        [pltpu.VMEM(a.shape, a.dtype) for a in inputs] + [pltpu.SemaphoreType.DMA((len(inputs),))],
        inputs,
        2 * block * chans * chans,
        x.size,
        far=len(inputs),
    )

    w_rounds, h_rounds = swaps("width"), swaps("height")
    sides = [shape((frames * rows, chans), BF16)] * len(w_rounds)
    lines = shape((len(h_rounds) * frames * cols, chans), BF16)
    mine, *sent = call(
        functools.partial(mix_kernel, frames, rows, cols, len(w_rounds), len(h_rounds)),
        "mix",
        [shape((block, chans), F32)] + sides + (sides + [lines, shape((block, chans), F32)]) * (chips - 1),
        [pltpu.VMEM((block, LANES), F32)],
        [partner, fields, table],
        2 * chips * frames * x.size,
    )
    borders, wholes = [], []
    for d in range(chips):
        for pairs in w_rounds:
            route = [(i * n_w + a, (i + 2 * d) % n_t * n_w + b) for i in range(n_t) for a, b in pairs]
            borders.append(lax.ppermute(sent.pop(0), ("tm", "width"), route))
        if d:
            route = [(i, (i + 2 * d) % n_t) for i in range(n_t)]
            borders.append(lax.ppermute(sent.pop(0), "tm", route))
            (whole,) = call(round_kernel, "round", [shape((block, chans), BF16)], [], [sent.pop(0)])
            wholes.append(lax.ppermute(whole, "tm", route))

    size = -(-(frames * cols + 2 * frames) // 16) * 16
    low, high, *ends = call(
        functools.partial(border_kernel, frames, rows, cols, len(w_rounds), chips),
        "border",
        [shape((frames * rows, chans), F32)] * 2 + [shape((size, chans), BF16)] * len(h_rounds),
        [],
        [mine] + borders,
    )
    ends = [lax.ppermute(e, "height", pairs) for e, pairs in zip(ends, h_rounds)]

    (out,) = call(
        functools.partial(finish_kernel, frames, rows, cols, len(h_rounds)),
        "finish",
        [shape((block, chans), BF16)],
        [pltpu.VMEM((block, chans), BF16)],
        [mine, low, high, spatial_taps.reshape(9, chans), gate, value_weight, out_weight] + ends + wholes,
        4 * block * chans * chans,
    )
    return out.reshape(latents.shape)


def solution(mesh):
    in_specs = (P("tm", "height", "width", None), P(), P(), P(), P(), P(), P())
    out_specs = P("tm", "height", "width", None)
    return jax.shard_map(body, mesh=mesh, in_specs=in_specs, out_specs=out_specs, check_vma=False)
```

time: 70.6 us -> 23.5 us (0.33)
  local copies, waits for them, and re-layouts: 29.9 us -> 0.03 us
  waiting for transfers between devices: 16 us -> 6 us
  starting transfers between devices: 17.7 us -> 13.4 us
  Pallas kernels: 0 us -> 3.79 us
  matrix products: 3.16 us -> 0 us
  other arithmetic: 3.01 us -> 0 us
    unnamed x10 -> x6, local copies, waits for them, and re-layouts: 13.4 us -> 0.02 us
    all_to_all x2 -> x0, waiting for transfers between devices: 8.92 us -> none  [the longest x1 5.68 us: body(): lax.all_to_all(result.reshape(block.shape), 'tm', split_axis=0, concat_ax...]
    all_to_all x2 -> x0, starting transfers between devices: 6.81 us -> none  [the longest x1 3.41 us: body(): lax.all_to_all(spatial, 'tm', split_axis=3, concat_axis=0, tiled=True)]
    convert_element_type x1 -> x0, local copies, waits for them, and re-layouts: 6.37 us -> none  [spatial_mix(): return total.astype(jnp.bfloat16)]
    all_to_all x3 -> x0, local copies, waits for them, and re-layouts: 4.5 us -> none  [the longest x2 4.46 us: body(): lax.all_to_all(spatial, 'tm', split_axis=3, concat_axis=0, tiled=True)]
    pallas_call x0 -> x5, Pallas kernels: none -> 3.79 us  [call(): pl.pallas_call(kernel, out_shape=tuple(outs), in_specs=[HBM] * far + [VME...]
    dot_general x3 -> x0, matrix products: 3.16 us -> none  [the longest x1 2.43 us: body(): jnp.dot(hidden, out_weight, preferred_element_type=jnp.float32)]
    ppermute x4 -> x8, starting transfers between devices: 10.9 us -> 13.4 us  [the longest x4 8.15 us: body(): borders.append(lax.ppermute(sent.pop(0), ('tm', 'width'), route))]
  transfers between devices with their start and end apart: 6 -> 8, of which waited for: 5 -> 3; matrix products, arithmetic and copies ran while one was open for 7% -> 0% of each run, Pallas kernels for 0% -> 7%
where the time goes in v3:
time: 23.5 us; the launch traced here: 23.3 us
  starting transfers between devices  13.4 us (57%)
  waiting for transfers between devices  6 us (26%)
  Pallas kernels  3.79 us (16%)
    ppermute x4, starting transfers between devices, body(): borders.append(lax.ppermute(sent.pop(0), ('tm', 'width'), route))  8.15 us
    pallas_call x5, Pallas kernels, call(): pl.pallas_call(kernel, out_shape=tuple(outs), in_specs=[HBM] * far + [VME...  3.79 us
    ppermute x1, starting transfers between devices, body(): wholes.append(lax.ppermute(whole, 'tm', route))  2.69 us
    ppermute x1, waiting for transfers between devices, body(): lax.ppermute(e, 'height', pairs)  2.58 us
    ppermute x4, waiting for transfers between devices, body(): borders.append(lax.ppermute(sent.pop(0), ('tm', 'width'), route))  1.89 us
    ppermute x1, starting transfers between devices, body(): lax.ppermute(e, 'height', pairs)  1.56 us
    ppermute x1, waiting for transfers between devices, body(): borders.append(lax.ppermute(sent.pop(0), 'tm', route))  1.52 us
    ppermute x1, starting transfers between devices, body(): borders.append(lax.ppermute(sent.pop(0), 'tm', route))  0.51 us
  transfers between devices with their start and end apart: 8, of which 3 were waited for; matrix products, arithmetic and copies ran while one was open for 0% of the time, Pallas kernels for 7%

profile of v3, /device:TPU:0, one launch (start us, length us, event | category | flops | bytes accessed | tf_op | source)
XLA Modules:
  0.0 23.3 jit_solution(12683290001361538453)
XLA Ops:
  0.0 0.5 %collective-permute-start = (bf16[256,512]{1,0:T(8,128)(2,1)}, bf16[256,512]{1,0:T(8,128)(2,1)S(1)}, u32[]{:S(2)}, u32[]{:S(2)}) collective-permute-start(bf16[256,512]{1,0:T(8,128)(2,1)} %bitcast.3), channel_id=1, source_target_pairs={{0,8},{8,0},{16,24},{24,16},{1,9},{9,1},{17,25},{25,17},{2,10},{10... | collective-permute-start | bytes 786440 | tf_op jit(solution)/shard_map/ppermute | solution.py:216
  0.5 1.6 %early.1 = (f32[256,512]{1,0:T(8,128)S(1)}, f32[512,512]{1,0:T(8,128)S(1)}, f32[24,8,512]{2,1,0:T(8,128)S(1)}) custom-call(bf16[16,512]{1,0:T(8,128)(2,1)} %refs_0_.1, f32[1,512]{1,0:T(1,128)} %bitcast.5, bf16[256,512]{1,0:T(8,128)(2,1)} %bitcast.4, bf16[512,512]{1,0:T(8,128)(2,1)} %refs_3_.1), custom_call_target="tpu_custom_call" | custom-call | flops 134217728 | bytes 2770944 | tf_op jit(solution)/shard_map/early/pallas_call | solution.py:19
  2.1 0.0 collective-permute-done.partner_ref
  2.1 0.5 %mix.1 = (f32[256,512]{1,0:T(8,128)S(1)}, bf16[32,512]{1,0:T(8,128)(2,1)S(1)}, bf16[32,512]{1,0:T(8,128)(2,1)S(1)}, bf16[32,512]{1,0:T(8,128)(2,1)S(1)}, bf16[32...) custom-call(bf16[256,512]{1,0:T(8,128)(2,1)S(1)} %collective-permute-done.partner_ref, ...), custom_call_target="tpu_custom_call" | custom-call | flops 2097152 | bytes 2916352 | tf_op jit(solution)/shard_map/mix/pallas_call | solution.py:19
  2.6 0.0 copy-start.1
  2.6 0.0 copy-start
  2.7 2.7 %collective-permute-start.7 = (bf16[256,512]{1,0:T(8,128)(2,1)S(1)}, bf16[256,512]{1,0:T(8,128)(2,1)S(1)}, u32[]{:S(2)}, u32[]{:S(2)}) collective-permute-start(bf16[256,512]{1,0:T(8,128)(2,1)S(1)} %round.1), channel_id=1, source_target_pairs={{0,16},{8,24},{16,0},{24,8},{1,17},{9,25},{17,1},{25,9},{2,18},{10... | collective-permute-start | bytes 786440 | tf_op jit(solution)/shard_map/ppermute | solution.py:253
  5.4 1.6 %collective-permute-start.1 = (bf16[32,512]{1,0:T(8,128)(2,1)S(1)}, bf16[32,512]{1,0:T(8,128)(2,1)S(1)}, u32[]{:S(2)}, u32[]{:S(2)}) collective-permute-start(bf16[32,512]{1,0:T(8,128)(2,1)S(1)} %get-tuple-element.21), channel_id=1, source_target_pairs={{0,1},{1,0},{2,3},{3,2},{8,9},{9,8},{10,11},{11,10},{16,17},{17,16... | collective-permute-start | bytes 98312 | tf_op jit(solution)/shard_map/ppermute | solution.py:248
  6.9 0.7 %collective-permute-start.2 = (bf16[32,512]{1,0:T(8,128)(2,1)S(1)}, bf16[32,512]{1,0:T(8,128)(2,1)S(1)}, u32[]{:S(2)}, u32[]{:S(2)}) collective-permute-start(bf16[32,512]{1,0:T(8,128)(2,1)S(1)} %get-tuple-element.22), channel_id=1, source_target_pairs={{0,0},{1,2},{2,1},{3,3},{8,8},{9,10},{10,9},{11,11},{16,16},{17,18... | collective-permute-start | bytes 98312 | tf_op jit(solution)/shard_map/ppermute | solution.py:248
  7.6 4.4 %collective-permute-start.3 = (bf16[32,512]{1,0:T(8,128)(2,1)S(1)}, bf16[32,512]{1,0:T(8,128)(2,1)S(1)}, u32[]{:S(2)}, u32[]{:S(2)}) collective-permute-start(bf16[32,512]{1,0:T(8,128)(2,1)S(1)} %get-tuple-element.23), channel_id=1, source_target_pairs={{0,17},{1,16},{2,19},{3,18},{8,25},{9,24},{10,27},{11,26},{16,1},{... | collective-permute-start | bytes 98312 | tf_op jit(solution)/shard_map/ppermute | solution.py:248
  12.0 1.5 %collective-permute-start.4 = (bf16[32,512]{1,0:T(8,128)(2,1)S(1)}, bf16[32,512]{1,0:T(8,128)(2,1)S(1)}, u32[]{:S(2)}, u32[]{:S(2)}) collective-permute-start(bf16[32,512]{1,0:T(8,128)(2,1)S(1)} %get-tuple-element.24), channel_id=1, source_target_pairs={{0,16},{1,18},{2,17},{3,19},{8,24},{9,26},{10,25},{11,27},{16,0},{... | collective-permute-start | bytes 98312 | tf_op jit(solution)/shard_map/ppermute | solution.py:248
  13.5 0.0 collective-permute-done.1.refs_0_
  13.5 0.5 %collective-permute-start.5 = (bf16[32,512]{1,0:T(8,128)(2,1)S(1)}, bf16[32,512]{1,0:T(8,128)(2,1)S(1)}, u32[]{:S(2)}, u32[]{:S(2)}) collective-permute-start(bf16[32,512]{1,0:T(8,128)(2,1)S(1)} %get-tuple-element.25), channel_id=1, source_target_pairs={{0,16},{8,24},{16,0},{24,8},{1,17},{9,25},{17,1},{25,9},{2,18},{10... | collective-permute-start | bytes 98312 | tf_op jit(solution)/shard_map/ppermute | solution.py:251
  14.0 0.0 collective-permute-done.2.refs_1_
  14.0 0.0 collective-permute-done.3.refs_2_
  14.0 1.9 %collective-permute-done.4.refs_3_ = bf16[32,512]{1,0:T(8,128)(2,1)S(1)} collective-permute-done((bf16[32,512]{1,0:T(8,128)(2,1)S(1)}, bf16[32,512]{1,0:T(8,128)(2,1)S(1)}, u32[]{:S(2)}, u32[]{:S(2)}) %collective-permute-start.4) | collective-permute-done | bytes 32800 | tf_op jit(solution)/shard_map/ppermute | solution.py:248
  15.9 1.5 %collective-permute-done.5.refs_4_ = bf16[32,512]{1,0:T(8,128)(2,1)S(1)} collective-permute-done((bf16[32,512]{1,0:T(8,128)(2,1)S(1)}, bf16[32,512]{1,0:T(8,128)(2,1)S(1)}, u32[]{:S(2)}, u32[]{:S(2)}) %collective-permute-start.5) | collective-permute-done | bytes 32800 | tf_op jit(solution)/shard_map/ppermute | solution.py:251
  17.4 0.0 copy-start.2
  17.4 0.1 border.1
  17.5 1.6 %collective-permute-start.6 = (bf16[48,512]{1,0:T(8,128)(2,1)S(1)}, bf16[48,512]{1,0:T(8,128)(2,1)S(1)}, u32[]{:S(2)}, u32[]{:S(2)}) collective-permute-start(bf16[48,512]{1,0:T(8,128)(2,1)S(1)} %get-tuple-element.29), channel_id=1, source_target_pairs={{0,4},{4,0},{1,5},{5,1},{2,6},{6,2},{3,7},{7,3},{8,12},{12,8},{9,1... | collective-permute-start | bytes 147464 | tf_op jit(solution)/shard_map/ppermute | solution.py:263
  19.1 0.0 copy-done.2
  19.1 2.6 %collective-permute-done.6.refs_0_ = bf16[48,512]{1,0:T(8,128)(2,1)S(1)} collective-permute-done((bf16[48,512]{1,0:T(8,128)(2,1)S(1)}, bf16[48,512]{1,0:T(8,128)(2,1)S(1)}, u32[]{:S(2)}, u32[]{:S(2)}) %collective-permute-start.6) | collective-permute-done | bytes 49184 | tf_op jit(solution)/shard_map/ppermute | solution.py:263
  21.7 0.0 collective-permute-done.7.refs_1_
  21.7 0.0 copy-done.1
  21.7 0.0 copy-done
  21.7 1.6 %finish.1 = bf16[256,512]{1,0:T(8,128)(2,1)} custom-call(f32[256,512]{1,0:T(8,128)S(1)} %get-tuple-element.20.mine_ref, f32[32,512]{1,0:T(8,128)S(1)} %get-tuple-element.26.low_ref, f32[32,512]{1,0:T(8,128)S(1)} %get-tuple-element.27.high_ref, f32[9,512]{1,0:T(8,128)S(1)} %reshape.14.taps_ref, f32[256,512]{1,0:T(8,128)S(1)} %get-tuple-element.28.gate_ref, ...), custom_call_target="tpu_custom_call" | custom-call | flops 268435456 | bytes 2820096 | tf_op jit(solution)/shard_map/finish/pallas_call | solution.py:19
  (2 shorter events, 0.0 us)
Async XLA Ops:
  0.0 2.1 %collective-permute-start = (bf16[256,512]{1,0:T(8,128)(2,1)}, bf16[256,512]{1,0:T(8,128)(2,1)S(1)}, u32[]{:S(2)}, u32[]{:S(2)}) collective-permute-start(bf16[256,512]{1,0:T(8,128)(2,1)} %bitcast.3), channel_id=1, source_target_pairs={{0,8},{8,0},{16,24},{24,16},{1,9},{9,1},{17,25},{25,17},{2,10},{10... | collective-permute-start | bytes 786440 | tf_op jit(solution)/shard_map/ppermute | solution.py:216
  2.6 19.1 %copy-start.1 = (bf16[512,512]{1,0:T(8,128)(2,1)S(1)}, bf16[512,512]{1,0:T(8,128)(2,1)}, u32[]{:S(2)}) copy-start(bf16[512,512]{1,0:T(8,128)(2,1)} %wo_ref.1) | copy-start | bytes 1572868
  2.6 19.0 %copy-start = (bf16[512,512]{1,0:T(8,128)(2,1)S(1)}, bf16[512,512]{1,0:T(8,128)(2,1)}, u32[]{:S(2)}) copy-start(bf16[512,512]{1,0:T(8,128)(2,1)} %wv_ref.1) | copy-start | bytes 1572868
  2.7 19.0 %collective-permute-start.7 = (bf16[256,512]{1,0:T(8,128)(2,1)S(1)}, bf16[256,512]{1,0:T(8,128)(2,1)S(1)}, u32[]{:S(2)}, u32[]{:S(2)}) collective-permute-start(bf16[256,512]{1,0:T(8,128)(2,1)S(1)} %round.1), channel_id=1, source_target_pairs={{0,16},{8,24},{16,0},{24,8},{1,17},{9,25},{17,1},{25,9},{2,18},{10... | collective-permute-start | bytes 786440 | tf_op jit(solution)/shard_map/ppermute | solution.py:253
  5.4 8.2 %collective-permute-start.1 = (bf16[32,512]{1,0:T(8,128)(2,1)S(1)}, bf16[32,512]{1,0:T(8,128)(2,1)S(1)}, u32[]{:S(2)}, u32[]{:S(2)}) collective-permute-start(bf16[32,512]{1,0:T(8,128)(2,1)S(1)} %get-tuple-element.21), channel_id=1, source_target_pairs={{0,1},{1,0},{2,3},{3,2},{8,9},{9,8},{10,11},{11,10},{16,17},{17,16... | collective-permute-start | bytes 98312 | tf_op jit(solution)/shard_map/ppermute | solution.py:248
  6.9 7.1 %collective-permute-start.2 = (bf16[32,512]{1,0:T(8,128)(2,1)S(1)}, bf16[32,512]{1,0:T(8,128)(2,1)S(1)}, u32[]{:S(2)}, u32[]{:S(2)}) collective-permute-start(bf16[32,512]{1,0:T(8,128)(2,1)S(1)} %get-tuple-element.22), channel_id=1, source_target_pairs={{0,0},{1,2},{2,1},{3,3},{8,8},{9,10},{10,9},{11,11},{16,16},{17,18... | collective-permute-start | bytes 98312 | tf_op jit(solution)/shard_map/ppermute | solution.py:248
  7.6 6.4 %collective-permute-start.3 = (bf16[32,512]{1,0:T(8,128)(2,1)S(1)}, bf16[32,512]{1,0:T(8,128)(2,1)S(1)}, u32[]{:S(2)}, u32[]{:S(2)}) collective-permute-start(bf16[32,512]{1,0:T(8,128)(2,1)S(1)} %get-tuple-element.23), channel_id=1, source_target_pairs={{0,17},{1,16},{2,19},{3,18},{8,25},{9,24},{10,27},{11,26},{16,1},{... | collective-permute-start | bytes 98312 | tf_op jit(solution)/shard_map/ppermute | solution.py:248
  12.0 3.9 %collective-permute-start.4 = (bf16[32,512]{1,0:T(8,128)(2,1)S(1)}, bf16[32,512]{1,0:T(8,128)(2,1)S(1)}, u32[]{:S(2)}, u32[]{:S(2)}) collective-permute-start(bf16[32,512]{1,0:T(8,128)(2,1)S(1)} %get-tuple-element.24), channel_id=1, source_target_pairs={{0,16},{1,18},{2,17},{3,19},{8,24},{9,26},{10,25},{11,27},{16,0},{... | collective-permute-start | bytes 98312 | tf_op jit(solution)/shard_map/ppermute | solution.py:248
  13.5 3.9 %collective-permute-start.5 = (bf16[32,512]{1,0:T(8,128)(2,1)S(1)}, bf16[32,512]{1,0:T(8,128)(2,1)S(1)}, u32[]{:S(2)}, u32[]{:S(2)}) collective-permute-start(bf16[32,512]{1,0:T(8,128)(2,1)S(1)} %get-tuple-element.25), channel_id=1, source_target_pairs={{0,16},{8,24},{16,0},{24,8},{1,17},{9,25},{17,1},{25,9},{2,18},{10... | collective-permute-start | bytes 98312 | tf_op jit(solution)/shard_map/ppermute | solution.py:251
  17.4 1.6 %copy-start.2 = (f32[3,3,512]{2,1,0:T(4,128)S(1)}, f32[3,3,512]{2,1,0:T(4,128)}, u32[]{:S(2)}) copy-start(f32[3,3,512]{2,1,0:T(4,128)} %param.8) | copy-start | bytes 55300
  17.5 4.2 %collective-permute-start.6 = (bf16[48,512]{1,0:T(8,128)(2,1)S(1)}, bf16[48,512]{1,0:T(8,128)(2,1)S(1)}, u32[]{:S(2)}, u32[]{:S(2)}) collective-permute-start(bf16[48,512]{1,0:T(8,128)(2,1)S(1)} %get-tuple-element.29), channel_id=1, source_target_pairs={{0,4},{4,0},{1,5},{5,1},{2,6},{6,2},{3,7},{7,3},{8,12},{12,8},{9,1... | collective-permute-start | bytes 147464 | tf_op jit(solution)/shard_map/ppermute | solution.py:263

commit v4 on v3

--- a/solution.py
+++ b/solution.py
@@ -88,13 +88,13 @@
     gate_ref[...] = v / (1.0 + jnp.exp(-v))
 
 
-def mix_kernel(frames, rows, cols, rounds_w, rounds_h, partner_ref, fields_ref, table_ref, mine_ref, *refs):
+def mix_kernel(frames, rows, cols, rounds_w, partner_ref, fields_ref, table_ref, mine_ref, *refs):
     *outs, held = refs
     sites = rows * cols
     block = frames * sites
     pad = 2 * frames
     shift = jnp.where(lax.rem(lax.axis_index("tm"), 2) == 1, frames, -frames)
-    odd_w, odd_h = position("width")[0], position("height")[0]
+    odd = position("width")[0]
     for lane in range(0, mine_ref.shape[1], LANES):
         span = slice(lane, lane + LANES)
         outs_left = list(outs)
@@ -112,21 +112,11 @@
             first = held[pl.ds(0, frames * rows, stride=cols), :].astype(BF16)
             last = held[pl.ds(cols - 1, frames * rows, stride=cols), :].astype(BF16)
             for k in range(rounds_w):
-                outs_left.pop(0)[:, span] = jnp.where(odd_w, last, first) if k else jnp.where(odd_w, first, last)
+                outs_left.pop(0)[:, span] = jnp.where(odd, last, first) if k else jnp.where(odd, first, last)
             if d == 0:
                 mine_ref[:, span] = held[...]
                 continue
-            top = jnp.concatenate([t[0] for t in totals], axis=0).astype(BF16)
-            bottom = jnp.concatenate([t[rows - 1] for t in totals], axis=0).astype(BF16)
-            lines_ref = outs_left.pop(0)
-            for k in range(rounds_h):
-                line = jnp.where(odd_h, bottom, top) if k else jnp.where(odd_h, top, bottom)
-                lines_ref[k * frames * cols : (k + 1) * frames * cols, span] = line
-            outs_left.pop(0)[:, span] = held[...]
-
-
-def round_kernel(x_ref, out_ref):
-    out_ref[...] = x_ref[...].astype(BF16)
+            outs_left.pop(0)[:, span] = held[...].astype(BF16)
 
 
 def later(d, value):
@@ -134,74 +124,106 @@
 
 
 def border_kernel(frames, rows, cols, rounds_w, chips, mine_ref, *refs):
-    ins, (low_ref, high_ref, *outs) = refs[: chips * rounds_w + chips - 1], refs[chips * rounds_w + chips - 1 :]
+    sides, wholes = refs[: chips * rounds_w], refs[chips * rounds_w : chips * rounds_w + chips - 1]
+    low_ref, high_ref, *outs = refs[chips * rounds_w + chips - 1 :]
     sites = rows * cols
     odd, _, _ = position("height")
     low = high = None
-    lines = []
     for d in range(chips):
-        sides, ins = ins[:rounds_w], ins[rounds_w:]
-        arrived = received("width", [s[...].astype(F32) for s in sides])
+        arrived = received("width", [s[...].astype(F32) for s in sides[d * rounds_w : (d + 1) * rounds_w]])
         if d == 0:
             low, high = arrived
         else:
             low, high = low + later(d, arrived[0]), high + later(d, arrived[1])
-            lines.append(ins[0])
-            ins = ins[1:]
     low_ref[...] = low
     high_ref[...] = high
-    size = frames * cols
-    fill = jnp.zeros((outs[0].shape[0] - size - 2 * frames, low.shape[1]), F32)
+    fill = jnp.zeros((outs[0].shape[0] - frames * cols - 2 * frames, low.shape[1]), F32)
+    ends = []
+    for r in (0, rows - 1):
+        lines = []
+        for t in range(frames):
+            at = t * sites + r * cols
+            line = mine_ref[at : at + cols]
+            for d, ref in enumerate(wholes, 1):
+                line = line + later(d, ref[at : at + cols].astype(F32))
+            lines.append(line)
+        lefts = [low[t * rows + r : t * rows + r + 1] for t in range(frames)]
+        rights = [high[t * rows + r : t * rows + r + 1] for t in range(frames)]
+        ends.append(jnp.concatenate(lines + lefts + rights + [fill], axis=0))
     for k, out in enumerate(outs):
-        ends = []
-        for r in (0, rows - 1):
-            line = [mine_ref[t * sites + r * cols : t * sites + (r + 1) * cols] for t in range(frames)]
-            lefts = [low[t * rows + r : t * rows + r + 1] for t in range(frames)]
-            rights = [high[t * rows + r : t * rows + r + 1] for t in range(frames)]
-            ends.append((jnp.concatenate(line, axis=0), jnp.concatenate(lefts + rights + [fill], axis=0)))
-        pick = lambda j: jnp.where(odd, ends[1][j], ends[0][j]) if k else jnp.where(odd, ends[0][j], ends[1][j])
-        line = pick(0)
-        for d, ref in enumerate(lines, 1):
-            line = line + later(d, ref[k * size : (k + 1) * size].astype(F32))
-        out[...] = jnp.concatenate([line, pick(1)], axis=0).astype(BF16)
-
-
-def finish_kernel(frames, rows, cols, rounds_h, mine_ref, low_ref, high_ref, taps_ref, gate_ref, wv_ref, wo_ref, *refs):
-    ends, wholes, (out_ref, mixed) = refs[:rounds_h], refs[rounds_h:-2], refs[-2:]
+        out[...] = (jnp.where(odd, ends[1], ends[0]) if k else jnp.where(odd, ends[0], ends[1])).astype(BF16)
+
+
+def shifted(line, left, right):
+    cols = line.shape[0]
+    place = lax.broadcasted_iota(jnp.int32, line.shape, 0)
+    before = jnp.where(place == 0, left, pltpu.roll(line, 1, 0))
+    after = jnp.where(place == cols - 1, right, pltpu.roll(line, cols - 1, 0))
+    return before, line, after
+
+
+def projected(mixed, gate, wv_ref, wo_ref):
+    value = jnp.dot(mixed, wv_ref[...], preferred_element_type=F32)
+    hidden = (value * gate).astype(BF16)
+    return jnp.dot(hidden, wo_ref[...], preferred_element_type=F32).astype(BF16)
+
+
+def inner_kernel(frames, rows, cols, mine_ref, low_ref, high_ref, taps_ref, gate_ref, wv_ref, wo_ref, *refs):
+    *wholes, out_ref, edges_ref, mixed = refs
     chans = mine_ref.shape[1]
     sites = rows * cols
-    place = lax.broadcasted_iota(jnp.int32, (cols, LANES), 0)
-    corner = frames * cols
     for lane in range(0, chans, LANES):
         span = slice(lane, lane + LANES)
         taps = [[taps_ref[3 * a + b : 3 * a + b + 1, span] for b in range(3)] for a in range(3)]
         low, high = low_ref[:, span], high_ref[:, span]
-        above, below = received("height", [e[:, span].astype(F32) for e in ends])
         for t in range(frames):
             at = t * sites
             tile = mine_ref[at : at + sites, span]
             for d, ref in enumerate(wholes, 1):
                 tile = tile + later(d, ref[at : at + sites, span].astype(F32))
-            lines = [tile[r * cols : (r + 1) * cols] for r in range(rows)]
-            lefts = [low[t * rows + r : t * rows + r + 1] for r in range(rows)]
-            rights = [high[t * rows + r : t * rows + r + 1] for r in range(rows)]
-            for end, where in ((above, 0), (below, rows + 1)):
-                lines.insert(where, end[t * cols : (t + 1) * cols])
-                lefts.insert(where, end[corner + t : corner + t + 1])
-                rights.insert(where, end[corner + frames + t : corner + frames + t + 1])
             totals = [None] * rows
-            for r in range(rows + 2):
-                before = jnp.where(place == 0, lefts[r], pltpu.roll(lines[r], 1, 0))
-                after = jnp.where(place == cols - 1, rights[r], pltpu.roll(lines[r], cols - 1, 0))
+            for r in range(rows):
+                row = t * rows + r
+                near = shifted(tile[r * cols : (r + 1) * cols], low[row : row + 1], high[row : row + 1])
                 for a in range(3):
-                    to = r - a
+                    to = r + 1 - a
                     if 0 <= to < rows:
-                        term = before * taps[a][0] + lines[r] * taps[a][1] + after * taps[a][2]
+                        term = near[0] * taps[a][0] + near[1] * taps[a][1] + near[2] * taps[a][2]
                         totals[to] = term if totals[to] is None else totals[to] + term
             mixed[at : at + sites, span] = jnp.concatenate(totals, axis=0).astype(BF16)
-    value = jnp.dot(mixed[...], wv_ref[...], preferred_element_type=F32)
-    hidden = (value * gate_ref[...]).astype(BF16)
-    out_ref[...] = jnp.dot(hidden, wo_ref[...], preferred_element_type=F32).astype(BF16)
+            edges_ref[t * cols : (t + 1) * cols, span] = totals[0]
+            edges_ref[(frames + t) * cols : (frames + t + 1) * cols, span] = totals[rows - 1]
+    out_ref[...] = projected(mixed[...], gate_ref[...], wv_ref, wo_ref)
+
+
+def edge_kernel(frames, rows, cols, rounds_h, edges_ref, taps_ref, gate_ref, wv_ref, wo_ref, inner_ref, *refs):
+    ends, out_ref = refs[:rounds_h], refs[rounds_h]
+    sites = rows * cols
+    size = frames * cols
+    odd, _, _ = position("height")
+    out_ref[...] = inner_ref[...]
+    taps = taps_ref[...]
+    mixed, gate = [], []
+    for k, end in enumerate(ends):
+        end = end[...].astype(F32)
+        first = jnp.logical_not(odd) if k else odd
+        lefts, rights = end[size : size + frames], end[size + frames : size + 2 * frames]
+        lower, upper = position("height")[1:]
+        exists = jnp.where(first, lower, upper)
+        tap = jnp.where(first, taps[0:3], taps[6:9])
+        total = jnp.where(first, edges_ref[0:size], edges_ref[size : 2 * size])
+        for t in range(frames):
+            near = shifted(end[t * cols : (t + 1) * cols], lefts[t : t + 1], rights[t : t + 1])
+            more = near[0] * tap[0:1] + near[1] * tap[1:2] + near[2] * tap[2:3]
+            mixed.append(total[t * cols : (t + 1) * cols] + jnp.where(exists, more, jnp.zeros_like(more)))
+            at = t * sites
+            gate.append(jnp.where(first, gate_ref[at : at + cols], gate_ref[at + sites - cols : at + sites]))
+    out = projected(jnp.concatenate(mixed, axis=0).astype(BF16), jnp.concatenate(gate, axis=0), wv_ref, wo_ref)
+    for t in range(frames):
+        new = [out[k * size + t * cols : k * size + (t + 1) * cols] for k in range(rounds_h)]
+        for at, other in ((t * sites, False), (t * sites + sites - cols, True)):
+            kept = new[1] if rounds_h > 1 else inner_ref[at : at + cols]
+            out_ref[at : at + cols] = jnp.where(odd, kept, new[0]) if other else jnp.where(odd, new[0], kept)
 
 
 def body(latents, spatial_taps, kernel_taps, skip_gain, gate_weight, value_weight, out_weight):
@@ -232,11 +254,10 @@
 
     w_rounds, h_rounds = swaps("width"), swaps("height")
     sides = [shape((frames * rows, chans), BF16)] * len(w_rounds)
-    lines = shape((len(h_rounds) * frames * cols, chans), BF16)
     mine, *sent = call(
-        functools.partial(mix_kernel, frames, rows, cols, len(w_rounds), len(h_rounds)),
+        functools.partial(mix_kernel, frames, rows, cols, len(w_rounds)),
         "mix",
-        [shape((block, chans), F32)] + sides + (sides + [lines, shape((block, chans), F32)]) * (chips - 1),
+        [shape((block, chans), F32)] + sides + (sides + [shape((block, chans), BF16)]) * (chips - 1),
         [pltpu.VMEM((block, LANES), F32)],
         [partner, fields, table],
         2 * chips * frames * x.size,
@@ -247,10 +268,7 @@
             route = [(i * n_w + a, (i + 2 * d) % n_t * n_w + b) for i in range(n_t) for a, b in pairs]
             borders.append(lax.ppermute(sent.pop(0), ("tm", "width"), route))
         if d:
-            route = [(i, (i + 2 * d) % n_t) for i in range(n_t)]
-            borders.append(lax.ppermute(sent.pop(0), "tm", route))
-            (whole,) = call(round_kernel, "round", [shape((block, chans), BF16)], [], [sent.pop(0)])
-            wholes.append(lax.ppermute(whole, "tm", route))
+            wholes.append(lax.ppermute(sent.pop(0), "tm", [(i, (i + 2 * d) % n_t) for i in range(n_t)]))
 
     size = -(-(frames * cols + 2 * frames) // 16) * 16
     low, high, *ends = call(
@@ -258,17 +276,26 @@
         "border",
         [shape((frames * rows, chans), F32)] * 2 + [shape((size, chans), BF16)] * len(h_rounds),
         [],
-        [mine] + borders,
+        [mine] + borders + wholes,
     )
     ends = [lax.ppermute(e, "height", pairs) for e, pairs in zip(ends, h_rounds)]
 
+    taps = spatial_taps.reshape(9, chans)
+    inner, edges = call(
+        functools.partial(inner_kernel, frames, rows, cols),
+        "inner",
+        [shape((block, chans), BF16), shape((2 * frames * cols, chans), F32)],
+        [pltpu.VMEM((block, chans), BF16)],
+        [mine, low, high, taps, gate, value_weight, out_weight] + wholes,
+        4 * block * chans * chans,
+    )
     (out,) = call(
-        functools.partial(finish_kernel, frames, rows, cols, len(h_rounds)),
-        "finish",
+        functools.partial(edge_kernel, frames, rows, cols, len(h_rounds)),
+        "edge",
         [shape((block, chans), BF16)],
-        [pltpu.VMEM((block, chans), BF16)],
-        [mine, low, high, spatial_taps.reshape(9, chans), gate, value_weight, out_weight] + ends + wholes,
-        4 * block * chans * chans,
+        [],
+        [edges, taps, gate, value_weight, out_weight, inner] + ends,
+        4 * frames * cols * chans * chans,
     )
     return out.reshape(latents.shape)
 

time: 23.5 us -> 21.4 us (0.911)
  waiting for transfers between devices: 6 us -> 4.17 us
  starting transfers between devices: 13.4 us -> 12.8 us
  Pallas kernels: 3.79 us -> 4.03 us
    ppermute x2 -> x1, waiting for transfers between devices: 1.53 us -> 0.01 us  [body(): lax.ppermute(sent.pop(0), 'tm', [(i, (i + 2 * d) % n_t) for i in range(n_...]
    ppermute x1, waiting for transfers between devices: 2.58 us -> 1.77 us  [body(): lax.ppermute(e, 'height', pairs)]
    ppermute x2 -> x1, starting transfers between devices: 3.2 us -> 2.68 us  [body(): lax.ppermute(sent.pop(0), 'tm', [(i, (i + 2 * d) % n_t) for i in range(n_...]
    ppermute x4, waiting for transfers between devices: 1.89 us -> 2.39 us  [body(): borders.append(lax.ppermute(sent.pop(0), ('tm', 'width'), route))]
    pallas_call x5, Pallas kernels: 3.79 us -> 4.03 us  [call(): pl.pallas_call(kernel, out_shape=tuple(outs), in_specs=[HBM] * far + [VME...]
  transfers between devices with their start and end apart: 8 -> 7, of which waited for: 3 -> 3; matrix products, arithmetic and copies ran while one was open for 0% -> 0% of each run, Pallas kernels for 7% -> 11%
where the time goes in v4:
time: 21.4 us; the launch traced here: 21.2 us
  starting transfers between devices  12.8 us (60%)
  waiting for transfers between devices  4.17 us (19%)
  Pallas kernels  4.03 us (19%)
    ppermute x4, starting transfers between devices, body(): borders.append(lax.ppermute(sent.pop(0), ('tm', 'width'), route))  8.15 us
    pallas_call x5, Pallas kernels, call(): pl.pallas_call(kernel, out_shape=tuple(outs), in_specs=[HBM] * far + [VME...  4.03 us
    ppermute x1, starting transfers between devices, body(): lax.ppermute(sent.pop(0), 'tm', [(i, (i + 2 * d) % n_t) for i in range(n_...  2.68 us
    ppermute x4, waiting for transfers between devices, body(): borders.append(lax.ppermute(sent.pop(0), ('tm', 'width'), route))  2.39 us
    ppermute x1, waiting for transfers between devices, body(): lax.ppermute(e, 'height', pairs)  1.77 us
    ppermute x1, starting transfers between devices, body(): lax.ppermute(e, 'height', pairs)  1.56 us
    ppermute x1, starting transfers between devices, body(): partner = lax.ppermute(x, 'tm', [(i, i ^ 1) for i in range(n_t)])  0.45 us
  transfers between devices with their start and end apart: 7, of which 3 were waited for; matrix products, arithmetic and copies ran while one was open for 0% of the time, Pallas kernels for 11%

profile of v4, /device:TPU:0, one launch (start us, length us, event | category | flops | bytes accessed | tf_op | source)
XLA Modules:
  0.0 21.2 jit_solution(7095533092324529367)
XLA Ops:
  0.0 0.5 %collective-permute-start = (bf16[256,512]{1,0:T(8,128)(2,1)}, bf16[256,512]{1,0:T(8,128)(2,1)S(1)}, u32[]{:S(2)}, u32[]{:S(2)}) collective-permute-start(bf16[256,512]{1,0:T(8,128)(2,1)} %bitcast.3), channel_id=1, source_target_pairs={{0,8},{8,0},{16,24},{24,16},{1,9},{9,1},{17,25},{25,17},{2,10},{10... | collective-permute-start | bytes 786440 | tf_op jit(solution)/shard_map/ppermute | solution.py:238
  0.5 1.6 %early.1 = (f32[256,512]{1,0:T(8,128)S(1)}, f32[512,512]{1,0:T(8,128)S(1)}, f32[24,8,512]{2,1,0:T(8,128)S(1)}) custom-call(bf16[16,512]{1,0:T(8,128)(2,1)} %refs_0_.1, f32[1,512]{1,0:T(1,128)} %bitcast.5, bf16[256,512]{1,0:T(8,128)(2,1)} %bitcast.4, bf16[512,512]{1,0:T(8,128)(2,1)} %refs_3_.1), custom_call_target="tpu_custom_call" | custom-call | flops 134217728 | bytes 2770944 | tf_op jit(solution)/shard_map/early/pallas_call | solution.py:19
  2.1 0.0 collective-permute-done.partner_ref
  2.1 0.0 copy-start.1
  2.1 0.5 %mix.1 = (f32[256,512]{1,0:T(8,128)S(1)}, bf16[32,512]{1,0:T(8,128)(2,1)S(1)}, bf16[32,512]{1,0:T(8,128)(2,1)S(1)}, bf16[32,512]{1,0:T(8,128)(2,1)S(1)}, bf16[32...) custom-call(bf16[256,512]{1,0:T(8,128)(2,1)S(1)} %collective-permute-done.partner_ref, ...), custom_call_target="tpu_custom_call" | custom-call | flops 2097152 | bytes 2621440 | tf_op jit(solution)/shard_map/mix/pallas_call | solution.py:19
  2.6 0.0 copy-start
  2.6 2.7 %collective-permute-start.5 = (bf16[256,512]{1,0:T(8,128)(2,1)S(1)}, bf16[256,512]{1,0:T(8,128)(2,1)S(1)}, u32[]{:S(2)}, u32[]{:S(2)}) collective-permute-start(bf16[256,512]{1,0:T(8,128)(2,1)S(1)} %get-tuple-element.26), channel_id=1, source_target_pairs={{0,16},{8,24},{16,0},{24,8},{1,17},{9,25},{17,1},{25,9},{2,18},{10... | collective-permute-start | bytes 786440 | tf_op jit(solution)/shard_map/ppermute | solution.py:271
  5.3 1.6 %collective-permute-start.1 = (bf16[32,512]{1,0:T(8,128)(2,1)S(1)}, bf16[32,512]{1,0:T(8,128)(2,1)S(1)}, u32[]{:S(2)}, u32[]{:S(2)}) collective-permute-start(bf16[32,512]{1,0:T(8,128)(2,1)S(1)} %get-tuple-element.22), channel_id=1, source_target_pairs={{0,1},{1,0},{2,3},{3,2},{8,9},{9,8},{10,11},{11,10},{16,17},{17,16... | collective-permute-start | bytes 98312 | tf_op jit(solution)/shard_map/ppermute | solution.py:269
  6.9 0.7 %collective-permute-start.2 = (bf16[32,512]{1,0:T(8,128)(2,1)S(1)}, bf16[32,512]{1,0:T(8,128)(2,1)S(1)}, u32[]{:S(2)}, u32[]{:S(2)}) collective-permute-start(bf16[32,512]{1,0:T(8,128)(2,1)S(1)} %get-tuple-element.23), channel_id=1, source_target_pairs={{0,0},{1,2},{2,1},{3,3},{8,8},{9,10},{10,9},{11,11},{16,16},{17,18... | collective-permute-start | bytes 98312 | tf_op jit(solution)/shard_map/ppermute | solution.py:269
  7.5 4.4 %collective-permute-start.3 = (bf16[32,512]{1,0:T(8,128)(2,1)S(1)}, bf16[32,512]{1,0:T(8,128)(2,1)S(1)}, u32[]{:S(2)}, u32[]{:S(2)}) collective-permute-start(bf16[32,512]{1,0:T(8,128)(2,1)S(1)} %get-tuple-element.24), channel_id=1, source_target_pairs={{0,17},{1,16},{2,19},{3,18},{8,25},{9,24},{10,27},{11,26},{16,1},{... | collective-permute-start | bytes 98312 | tf_op jit(solution)/shard_map/ppermute | solution.py:269
  11.9 1.5 %collective-permute-start.4 = (bf16[32,512]{1,0:T(8,128)(2,1)S(1)}, bf16[32,512]{1,0:T(8,128)(2,1)S(1)}, u32[]{:S(2)}, u32[]{:S(2)}) collective-permute-start(bf16[32,512]{1,0:T(8,128)(2,1)S(1)} %get-tuple-element.25), channel_id=1, source_target_pairs={{0,16},{1,18},{2,17},{3,19},{8,24},{9,26},{10,25},{11,27},{16,0},{... | collective-permute-start | bytes 98312 | tf_op jit(solution)/shard_map/ppermute | solution.py:269
  13.5 0.0 collective-permute-done.1.refs_0_
  13.5 0.0 collective-permute-done.2.refs_1_
  13.5 0.4 %collective-permute-done.3.refs_2_ = bf16[32,512]{1,0:T(8,128)(2,1)S(1)} collective-permute-done((bf16[32,512]{1,0:T(8,128)(2,1)S(1)}, bf16[32,512]{1,0:T(8,128)(2,1)S(1)}, u32[]{:S(2)}, u32[]{:S(2)}) %collective-permute-start.3) | collective-permute-done | bytes 32800 | tf_op jit(solution)/shard_map/ppermute | solution.py:269
  13.8 2.0 %collective-permute-done.4.refs_3_ = bf16[32,512]{1,0:T(8,128)(2,1)S(1)} collective-permute-done((bf16[32,512]{1,0:T(8,128)(2,1)S(1)}, bf16[32,512]{1,0:T(8,128)(2,1)S(1)}, u32[]{:S(2)}, u32[]{:S(2)}) %collective-permute-start.4) | collective-permute-done | bytes 32800 | tf_op jit(solution)/shard_map/ppermute | solution.py:269
  15.8 0.0 collective-permute-done.5.refs_4_.refs_0_
  15.9 0.0 copy-start.2
  15.9 0.1 border.1
  15.9 1.6 %collective-permute-start.6 = (bf16[48,512]{1,0:T(8,128)(2,1)S(1)}, bf16[48,512]{1,0:T(8,128)(2,1)S(1)}, u32[]{:S(2)}, u32[]{:S(2)}) collective-permute-start(bf16[48,512]{1,0:T(8,128)(2,1)S(1)} %get-tuple-element.32), channel_id=1, source_target_pairs={{0,4},{4,0},{1,5},{5,1},{2,6},{6,2},{3,7},{7,3},{8,12},{12,8},{9,1... | collective-permute-start | bytes 147464 | tf_op jit(solution)/shard_map/ppermute | solution.py:281
  17.5 0.0 copy-done.2
  17.5 0.0 copy-done.1
  17.5 0.0 copy-done
  17.5 0.8 %inner.1 = (bf16[256,512]{1,0:T(8,128)(2,1)S(1)}, f32[64,512]{1,0:T(8,128)S(1)}) custom-call(f32[256,512]{1,0:T(8,128)S(1)} %get-tuple-element.21.mine_ref, f32[32,512]{1,0:T(8,128)S(1)} %get-tuple-element.27.low_ref, f32[32,512]{1,0:T(8,128)S(1)} %get-tuple-element.28.high_ref, f32[9,512]{1,0:T(8,128)S(1)} %reshape.14.taps_ref, ...), custom_call_target="tpu_custom_call" | custom-call | flops 268435456 | bytes 2902016 | tf_op jit(solution)/shard_map/inner/pallas_call | solution.py:19
  18.3 1.8 %collective-permute-done.6.refs_0_ = bf16[48,512]{1,0:T(8,128)(2,1)S(1)} collective-permute-done((bf16[48,512]{1,0:T(8,128)(2,1)S(1)}, bf16[48,512]{1,0:T(8,128)(2,1)S(1)}, u32[]{:S(2)}, u32[]{:S(2)}) %collective-permute-start.6) | collective-permute-done | bytes 49184 | tf_op jit(solution)/shard_map/ppermute | solution.py:281
  20.1 1.1 %edge.1 = bf16[256,512]{1,0:T(8,128)(2,1)} custom-call(f32[64,512]{1,0:T(8,128)S(1)} %get-tuple-element.30.edges_ref, f32[9,512]{1,0:T(8,128)S(1)} %reshape.14.taps_ref, f32[256,512]{1,0:T(8,128)S(1)} %get-tuple-element.29.gate_ref, bf16[512,512]{1,0:T(8,128)(2,1)S(1)} %copy-done, bf16[512,512]{1,0:T(8,128)(2,1)S(1)} %copy-done.1, ...), custom_call_target="tpu_custom_call" | custom-call | flops 33554432 | bytes 2295808 | tf_op jit(solution)/shard_map/edge/pallas_call | solution.py:19
  (1 shorter events, 0.0 us)
Async XLA Ops:
  0.0 2.1 %collective-permute-start = (bf16[256,512]{1,0:T(8,128)(2,1)}, bf16[256,512]{1,0:T(8,128)(2,1)S(1)}, u32[]{:S(2)}, u32[]{:S(2)}) collective-permute-start(bf16[256,512]{1,0:T(8,128)(2,1)} %bitcast.3), channel_id=1, source_target_pairs={{0,8},{8,0},{16,24},{24,16},{1,9},{9,1},{17,25},{25,17},{2,10},{10... | collective-permute-start | bytes 786440 | tf_op jit(solution)/shard_map/ppermute | solution.py:238
  2.1 15.4 %copy-start.1 = (bf16[512,512]{1,0:T(8,128)(2,1)S(1)}, bf16[512,512]{1,0:T(8,128)(2,1)}, u32[]{:S(2)}) copy-start(bf16[512,512]{1,0:T(8,128)(2,1)} %wo_ref.3) | copy-start | bytes 1572868
  2.6 14.9 %copy-start = (bf16[512,512]{1,0:T(8,128)(2,1)S(1)}, bf16[512,512]{1,0:T(8,128)(2,1)}, u32[]{:S(2)}) copy-start(bf16[512,512]{1,0:T(8,128)(2,1)} %wv_ref.3) | copy-start | bytes 1572868
  2.6 13.2 %collective-permute-start.5 = (bf16[256,512]{1,0:T(8,128)(2,1)S(1)}, bf16[256,512]{1,0:T(8,128)(2,1)S(1)}, u32[]{:S(2)}, u32[]{:S(2)}) collective-permute-start(bf16[256,512]{1,0:T(8,128)(2,1)S(1)} %get-tuple-element.26), channel_id=1, source_target_pairs={{0,16},{8,24},{16,0},{24,8},{1,17},{9,25},{17,1},{25,9},{2,18},{10... | collective-permute-start | bytes 786440 | tf_op jit(solution)/shard_map/ppermute | solution.py:271
  5.3 8.2 %collective-permute-start.1 = (bf16[32,512]{1,0:T(8,128)(2,1)S(1)}, bf16[32,512]{1,0:T(8,128)(2,1)S(1)}, u32[]{:S(2)}, u32[]{:S(2)}) collective-permute-start(bf16[32,512]{1,0:T(8,128)(2,1)S(1)} %get-tuple-element.22), channel_id=1, source_target_pairs={{0,1},{1,0},{2,3},{3,2},{8,9},{9,8},{10,11},{11,10},{16,17},{17,16... | collective-permute-start | bytes 98312 | tf_op jit(solution)/shard_map/ppermute | solution.py:269
  6.9 6.6 %collective-permute-start.2 = (bf16[32,512]{1,0:T(8,128)(2,1)S(1)}, bf16[32,512]{1,0:T(8,128)(2,1)S(1)}, u32[]{:S(2)}, u32[]{:S(2)}) collective-permute-start(bf16[32,512]{1,0:T(8,128)(2,1)S(1)} %get-tuple-element.23), channel_id=1, source_target_pairs={{0,0},{1,2},{2,1},{3,3},{8,8},{9,10},{10,9},{11,11},{16,16},{17,18... | collective-permute-start | bytes 98312 | tf_op jit(solution)/shard_map/ppermute | solution.py:269
  7.5 6.3 %collective-permute-start.3 = (bf16[32,512]{1,0:T(8,128)(2,1)S(1)}, bf16[32,512]{1,0:T(8,128)(2,1)S(1)}, u32[]{:S(2)}, u32[]{:S(2)}) collective-permute-start(bf16[32,512]{1,0:T(8,128)(2,1)S(1)} %get-tuple-element.24), channel_id=1, source_target_pairs={{0,17},{1,16},{2,19},{3,18},{8,25},{9,24},{10,27},{11,26},{16,1},{... | collective-permute-start | bytes 98312 | tf_op jit(solution)/shard_map/ppermute | solution.py:269
  11.9 3.9 %collective-permute-start.4 = (bf16[32,512]{1,0:T(8,128)(2,1)S(1)}, bf16[32,512]{1,0:T(8,128)(2,1)S(1)}, u32[]{:S(2)}, u32[]{:S(2)}) collective-permute-start(bf16[32,512]{1,0:T(8,128)(2,1)S(1)} %get-tuple-element.25), channel_id=1, source_target_pairs={{0,16},{1,18},{2,17},{3,19},{8,24},{9,26},{10,25},{11,27},{16,0},{... | collective-permute-start | bytes 98312 | tf_op jit(solution)/shard_map/ppermute | solution.py:269
  15.9 1.7 %copy-start.2 = (f32[3,3,512]{2,1,0:T(4,128)S(1)}, f32[3,3,512]{2,1,0:T(4,128)}, u32[]{:S(2)}) copy-start(f32[3,3,512]{2,1,0:T(4,128)} %param.8) | copy-start | bytes 55300
  15.9 4.2 %collective-permute-start.6 = (bf16[48,512]{1,0:T(8,128)(2,1)S(1)}, bf16[48,512]{1,0:T(8,128)(2,1)S(1)}, u32[]{:S(2)}, u32[]{:S(2)}) collective-permute-start(bf16[48,512]{1,0:T(8,128)(2,1)S(1)} %get-tuple-element.32), channel_id=1, source_target_pairs={{0,4},{4,0},{1,5},{5,1},{2,6},{6,2},{3,7},{7,3},{8,12},{12,8},{9,1... | collective-permute-start | bytes 147464 | tf_op jit(solution)/shard_map/ppermute | solution.py:281

commit v5 on v4

--- a/solution.py
+++ b/solution.py
@@ -44,17 +44,16 @@
     return lax.rem(i, 2) == 1, i > 0, i < n - 1
 
 
-def received(axis, arrived):
-    odd, lower, upper = position(axis)
-    even_low, even_high = arrived[-1], arrived[0]
-    low = jnp.where(odd, arrived[0], even_low)
-    high = jnp.where(odd, arrived[-1], even_high)
-    zero = jnp.zeros_like(low)
-    return jnp.where(lower, low, zero), jnp.where(upper, high, zero)
+def right_core():
+    return lax.rem(lax.axis_index("tm"), 2) == 1
+
+
+def outer_column(ref, lines, cols):
+    return jnp.where(right_core(), ref[pl.ds(cols - 1, lines, stride=cols), :], ref[pl.ds(0, lines, stride=cols), :])
 
 
 def early_kernel(frames, rows, cols, *refs):
-    far, (gate_ref, fields_ref, table_ref), near, arrived = refs[:4], refs[4:7], refs[7:11], refs[11]
+    far, (gate_ref, fields_ref, table_ref, side_ref), near, (arrived, held) = refs[:4], refs[4:8], refs[8:12], refs[12:]
     copies = [pltpu.make_async_copy(a, b, arrived.at[i]) for i, (a, b) in enumerate(zip(far, near))]
     for copy in copies:
         copy.start()
@@ -73,6 +72,8 @@
     copies[2].wait()
     for lane in range(0, chans, LANES):
         span = slice(lane, lane + LANES)
+        held[...] = x_ref[:, span].astype(F32)
+        side_ref[:, span] = outer_column(held, frames * rows, cols)
         for d in range(fields_ref.shape[0] // block):
             totals = [None] * frames
             for s in range(frames):
@@ -88,53 +89,69 @@
     gate_ref[...] = v / (1.0 + jnp.exp(-v))
 
 
-def mix_kernel(frames, rows, cols, rounds_w, partner_ref, fields_ref, table_ref, mine_ref, *refs):
+def mix_kernel(frames, rows, cols, partner_ref, fields_ref, table_ref, side_ref, mine_ref, *refs):
     *outs, held = refs
     sites = rows * cols
+    lines = frames * rows
     block = frames * sites
     pad = 2 * frames
-    shift = jnp.where(lax.rem(lax.axis_index("tm"), 2) == 1, frames, -frames)
-    odd = position("width")[0]
+    shift = jnp.where(right_core(), frames, -frames)
     for lane in range(0, mine_ref.shape[1], LANES):
         span = slice(lane, lane + LANES)
-        outs_left = list(outs)
+        held[...] = partner_ref[:, span].astype(F32)
+        near = [side_ref[s * rows : (s + 1) * rows, span] for s in range(frames)]
+        far = outer_column(held, lines, cols)
         for d in range(fields_ref.shape[0] // block):
             totals = []
             for t in range(frames):
                 at = d * block + t * sites
                 totals.append(fields_ref[at : at + sites, span].reshape(rows, cols, LANES))
+            base = pad + 2 * d * frames
             for s in range(frames):
                 x = partner_ref[s * sites : (s + 1) * sites, span].astype(F32).reshape(rows, cols, LANES)
                 for t in range(frames):
-                    totals[t] = totals[t] + table_ref[pad + 2 * d * frames + shift + t - s, :, span] * x
+                    totals[t] = totals[t] + table_ref[base + shift + t - s, :, span] * x
             for t in range(frames):
                 held[t * sites : (t + 1) * sites, :] = totals[t].reshape(sites, LANES)
-            first = held[pl.ds(0, frames * rows, stride=cols), :].astype(BF16)
-            last = held[pl.ds(cols - 1, frames * rows, stride=cols), :].astype(BF16)
-            for k in range(rounds_w):
-                outs_left.pop(0)[:, span] = jnp.where(odd, last, first) if k else jnp.where(odd, first, last)
-            if d == 0:
+            if d:
+                outs[2 * d][:, span] = held[...].astype(BF16)
+            else:
                 mine_ref[:, span] = held[...]
-                continue
-            outs_left.pop(0)[:, span] = held[...].astype(BF16)
+            ends = []
+            for t in range(frames):
+                end = jnp.zeros((rows, LANES), F32)
+                for s in range(frames):
+                    end = end + table_ref[base - shift + t - s, :, span] * near[s]
+                    if d or t >= s:
+                        end = end + table_ref[base + t - s, :, span] * far[s * rows : (s + 1) * rows]
+                ends.append(end)
+            column = jnp.concatenate([outer_column(held, lines, cols)] + ends, axis=0)
+            outs[2 * d - 1 if d else 0][:, span] = column.astype(BF16)
 
 
 def later(d, value):
     return jnp.where(lax.div(lax.axis_index("tm"), 2) >= d, value, jnp.zeros_like(value))
 
 
-def border_kernel(frames, rows, cols, rounds_w, chips, mine_ref, *refs):
-    sides, wholes = refs[: chips * rounds_w], refs[chips * rounds_w : chips * rounds_w + chips - 1]
-    low_ref, high_ref, *outs = refs[chips * rounds_w + chips - 1 :]
+def side_kernel(lines, *refs):
+    *arrived, own_ref, other_ref = refs
+    _, lower, upper = position("width")
+    exists = jnp.where(right_core(), upper, lower)
+    total = 0.0
+    for d, ref in enumerate(arrived):
+        total = total + later(d, ref[...].astype(F32))
+    total = jnp.where(exists, total, jnp.zeros_like(total))
+    other_ref[...] = total[:lines].astype(BF16)
+    own_ref[...] = total[lines:]
+
+
+def border_kernel(frames, rows, cols, mine_ref, own_ref, other_ref, *refs):
+    n = sum(ref.shape == mine_ref.shape for ref in refs)
+    wholes, (low_ref, high_ref, *outs) = refs[:n], refs[n:]
     sites = rows * cols
     odd, _, _ = position("height")
-    low = high = None
-    for d in range(chips):
-        arrived = received("width", [s[...].astype(F32) for s in sides[d * rounds_w : (d + 1) * rounds_w]])
-        if d == 0:
-            low, high = arrived
-        else:
-            low, high = low + later(d, arrived[0]), high + later(d, arrived[1])
+    right, own, other = right_core(), own_ref[...], other_ref[...].astype(F32)
+    low, high = jnp.where(right, other, own), jnp.where(right, own, other)
     low_ref[...] = low
     high_ref[...] = high
     fill = jnp.zeros((outs[0].shape[0] - frames * cols - 2 * frames, low.shape[1]), F32)
@@ -237,46 +254,61 @@
 
     partner = lax.ppermute(x, "tm", [(i, i ^ 1) for i in range(n_t)])
     inputs = [kernel_taps, skip_gain.reshape(1, chans), x, gate_weight]
-    gate, fields, table = call(
+    lines = frames * rows
+    gate, fields, table, side = call(
         functools.partial(early_kernel, frames, rows, cols),
         "early",
         [
             shape((block, chans), F32),
             shape((chips * block, chans), F32),
             shape((lags + 2 * frames, cols, chans), F32),
+            shape((lines, chans), F32),
         ],
-        [pltpu.VMEM(a.shape, a.dtype) for a in inputs] + [pltpu.SemaphoreType.DMA((len(inputs),))],
+        [pltpu.VMEM(a.shape, a.dtype) for a in inputs]
+        + [pltpu.SemaphoreType.DMA((len(inputs),)), pltpu.VMEM((block, LANES), F32)],
         inputs,
         2 * block * chans * chans,
         x.size,
         far=len(inputs),
     )
 
-    w_rounds, h_rounds = swaps("width"), swaps("height")
-    sides = [shape((frames * rows, chans), BF16)] * len(w_rounds)
+    h_rounds = swaps("height")
+    column = shape((2 * lines, chans), BF16)
     mine, *sent = call(
-        functools.partial(mix_kernel, frames, rows, cols, len(w_rounds)),
+        functools.partial(mix_kernel, frames, rows, cols),
         "mix",
-        [shape((block, chans), F32)] + sides + (sides + [shape((block, chans), BF16)]) * (chips - 1),
+        [shape((block, chans), F32), column] + [column, shape((block, chans), BF16)] * (chips - 1),
         [pltpu.VMEM((block, LANES), F32)],
-        [partner, fields, table],
+        [partner, fields, table, side],
         2 * chips * frames * x.size,
     )
-    borders, wholes = [], []
+    columns, wholes = [], []
     for d in range(chips):
-        for pairs in w_rounds:
-            route = [(i * n_w + a, (i + 2 * d) % n_t * n_w + b) for i in range(n_t) for a, b in pairs]
-            borders.append(lax.ppermute(sent.pop(0), ("tm", "width"), route))
+        route = []
+        for i in range(n_t):
+            for j in range(n_w):
+                to = j + (1 if i % 2 else -1)
+                core, to = (1 - i % 2, to) if 0 <= to < n_w else (i % 2, j)
+                route.append((i * n_w + j, ((i // 2 + d) % chips * 2 + core) * n_w + to))
+        columns.append(lax.ppermute(sent.pop(0), ("tm", "width"), route))
         if d:
             wholes.append(lax.ppermute(sent.pop(0), "tm", [(i, (i + 2 * d) % n_t) for i in range(n_t)]))
 
+    own, other = call(
+        functools.partial(side_kernel, lines),
+        "side",
+        [shape((lines, chans), F32), shape((lines, chans), BF16)],
+        [],
+        columns,
+    )
+    other = lax.ppermute(other, "tm", [(i, i ^ 1) for i in range(n_t)])
     size = -(-(frames * cols + 2 * frames) // 16) * 16
     low, high, *ends = call(
-        functools.partial(border_kernel, frames, rows, cols, len(w_rounds), chips),
+        functools.partial(border_kernel, frames, rows, cols),
         "border",
-        [shape((frames * rows, chans), F32)] * 2 + [shape((size, chans), BF16)] * len(h_rounds),
+        [shape((lines, chans), F32)] * 2 + [shape((size, chans), BF16)] * len(h_rounds),
         [],
-        [mine] + borders + wholes,
+        [mine, own, other] + wholes,
     )
     ends = [lax.ppermute(e, "height", pairs) for e, pairs in zip(ends, h_rounds)]
 

time: 21.4 us -> 20.3 us (0.949)
  starting transfers between devices: 12.8 us -> 6.67 us
  waiting for transfers between devices: 4.17 us -> 9.01 us
    ppermute x4 -> x3, starting transfers between devices: 8.15 us -> 1.4 us  [the longest x2 0.74 us: body(): columns.append(lax.ppermute(sent.pop(0), ('tm', 'width'), route))]
    ppermute x4 -> x3, waiting for transfers between devices: 2.39 us -> 7.76 us  [the longest x2 6.9 us: body(): columns.append(lax.ppermute(sent.pop(0), ('tm', 'width'), route))]
    ppermute x1, starting transfers between devices: 1.56 us -> 2.23 us  [body(): lax.ppermute(e, 'height', pairs)]
    ppermute x1, waiting for transfers between devices: 1.77 us -> 1.24 us  [body(): lax.ppermute(e, 'height', pairs)]
    pallas_call x5 -> x6, Pallas kernels: 4.03 us -> 4.24 us  [call(): pl.pallas_call(kernel, out_shape=tuple(outs), in_specs=[HBM] * far + [VME...]
  transfers between devices with their start and end apart: 7 -> 6, of which waited for: 3 -> 3; matrix products, arithmetic and copies ran while one was open for 0% -> 0% of each run, Pallas kernels for 11% -> 13%
where the time goes in v5:
time: 20.3 us; the launch traced here: 20.1 us
  waiting for transfers between devices  9.01 us (44%)
  starting transfers between devices  6.67 us (33%)
  Pallas kernels  4.24 us (21%)
    ppermute x2, waiting for transfers between devices, body(): columns.append(lax.ppermute(sent.pop(0), ('tm', 'width'), route))  6.9 us
    pallas_call x6, Pallas kernels, call(): pl.pallas_call(kernel, out_shape=tuple(outs), in_specs=[HBM] * far + [VME...  4.24 us
    ppermute x1, starting transfers between devices, body(): lax.ppermute(sent.pop(0), 'tm', [(i, (i + 2 * d) % n_t) for i in range(n_...  2.58 us
    ppermute x1, starting transfers between devices, body(): lax.ppermute(e, 'height', pairs)  2.23 us
    ppermute x1, waiting for transfers between devices, body(): lax.ppermute(e, 'height', pairs)  1.24 us
    ppermute x1, waiting for transfers between devices, body(): other = lax.ppermute(other, 'tm', [(i, i ^ 1) for i in range(n_t)])  0.86 us
    ppermute x2, starting transfers between devices, body(): columns.append(lax.ppermute(sent.pop(0), ('tm', 'width'), route))  0.74 us
    ppermute x1, starting transfers between devices, body(): other = lax.ppermute(other, 'tm', [(i, i ^ 1) for i in range(n_t)])  0.66 us
  transfers between devices with their start and end apart: 6, of which 3 were waited for; matrix products, arithmetic and copies ran while one was open for 0% of the time, Pallas kernels for 13%

profile of v5, /device:TPU:0, one launch (start us, length us, event | category | flops | bytes accessed | tf_op | source)
XLA Modules:
  0.0 20.1 jit_solution(92953715866077545)
XLA Ops:
  0.0 0.5 %collective-permute-start = (bf16[256,512]{1,0:T(8,128)(2,1)}, bf16[256,512]{1,0:T(8,128)(2,1)S(1)}, u32[]{:S(2)}, u32[]{:S(2)}) collective-permute-start(bf16[256,512]{1,0:T(8,128)(2,1)} %bitcast.3), channel_id=1, source_target_pairs={{0,8},{8,0},{16,24},{24,16},{1,9},{9,1},{17,25},{25,17},{2,10},{10... | collective-permute-start | bytes 786440 | tf_op jit(solution)/shard_map/ppermute | solution.py:255
  0.5 1.7 %early.1 = (f32[256,512]{1,0:T(8,128)S(1)}, f32[512,512]{1,0:T(8,128)S(1)}, f32[24,8,512]{2,1,0:T(8,128)S(1)}, f32[32,512]{1,0:T(8,128)S(1)}) custom-call(bf16[16,512]{1,0:T(8,128)(2,1)} %refs_0_.1, f32[1,512]{1,0:T(1,128)} %bitcast.5, bf16[256,512]{1,0:T(8,128)(2,1)} %bitcast.4, bf16[512,512]{1,0:T(8,128)(2,1)} %refs_3_.1), custom_call_target="tpu_custom_call" | custom-call | flops 134217728 | bytes 2836480 | tf_op jit(solution)/shard_map/early/pallas_call | solution.py:19
  2.2 0.0 collective-permute-done.partner_ref
  2.2 0.0 copy-start.2
  2.2 0.6 %mix.1 = (f32[256,512]{1,0:T(8,128)S(1)}, bf16[64,512]{1,0:T(8,128)(2,1)S(1)}, bf16[64,512]{1,0:T(8,128)(2,1)S(1)}, bf16[256,512]{1,0:T(8,128)(2,1)S(1)}) custom-call(bf16[256,512]{1,0:T(8,128)(2,1)S(1)} %collective-permute-done.partner_ref, f32[512,512]{1,0:T(8,128)S(1)} %get-tuple-element.20.fields_ref, f32[24,8,512]{2,1,0:T(8,128)S(1)} %get-tuple-element.21.table_ref, ...), custom_call_target="tpu_custom_call" | custom-call | flops 2097152 | bytes 2686976 | tf_op jit(solution)/shard_map/mix/pallas_call | solution.py:19
  2.8 2.6 %collective-permute-start.4 = (bf16[256,512]{1,0:T(8,128)(2,1)S(1)}, bf16[256,512]{1,0:T(8,128)(2,1)S(1)}, u32[]{:S(2)}, u32[]{:S(2)}) collective-permute-start(bf16[256,512]{1,0:T(8,128)(2,1)S(1)} %get-tuple-element.28), channel_id=1, source_target_pairs={{0,16},{8,24},{16,0},{24,8},{1,17},{9,25},{17,1},{25,9},{2,18},{10... | collective-permute-start | bytes 786440 | tf_op jit(solution)/shard_map/ppermute | solution.py:295
  5.4 0.7 %collective-permute-start.1 = (bf16[64,512]{1,0:T(8,128)(2,1)S(1)}, bf16[64,512]{1,0:T(8,128)(2,1)S(1)}, u32[]{:S(2)}, u32[]{:S(2)}) collective-permute-start(bf16[64,512]{1,0:T(8,128)(2,1)S(1)} %get-tuple-element.24), channel_id=1, source_target_pairs={{0,0},{1,8},{2,9},{3,10},{8,1},{9,2},{10,3},{11,11},{16,16},{17,24... | collective-permute-start | bytes 196616 | tf_op jit(solution)/shard_map/ppermute | solution.py:293
  6.0 0.0 copy-start
  6.1 0.0 copy-start.1
  6.1 0.1 collective-permute-start.2
  6.2 0.0 collective-permute-done.1.refs_0_
  6.2 6.9 %collective-permute-done.2.refs_1_ = bf16[64,512]{1,0:T(8,128)(2,1)S(1)} collective-permute-done((bf16[64,512]{1,0:T(8,128)(2,1)S(1)}, bf16[64,512]{1,0:T(8,128)(2,1)S(1)}, u32[]{:S(2)}, u32[]{:S(2)}) %collective-permute-start.2) | collective-permute-done | bytes 65568 | tf_op jit(solution)/shard_map/ppermute | solution.py:293
  13.1 0.7 %collective-permute-start.3 = (bf16[32,512]{1,0:T(8,128)(2,1)S(1)}, bf16[32,512]{1,0:T(8,128)(2,1)S(1)}, u32[]{:S(2)}, u32[]{:S(2)}) collective-permute-start(bf16[32,512]{1,0:T(8,128)(2,1)S(1)} %get-tuple-element.27), channel_id=1, source_target_pairs={{0,8},{8,0},{16,24},{24,16},{1,9},{9,1},{17,25},{25,17},{2,10},{10... | collective-permute-start | bytes 98312 | tf_op jit(solution)/shard_map/ppermute | solution.py:304
  13.8 0.9 %collective-permute-done.3.other_ref = bf16[32,512]{1,0:T(8,128)(2,1)S(1)} collective-permute-done((bf16[32,512]{1,0:T(8,128)(2,1)S(1)}, bf16[32,512]{1,0:T(8,128)(2,1)S(1)}, u32[]{:S(2)}, u32[]{:S(2)}) %collective-permute-start.3) | collective-permute-done | bytes 32800 | tf_op jit(solution)/shard_map/ppermute | solution.py:304
  14.6 0.0 collective-permute-done.4.refs_0_
  14.6 0.1 border.1
  14.7 2.2 %collective-permute-start.5 = (bf16[48,512]{1,0:T(8,128)(2,1)S(1)}, bf16[48,512]{1,0:T(8,128)(2,1)S(1)}, u32[]{:S(2)}, u32[]{:S(2)}) collective-permute-start(bf16[48,512]{1,0:T(8,128)(2,1)S(1)} %get-tuple-element.34), channel_id=1, source_target_pairs={{0,4},{4,0},{1,5},{5,1},{2,6},{6,2},{3,7},{7,3},{8,12},{12,8},{9,1... | collective-permute-start | bytes 147464 | tf_op jit(solution)/shard_map/ppermute | solution.py:313
  16.9 0.0 copy-done.2
  16.9 0.0 copy-done
  17.0 0.0 copy-done.1
  17.0 0.8 %inner.1 = (bf16[256,512]{1,0:T(8,128)(2,1)S(1)}, f32[64,512]{1,0:T(8,128)S(1)}) custom-call(f32[256,512]{1,0:T(8,128)S(1)} %get-tuple-element.23.mine_ref, f32[32,512]{1,0:T(8,128)S(1)} %get-tuple-element.29.low_ref, f32[32,512]{1,0:T(8,128)S(1)} %get-tuple-element.30.high_ref, f32[9,512]{1,0:T(8,128)S(1)} %reshape.14.taps_ref, ...), custom_call_target="tpu_custom_call" | custom-call | flops 268435456 | bytes 2902016 | tf_op jit(solution)/shard_map/inner/pallas_call | solution.py:19
  17.8 1.2 %collective-permute-done.5.refs_0_ = bf16[48,512]{1,0:T(8,128)(2,1)S(1)} collective-permute-done((bf16[48,512]{1,0:T(8,128)(2,1)S(1)}, bf16[48,512]{1,0:T(8,128)(2,1)S(1)}, u32[]{:S(2)}, u32[]{:S(2)}) %collective-permute-start.5) | collective-permute-done | bytes 49184 | tf_op jit(solution)/shard_map/ppermute | solution.py:313
  19.0 1.1 %edge.1 = bf16[256,512]{1,0:T(8,128)(2,1)} custom-call(f32[64,512]{1,0:T(8,128)S(1)} %get-tuple-element.32.edges_ref, f32[9,512]{1,0:T(8,128)S(1)} %reshape.14.taps_ref, f32[256,512]{1,0:T(8,128)S(1)} %get-tuple-element.31.gate_ref, bf16[512,512]{1,0:T(8,128)(2,1)S(1)} %copy-done, bf16[512,512]{1,0:T(8,128)(2,1)S(1)} %copy-done.1, ...), custom_call_target="tpu_custom_call" | custom-call | flops 33554432 | bytes 2295808 | tf_op jit(solution)/shard_map/edge/pallas_call | solution.py:19
  (2 shorter events, 0.0 us)
Async XLA Ops:
  0.0 2.2 %collective-permute-start = (bf16[256,512]{1,0:T(8,128)(2,1)}, bf16[256,512]{1,0:T(8,128)(2,1)S(1)}, u32[]{:S(2)}, u32[]{:S(2)}) collective-permute-start(bf16[256,512]{1,0:T(8,128)(2,1)} %bitcast.3), channel_id=1, source_target_pairs={{0,8},{8,0},{16,24},{24,16},{1,9},{9,1},{17,25},{25,17},{2,10},{10... | collective-permute-start | bytes 786440 | tf_op jit(solution)/shard_map/ppermute | solution.py:255
  2.2 14.7 %copy-start.2 = (f32[3,3,512]{2,1,0:T(4,128)S(1)}, f32[3,3,512]{2,1,0:T(4,128)}, u32[]{:S(2)}) copy-start(f32[3,3,512]{2,1,0:T(4,128)} %param.8) | copy-start | bytes 55300
  2.8 11.8 %collective-permute-start.4 = (bf16[256,512]{1,0:T(8,128)(2,1)S(1)}, bf16[256,512]{1,0:T(8,128)(2,1)S(1)}, u32[]{:S(2)}, u32[]{:S(2)}) collective-permute-start(bf16[256,512]{1,0:T(8,128)(2,1)S(1)} %get-tuple-element.28), channel_id=1, source_target_pairs={{0,16},{8,24},{16,0},{24,8},{1,17},{9,25},{17,1},{25,9},{2,18},{10... | collective-permute-start | bytes 786440 | tf_op jit(solution)/shard_map/ppermute | solution.py:295
  5.4 0.8 %collective-permute-start.1 = (bf16[64,512]{1,0:T(8,128)(2,1)S(1)}, bf16[64,512]{1,0:T(8,128)(2,1)S(1)}, u32[]{:S(2)}, u32[]{:S(2)}) collective-permute-start(bf16[64,512]{1,0:T(8,128)(2,1)S(1)} %get-tuple-element.24), channel_id=1, source_target_pairs={{0,0},{1,8},{2,9},{3,10},{8,1},{9,2},{10,3},{11,11},{16,16},{17,24... | collective-permute-start | bytes 196616 | tf_op jit(solution)/shard_map/ppermute | solution.py:293
  6.0 10.9 %copy-start = (bf16[512,512]{1,0:T(8,128)(2,1)S(1)}, bf16[512,512]{1,0:T(8,128)(2,1)}, u32[]{:S(2)}) copy-start(bf16[512,512]{1,0:T(8,128)(2,1)} %wv_ref.3) | copy-start | bytes 1572868
  6.1 10.9 %copy-start.1 = (bf16[512,512]{1,0:T(8,128)(2,1)S(1)}, bf16[512,512]{1,0:T(8,128)(2,1)}, u32[]{:S(2)}) copy-start(bf16[512,512]{1,0:T(8,128)(2,1)} %wo_ref.3) | copy-start | bytes 1572868
  6.1 7.0 %collective-permute-start.2 = (bf16[64,512]{1,0:T(8,128)(2,1)S(1)}, bf16[64,512]{1,0:T(8,128)(2,1)S(1)}, u32[]{:S(2)}, u32[]{:S(2)}) collective-permute-start(bf16[64,512]{1,0:T(8,128)(2,1)S(1)} %get-tuple-element.25), channel_id=1, source_target_pairs={{0,16},{1,24},{2,25},{3,26},{8,17},{9,18},{10,19},{11,27},{16,0},{... | collective-permute-start | bytes 196616 | tf_op jit(solution)/shard_map/ppermute | solution.py:293
  13.1 1.5 %collective-permute-start.3 = (bf16[32,512]{1,0:T(8,128)(2,1)S(1)}, bf16[32,512]{1,0:T(8,128)(2,1)S(1)}, u32[]{:S(2)}, u32[]{:S(2)}) collective-permute-start(bf16[32,512]{1,0:T(8,128)(2,1)S(1)} %get-tuple-element.27), channel_id=1, source_target_pairs={{0,8},{8,0},{16,24},{24,16},{1,9},{9,1},{17,25},{25,17},{2,10},{10... | collective-permute-start | bytes 98312 | tf_op jit(solution)/shard_map/ppermute | solution.py:304
  14.7 4.3 %collective-permute-start.5 = (bf16[48,512]{1,0:T(8,128)(2,1)S(1)}, bf16[48,512]{1,0:T(8,128)(2,1)S(1)}, u32[]{:S(2)}, u32[]{:S(2)}) collective-permute-start(bf16[48,512]{1,0:T(8,128)(2,1)S(1)} %get-tuple-element.34), channel_id=1, source_target_pairs={{0,4},{4,0},{1,5},{5,1},{2,6},{6,2},{3,7},{7,3},{8,12},{12,8},{9,1... | collective-permute-start | bytes 147464 | tf_op jit(solution)/shard_map/ppermute | solution.py:313

commit v6 on v5

--- a/solution.py
+++ b/solution.py
@@ -44,12 +44,21 @@
     return lax.rem(i, 2) == 1, i > 0, i < n - 1
 
 
-def right_core():
+def second():
     return lax.rem(lax.axis_index("tm"), 2) == 1
 
 
+def on_right():
+    return lax.rem(lax.axis_index("tm") + lax.axis_index("width"), 2) == 0
+
+
+def facing(core, column, columns):
+    to = column + (1 if (core + column) % 2 == 0 else -1)
+    return to if 0 <= to < columns else column
+
+
 def outer_column(ref, lines, cols):
-    return jnp.where(right_core(), ref[pl.ds(cols - 1, lines, stride=cols), :], ref[pl.ds(0, lines, stride=cols), :])
+    return jnp.where(on_right(), ref[pl.ds(cols - 1, lines, stride=cols), :], ref[pl.ds(0, lines, stride=cols), :])
 
 
 def early_kernel(frames, rows, cols, *refs):
@@ -95,7 +104,7 @@
     lines = frames * rows
     block = frames * sites
     pad = 2 * frames
-    shift = jnp.where(right_core(), frames, -frames)
+    shift = jnp.where(second(), frames, -frames)
     for lane in range(0, mine_ref.shape[1], LANES):
         span = slice(lane, lane + LANES)
         held[...] = partner_ref[:, span].astype(F32)
@@ -136,13 +145,13 @@
 def side_kernel(lines, *refs):
     *arrived, own_ref, other_ref = refs
     _, lower, upper = position("width")
-    exists = jnp.where(right_core(), upper, lower)
+    exists = jnp.where(on_right(), upper, lower)
     total = 0.0
     for d, ref in enumerate(arrived):
         total = total + later(d, ref[...].astype(F32))
     total = jnp.where(exists, total, jnp.zeros_like(total))
-    other_ref[...] = total[:lines].astype(BF16)
-    own_ref[...] = total[lines:]
+    own_ref[...] = total[:lines]
+    other_ref[...] = total[lines:].astype(BF16)
 
 
 def border_kernel(frames, rows, cols, mine_ref, own_ref, other_ref, *refs):
@@ -150,7 +159,7 @@
     wholes, (low_ref, high_ref, *outs) = refs[:n], refs[n:]
     sites = rows * cols
     odd, _, _ = position("height")
-    right, own, other = right_core(), own_ref[...], other_ref[...].astype(F32)
+    right, own, other = on_right(), own_ref[...], other_ref[...].astype(F32)
     low, high = jnp.where(right, other, own), jnp.where(right, own, other)
     low_ref[...] = low
     high_ref[...] = high
@@ -284,12 +293,9 @@
     )
     columns, wholes = [], []
     for d in range(chips):
-        route = []
-        for i in range(n_t):
-            for j in range(n_w):
-                to = j + (1 if i % 2 else -1)
-                core, to = (1 - i % 2, to) if 0 <= to < n_w else (i % 2, j)
-                route.append((i * n_w + j, ((i // 2 + d) % chips * 2 + core) * n_w + to))
+        route = [
+            (i * n_w + j, (i + 2 * d) % n_t * n_w + facing(i % 2, j, n_w)) for i in range(n_t) for j in range(n_w)
+        ]
         columns.append(lax.ppermute(sent.pop(0), ("tm", "width"), route))
         if d:
             wholes.append(lax.ppermute(sent.pop(0), "tm", [(i, (i + 2 * d) % n_t) for i in range(n_t)]))

time: 20.3 us -> 21 us (1.034)
  starting transfers between devices: 6.67 us -> 8.2 us
  waiting for transfers between devices: 9.01 us -> 8.12 us
    ppermute x2, starting transfers between devices: 0.74 us -> 3.54 us  [body(): columns.append(lax.ppermute(sent.pop(0), ('tm', 'width'), route))]
    ppermute x2, waiting for transfers between devices: 6.9 us -> 5.15 us  [body(): columns.append(lax.ppermute(sent.pop(0), ('tm', 'width'), route))]
    ppermute x1, starting transfers between devices: 2.23 us -> 1.56 us  [body(): lax.ppermute(e, 'height', pairs)]
    ppermute x1, starting transfers between devices: 0.66 us -> 0.07 us  [body(): other = lax.ppermute(other, 'tm', [(i, i ^ 1) for i in range(n_t)])]
    ppermute x1, waiting for transfers between devices: 1.24 us -> 1.77 us  [body(): lax.ppermute(e, 'height', pairs)]
    ppermute x1, waiting for transfers between devices: 0.86 us -> 1.19 us  [body(): other = lax.ppermute(other, 'tm', [(i, i ^ 1) for i in range(n_t)])]
  transfers between devices with their start and end apart: 6 -> 6, of which waited for: 3 -> 4; matrix products, arithmetic and copies ran while one was open for 0% -> 0% of each run, Pallas kernels for 13% -> 12%
where the time goes in v6:
time: 21 us; the launch traced here: 20.7 us
  starting transfers between devices  8.2 us (39%)
  waiting for transfers between devices  8.12 us (39%)
  Pallas kernels  4.24 us (20%)
    ppermute x2, waiting for transfers between devices, body(): columns.append(lax.ppermute(sent.pop(0), ('tm', 'width'), route))  5.15 us
    pallas_call x6, Pallas kernels, call(): pl.pallas_call(kernel, out_shape=tuple(outs), in_specs=[HBM] * far + [VME...  4.24 us
    ppermute x2, starting transfers between devices, body(): columns.append(lax.ppermute(sent.pop(0), ('tm', 'width'), route))  3.54 us
    ppermute x1, starting transfers between devices, body(): lax.ppermute(sent.pop(0), 'tm', [(i, (i + 2 * d) % n_t) for i in range(n_...  2.58 us
    ppermute x1, waiting for transfers between devices, body(): lax.ppermute(e, 'height', pairs)  1.77 us
    ppermute x1, starting transfers between devices, body(): lax.ppermute(e, 'height', pairs)  1.56 us
    ppermute x1, waiting for transfers between devices, body(): other = lax.ppermute(other, 'tm', [(i, i ^ 1) for i in range(n_t)])  1.19 us
    ppermute x1, starting transfers between devices, body(): partner = lax.ppermute(x, 'tm', [(i, i ^ 1) for i in range(n_t)])  0.45 us
  transfers between devices with their start and end apart: 6, of which 4 were waited for; matrix products, arithmetic and copies ran while one was open for 0% of the time, Pallas kernels for 12%

profile of v6, /device:TPU:0, one launch (start us, length us, event | category | flops | bytes accessed | tf_op | source)
XLA Modules:
  0.0 20.7 jit_solution(1949419160258797957)
XLA Ops:
  0.0 0.5 %collective-permute-start = (bf16[256,512]{1,0:T(8,128)(2,1)}, bf16[256,512]{1,0:T(8,128)(2,1)S(1)}, u32[]{:S(2)}, u32[]{:S(2)}) collective-permute-start(bf16[256,512]{1,0:T(8,128)(2,1)} %bitcast.3), channel_id=1, source_target_pairs={{0,8},{8,0},{16,24},{24,16},{1,9},{9,1},{17,25},{25,17},{2,10},{10... | collective-permute-start | bytes 786440 | tf_op jit(solution)/shard_map/ppermute | solution.py:264
  0.5 1.7 %early.1 = (f32[256,512]{1,0:T(8,128)S(1)}, f32[512,512]{1,0:T(8,128)S(1)}, f32[24,8,512]{2,1,0:T(8,128)S(1)}, f32[32,512]{1,0:T(8,128)S(1)}) custom-call(bf16[16,512]{1,0:T(8,128)(2,1)} %refs_0_.1, f32[1,512]{1,0:T(1,128)} %bitcast.5, bf16[256,512]{1,0:T(8,128)(2,1)} %bitcast.4, bf16[512,512]{1,0:T(8,128)(2,1)} %refs_3_.1), custom_call_target="tpu_custom_call" | custom-call | flops 134217728 | bytes 2836480 | tf_op jit(solution)/shard_map/early/pallas_call | solution.py:19
  2.2 0.0 collective-permute-done.partner_ref
  2.2 0.0 copy-start.2
  2.2 0.6 %mix.1 = (f32[256,512]{1,0:T(8,128)S(1)}, bf16[64,512]{1,0:T(8,128)(2,1)S(1)}, bf16[64,512]{1,0:T(8,128)(2,1)S(1)}, bf16[256,512]{1,0:T(8,128)(2,1)S(1)}) custom-call(bf16[256,512]{1,0:T(8,128)(2,1)S(1)} %collective-permute-done.partner_ref, f32[512,512]{1,0:T(8,128)S(1)} %get-tuple-element.20.fields_ref, f32[24,8,512]{2,1,0:T(8,128)S(1)} %get-tuple-element.21.table_ref, ...), custom_call_target="tpu_custom_call" | custom-call | flops 2097152 | bytes 2686976 | tf_op jit(solution)/shard_map/mix/pallas_call | solution.py:19
  2.8 2.6 %collective-permute-start.4 = (bf16[256,512]{1,0:T(8,128)(2,1)S(1)}, bf16[256,512]{1,0:T(8,128)(2,1)S(1)}, u32[]{:S(2)}, u32[]{:S(2)}) collective-permute-start(bf16[256,512]{1,0:T(8,128)(2,1)S(1)} %get-tuple-element.28), channel_id=1, source_target_pairs={{0,16},{8,24},{16,0},{24,8},{1,17},{9,25},{17,1},{25,9},{2,18},{10... | collective-permute-start | bytes 786440 | tf_op jit(solution)/shard_map/ppermute | solution.py:301
  5.4 3.5 %collective-permute-start.1 = (bf16[64,512]{1,0:T(8,128)(2,1)S(1)}, bf16[64,512]{1,0:T(8,128)(2,1)S(1)}, u32[]{:S(2)}, u32[]{:S(2)}) collective-permute-start(bf16[64,512]{1,0:T(8,128)(2,1)S(1)} %get-tuple-element.24), channel_id=1, source_target_pairs={{0,1},{1,0},{2,3},{3,2},{8,8},{9,10},{10,9},{11,11},{16,17},{17,16... | collective-permute-start | bytes 196616 | tf_op jit(solution)/shard_map/ppermute | solution.py:299
  8.9 0.0 copy-start
  8.9 0.0 copy-start.1
  8.9 0.1 collective-permute-start.2
  9.0 2.6 %collective-permute-done.1.refs_0_ = bf16[64,512]{1,0:T(8,128)(2,1)S(1)} collective-permute-done((bf16[64,512]{1,0:T(8,128)(2,1)S(1)}, bf16[64,512]{1,0:T(8,128)(2,1)S(1)}, u32[]{:S(2)}, u32[]{:S(2)}) %collective-permute-start.1) | collective-permute-done | bytes 65568 | tf_op jit(solution)/shard_map/ppermute | solution.py:299
  11.5 2.6 %collective-permute-done.2.refs_1_ = bf16[64,512]{1,0:T(8,128)(2,1)S(1)} collective-permute-done((bf16[64,512]{1,0:T(8,128)(2,1)S(1)}, bf16[64,512]{1,0:T(8,128)(2,1)S(1)}, u32[]{:S(2)}, u32[]{:S(2)}) %collective-permute-start.2) | collective-permute-done | bytes 65568 | tf_op jit(solution)/shard_map/ppermute | solution.py:299
  14.2 0.1 collective-permute-start.3
  14.2 1.2 %collective-permute-done.3.other_ref = bf16[32,512]{1,0:T(8,128)(2,1)S(1)} collective-permute-done((bf16[32,512]{1,0:T(8,128)(2,1)S(1)}, bf16[32,512]{1,0:T(8,128)(2,1)S(1)}, u32[]{:S(2)}, u32[]{:S(2)}) %collective-permute-start.3) | collective-permute-done | bytes 32800 | tf_op jit(solution)/shard_map/ppermute | solution.py:310
  15.4 0.0 collective-permute-done.4.refs_0_
  15.4 0.1 border.1
  15.5 1.6 %collective-permute-start.5 = (bf16[48,512]{1,0:T(8,128)(2,1)S(1)}, bf16[48,512]{1,0:T(8,128)(2,1)S(1)}, u32[]{:S(2)}, u32[]{:S(2)}) collective-permute-start(bf16[48,512]{1,0:T(8,128)(2,1)S(1)} %get-tuple-element.34), channel_id=1, source_target_pairs={{0,4},{4,0},{1,5},{5,1},{2,6},{6,2},{3,7},{7,3},{8,12},{12,8},{9,1... | collective-permute-start | bytes 147464 | tf_op jit(solution)/shard_map/ppermute | solution.py:319
  17.1 0.0 copy-done.2
  17.1 0.0 copy-done
  17.1 0.0 copy-done.1
  17.1 0.8 %inner.1 = (bf16[256,512]{1,0:T(8,128)(2,1)S(1)}, f32[64,512]{1,0:T(8,128)S(1)}) custom-call(f32[256,512]{1,0:T(8,128)S(1)} %get-tuple-element.23.mine_ref, f32[32,512]{1,0:T(8,128)S(1)} %get-tuple-element.29.low_ref, f32[32,512]{1,0:T(8,128)S(1)} %get-tuple-element.30.high_ref, f32[9,512]{1,0:T(8,128)S(1)} %reshape.14.taps_ref, ...), custom_call_target="tpu_custom_call" | custom-call | flops 268435456 | bytes 2902016 | tf_op jit(solution)/shard_map/inner/pallas_call | solution.py:19
  17.9 1.8 %collective-permute-done.5.refs_0_ = bf16[48,512]{1,0:T(8,128)(2,1)S(1)} collective-permute-done((bf16[48,512]{1,0:T(8,128)(2,1)S(1)}, bf16[48,512]{1,0:T(8,128)(2,1)S(1)}, u32[]{:S(2)}, u32[]{:S(2)}) %collective-permute-start.5) | collective-permute-done | bytes 49184 | tf_op jit(solution)/shard_map/ppermute | solution.py:319
  19.6 1.1 %edge.1 = bf16[256,512]{1,0:T(8,128)(2,1)} custom-call(f32[64,512]{1,0:T(8,128)S(1)} %get-tuple-element.32.edges_ref, f32[9,512]{1,0:T(8,128)S(1)} %reshape.14.taps_ref, f32[256,512]{1,0:T(8,128)S(1)} %get-tuple-element.31.gate_ref, bf16[512,512]{1,0:T(8,128)(2,1)S(1)} %copy-done, bf16[512,512]{1,0:T(8,128)(2,1)S(1)} %copy-done.1, ...), custom_call_target="tpu_custom_call" | custom-call | flops 33554432 | bytes 2295808 | tf_op jit(solution)/shard_map/edge/pallas_call | solution.py:19
  (2 shorter events, 0.0 us)
Async XLA Ops:
  0.0 2.2 %collective-permute-start = (bf16[256,512]{1,0:T(8,128)(2,1)}, bf16[256,512]{1,0:T(8,128)(2,1)S(1)}, u32[]{:S(2)}, u32[]{:S(2)}) collective-permute-start(bf16[256,512]{1,0:T(8,128)(2,1)} %bitcast.3), channel_id=1, source_target_pairs={{0,8},{8,0},{16,24},{24,16},{1,9},{9,1},{17,25},{25,17},{2,10},{10... | collective-permute-start | bytes 786440 | tf_op jit(solution)/shard_map/ppermute | solution.py:264
  2.2 14.9 %copy-start.2 = (f32[3,3,512]{2,1,0:T(4,128)S(1)}, f32[3,3,512]{2,1,0:T(4,128)}, u32[]{:S(2)}) copy-start(f32[3,3,512]{2,1,0:T(4,128)} %param.8) | copy-start | bytes 55300
  2.8 12.6 %collective-permute-start.4 = (bf16[256,512]{1,0:T(8,128)(2,1)S(1)}, bf16[256,512]{1,0:T(8,128)(2,1)S(1)}, u32[]{:S(2)}, u32[]{:S(2)}) collective-permute-start(bf16[256,512]{1,0:T(8,128)(2,1)S(1)} %get-tuple-element.28), channel_id=1, source_target_pairs={{0,16},{8,24},{16,0},{24,8},{1,17},{9,25},{17,1},{25,9},{2,18},{10... | collective-permute-start | bytes 786440 | tf_op jit(solution)/shard_map/ppermute | solution.py:301
  5.4 6.1 %collective-permute-start.1 = (bf16[64,512]{1,0:T(8,128)(2,1)S(1)}, bf16[64,512]{1,0:T(8,128)(2,1)S(1)}, u32[]{:S(2)}, u32[]{:S(2)}) collective-permute-start(bf16[64,512]{1,0:T(8,128)(2,1)S(1)} %get-tuple-element.24), channel_id=1, source_target_pairs={{0,1},{1,0},{2,3},{3,2},{8,8},{9,10},{10,9},{11,11},{16,17},{17,16... | collective-permute-start | bytes 196616 | tf_op jit(solution)/shard_map/ppermute | solution.py:299
  8.9 8.2 %copy-start = (bf16[512,512]{1,0:T(8,128)(2,1)S(1)}, bf16[512,512]{1,0:T(8,128)(2,1)}, u32[]{:S(2)}) copy-start(bf16[512,512]{1,0:T(8,128)(2,1)} %wv_ref.3) | copy-start | bytes 1572868
  8.9 8.2 %copy-start.1 = (bf16[512,512]{1,0:T(8,128)(2,1)S(1)}, bf16[512,512]{1,0:T(8,128)(2,1)}, u32[]{:S(2)}) copy-start(bf16[512,512]{1,0:T(8,128)(2,1)} %wo_ref.3) | copy-start | bytes 1572868
  8.9 5.2 %collective-permute-start.2 = (bf16[64,512]{1,0:T(8,128)(2,1)S(1)}, bf16[64,512]{1,0:T(8,128)(2,1)S(1)}, u32[]{:S(2)}, u32[]{:S(2)}) collective-permute-start(bf16[64,512]{1,0:T(8,128)(2,1)S(1)} %get-tuple-element.25), channel_id=1, source_target_pairs={{0,17},{1,16},{2,19},{3,18},{8,24},{9,26},{10,25},{11,27},{16,1},{... | collective-permute-start | bytes 196616 | tf_op jit(solution)/shard_map/ppermute | solution.py:299
  14.2 1.3 %collective-permute-start.3 = (bf16[32,512]{1,0:T(8,128)(2,1)S(1)}, bf16[32,512]{1,0:T(8,128)(2,1)S(1)}, u32[]{:S(2)}, u32[]{:S(2)}) collective-permute-start(bf16[32,512]{1,0:T(8,128)(2,1)S(1)} %get-tuple-element.27), channel_id=1, source_target_pairs={{0,8},{8,0},{16,24},{24,16},{1,9},{9,1},{17,25},{25,17},{2,10},{10... | collective-permute-start | bytes 98312 | tf_op jit(solution)/shard_map/ppermute | solution.py:310
  15.5 4.2 %collective-permute-start.5 = (bf16[48,512]{1,0:T(8,128)(2,1)S(1)}, bf16[48,512]{1,0:T(8,128)(2,1)S(1)}, u32[]{:S(2)}, u32[]{:S(2)}) collective-permute-start(bf16[48,512]{1,0:T(8,128)(2,1)S(1)} %get-tuple-element.34), channel_id=1, source_target_pairs={{0,4},{4,0},{1,5},{5,1},{2,6},{6,2},{3,7},{7,3},{8,12},{12,8},{9,1... | collective-permute-start | bytes 147464 | tf_op jit(solution)/shard_map/ppermute | solution.py:319

commit v7 on v6

--- a/solution.py
+++ b/solution.py
@@ -255,7 +255,7 @@
 def body(latents, spatial_taps, kernel_taps, skip_gain, gate_weight, value_weight, out_weight):
     frames, rows, cols, chans = latents.shape
     lags = kernel_taps.shape[0]
-    n_t, n_w = lax.axis_size("tm"), lax.axis_size("width")
+    n_t, n_h, n_w = lax.axis_size("tm"), lax.axis_size("height"), lax.axis_size("width")
     chips = n_t // 2
     block = frames * rows * cols
     shape = jax.ShapeDtypeStruct
@@ -293,10 +293,15 @@
     )
     columns, wholes = [], []
     for d in range(chips):
-        route = [
-            (i * n_w + j, (i + 2 * d) % n_t * n_w + facing(i % 2, j, n_w)) for i in range(n_t) for j in range(n_w)
-        ]
-        columns.append(lax.ppermute(sent.pop(0), ("tm", "width"), route))
+        route = []
+        for i in range(n_t):
+            for h in range(n_h):
+                for j in range(n_w):
+                    to = facing(i % 2, j, n_w)
+                    row = h ^ 1 if to == j and n_h % 2 == 0 else h
+                    source = (i * n_h + h) * n_w + j
+                    route.append((source, ((i + 2 * d) % n_t * n_h + row) * n_w + to))
+        columns.append(lax.ppermute(sent.pop(0), ("tm", "height", "width"), route))
         if d:
             wholes.append(lax.ppermute(sent.pop(0), "tm", [(i, (i + 2 * d) % n_t) for i in range(n_t)]))
 

time: 21 us -> 19.3 us (0.919)
  starting transfers between devices: 8.2 us -> 6.46 us
    ppermute x2, starting transfers between devices: 3.54 us -> 1.58 us  [body(): columns.append(lax.ppermute(sent.pop(0), ('tm', 'height', 'width'), route))]
    ppermute x1, waiting for transfers between devices: 0.01 us -> 0.27 us  [body(): lax.ppermute(sent.pop(0), 'tm', [(i, (i + 2 * d) % n_t) for i in range(n_...]
    ppermute x1, waiting for transfers between devices: 1.77 us -> 1.54 us  [body(): lax.ppermute(e, 'height', pairs)]
    ppermute x1, starting transfers between devices: 1.56 us -> 1.78 us  [body(): lax.ppermute(e, 'height', pairs)]
  transfers between devices with their start and end apart: 6 -> 6, of which waited for: 4 -> 5; matrix products, arithmetic and copies ran while one was open for 0% -> 0% of each run, Pallas kernels for 12% -> 13%
where the time goes in v7:
time: 19.3 us; the launch traced here: 19 us
  waiting for transfers between devices  8.23 us (43%)
  starting transfers between devices  6.46 us (33%)
  Pallas kernels  4.24 us (22%)
    ppermute x2, waiting for transfers between devices, body(): columns.append(lax.ppermute(sent.pop(0), ('tm', 'height', 'width'), route))  5.22 us
    pallas_call x6, Pallas kernels, call(): pl.pallas_call(kernel, out_shape=tuple(outs), in_specs=[HBM] * far + [VME...  4.24 us
    ppermute x1, starting transfers between devices, body(): lax.ppermute(sent.pop(0), 'tm', [(i, (i + 2 * d) % n_t) for i in range(n_...  2.58 us
    ppermute x1, starting transfers between devices, body(): lax.ppermute(e, 'height', pairs)  1.78 us
    ppermute x2, starting transfers between devices, body(): columns.append(lax.ppermute(sent.pop(0), ('tm', 'height', 'width'), route))  1.58 us
    ppermute x1, waiting for transfers between devices, body(): lax.ppermute(e, 'height', pairs)  1.54 us
    ppermute x1, waiting for transfers between devices, body(): other = lax.ppermute(other, 'tm', [(i, i ^ 1) for i in range(n_t)])  1.19 us
    ppermute x1, starting transfers between devices, body(): partner = lax.ppermute(x, 'tm', [(i, i ^ 1) for i in range(n_t)])  0.45 us
  transfers between devices with their start and end apart: 6, of which 5 were waited for; matrix products, arithmetic and copies ran while one was open for 0% of the time, Pallas kernels for 13%

profile of v7, /device:TPU:0, one launch (start us, length us, event | category | flops | bytes accessed | tf_op | source)
XLA Modules:
  0.0 19.0 jit_solution(16641846359806939329)
XLA Ops:
  0.0 0.5 %collective-permute-start = (bf16[256,512]{1,0:T(8,128)(2,1)}, bf16[256,512]{1,0:T(8,128)(2,1)S(1)}, u32[]{:S(2)}, u32[]{:S(2)}) collective-permute-start(bf16[256,512]{1,0:T(8,128)(2,1)} %bitcast.3), channel_id=1, source_target_pairs={{0,8},{8,0},{16,24},{24,16},{1,9},{9,1},{17,25},{25,17},{2,10},{10... | collective-permute-start | bytes 786440 | tf_op jit(solution)/shard_map/ppermute | solution.py:264
  0.5 1.7 %early.1 = (f32[256,512]{1,0:T(8,128)S(1)}, f32[512,512]{1,0:T(8,128)S(1)}, f32[24,8,512]{2,1,0:T(8,128)S(1)}, f32[32,512]{1,0:T(8,128)S(1)}) custom-call(bf16[16,512]{1,0:T(8,128)(2,1)} %refs_0_.1, f32[1,512]{1,0:T(1,128)} %bitcast.5, bf16[256,512]{1,0:T(8,128)(2,1)} %bitcast.4, bf16[512,512]{1,0:T(8,128)(2,1)} %refs_3_.1), custom_call_target="tpu_custom_call" | custom-call | flops 134217728 | bytes 2836480 | tf_op jit(solution)/shard_map/early/pallas_call | solution.py:19
  2.2 0.0 collective-permute-done.partner_ref
  2.2 0.0 copy-start.2
  2.2 0.6 %mix.1 = (f32[256,512]{1,0:T(8,128)S(1)}, bf16[64,512]{1,0:T(8,128)(2,1)S(1)}, bf16[64,512]{1,0:T(8,128)(2,1)S(1)}, bf16[256,512]{1,0:T(8,128)(2,1)S(1)}) custom-call(bf16[256,512]{1,0:T(8,128)(2,1)S(1)} %collective-permute-done.partner_ref, f32[512,512]{1,0:T(8,128)S(1)} %get-tuple-element.20.fields_ref, f32[24,8,512]{2,1,0:T(8,128)S(1)} %get-tuple-element.21.table_ref, ...), custom_call_target="tpu_custom_call" | custom-call | flops 2097152 | bytes 2686976 | tf_op jit(solution)/shard_map/mix/pallas_call | solution.py:19
  2.8 2.6 %collective-permute-start.4 = (bf16[256,512]{1,0:T(8,128)(2,1)S(1)}, bf16[256,512]{1,0:T(8,128)(2,1)S(1)}, u32[]{:S(2)}, u32[]{:S(2)}) collective-permute-start(bf16[256,512]{1,0:T(8,128)(2,1)S(1)} %get-tuple-element.28), channel_id=1, source_target_pairs={{0,16},{8,24},{16,0},{24,8},{1,17},{9,25},{17,1},{25,9},{2,18},{10... | collective-permute-start | bytes 786440 | tf_op jit(solution)/shard_map/ppermute | solution.py:306
  5.4 1.6 %collective-permute-start.1 = (bf16[64,512]{1,0:T(8,128)(2,1)S(1)}, bf16[64,512]{1,0:T(8,128)(2,1)S(1)}, u32[]{:S(2)}, u32[]{:S(2)}) collective-permute-start(bf16[64,512]{1,0:T(8,128)(2,1)S(1)} %get-tuple-element.24), channel_id=1, source_target_pairs={{0,1},{1,0},{2,3},{3,2},{4,5},{5,4},{6,7},{7,6},{8,12},{9,10},{10,... | collective-permute-start | bytes 196616 | tf_op jit(solution)/shard_map/ppermute | solution.py:304
  7.0 0.0 copy-start
  7.0 0.0 copy-start.1
  7.0 0.0 collective-permute-start.2
  7.0 2.7 %collective-permute-done.1.refs_0_ = bf16[64,512]{1,0:T(8,128)(2,1)S(1)} collective-permute-done((bf16[64,512]{1,0:T(8,128)(2,1)S(1)}, bf16[64,512]{1,0:T(8,128)(2,1)S(1)}, u32[]{:S(2)}, u32[]{:S(2)}) %collective-permute-start.1) | collective-permute-done | bytes 65568 | tf_op jit(solution)/shard_map/ppermute | solution.py:304
  9.6 2.5 %collective-permute-done.2.refs_1_ = bf16[64,512]{1,0:T(8,128)(2,1)S(1)} collective-permute-done((bf16[64,512]{1,0:T(8,128)(2,1)S(1)}, bf16[64,512]{1,0:T(8,128)(2,1)S(1)}, u32[]{:S(2)}, u32[]{:S(2)}) %collective-permute-start.2) | collective-permute-done | bytes 65568 | tf_op jit(solution)/shard_map/ppermute | solution.py:304
  12.2 0.1 collective-permute-start.3
  12.3 1.2 %collective-permute-done.3.other_ref = bf16[32,512]{1,0:T(8,128)(2,1)S(1)} collective-permute-done((bf16[32,512]{1,0:T(8,128)(2,1)S(1)}, bf16[32,512]{1,0:T(8,128)(2,1)S(1)}, u32[]{:S(2)}, u32[]{:S(2)}) %collective-permute-start.3) | collective-permute-done | bytes 32800 | tf_op jit(solution)/shard_map/ppermute | solution.py:315
  13.5 0.3 %collective-permute-done.4.refs_0_ = bf16[256,512]{1,0:T(8,128)(2,1)S(1)} collective-permute-done((bf16[256,512]{1,0:T(8,128)(2,1)S(1)}, bf16[256,512]{1,0:T(8,128)(2,1)S(1)}, u32[]{:S(2)}, u32[]{:S(2)}) %collective-permute-start.4) | collective-permute-done | bytes 262176 | tf_op jit(solution)/shard_map/ppermute | solution.py:306
  13.8 0.1 border.1
  13.8 1.8 %collective-permute-start.5 = (bf16[48,512]{1,0:T(8,128)(2,1)S(1)}, bf16[48,512]{1,0:T(8,128)(2,1)S(1)}, u32[]{:S(2)}, u32[]{:S(2)}) collective-permute-start(bf16[48,512]{1,0:T(8,128)(2,1)S(1)} %get-tuple-element.34), channel_id=1, source_target_pairs={{0,4},{4,0},{1,5},{5,1},{2,6},{6,2},{3,7},{7,3},{8,12},{12,8},{9,1... | collective-permute-start | bytes 147464 | tf_op jit(solution)/shard_map/ppermute | solution.py:324
  15.6 0.0 copy-done.2
  15.6 0.0 copy-done
  15.6 0.0 copy-done.1
  15.6 0.8 %inner.1 = (bf16[256,512]{1,0:T(8,128)(2,1)S(1)}, f32[64,512]{1,0:T(8,128)S(1)}) custom-call(f32[256,512]{1,0:T(8,128)S(1)} %get-tuple-element.23.mine_ref, f32[32,512]{1,0:T(8,128)S(1)} %get-tuple-element.29.low_ref, f32[32,512]{1,0:T(8,128)S(1)} %get-tuple-element.30.high_ref, f32[9,512]{1,0:T(8,128)S(1)} %reshape.14.taps_ref, ...), custom_call_target="tpu_custom_call" | custom-call | flops 268435456 | bytes 2902016 | tf_op jit(solution)/shard_map/inner/pallas_call | solution.py:19
  16.4 1.5 %collective-permute-done.5.refs_0_ = bf16[48,512]{1,0:T(8,128)(2,1)S(1)} collective-permute-done((bf16[48,512]{1,0:T(8,128)(2,1)S(1)}, bf16[48,512]{1,0:T(8,128)(2,1)S(1)}, u32[]{:S(2)}, u32[]{:S(2)}) %collective-permute-start.5) | collective-permute-done | bytes 49184 | tf_op jit(solution)/shard_map/ppermute | solution.py:324
  18.0 1.1 %edge.1 = bf16[256,512]{1,0:T(8,128)(2,1)} custom-call(f32[64,512]{1,0:T(8,128)S(1)} %get-tuple-element.32.edges_ref, f32[9,512]{1,0:T(8,128)S(1)} %reshape.14.taps_ref, f32[256,512]{1,0:T(8,128)S(1)} %get-tuple-element.31.gate_ref, bf16[512,512]{1,0:T(8,128)(2,1)S(1)} %copy-done, bf16[512,512]{1,0:T(8,128)(2,1)S(1)} %copy-done.1, ...), custom_call_target="tpu_custom_call" | custom-call | flops 33554432 | bytes 2295808 | tf_op jit(solution)/shard_map/edge/pallas_call | solution.py:19
  (2 shorter events, 0.0 us)
Async XLA Ops:
  0.0 2.2 %collective-permute-start = (bf16[256,512]{1,0:T(8,128)(2,1)}, bf16[256,512]{1,0:T(8,128)(2,1)S(1)}, u32[]{:S(2)}, u32[]{:S(2)}) collective-permute-start(bf16[256,512]{1,0:T(8,128)(2,1)} %bitcast.3), channel_id=1, source_target_pairs={{0,8},{8,0},{16,24},{24,16},{1,9},{9,1},{17,25},{25,17},{2,10},{10... | collective-permute-start | bytes 786440 | tf_op jit(solution)/shard_map/ppermute | solution.py:264
  2.2 13.4 %copy-start.2 = (f32[3,3,512]{2,1,0:T(4,128)S(1)}, f32[3,3,512]{2,1,0:T(4,128)}, u32[]{:S(2)}) copy-start(f32[3,3,512]{2,1,0:T(4,128)} %param.8) | copy-start | bytes 55300
  2.8 11.0 %collective-permute-start.4 = (bf16[256,512]{1,0:T(8,128)(2,1)S(1)}, bf16[256,512]{1,0:T(8,128)(2,1)S(1)}, u32[]{:S(2)}, u32[]{:S(2)}) collective-permute-start(bf16[256,512]{1,0:T(8,128)(2,1)S(1)} %get-tuple-element.28), channel_id=1, source_target_pairs={{0,16},{8,24},{16,0},{24,8},{1,17},{9,25},{17,1},{25,9},{2,18},{10... | collective-permute-start | bytes 786440 | tf_op jit(solution)/shard_map/ppermute | solution.py:306
  5.4 4.3 %collective-permute-start.1 = (bf16[64,512]{1,0:T(8,128)(2,1)S(1)}, bf16[64,512]{1,0:T(8,128)(2,1)S(1)}, u32[]{:S(2)}, u32[]{:S(2)}) collective-permute-start(bf16[64,512]{1,0:T(8,128)(2,1)S(1)} %get-tuple-element.24), channel_id=1, source_target_pairs={{0,1},{1,0},{2,3},{3,2},{4,5},{5,4},{6,7},{7,6},{8,12},{9,10},{10,... | collective-permute-start | bytes 196616 | tf_op jit(solution)/shard_map/ppermute | solution.py:304
  7.0 8.7 %copy-start = (bf16[512,512]{1,0:T(8,128)(2,1)S(1)}, bf16[512,512]{1,0:T(8,128)(2,1)}, u32[]{:S(2)}) copy-start(bf16[512,512]{1,0:T(8,128)(2,1)} %wv_ref.3) | copy-start | bytes 1572868
  7.0 8.7 %copy-start.1 = (bf16[512,512]{1,0:T(8,128)(2,1)S(1)}, bf16[512,512]{1,0:T(8,128)(2,1)}, u32[]{:S(2)}) copy-start(bf16[512,512]{1,0:T(8,128)(2,1)} %wo_ref.3) | copy-start | bytes 1572868
  7.0 5.2 %collective-permute-start.2 = (bf16[64,512]{1,0:T(8,128)(2,1)S(1)}, bf16[64,512]{1,0:T(8,128)(2,1)S(1)}, u32[]{:S(2)}, u32[]{:S(2)}) collective-permute-start(bf16[64,512]{1,0:T(8,128)(2,1)S(1)} %get-tuple-element.25), channel_id=1, source_target_pairs={{0,17},{1,16},{2,19},{3,18},{4,21},{5,20},{6,23},{7,22},{8,28},{9,... | collective-permute-start | bytes 196616 | tf_op jit(solution)/shard_map/ppermute | solution.py:304
  12.2 1.3 %collective-permute-start.3 = (bf16[32,512]{1,0:T(8,128)(2,1)S(1)}, bf16[32,512]{1,0:T(8,128)(2,1)S(1)}, u32[]{:S(2)}, u32[]{:S(2)}) collective-permute-start(bf16[32,512]{1,0:T(8,128)(2,1)S(1)} %get-tuple-element.27), channel_id=1, source_target_pairs={{0,8},{8,0},{16,24},{24,16},{1,9},{9,1},{17,25},{25,17},{2,10},{10... | collective-permute-start | bytes 98312 | tf_op jit(solution)/shard_map/ppermute | solution.py:315
  13.8 4.2 %collective-permute-start.5 = (bf16[48,512]{1,0:T(8,128)(2,1)S(1)}, bf16[48,512]{1,0:T(8,128)(2,1)S(1)}, u32[]{:S(2)}, u32[]{:S(2)}) collective-permute-start(bf16[48,512]{1,0:T(8,128)(2,1)S(1)} %get-tuple-element.34), channel_id=1, source_target_pairs={{0,4},{4,0},{1,5},{5,1},{2,6},{6,2},{3,7},{7,3},{8,12},{12,8},{9,1... | collective-permute-start | bytes 147464 | tf_op jit(solution)/shard_map/ppermute | solution.py:324

commit v8 on v7

--- a/solution.py
+++ b/solution.py
@@ -8,6 +8,7 @@
 from jax.sharding import PartitionSpec as P
 
 LANES = 128
+LATER = 8 * 10**9
 F32, BF16 = jnp.float32, jnp.bfloat16
 VMEM = pl.BlockSpec(memory_space=pltpu.VMEM)
 HBM = pl.BlockSpec(memory_space=pltpu.HBM)
@@ -98,13 +99,14 @@
     gate_ref[...] = v / (1.0 + jnp.exp(-v))
 
 
-def mix_kernel(frames, rows, cols, partner_ref, fields_ref, table_ref, side_ref, mine_ref, *refs):
+def mix_kernel(frames, rows, cols, rounds_h, partner_ref, fields_ref, table_ref, side_ref, mine_ref, *refs):
     *outs, held = refs
     sites = rows * cols
     lines = frames * rows
     block = frames * sites
     pad = 2 * frames
     shift = jnp.where(second(), frames, -frames)
+    odd = position("height")[0]
     for lane in range(0, mine_ref.shape[1], LANES):
         span = slice(lane, lane + LANES)
         held[...] = partner_ref[:, span].astype(F32)
@@ -123,7 +125,10 @@
             for t in range(frames):
                 held[t * sites : (t + 1) * sites, :] = totals[t].reshape(sites, LANES)
             if d:
-                outs[2 * d][:, span] = held[...].astype(BF16)
+                outs[3 * d][:, span] = held[...].astype(BF16)
+                ends = [jnp.concatenate([t[r] for t in totals], axis=0) for r in (0, rows - 1)]
+                line = [jnp.where(odd, *(ends[::-1] if k else ends)) for k in range(rounds_h)]
+                outs[3 * d - 1][:, span] = jnp.concatenate(line, axis=0).astype(BF16)
             else:
                 mine_ref[:, span] = held[...]
             ends = []
@@ -135,7 +140,7 @@
                         end = end + table_ref[base + t - s, :, span] * far[s * rows : (s + 1) * rows]
                 ends.append(end)
             column = jnp.concatenate([outer_column(held, lines, cols)] + ends, axis=0)
-            outs[2 * d - 1 if d else 0][:, span] = column.astype(BF16)
+            outs[3 * d - 2 if d else 0][:, span] = column.astype(BF16)
 
 
 def later(d, value):
@@ -154,30 +159,26 @@
     other_ref[...] = total[lines:].astype(BF16)
 
 
-def border_kernel(frames, rows, cols, mine_ref, own_ref, other_ref, *refs):
-    n = sum(ref.shape == mine_ref.shape for ref in refs)
-    wholes, (low_ref, high_ref, *outs) = refs[:n], refs[n:]
+def border_kernel(frames, rows, cols, chips, mine_ref, own_ref, other_ref, *refs):
+    arrived, (low_ref, high_ref, *outs) = refs[: chips - 1], refs[chips - 1 :]
     sites = rows * cols
     odd, _, _ = position("height")
     right, own, other = on_right(), own_ref[...], other_ref[...].astype(F32)
     low, high = jnp.where(right, other, own), jnp.where(right, own, other)
     low_ref[...] = low
     high_ref[...] = high
-    fill = jnp.zeros((outs[0].shape[0] - frames * cols - 2 * frames, low.shape[1]), F32)
-    ends = []
+    size = frames * cols
+    fill = jnp.zeros((outs[0].shape[0] - size - 2 * frames, low.shape[1]), F32)
+    lines, corners = [], []
     for r in (0, rows - 1):
-        lines = []
-        for t in range(frames):
-            at = t * sites + r * cols
-            line = mine_ref[at : at + cols]
-            for d, ref in enumerate(wholes, 1):
-                line = line + later(d, ref[at : at + cols].astype(F32))
-            lines.append(line)
-        lefts = [low[t * rows + r : t * rows + r + 1] for t in range(frames)]
-        rights = [high[t * rows + r : t * rows + r + 1] for t in range(frames)]
-        ends.append(jnp.concatenate(lines + lefts + rights + [fill], axis=0))
+        lines.append(jnp.concatenate([mine_ref[t * sites + r * cols : t * sites + (r + 1) * cols] for t in range(frames)]))
+        ends = [side[t * rows + r : t * rows + r + 1] for side in (low, high) for t in range(frames)]
+        corners.append(jnp.concatenate(ends + [fill]))
     for k, out in enumerate(outs):
-        out[...] = (jnp.where(odd, ends[1], ends[0]) if k else jnp.where(odd, ends[0], ends[1])).astype(BF16)
+        line = jnp.where(odd, *(lines[::-1] if k else lines))
+        for d, ref in enumerate(arrived, 1):
+            line = line + later(d, ref[k * size : (k + 1) * size].astype(F32))
+        out[...] = jnp.concatenate([line, jnp.where(odd, *(corners[::-1] if k else corners))]).astype(BF16)
 
 
 def shifted(line, left, right):
@@ -283,27 +284,29 @@
 
     h_rounds = swaps("height")
     column = shape((2 * lines, chans), BF16)
+    row = shape((len(h_rounds) * frames * cols, chans), BF16)
     mine, *sent = call(
-        functools.partial(mix_kernel, frames, rows, cols),
+        functools.partial(mix_kernel, frames, rows, cols, len(h_rounds)),
         "mix",
-        [shape((block, chans), F32), column] + [column, shape((block, chans), BF16)] * (chips - 1),
+        [shape((block, chans), F32), column] + [column, row, shape((block, chans), BF16)] * (chips - 1),
         [pltpu.VMEM((block, LANES), F32)],
         [partner, fields, table, side],
         2 * chips * frames * x.size,
     )
-    columns, wholes = [], []
+    columns, arrived, wholes = [], [], []
     for d in range(chips):
         route = []
         for i in range(n_t):
             for h in range(n_h):
                 for j in range(n_w):
                     to = facing(i % 2, j, n_w)
-                    row = h ^ 1 if to == j and n_h % 2 == 0 else h
+                    beside = h ^ 1 if to == j and n_h % 2 == 0 else h
                     source = (i * n_h + h) * n_w + j
-                    route.append((source, ((i + 2 * d) % n_t * n_h + row) * n_w + to))
+                    route.append((source, ((i + 2 * d) % n_t * n_h + beside) * n_w + to))
         columns.append(lax.ppermute(sent.pop(0), ("tm", "height", "width"), route))
         if d:
-            wholes.append(lax.ppermute(sent.pop(0), "tm", [(i, (i + 2 * d) % n_t) for i in range(n_t)]))
+            for kept in (arrived, wholes):
+                kept.append(lax.ppermute(sent.pop(0), "tm", [(i, (i + 2 * d) % n_t) for i in range(n_t)]))
 
     own, other = call(
         functools.partial(side_kernel, lines),
@@ -311,15 +314,16 @@
         [shape((lines, chans), F32), shape((lines, chans), BF16)],
         [],
         columns,
+        LATER,
     )
     other = lax.ppermute(other, "tm", [(i, i ^ 1) for i in range(n_t)])
     size = -(-(frames * cols + 2 * frames) // 16) * 16
     low, high, *ends = call(
-        functools.partial(border_kernel, frames, rows, cols),
+        functools.partial(border_kernel, frames, rows, cols, chips),
         "border",
         [shape((lines, chans), F32)] * 2 + [shape((size, chans), BF16)] * len(h_rounds),
         [],
-        [mine, own, other] + wholes,
+        [mine, own, other] + arrived,
     )
     ends = [lax.ppermute(e, "height", pairs) for e, pairs in zip(ends, h_rounds)]
 

time: 19.3 us -> 18.9 us (0.979)
  waiting for transfers between devices: 8.23 us -> 6.11 us
  starting transfers between devices: 6.46 us -> 8.2 us
    ppermute x2, waiting for transfers between devices: 5.22 us -> 1.79 us  [body(): columns.append(lax.ppermute(sent.pop(0), ('tm', 'height', 'width'), route))]
    ppermute x1 -> x2, waiting for transfers between devices: 0.27 us -> 3.67 us  [body(): lax.ppermute(sent.pop(0), 'tm', [(i, (i + 2 * d) % n_t) for i in range(n_...]
    ppermute x2, starting transfers between devices: 1.58 us -> 4.05 us  [body(): columns.append(lax.ppermute(sent.pop(0), ('tm', 'height', 'width'), route))]
    ppermute x1, waiting for transfers between devices: 1.54 us -> 0.01 us  [body(): lax.ppermute(e, 'height', pairs)]
    ppermute x1 -> x2, starting transfers between devices: 2.58 us -> 2.03 us  [body(): lax.ppermute(sent.pop(0), 'tm', [(i, (i + 2 * d) % n_t) for i in range(n_...]
    ppermute x1, waiting for transfers between devices: 1.19 us -> 0.64 us  [body(): other = lax.ppermute(other, 'tm', [(i, i ^ 1) for i in range(n_t)])]
  transfers between devices with their start and end apart: 6 -> 7, of which waited for: 5 -> 4; matrix products, arithmetic and copies ran while one was open for 0% -> 0% of each run, Pallas kernels for 13% -> 14%
where the time goes in v8:
time: 18.9 us; the launch traced here: 18.7 us
  starting transfers between devices  8.2 us (43%)
  waiting for transfers between devices  6.11 us (32%)
  Pallas kernels  4.25 us (22%)
    pallas_call x6, Pallas kernels, call(): pl.pallas_call(kernel, out_shape=tuple(outs), in_specs=[HBM] * far + [VME...  4.25 us
    ppermute x2, starting transfers between devices, body(): columns.append(lax.ppermute(sent.pop(0), ('tm', 'height', 'width'), route))  4.05 us
    ppermute x2, waiting for transfers between devices, body(): lax.ppermute(sent.pop(0), 'tm', [(i, (i + 2 * d) % n_t) for i in range(n_...  3.67 us
    ppermute x2, starting transfers between devices, body(): lax.ppermute(sent.pop(0), 'tm', [(i, (i + 2 * d) % n_t) for i in range(n_...  2.03 us
    ppermute x2, waiting for transfers between devices, body(): columns.append(lax.ppermute(sent.pop(0), ('tm', 'height', 'width'), route))  1.79 us
    ppermute x1, starting transfers between devices, body(): lax.ppermute(e, 'height', pairs)  1.61 us
    ppermute x1, waiting for transfers between devices, body(): other = lax.ppermute(other, 'tm', [(i, i ^ 1) for i in range(n_t)])  0.64 us
    ppermute x1, starting transfers between devices, body(): partner = lax.ppermute(x, 'tm', [(i, i ^ 1) for i in range(n_t)])  0.45 us
  transfers between devices with their start and end apart: 7, of which 4 were waited for; matrix products, arithmetic and copies ran while one was open for 0% of the time, Pallas kernels for 14%

profile of v8, /device:TPU:0, one launch (start us, length us, event | category | flops | bytes accessed | tf_op | source)
XLA Modules:
  0.0 18.7 jit_solution(7393496991469680396)
XLA Ops:
  0.0 0.5 %collective-permute-start = (bf16[256,512]{1,0:T(8,128)(2,1)}, bf16[256,512]{1,0:T(8,128)(2,1)S(1)}, u32[]{:S(2)}, u32[]{:S(2)}) collective-permute-start(bf16[256,512]{1,0:T(8,128)(2,1)} %bitcast.3), channel_id=1, source_target_pairs={{0,8},{8,0},{16,24},{24,16},{1,9},{9,1},{17,25},{25,17},{2,10},{10... | collective-permute-start | bytes 786440 | tf_op jit(solution)/shard_map/ppermute | solution.py:265
  0.5 1.7 %early.1 = (f32[256,512]{1,0:T(8,128)S(1)}, f32[512,512]{1,0:T(8,128)S(1)}, f32[24,8,512]{2,1,0:T(8,128)S(1)}, f32[32,512]{1,0:T(8,128)S(1)}) custom-call(bf16[16,512]{1,0:T(8,128)(2,1)} %refs_0_.1, f32[1,512]{1,0:T(1,128)} %bitcast.5, bf16[256,512]{1,0:T(8,128)(2,1)} %bitcast.4, bf16[512,512]{1,0:T(8,128)(2,1)} %refs_3_.1), custom_call_target="tpu_custom_call" | custom-call | flops 134217728 | bytes 2836480 | tf_op jit(solution)/shard_map/early/pallas_call | solution.py:20
  2.2 0.0 collective-permute-done.partner_ref
  2.2 0.6 %mix.1 = (f32[256,512]{1,0:T(8,128)S(1)}, bf16[64,512]{1,0:T(8,128)(2,1)S(1)}, bf16[64,512]{1,0:T(8,128)(2,1)S(1)}, bf16[32,512]{1,0:T(8,128)(2,1)S(1)}, bf16[256,512]{1,0:T(8,128)(2,1)S(1)}) custom-call(bf16[256,512]{1,0:T(8,128)(2,1)S(1)} %collective-permute-done.partner_ref, f32[512,512]{1,0:T(8,128)S(1)} %get-tuple-element.21.fields_ref, ...), custom_call_target="tpu_custom_call" | custom-call | flops 2097152 | bytes 2719744 | tf_op jit(solution)/shard_map/mix/pallas_call | solution.py:20
  2.8 2.6 %collective-permute-start.1 = (bf16[64,512]{1,0:T(8,128)(2,1)S(1)}, bf16[64,512]{1,0:T(8,128)(2,1)S(1)}, u32[]{:S(2)}, u32[]{:S(2)}) collective-permute-start(bf16[64,512]{1,0:T(8,128)(2,1)S(1)} %get-tuple-element.25), channel_id=1, source_target_pairs={{0,1},{1,0},{2,3},{3,2},{4,5},{5,4},{6,7},{7,6},{8,12},{9,10},{10,... | collective-permute-start | bytes 196616 | tf_op jit(solution)/shard_map/ppermute | solution.py:306
  5.4 1.4 %collective-permute-start.2 = (bf16[64,512]{1,0:T(8,128)(2,1)S(1)}, bf16[64,512]{1,0:T(8,128)(2,1)S(1)}, u32[]{:S(2)}, u32[]{:S(2)}) collective-permute-start(bf16[64,512]{1,0:T(8,128)(2,1)S(1)} %get-tuple-element.26), channel_id=1, source_target_pairs={{0,17},{1,16},{2,19},{3,18},{4,21},{5,20},{6,23},{7,22},{8,28},{9,... | collective-permute-start | bytes 196616 | tf_op jit(solution)/shard_map/ppermute | solution.py:306
  6.8 0.1 collective-permute-start.4
  7.0 1.9 %collective-permute-start.5 = (bf16[256,512]{1,0:T(8,128)(2,1)S(1)}, bf16[256,512]{1,0:T(8,128)(2,1)S(1)}, u32[]{:S(2)}, u32[]{:S(2)}) collective-permute-start(bf16[256,512]{1,0:T(8,128)(2,1)S(1)} %get-tuple-element.33), channel_id=1, source_target_pairs={{0,16},{8,24},{16,0},{24,8},{1,17},{9,25},{17,1},{25,9},{2,18},{10... | collective-permute-start | bytes 786440 | tf_op jit(solution)/shard_map/ppermute | solution.py:309
  8.9 0.0 collective-permute-done.1.refs_0_
  8.9 1.8 %collective-permute-done.2.refs_1_ = bf16[64,512]{1,0:T(8,128)(2,1)S(1)} collective-permute-done((bf16[64,512]{1,0:T(8,128)(2,1)S(1)}, bf16[64,512]{1,0:T(8,128)(2,1)S(1)}, u32[]{:S(2)}, u32[]{:S(2)}) %collective-permute-start.2) | collective-permute-done | bytes 65568 | tf_op jit(solution)/shard_map/ppermute | solution.py:306
  10.7 0.0 copy-start.1
  10.7 0.0 copy-start
  10.7 0.1 collective-permute-start.3
  10.8 0.6 %collective-permute-done.4.refs_0_ = bf16[32,512]{1,0:T(8,128)(2,1)S(1)} collective-permute-done((bf16[32,512]{1,0:T(8,128)(2,1)S(1)}, bf16[32,512]{1,0:T(8,128)(2,1)S(1)}, u32[]{:S(2)}, u32[]{:S(2)}) %collective-permute-start.4) | collective-permute-done | bytes 32800 | tf_op jit(solution)/shard_map/ppermute | solution.py:309
  11.4 0.6 %collective-permute-done.3.other_ref = bf16[32,512]{1,0:T(8,128)(2,1)S(1)} collective-permute-done((bf16[32,512]{1,0:T(8,128)(2,1)S(1)}, bf16[32,512]{1,0:T(8,128)(2,1)S(1)}, u32[]{:S(2)}, u32[]{:S(2)}) %collective-permute-start.3) | collective-permute-done | bytes 32800 | tf_op jit(solution)/shard_map/ppermute | solution.py:319
  12.0 0.0 copy-start.2
  12.1 1.6 %collective-permute-start.6 = (bf16[48,512]{1,0:T(8,128)(2,1)S(1)}, bf16[48,512]{1,0:T(8,128)(2,1)S(1)}, u32[]{:S(2)}, u32[]{:S(2)}) collective-permute-start(bf16[48,512]{1,0:T(8,128)(2,1)S(1)} %get-tuple-element.36), channel_id=1, source_target_pairs={{0,4},{4,0},{1,5},{5,1},{2,6},{6,2},{3,7},{7,3},{8,12},{12,8},{9,1... | collective-permute-start | bytes 147464 | tf_op jit(solution)/shard_map/ppermute | solution.py:328
  13.7 0.0 copy-done.2
  13.7 3.1 %collective-permute-done.5.refs_0_ = bf16[256,512]{1,0:T(8,128)(2,1)S(1)} collective-permute-done((bf16[256,512]{1,0:T(8,128)(2,1)S(1)}, bf16[256,512]{1,0:T(8,128)(2,1)S(1)}, u32[]{:S(2)}, u32[]{:S(2)}) %collective-permute-start.5) | collective-permute-done | bytes 262176 | tf_op jit(solution)/shard_map/ppermute | solution.py:309
  16.8 0.0 copy-done.1
  16.8 0.0 copy-done
  16.8 0.8 %inner.1 = (bf16[256,512]{1,0:T(8,128)(2,1)S(1)}, f32[64,512]{1,0:T(8,128)S(1)}) custom-call(f32[256,512]{1,0:T(8,128)S(1)} %get-tuple-element.24.mine_ref, f32[32,512]{1,0:T(8,128)S(1)} %get-tuple-element.30.low_ref, f32[32,512]{1,0:T(8,128)S(1)} %get-tuple-element.31.high_ref, f32[9,512]{1,0:T(8,128)S(1)} %reshape.14.taps_ref, ...), custom_call_target="tpu_custom_call" | custom-call | flops 268435456 | bytes 2902016 | tf_op jit(solution)/shard_map/inner/pallas_call | solution.py:20
  17.6 0.0 collective-permute-done.6.refs_0_
  17.6 1.1 %edge.1 = bf16[256,512]{1,0:T(8,128)(2,1)} custom-call(f32[64,512]{1,0:T(8,128)S(1)} %get-tuple-element.34.edges_ref, f32[9,512]{1,0:T(8,128)S(1)} %reshape.14.taps_ref, f32[256,512]{1,0:T(8,128)S(1)} %get-tuple-element.32.gate_ref, bf16[512,512]{1,0:T(8,128)(2,1)S(1)} %copy-done, bf16[512,512]{1,0:T(8,128)(2,1)S(1)} %copy-done.1, ...), custom_call_target="tpu_custom_call" | custom-call | flops 33554432 | bytes 2295808 | tf_op jit(solution)/shard_map/edge/pallas_call | solution.py:20
  (3 shorter events, 0.1 us)
Async XLA Ops:
  0.0 2.2 %collective-permute-start = (bf16[256,512]{1,0:T(8,128)(2,1)}, bf16[256,512]{1,0:T(8,128)(2,1)S(1)}, u32[]{:S(2)}, u32[]{:S(2)}) collective-permute-start(bf16[256,512]{1,0:T(8,128)(2,1)} %bitcast.3), channel_id=1, source_target_pairs={{0,8},{8,0},{16,24},{24,16},{1,9},{9,1},{17,25},{25,17},{2,10},{10... | collective-permute-start | bytes 786440 | tf_op jit(solution)/shard_map/ppermute | solution.py:265
  2.8 6.1 %collective-permute-start.1 = (bf16[64,512]{1,0:T(8,128)(2,1)S(1)}, bf16[64,512]{1,0:T(8,128)(2,1)S(1)}, u32[]{:S(2)}, u32[]{:S(2)}) collective-permute-start(bf16[64,512]{1,0:T(8,128)(2,1)S(1)} %get-tuple-element.25), channel_id=1, source_target_pairs={{0,1},{1,0},{2,3},{3,2},{4,5},{5,4},{6,7},{7,6},{8,12},{9,10},{10,... | collective-permute-start | bytes 196616 | tf_op jit(solution)/shard_map/ppermute | solution.py:306
  5.4 5.2 %collective-permute-start.2 = (bf16[64,512]{1,0:T(8,128)(2,1)S(1)}, bf16[64,512]{1,0:T(8,128)(2,1)S(1)}, u32[]{:S(2)}, u32[]{:S(2)}) collective-permute-start(bf16[64,512]{1,0:T(8,128)(2,1)S(1)} %get-tuple-element.26), channel_id=1, source_target_pairs={{0,17},{1,16},{2,19},{3,18},{4,21},{5,20},{6,23},{7,22},{8,28},{9,... | collective-permute-start | bytes 196616 | tf_op jit(solution)/shard_map/ppermute | solution.py:306
  6.8 4.5 %collective-permute-start.4 = (bf16[32,512]{1,0:T(8,128)(2,1)S(1)}, bf16[32,512]{1,0:T(8,128)(2,1)S(1)}, u32[]{:S(2)}, u32[]{:S(2)}) collective-permute-start(bf16[32,512]{1,0:T(8,128)(2,1)S(1)} %get-tuple-element.29), channel_id=1, source_target_pairs={{0,16},{8,24},{16,0},{24,8},{1,17},{9,25},{17,1},{25,9},{2,18},{10... | collective-permute-start | bytes 98312 | tf_op jit(solution)/shard_map/ppermute | solution.py:309
  7.0 9.8 %collective-permute-start.5 = (bf16[256,512]{1,0:T(8,128)(2,1)S(1)}, bf16[256,512]{1,0:T(8,128)(2,1)S(1)}, u32[]{:S(2)}, u32[]{:S(2)}) collective-permute-start(bf16[256,512]{1,0:T(8,128)(2,1)S(1)} %get-tuple-element.33), channel_id=1, source_target_pairs={{0,16},{8,24},{16,0},{24,8},{1,17},{9,25},{17,1},{25,9},{2,18},{10... | collective-permute-start | bytes 786440 | tf_op jit(solution)/shard_map/ppermute | solution.py:309
  10.7 6.1 %copy-start.1 = (bf16[512,512]{1,0:T(8,128)(2,1)S(1)}, bf16[512,512]{1,0:T(8,128)(2,1)}, u32[]{:S(2)}) copy-start(bf16[512,512]{1,0:T(8,128)(2,1)} %wo_ref.3) | copy-start | bytes 1572868
  10.7 6.1 %copy-start = (bf16[512,512]{1,0:T(8,128)(2,1)S(1)}, bf16[512,512]{1,0:T(8,128)(2,1)}, u32[]{:S(2)}) copy-start(bf16[512,512]{1,0:T(8,128)(2,1)} %wv_ref.3) | copy-start | bytes 1572868
  10.7 1.3 %collective-permute-start.3 = (bf16[32,512]{1,0:T(8,128)(2,1)S(1)}, bf16[32,512]{1,0:T(8,128)(2,1)S(1)}, u32[]{:S(2)}, u32[]{:S(2)}) collective-permute-start(bf16[32,512]{1,0:T(8,128)(2,1)S(1)} %get-tuple-element.28), channel_id=1, source_target_pairs={{0,8},{8,0},{16,24},{24,16},{1,9},{9,1},{17,25},{25,17},{2,10},{10... | collective-permute-start | bytes 98312 | tf_op jit(solution)/shard_map/ppermute | solution.py:319
  12.0 1.7 %copy-start.2 = (f32[3,3,512]{2,1,0:T(4,128)S(1)}, f32[3,3,512]{2,1,0:T(4,128)}, u32[]{:S(2)}) copy-start(f32[3,3,512]{2,1,0:T(4,128)} %param.8) | copy-start | bytes 55300
  12.1 5.5 %collective-permute-start.6 = (bf16[48,512]{1,0:T(8,128)(2,1)S(1)}, bf16[48,512]{1,0:T(8,128)(2,1)S(1)}, u32[]{:S(2)}, u32[]{:S(2)}) collective-permute-start(bf16[48,512]{1,0:T(8,128)(2,1)S(1)} %get-tuple-element.36), channel_id=1, source_target_pairs={{0,4},{4,0},{1,5},{5,1},{2,6},{6,2},{3,7},{7,3},{8,12},{12,8},{9,1... | collective-permute-start | bytes 147464 | tf_op jit(solution)/shard_map/ppermute | solution.py:328

commit v9 on v8

--- a/solution.py
+++ b/solution.py
@@ -62,12 +62,17 @@
     return jnp.where(on_right(), ref[pl.ds(cols - 1, lines, stride=cols), :], ref[pl.ds(0, lines, stride=cols), :])
 
 
+def gate_kernel(x_ref, w_ref, gate_ref):
+    v = jnp.dot(x_ref[...], w_ref[...], preferred_element_type=F32)
+    gate_ref[...] = v / (1.0 + jnp.exp(-v))
+
+
 def early_kernel(frames, rows, cols, *refs):
-    far, (gate_ref, fields_ref, table_ref, side_ref), near, (arrived, held) = refs[:4], refs[4:8], refs[8:12], refs[12:]
+    far, (fields_ref, table_ref, side_ref), near, (arrived, held) = refs[:3], refs[3:6], refs[6:9], refs[9:]
     copies = [pltpu.make_async_copy(a, b, arrived.at[i]) for i, (a, b) in enumerate(zip(far, near))]
     for copy in copies:
         copy.start()
-    taps_ref, skip_ref, x_ref, w_ref = near
+    taps_ref, skip_ref, x_ref = near
     lags, chans = taps_ref.shape
     copies[0].wait()
     copies[1].wait()
@@ -94,9 +99,13 @@
             for t in range(frames):
                 at = d * block + t * sites
                 fields_ref[at : at + sites, span] = totals[t].reshape(sites, LANES)
-    copies[3].wait()
-    v = jnp.dot(x_ref[...], w_ref[...], preferred_element_type=F32)
-    gate_ref[...] = v / (1.0 + jnp.exp(-v))
+
+
+def reordered(lines, rounds_h, back=False):
+    if rounds_h > 1:
+        return lines[:1] + lines[2:] + lines[1:2] if back else lines[:1] + lines[-1:] + lines[1:-1]
+    odd = position("height")[0]
+    return [jnp.where(odd, a, b) for a, b in zip(lines, lines[::-1])]
 
 
 def mix_kernel(frames, rows, cols, rounds_h, partner_ref, fields_ref, table_ref, side_ref, mine_ref, *refs):
@@ -106,7 +115,6 @@
     block = frames * sites
     pad = 2 * frames
     shift = jnp.where(second(), frames, -frames)
-    odd = position("height")[0]
     for lane in range(0, mine_ref.shape[1], LANES):
         span = slice(lane, lane + LANES)
         held[...] = partner_ref[:, span].astype(F32)
@@ -125,10 +133,10 @@
             for t in range(frames):
                 held[t * sites : (t + 1) * sites, :] = totals[t].reshape(sites, LANES)
             if d:
-                outs[3 * d][:, span] = held[...].astype(BF16)
-                ends = [jnp.concatenate([t[r] for t in totals], axis=0) for r in (0, rows - 1)]
-                line = [jnp.where(odd, *(ends[::-1] if k else ends)) for k in range(rounds_h)]
-                outs[3 * d - 1][:, span] = jnp.concatenate(line, axis=0).astype(BF16)
+                tiles = [jnp.concatenate([t[r] for t in totals]) for r in range(rows)]
+                tiles = reordered(tiles, rounds_h)
+                outs[3 * d - 1][:, span] = jnp.concatenate(tiles[:2]).astype(BF16)
+                outs[3 * d][:, span] = jnp.concatenate(tiles[2:]).astype(BF16)
             else:
                 mine_ref[:, span] = held[...]
             ends = []
@@ -152,7 +160,7 @@
     _, lower, upper = position("width")
     exists = jnp.where(on_right(), upper, lower)
     total = 0.0
-    for d, ref in enumerate(arrived):
+    for d, ref in enumerate(arrived[::-1]):
         total = total + later(d, ref[...].astype(F32))
     total = jnp.where(exists, total, jnp.zeros_like(total))
     own_ref[...] = total[:lines]
@@ -168,16 +176,20 @@
     low_ref[...] = low
     high_ref[...] = high
     size = frames * cols
-    fill = jnp.zeros((outs[0].shape[0] - size - 2 * frames, low.shape[1]), F32)
     lines, corners = [], []
     for r in (0, rows - 1):
         lines.append(jnp.concatenate([mine_ref[t * sites + r * cols : t * sites + (r + 1) * cols] for t in range(frames)]))
         ends = [side[t * rows + r : t * rows + r + 1] for side in (low, high) for t in range(frames)]
-        corners.append(jnp.concatenate(ends + [fill]))
+        corners.append(jnp.concatenate(ends))
     for k, out in enumerate(outs):
         line = jnp.where(odd, *(lines[::-1] if k else lines))
         for d, ref in enumerate(arrived, 1):
-            line = line + later(d, ref[k * size : (k + 1) * size].astype(F32))
+            if len(outs) > 1:
+                ends = [ref[i * size : (i + 1) * size].astype(F32) for i in range(2)]
+                more = jnp.where(odd, *(ends[::-1] if k else ends))
+            else:
+                more = ref[:size].astype(F32)
+            line = line + later(d, more)
         out[...] = jnp.concatenate([line, jnp.where(odd, *(corners[::-1] if k else corners))]).astype(BF16)
 
 
@@ -195,23 +207,33 @@
     return jnp.dot(hidden, wo_ref[...], preferred_element_type=F32).astype(BF16)
 
 
-def inner_kernel(frames, rows, cols, mine_ref, low_ref, high_ref, taps_ref, gate_ref, wv_ref, wo_ref, *refs):
-    *wholes, out_ref, edges_ref, mixed = refs
+def inner_kernel(
+    frames, rows, cols, rounds_h, mine_ref, low_ref, high_ref, taps_ref, gate_ref, wv_ref, wo_ref, *refs
+):
+    *parts, out_ref, edges_ref, mixed = refs
+    firsts, rests = parts[: len(parts) // 2], parts[len(parts) // 2 :]
     chans = mine_ref.shape[1]
     sites = rows * cols
+    size = frames * cols
     for lane in range(0, chans, LANES):
         span = slice(lane, lane + LANES)
         taps = [[taps_ref[3 * a + b : 3 * a + b + 1, span] for b in range(3)] for a in range(3)]
         low, high = low_ref[:, span], high_ref[:, span]
+        lines = [
+            jnp.concatenate([mine_ref[t * sites + r * cols : t * sites + (r + 1) * cols, span] for t in range(frames)])
+            for r in range(rows)
+        ]
+        for d, (first, rest) in enumerate(zip(firsts, rests), 1):
+            more = [first[i * size : (i + 1) * size, span].astype(F32) for i in range(2)]
+            more += [rest[i * size : (i + 1) * size, span].astype(F32) for i in range(rows - 2)]
+            more = reordered(more, rounds_h, back=True)
+            lines = [line + later(d, other) for line, other in zip(lines, more)]
         for t in range(frames):
             at = t * sites
-            tile = mine_ref[at : at + sites, span]
-            for d, ref in enumerate(wholes, 1):
-                tile = tile + later(d, ref[at : at + sites, span].astype(F32))
             totals = [None] * rows
             for r in range(rows):
                 row = t * rows + r
-                near = shifted(tile[r * cols : (r + 1) * cols], low[row : row + 1], high[row : row + 1])
+                near = shifted(lines[r][t * cols : (t + 1) * cols], low[row : row + 1], high[row : row + 1])
                 for a in range(3):
                     to = r + 1 - a
                     if 0 <= to < rows:
@@ -263,13 +285,12 @@
     x = latents.reshape(block, chans)
 
     partner = lax.ppermute(x, "tm", [(i, i ^ 1) for i in range(n_t)])
-    inputs = [kernel_taps, skip_gain.reshape(1, chans), x, gate_weight]
+    inputs = [kernel_taps, skip_gain.reshape(1, chans), x]
     lines = frames * rows
-    gate, fields, table, side = call(
+    fields, table, side = call(
         functools.partial(early_kernel, frames, rows, cols),
         "early",
         [
-            shape((block, chans), F32),
             shape((chips * block, chans), F32),
             shape((lags + 2 * frames, cols, chans), F32),
             shape((lines, chans), F32),
@@ -277,24 +298,27 @@
         [pltpu.VMEM(a.shape, a.dtype) for a in inputs]
         + [pltpu.SemaphoreType.DMA((len(inputs),)), pltpu.VMEM((block, LANES), F32)],
         inputs,
-        2 * block * chans * chans,
-        x.size,
+        2 * chips * frames * x.size,
         far=len(inputs),
+    )
+    (gate,) = call(
+        gate_kernel, "gate", [shape((block, chans), F32)], [], [x, gate_weight], 2 * block * chans * chans, x.size
     )
 
     h_rounds = swaps("height")
     column = shape((2 * lines, chans), BF16)
-    row = shape((len(h_rounds) * frames * cols, chans), BF16)
+    parts = [shape((n * frames * cols, chans), BF16) for n in (2, rows - 2)]
     mine, *sent = call(
         functools.partial(mix_kernel, frames, rows, cols, len(h_rounds)),
         "mix",
-        [shape((block, chans), F32), column] + [column, row, shape((block, chans), BF16)] * (chips - 1),
+        [shape((block, chans), F32), column] + ([column] + parts) * (chips - 1),
         [pltpu.VMEM((block, LANES), F32)],
         [partner, fields, table, side],
         2 * chips * frames * x.size,
     )
-    columns, arrived, wholes = [], [], []
-    for d in range(chips):
+    columns, firsts, rests = [], [], []
+    sent = [sent[0:1]] + [sent[i : i + 3] for i in range(1, len(sent), 3)]
+    for d in reversed(range(chips)):
         route = []
         for i in range(n_t):
             for h in range(n_h):
@@ -303,10 +327,10 @@
                     beside = h ^ 1 if to == j and n_h % 2 == 0 else h
                     source = (i * n_h + h) * n_w + j
                     route.append((source, ((i + 2 * d) % n_t * n_h + beside) * n_w + to))
-        columns.append(lax.ppermute(sent.pop(0), ("tm", "height", "width"), route))
-        if d:
-            for kept in (arrived, wholes):
-                kept.append(lax.ppermute(sent.pop(0), "tm", [(i, (i + 2 * d) % n_t) for i in range(n_t)]))
+        columns.append(lax.ppermute(sent[d].pop(0), ("tm", "height", "width"), route))
+    for d in range(1, chips):
+        for kept in (firsts, rests):
+            kept.append(lax.ppermute(sent[d].pop(0), "tm", [(i, (i + 2 * d) % n_t) for i in range(n_t)]))
 
     own, other = call(
         functools.partial(side_kernel, lines),
@@ -317,23 +341,23 @@
         LATER,
     )
     other = lax.ppermute(other, "tm", [(i, i ^ 1) for i in range(n_t)])
-    size = -(-(frames * cols + 2 * frames) // 16) * 16
+    size = frames * cols + 2 * frames
     low, high, *ends = call(
         functools.partial(border_kernel, frames, rows, cols, chips),
         "border",
         [shape((lines, chans), F32)] * 2 + [shape((size, chans), BF16)] * len(h_rounds),
         [],
-        [mine, own, other] + arrived,
+        [mine, own, other] + firsts,
     )
     ends = [lax.ppermute(e, "height", pairs) for e, pairs in zip(ends, h_rounds)]
 
     taps = spatial_taps.reshape(9, chans)
     inner, edges = call(
-        functools.partial(inner_kernel, frames, rows, cols),
+        functools.partial(inner_kernel, frames, rows, cols, len(h_rounds)),
         "inner",
         [shape((block, chans), BF16), shape((2 * frames * cols, chans), F32)],
         [pltpu.VMEM((block, chans), BF16)],
-        [mine, low, high, taps, gate, value_weight, out_weight] + wholes,
+        [mine, low, high, taps, gate, value_weight, out_weight] + firsts + rests,
         4 * block * chans * chans,
     )
     (out,) = call(

time: 18.9 us -> 17.4 us (0.921)
  waiting for transfers between devices: 6.11 us -> 4.06 us
  starting transfers between devices: 8.2 us -> 8.52 us
  local copies, waits for them, and re-layouts: 0.03 us -> 0.24 us
    ppermute x4, waiting for transfers between devices: 5.46 us -> 3.45 us  [the longest x2 1.79 us: body(): lax.ppermute(sent[d].pop(0), ('tm', 'height', 'width'), route)]
    ppermute x1, waiting for transfers between devices: 0.64 us -> 0.12 us  [body(): other = lax.ppermute(other, 'tm', [(i, i ^ 1) for i in range(n_t)])]
    ppermute x1, waiting for transfers between devices: 0.01 us -> 0.45 us  [body(): lax.ppermute(e, 'height', pairs)]
    ppermute x4, starting transfers between devices: 6.07 us -> 6.44 us  [the longest x2 4.42 us: body(): lax.ppermute(sent[d].pop(0), ('tm', 'height', 'width'), route)]
    unnamed x6 -> x10, local copies, waits for them, and re-layouts: 0.01 us -> 0.23 us
    pallas_call x6 -> x7, Pallas kernels: 4.25 us -> 4.27 us  [call(): pl.pallas_call(kernel, out_shape=tuple(outs), in_specs=[HBM] * far + [VME...]
  transfers between devices with their start and end apart: 7 -> 7, of which waited for: 4 -> 5; matrix products, arithmetic and copies ran while one was open for 0% -> 0% of each run, Pallas kernels for 14% -> 15%
where the time goes in v9:
time: 17.4 us; the launch traced here: 17.2 us
  starting transfers between devices  8.52 us (49%)
  Pallas kernels  4.27 us (25%)
  waiting for transfers between devices  4.06 us (23%)
  local copies, waits for them, and re-layouts  0.24 us (1%)
    ppermute x2, starting transfers between devices, body(): lax.ppermute(sent[d].pop(0), ('tm', 'height', 'width'), route)  4.42 us
    pallas_call x7, Pallas kernels, call(): pl.pallas_call(kernel, out_shape=tuple(outs), in_specs=[HBM] * far + [VME...  4.27 us
    ppermute x2, starting transfers between devices, body(): lax.ppermute(sent[d].pop(0), 'tm', [(i, (i + 2 * d) % n_t) for i in range...  2.03 us
    ppermute x2, waiting for transfers between devices, body(): lax.ppermute(sent[d].pop(0), ('tm', 'height', 'width'), route)  1.79 us
    ppermute x2, waiting for transfers between devices, body(): lax.ppermute(sent[d].pop(0), 'tm', [(i, (i + 2 * d) % n_t) for i in range...  1.66 us
    ppermute x1, starting transfers between devices, body(): lax.ppermute(e, 'height', pairs)  1.56 us
    ppermute x1, starting transfers between devices, body(): partner = lax.ppermute(x, 'tm', [(i, i ^ 1) for i in range(n_t)])  0.45 us
    ppermute x1, waiting for transfers between devices, body(): lax.ppermute(e, 'height', pairs)  0.45 us
  transfers between devices with their start and end apart: 7, of which 5 were waited for; matrix products, arithmetic and copies ran while one was open for 0% of the time, Pallas kernels for 15%

profile of v9, /device:TPU:0, one launch (start us, length us, event | category | flops | bytes accessed | tf_op | source)
XLA Modules:
  0.0 17.2 jit_solution(16330487358629257604)
XLA Ops:
  0.0 0.5 %collective-permute-start = (bf16[256,512]{1,0:T(8,128)(2,1)}, bf16[256,512]{1,0:T(8,128)(2,1)S(1)}, u32[]{:S(2)}, u32[]{:S(2)}) collective-permute-start(bf16[256,512]{1,0:T(8,128)(2,1)} %bitcast.3), channel_id=1, source_target_pairs={{0,8},{8,0},{16,24},{24,16},{1,9},{9,1},{17,25},{25,17},{2,10},{10... | collective-permute-start | bytes 786440 | tf_op jit(solution)/shard_map/ppermute | solution.py:287
  0.5 1.3 %early.1 = (f32[512,512]{1,0:T(8,128)S(1)}, f32[24,8,512]{2,1,0:T(8,128)S(1)}, f32[32,512]{1,0:T(8,128)S(1)}) custom-call(bf16[16,512]{1,0:T(8,128)(2,1)} %refs_0_.1, f32[1,512]{1,0:T(1,128)} %bitcast.6, bf16[256,512]{1,0:T(8,128)(2,1)} %bitcast.4), custom_call_target="tpu_custom_call" | custom-call | flops 2097152 | bytes 1787904 | tf_op jit(solution)/shard_map/early/pallas_call | solution.py:20
  1.8 0.0 collective-permute-done.partner_ref
  1.8 0.6 %mix.1 = (f32[256,512]{1,0:T(8,128)S(1)}, bf16[64,512]{1,0:T(8,128)(2,1)S(1)}, bf16[64,512]{1,0:T(8,128)(2,1)S(1)}, bf16[64,512]{1,0:T(8,128)(2,1)S(1)}, bf16[192,512]{1,0:T(8,128)(2,1)S(1)}) custom-call(bf16[256,512]{1,0:T(8,128)(2,1)S(1)} %collective-permute-done.partner_ref, f32[512,512]{1,0:T(8,128)S(1)} %get-tuple-element.20.fields_ref, ...), custom_call_target="tpu_custom_call" | custom-call | flops 2097152 | bytes 2686976 | tf_op jit(solution)/shard_map/mix/pallas_call | solution.py:20
  2.4 4.0 %collective-permute-start.1 = (bf16[64,512]{1,0:T(8,128)(2,1)S(1)}, bf16[64,512]{1,0:T(8,128)(2,1)S(1)}, u32[]{:S(2)}, u32[]{:S(2)}) collective-permute-start(bf16[64,512]{1,0:T(8,128)(2,1)S(1)} %get-tuple-element.24), channel_id=1, source_target_pairs={{0,17},{1,16},{2,19},{3,18},{4,21},{5,20},{6,23},{7,22},{8,28},{9,... | collective-permute-start | bytes 196616 | tf_op jit(solution)/shard_map/ppermute | solution.py:330
  6.4 0.4 %collective-permute-start.2 = (bf16[64,512]{1,0:T(8,128)(2,1)S(1)}, bf16[64,512]{1,0:T(8,128)(2,1)S(1)}, u32[]{:S(2)}, u32[]{:S(2)}) collective-permute-start(bf16[64,512]{1,0:T(8,128)(2,1)S(1)} %get-tuple-element.25), channel_id=1, source_target_pairs={{0,1},{1,0},{2,3},{3,2},{4,5},{5,4},{6,7},{7,6},{8,12},{9,10},{10,... | collective-permute-start | bytes 196616 | tf_op jit(solution)/shard_map/ppermute | solution.py:330
  6.9 0.2 %collective-permute-start.4 = (bf16[64,512]{1,0:T(8,128)(2,1)S(1)}, bf16[64,512]{1,0:T(8,128)(2,1)S(1)}, u32[]{:S(2)}, u32[]{:S(2)}) collective-permute-start(bf16[64,512]{1,0:T(8,128)(2,1)S(1)} %get-tuple-element.28), channel_id=1, source_target_pairs={{0,16},{8,24},{16,0},{24,8},{1,17},{9,25},{17,1},{25,9},{2,18},{10... | collective-permute-start | bytes 196616 | tf_op jit(solution)/shard_map/ppermute | solution.py:333
  7.1 1.8 %collective-permute-start.5 = (bf16[192,512]{1,0:T(8,128)(2,1)S(1)}, bf16[192,512]{1,0:T(8,128)(2,1)S(1)}, u32[]{:S(2)}, u32[]{:S(2)}) collective-permute-start(bf16[192,512]{1,0:T(8,128)(2,1)S(1)} %get-tuple-element.31), channel_id=1, source_target_pairs={{0,16},{8,24},{16,0},{24,8},{1,17},{9,25},{17,1},{25,9},{2,18},{10... | collective-permute-start | bytes 589832 | tf_op jit(solution)/shard_map/ppermute | solution.py:333
  8.9 0.0 collective-permute-done.1.refs_0_
  8.9 1.8 %collective-permute-done.2.refs_1_ = bf16[64,512]{1,0:T(8,128)(2,1)S(1)} collective-permute-done((bf16[64,512]{1,0:T(8,128)(2,1)S(1)}, bf16[64,512]{1,0:T(8,128)(2,1)S(1)}, u32[]{:S(2)}, u32[]{:S(2)}) %collective-permute-start.2) | collective-permute-done | bytes 65568 | tf_op jit(solution)/shard_map/ppermute | solution.py:330
  10.7 0.0 copy-start.3
  10.7 0.1 collective-permute-start.3
  10.8 1.1 %collective-permute-done.4.refs_0_ = bf16[64,512]{1,0:T(8,128)(2,1)S(1)} collective-permute-done((bf16[64,512]{1,0:T(8,128)(2,1)S(1)}, bf16[64,512]{1,0:T(8,128)(2,1)S(1)}, u32[]{:S(2)}, u32[]{:S(2)}) %collective-permute-start.4) | collective-permute-done | bytes 65568 | tf_op jit(solution)/shard_map/ppermute | solution.py:333
  11.9 0.1 collective-permute-done.3.other_ref
  12.0 0.0 copy-start.4
  12.0 0.0 copy-start.2
  12.1 1.6 %collective-permute-start.6 = (bf16[40,512]{1,0:T(8,128)(2,1)S(1)}, bf16[40,512]{1,0:T(8,128)(2,1)S(1)}, u32[]{:S(2)}, u32[]{:S(2)}) collective-permute-start(bf16[40,512]{1,0:T(8,128)(2,1)S(1)} %get-tuple-element.34), channel_id=1, source_target_pairs={{0,4},{4,0},{1,5},{5,1},{2,6},{6,2},{3,7},{7,3},{8,12},{12,8},{9,1... | collective-permute-start | bytes 122888 | tf_op jit(solution)/shard_map/ppermute | solution.py:352
  13.6 0.0 copy-done.4
  13.6 0.0 copy-done.3
  13.6 0.0 copy-done.2
  13.6 0.0 copy-start
  13.7 0.0 copy-start.1
  13.7 0.4 %gate.1.gate_ref = f32[256,512]{1,0:T(8,128)S(1)} custom-call(bf16[256,512]{1,0:T(8,128)(2,1)S(1)} %bitcast.5, bf16[512,512]{1,0:T(8,128)(2,1)S(1)} %copy-done.3), custom_call_target="tpu_custom_call" | custom-call | flops 134217728 | bytes 1310720 | tf_op jit(solution)/shard_map/gate/pallas_call | solution.py:20
  14.1 0.6 %collective-permute-done.5.refs_1_ = bf16[192,512]{1,0:T(8,128)(2,1)S(1)} collective-permute-done((bf16[192,512]{1,0:T(8,128)(2,1)S(1)}, bf16[192,512]{1,0:T(8,128)(2,1)S(1)}, u32[]{:S(2)}, u32[]{:S(2)}) %collective-permute-start.5) | collective-permute-done | bytes 196640 | tf_op jit(solution)/shard_map/ppermute | solution.py:333
  14.6 0.0 copy-done
  14.7 0.2 copy-done.1
  14.9 0.8 %inner.1 = (bf16[256,512]{1,0:T(8,128)(2,1)S(1)}, f32[64,512]{1,0:T(8,128)S(1)}) custom-call(f32[256,512]{1,0:T(8,128)S(1)} %get-tuple-element.23.mine_ref, f32[32,512]{1,0:T(8,128)S(1)} %get-tuple-element.29.low_ref, f32[32,512]{1,0:T(8,128)S(1)} %get-tuple-element.30.high_ref, f32[9,512]{1,0:T(8,128)S(1)} %reshape.14.taps_ref, ...), custom_call_target="tpu_custom_call" | custom-call | flops 268435456 | bytes 2902016 | tf_op jit(solution)/shard_map/inner/pallas_call | solution.py:20
  15.7 0.4 %collective-permute-done.6.refs_0_ = bf16[40,512]{1,0:T(8,128)(2,1)S(1)} collective-permute-done((bf16[40,512]{1,0:T(8,128)(2,1)S(1)}, bf16[40,512]{1,0:T(8,128)(2,1)S(1)}, u32[]{:S(2)}, u32[]{:S(2)}) %collective-permute-start.6) | collective-permute-done | bytes 40992 | tf_op jit(solution)/shard_map/ppermute | solution.py:352
  16.1 1.1 %edge.1 = bf16[256,512]{1,0:T(8,128)(2,1)} custom-call(f32[64,512]{1,0:T(8,128)S(1)} %get-tuple-element.32.edges_ref, f32[9,512]{1,0:T(8,128)S(1)} %reshape.14.taps_ref, f32[256,512]{1,0:T(8,128)S(1)} %gate.1.gate_ref, bf16[512,512]{1,0:T(8,128)(2,1)S(1)} %copy-done, bf16[512,512]{1,0:T(8,128)(2,1)S(1)} %copy-done.1, ...), custom_call_target="tpu_custom_call" | custom-call | flops 33554432 | bytes 2287616 | tf_op jit(solution)/shard_map/edge/pallas_call | solution.py:20
  (3 shorter events, 0.1 us)
Async XLA Ops:
  0.0 1.8 %collective-permute-start = (bf16[256,512]{1,0:T(8,128)(2,1)}, bf16[256,512]{1,0:T(8,128)(2,1)S(1)}, u32[]{:S(2)}, u32[]{:S(2)}) collective-permute-start(bf16[256,512]{1,0:T(8,128)(2,1)} %bitcast.3), channel_id=1, source_target_pairs={{0,8},{8,0},{16,24},{24,16},{1,9},{9,1},{17,25},{25,17},{2,10},{10... | collective-permute-start | bytes 786440 | tf_op jit(solution)/shard_map/ppermute | solution.py:287
  2.4 6.4 %collective-permute-start.1 = (bf16[64,512]{1,0:T(8,128)(2,1)S(1)}, bf16[64,512]{1,0:T(8,128)(2,1)S(1)}, u32[]{:S(2)}, u32[]{:S(2)}) collective-permute-start(bf16[64,512]{1,0:T(8,128)(2,1)S(1)} %get-tuple-element.24), channel_id=1, source_target_pairs={{0,17},{1,16},{2,19},{3,18},{4,21},{5,20},{6,23},{7,22},{8,28},{9,... | collective-permute-start | bytes 196616 | tf_op jit(solution)/shard_map/ppermute | solution.py:330
  6.4 4.3 %collective-permute-start.2 = (bf16[64,512]{1,0:T(8,128)(2,1)S(1)}, bf16[64,512]{1,0:T(8,128)(2,1)S(1)}, u32[]{:S(2)}, u32[]{:S(2)}) collective-permute-start(bf16[64,512]{1,0:T(8,128)(2,1)S(1)} %get-tuple-element.25), channel_id=1, source_target_pairs={{0,1},{1,0},{2,3},{3,2},{4,5},{5,4},{6,7},{7,6},{8,12},{9,10},{10,... | collective-permute-start | bytes 196616 | tf_op jit(solution)/shard_map/ppermute | solution.py:330
  6.9 5.0 %collective-permute-start.4 = (bf16[64,512]{1,0:T(8,128)(2,1)S(1)}, bf16[64,512]{1,0:T(8,128)(2,1)S(1)}, u32[]{:S(2)}, u32[]{:S(2)}) collective-permute-start(bf16[64,512]{1,0:T(8,128)(2,1)S(1)} %get-tuple-element.28), channel_id=1, source_target_pairs={{0,16},{8,24},{16,0},{24,8},{1,17},{9,25},{17,1},{25,9},{2,18},{10... | collective-permute-start | bytes 196616 | tf_op jit(solution)/shard_map/ppermute | solution.py:333
  7.1 7.6 %collective-permute-start.5 = (bf16[192,512]{1,0:T(8,128)(2,1)S(1)}, bf16[192,512]{1,0:T(8,128)(2,1)S(1)}, u32[]{:S(2)}, u32[]{:S(2)}) collective-permute-start(bf16[192,512]{1,0:T(8,128)(2,1)S(1)} %get-tuple-element.31), channel_id=1, source_target_pairs={{0,16},{8,24},{16,0},{24,8},{1,17},{9,25},{17,1},{25,9},{2,18},{10... | collective-permute-start | bytes 589832 | tf_op jit(solution)/shard_map/ppermute | solution.py:333
  10.7 3.0 %copy-start.3 = (bf16[512,512]{1,0:T(8,128)(2,1)S(1)}, bf16[512,512]{1,0:T(8,128)(2,1)}, u32[]{:S(2)}) copy-start(bf16[512,512]{1,0:T(8,128)(2,1)} %w_ref.1) | copy-start | bytes 1572868
  10.7 1.3 %collective-permute-start.3 = (bf16[32,512]{1,0:T(8,128)(2,1)S(1)}, bf16[32,512]{1,0:T(8,128)(2,1)S(1)}, u32[]{:S(2)}, u32[]{:S(2)}) collective-permute-start(bf16[32,512]{1,0:T(8,128)(2,1)S(1)} %get-tuple-element.27), channel_id=1, source_target_pairs={{0,8},{8,0},{16,24},{24,16},{1,9},{9,1},{17,25},{25,17},{2,10},{10... | collective-permute-start | bytes 98312 | tf_op jit(solution)/shard_map/ppermute | solution.py:343
  12.0 1.6 %copy-start.4 = (f32[3,3,512]{2,1,0:T(4,128)S(1)}, f32[3,3,512]{2,1,0:T(4,128)}, u32[]{:S(2)}) copy-start(f32[3,3,512]{2,1,0:T(4,128)} %param.8) | copy-start | bytes 55300
  12.0 1.6 %copy-start.2 = (bf16[4,8,8,512]{3,2,1,0:T(8,128)(2,1)S(1)}, bf16[4,8,8,512]{3,2,1,0:T(8,128)(2,1)}, u32[]{:S(2)}) copy-start(bf16[4,8,8,512]{3,2,1,0:T(8,128)(2,1)} %param.7) | copy-start | bytes 786436
  12.1 4.1 %collective-permute-start.6 = (bf16[40,512]{1,0:T(8,128)(2,1)S(1)}, bf16[40,512]{1,0:T(8,128)(2,1)S(1)}, u32[]{:S(2)}, u32[]{:S(2)}) collective-permute-start(bf16[40,512]{1,0:T(8,128)(2,1)S(1)} %get-tuple-element.34), channel_id=1, source_target_pairs={{0,4},{4,0},{1,5},{5,1},{2,6},{6,2},{3,7},{7,3},{8,12},{12,8},{9,1... | collective-permute-start | bytes 122888 | tf_op jit(solution)/shard_map/ppermute | solution.py:352
  13.6 1.0 %copy-start = (bf16[512,512]{1,0:T(8,128)(2,1)S(1)}, bf16[512,512]{1,0:T(8,128)(2,1)}, u32[]{:S(2)}) copy-start(bf16[512,512]{1,0:T(8,128)(2,1)} %wv_ref.3) | copy-start | bytes 1572868
  13.7 1.2 %copy-start.1 = (bf16[512,512]{1,0:T(8,128)(2,1)S(1)}, bf16[512,512]{1,0:T(8,128)(2,1)}, u32[]{:S(2)}) copy-start(bf16[512,512]{1,0:T(8,128)(2,1)} %wo_ref.3) | copy-start | bytes 1572868

commit v10 on v9

--- a/solution.py
+++ b/solution.py
@@ -14,15 +14,16 @@
 HBM = pl.BlockSpec(memory_space=pltpu.HBM)
 
 
-def call(kernel, name, outs, scratch, operands, flops=0, exps=0, far=0):
+def call(kernel, name, outs, scratch, operands, flops=0, exps=0, far=0, far_outs=0, aliases={}):
     operands = [pltpu.with_memory_space_constraint(a, pltpu.HBM) for a in operands[:far]] + list(operands[far:])
     moved = sum(a.size * a.dtype.itemsize for a in operands) + sum(a.size * a.dtype.itemsize for a in outs)
     return pl.pallas_call(
         kernel,
         out_shape=tuple(outs),
         in_specs=[HBM] * far + [VMEM] * (len(operands) - far),
-        out_specs=(VMEM,) * len(outs),
+        out_specs=(HBM,) * far_outs + (VMEM,) * (len(outs) - far_outs),
         scratch_shapes=scratch,
+        input_output_aliases=aliases,
         compiler_params=pltpu.CompilerParams(vmem_limit_bytes=24 * 1024 * 1024),
         cost_estimate=pl.CostEstimate(flops=flops, bytes_accessed=moved, transcendentals=exps),
         name=name,
@@ -68,7 +69,7 @@
 
 
 def early_kernel(frames, rows, cols, *refs):
-    far, (fields_ref, table_ref, side_ref), near, (arrived, held) = refs[:3], refs[3:6], refs[6:9], refs[9:]
+    far, (table_ref, side_ref, *fields), near, (arrived, held) = refs[:3], refs[3:-5], refs[-5:-2], refs[-2:]
     copies = [pltpu.make_async_copy(a, b, arrived.at[i]) for i, (a, b) in enumerate(zip(far, near))]
     for copy in copies:
         copy.start()
@@ -83,13 +84,12 @@
         tap = taps[lag : lag + 1] + (skip_ref[...] if lag == 0 else 0.0)
         table_ref[pad + lag] = jnp.broadcast_to(tap, (cols, chans))
     sites = rows * cols
-    block = frames * sites
     copies[2].wait()
     for lane in range(0, chans, LANES):
         span = slice(lane, lane + LANES)
         held[...] = x_ref[:, span].astype(F32)
         side_ref[:, span] = outer_column(held, frames * rows, cols)
-        for d in range(fields_ref.shape[0] // block):
+        for d, field in enumerate(fields):
             totals = [None] * frames
             for s in range(frames):
                 x = x_ref[s * sites : (s + 1) * sites, span].astype(F32).reshape(rows, cols, LANES)
@@ -97,8 +97,7 @@
                     term = table_ref[pad + 2 * d * frames + t - s, :, span] * x
                     totals[t] = term if totals[t] is None else totals[t] + term
             for t in range(frames):
-                at = d * block + t * sites
-                fields_ref[at : at + sites, span] = totals[t].reshape(sites, LANES)
+                field[t * sites : (t + 1) * sites, span] = totals[t].reshape(sites, LANES)
 
 
 def reordered(lines, rounds_h, back=False):
@@ -108,63 +107,73 @@
     return [jnp.where(odd, a, b) for a, b in zip(lines, lines[::-1])]
 
 
-def mix_kernel(frames, rows, cols, rounds_h, partner_ref, fields_ref, table_ref, side_ref, mine_ref, *refs):
-    *outs, held = refs
+def column_kernel(frames, rows, cols, partner_ref, side_ref, out_ref, held):
+    lines = frames * rows
+    for lane in range(0, out_ref.shape[1], LANES):
+        span = slice(lane, lane + LANES)
+        held[...] = partner_ref[:, span].astype(F32)
+        out_ref[:, span] = jnp.concatenate([side_ref[:, span], outer_column(held, lines, cols)]).astype(BF16)
+
+
+def shift(frames):
+    return jnp.where(second(), frames, -frames)
+
+
+def with_partner(frames, rows, cols, d, field_ref, partner_ref, table_ref, span):
     sites = rows * cols
-    lines = frames * rows
-    block = frames * sites
-    pad = 2 * frames
-    shift = jnp.where(second(), frames, -frames)
+    base = 2 * frames + 2 * d * frames + shift(frames)
+    totals = [field_ref[t * sites : (t + 1) * sites, span].reshape(rows, cols, LANES) for t in range(frames)]
+    for s in range(frames):
+        x = partner_ref[s * sites : (s + 1) * sites, span].astype(F32).reshape(rows, cols, LANES)
+        for t in range(frames):
+            totals[t] = totals[t] + table_ref[base + t - s, :, span] * x
+    return totals
+
+
+def later_kernel(frames, rows, cols, rounds_h, partner_ref, table_ref, *refs):
+    fields, outs = refs[: len(refs) // 3], refs[len(refs) // 3 :]
+    for d, field in enumerate(fields, 1):
+        for lane in range(0, field.shape[1], LANES):
+            span = slice(lane, lane + LANES)
+            totals = with_partner(frames, rows, cols, d, field, partner_ref, table_ref, span)
+            tiles = reordered([jnp.concatenate([t[r] for t in totals]) for r in range(rows)], rounds_h)
+            outs[2 * d - 2][:, span] = jnp.concatenate(tiles[:2]).astype(BF16)
+            outs[2 * d - 1][:, span] = jnp.concatenate(tiles[2:]).astype(BF16)
+
+
+def own_kernel(frames, rows, cols, partner_ref, table_ref, field_ref, mine_ref):
     for lane in range(0, mine_ref.shape[1], LANES):
         span = slice(lane, lane + LANES)
-        held[...] = partner_ref[:, span].astype(F32)
-        near = [side_ref[s * rows : (s + 1) * rows, span] for s in range(frames)]
-        far = outer_column(held, lines, cols)
-        for d in range(fields_ref.shape[0] // block):
-            totals = []
-            for t in range(frames):
-                at = d * block + t * sites
-                totals.append(fields_ref[at : at + sites, span].reshape(rows, cols, LANES))
-            base = pad + 2 * d * frames
-            for s in range(frames):
-                x = partner_ref[s * sites : (s + 1) * sites, span].astype(F32).reshape(rows, cols, LANES)
-                for t in range(frames):
-                    totals[t] = totals[t] + table_ref[base + shift + t - s, :, span] * x
-            for t in range(frames):
-                held[t * sites : (t + 1) * sites, :] = totals[t].reshape(sites, LANES)
-            if d:
-                tiles = [jnp.concatenate([t[r] for t in totals]) for r in range(rows)]
-                tiles = reordered(tiles, rounds_h)
-                outs[3 * d - 1][:, span] = jnp.concatenate(tiles[:2]).astype(BF16)
-                outs[3 * d][:, span] = jnp.concatenate(tiles[2:]).astype(BF16)
-            else:
-                mine_ref[:, span] = held[...]
-            ends = []
-            for t in range(frames):
-                end = jnp.zeros((rows, LANES), F32)
-                for s in range(frames):
-                    end = end + table_ref[base - shift + t - s, :, span] * near[s]
-                    if d or t >= s:
-                        end = end + table_ref[base + t - s, :, span] * far[s * rows : (s + 1) * rows]
-                ends.append(end)
-            column = jnp.concatenate([outer_column(held, lines, cols)] + ends, axis=0)
-            outs[3 * d - 2 if d else 0][:, span] = column.astype(BF16)
+        totals = with_partner(frames, rows, cols, 0, field_ref, partner_ref, table_ref, span)
+        mine_ref[:, span] = jnp.concatenate(totals).reshape(mine_ref.shape[0], LANES)
 
 
 def later(d, value):
     return jnp.where(lax.div(lax.axis_index("tm"), 2) >= d, value, jnp.zeros_like(value))
 
 
-def side_kernel(lines, *refs):
+def side_kernel(frames, rows, table_ref, *refs):
     *arrived, own_ref, other_ref = refs
     _, lower, upper = position("width")
     exists = jnp.where(on_right(), upper, lower)
-    total = 0.0
-    for d, ref in enumerate(arrived[::-1]):
-        total = total + later(d, ref[...].astype(F32))
-    total = jnp.where(exists, total, jnp.zeros_like(total))
-    own_ref[...] = total[:lines]
-    other_ref[...] = total[lines:].astype(BF16)
+    for lane in range(0, own_ref.shape[1], LANES):
+        span = slice(lane, lane + LANES)
+        totals = [jnp.zeros((rows, LANES), F32)] * (2 * frames)
+        for d, ref in enumerate(arrived[::-1]):
+            column = later(d, ref[:, span].astype(F32))
+            base = 2 * frames + 2 * d * frames
+            for t in range(2 * frames):
+                for s in range(2 * frames):
+                    lag = t % frames - s % frames
+                    if t // frames == s // frames:
+                        if d == 0 and lag < 0:
+                            continue
+                    else:
+                        lag = lag + (shift(frames) if t < frames else -shift(frames))
+                    totals[t] = totals[t] + table_ref[base + lag, :, span] * column[s * rows : (s + 1) * rows]
+        totals = [jnp.where(exists, total, jnp.zeros_like(total)) for total in totals]
+        own_ref[:, span] = jnp.concatenate(totals[:frames])
+        other_ref[:, span] = jnp.concatenate(totals[frames:]).astype(BF16)
 
 
 def border_kernel(frames, rows, cols, chips, mine_ref, own_ref, other_ref, *refs):
@@ -210,7 +219,7 @@
 def inner_kernel(
     frames, rows, cols, rounds_h, mine_ref, low_ref, high_ref, taps_ref, gate_ref, wv_ref, wo_ref, *refs
 ):
-    *parts, out_ref, edges_ref, mixed = refs
+    *parts, out_ref, edges_ref, mixed, held, done = refs
     firsts, rests = parts[: len(parts) // 2], parts[len(parts) // 2 :]
     chans = mine_ref.shape[1]
     sites = rows * cols
@@ -240,39 +249,47 @@
                         term = near[0] * taps[a][0] + near[1] * taps[a][1] + near[2] * taps[a][2]
                         totals[to] = term if totals[to] is None else totals[to] + term
             mixed[at : at + sites, span] = jnp.concatenate(totals, axis=0).astype(BF16)
-            edges_ref[t * cols : (t + 1) * cols, span] = totals[0]
-            edges_ref[(frames + t) * cols : (frames + t + 1) * cols, span] = totals[rows - 1]
-    out_ref[...] = projected(mixed[...], gate_ref[...], wv_ref, wo_ref)
-
-
-def edge_kernel(frames, rows, cols, rounds_h, edges_ref, taps_ref, gate_ref, wv_ref, wo_ref, inner_ref, *refs):
-    ends, out_ref = refs[:rounds_h], refs[rounds_h]
+            for k, edge in enumerate((totals[:2], totals[-2:])):
+                edges_ref[2 * (k * size + t * cols) : 2 * (k * size + (t + 1) * cols), span] = jnp.concatenate(edge)
+    held[...] = projected(mixed[...], gate_ref[...], wv_ref, wo_ref)
+    copy = pltpu.make_async_copy(held, out_ref, done)
+    copy.start()
+    copy.wait()
+
+
+def edge_kernel(frames, rows, cols, rounds_h, inner_ref, edges_ref, taps_ref, gate_ref, wv_ref, wo_ref, *refs):
+    ends, (out_ref, held, done) = refs[:rounds_h], refs[rounds_h:]
     sites = rows * cols
     size = frames * cols
-    odd, _, _ = position("height")
-    out_ref[...] = inner_ref[...]
+    odd, lower, upper = position("height")
     taps = taps_ref[...]
-    mixed, gate = [], []
+    mixed, gate, starts = [], [], []
     for k, end in enumerate(ends):
         end = end[...].astype(F32)
         first = jnp.logical_not(odd) if k else odd
         lefts, rights = end[size : size + frames], end[size + frames : size + 2 * frames]
-        lower, upper = position("height")[1:]
         exists = jnp.where(first, lower, upper)
         tap = jnp.where(first, taps[0:3], taps[6:9])
-        total = jnp.where(first, edges_ref[0:size], edges_ref[size : 2 * size])
+        total = jnp.where(first, edges_ref[: 2 * size], edges_ref[2 * size :])
         for t in range(frames):
             near = shifted(end[t * cols : (t + 1) * cols], lefts[t : t + 1], rights[t : t + 1])
             more = near[0] * tap[0:1] + near[1] * tap[1:2] + near[2] * tap[2:3]
-            mixed.append(total[t * cols : (t + 1) * cols] + jnp.where(exists, more, jnp.zeros_like(more)))
+            more = jnp.where(exists, more, jnp.zeros_like(more))
+            none = jnp.zeros_like(more)
+            mixed.append(total[2 * t * cols : (2 * t + 1) * cols] + jnp.where(first, more, none))
+            mixed.append(total[(2 * t + 1) * cols : (2 * t + 2) * cols] + jnp.where(first, none, more))
             at = t * sites
-            gate.append(jnp.where(first, gate_ref[at : at + cols], gate_ref[at + sites - cols : at + sites]))
-    out = projected(jnp.concatenate(mixed, axis=0).astype(BF16), jnp.concatenate(gate, axis=0), wv_ref, wo_ref)
-    for t in range(frames):
-        new = [out[k * size + t * cols : k * size + (t + 1) * cols] for k in range(rounds_h)]
-        for at, other in ((t * sites, False), (t * sites + sites - cols, True)):
-            kept = new[1] if rounds_h > 1 else inner_ref[at : at + cols]
-            out_ref[at : at + cols] = jnp.where(odd, kept, new[0]) if other else jnp.where(odd, new[0], kept)
+            gate.append(jnp.where(first, gate_ref[at : at + 2 * cols], gate_ref[at + sites - 2 * cols : at + sites]))
+            starts.append(pl.multiple_of(at + jnp.where(first, 0, sites - 2 * cols), 2 * cols))
+    held[...] = projected(jnp.concatenate(mixed).astype(BF16), jnp.concatenate(gate), wv_ref, wo_ref)
+    copies = [
+        pltpu.make_async_copy(held.at[pl.ds(2 * i * cols, 2 * cols)], out_ref.at[pl.ds(at, 2 * cols)], done.at[i])
+        for i, at in enumerate(starts)
+    ]
+    for copy in copies:
+        copy.start()
+    for copy in copies:
+        copy.wait()
 
 
 def body(latents, spatial_taps, kernel_taps, skip_gain, gate_weight, value_weight, out_weight):
@@ -287,14 +304,11 @@
     partner = lax.ppermute(x, "tm", [(i, i ^ 1) for i in range(n_t)])
     inputs = [kernel_taps, skip_gain.reshape(1, chans), x]
     lines = frames * rows
-    fields, table, side = call(
+    field = shape((block, chans), F32)
+    table, side, *fields = call(
         functools.partial(early_kernel, frames, rows, cols),
         "early",
-        [
-            shape((chips * block, chans), F32),
-            shape((lags + 2 * frames, cols, chans), F32),
-            shape((lines, chans), F32),
-        ],
+        [shape((lags + 2 * frames, cols, chans), F32), shape((lines, chans), F32)] + [field] * chips,
         [pltpu.VMEM(a.shape, a.dtype) for a in inputs]
         + [pltpu.SemaphoreType.DMA((len(inputs),)), pltpu.VMEM((block, LANES), F32)],
         inputs,
@@ -306,18 +320,31 @@
     )
 
     h_rounds = swaps("height")
-    column = shape((2 * lines, chans), BF16)
+    (column,) = call(
+        functools.partial(column_kernel, frames, rows, cols),
+        "column",
+        [shape((2 * lines, chans), BF16)],
+        [pltpu.VMEM((block, LANES), F32)],
+        [partner, side],
+    )
     parts = [shape((n * frames * cols, chans), BF16) for n in (2, rows - 2)]
-    mine, *sent = call(
-        functools.partial(mix_kernel, frames, rows, cols, len(h_rounds)),
-        "mix",
-        [shape((block, chans), F32), column] + ([column] + parts) * (chips - 1),
-        [pltpu.VMEM((block, LANES), F32)],
-        [partner, fields, table, side],
-        2 * chips * frames * x.size,
+    sent = call(
+        functools.partial(later_kernel, frames, rows, cols, len(h_rounds)),
+        "later",
+        parts * (chips - 1),
+        [],
+        [partner, table] + fields[1:],
+        2 * (chips - 1) * frames * x.size,
+    )
+    (mine,) = call(
+        functools.partial(own_kernel, frames, rows, cols),
+        "own",
+        [field],
+        [],
+        [partner, table, fields[0]],
+        2 * frames * x.size,
     )
     columns, firsts, rests = [], [], []
-    sent = [sent[0:1]] + [sent[i : i + 3] for i in range(1, len(sent), 3)]
     for d in reversed(range(chips)):
         route = []
         for i in range(n_t):
@@ -327,17 +354,18 @@
                     beside = h ^ 1 if to == j and n_h % 2 == 0 else h
                     source = (i * n_h + h) * n_w + j
                     route.append((source, ((i + 2 * d) % n_t * n_h + beside) * n_w + to))
-        columns.append(lax.ppermute(sent[d].pop(0), ("tm", "height", "width"), route))
+        columns.append(lax.ppermute(column, ("tm", "height", "width"), route))
     for d in range(1, chips):
-        for kept in (firsts, rests):
-            kept.append(lax.ppermute(sent[d].pop(0), "tm", [(i, (i + 2 * d) % n_t) for i in range(n_t)]))
+        route = [(i, (i + 2 * d) % n_t) for i in range(n_t)]
+        firsts.append(lax.ppermute(sent[2 * d - 2], "tm", route))
+        rests.append(lax.ppermute(sent[2 * d - 1], "tm", route))
 
     own, other = call(
-        functools.partial(side_kernel, lines),
+        functools.partial(side_kernel, frames, rows),
         "side",
         [shape((lines, chans), F32), shape((lines, chans), BF16)],
         [],
-        columns,
+        [table] + columns,
         LATER,
     )
     other = lax.ppermute(other, "tm", [(i, i ^ 1) for i in range(n_t)])
@@ -355,18 +383,25 @@
     inner, edges = call(
         functools.partial(inner_kernel, frames, rows, cols, len(h_rounds)),
         "inner",
-        [shape((block, chans), BF16), shape((2 * frames * cols, chans), F32)],
-        [pltpu.VMEM((block, chans), BF16)],
+        [shape((block, chans), BF16), shape((4 * frames * cols, chans), F32)],
+        [pltpu.VMEM((block, chans), BF16)] * 2 + [pltpu.SemaphoreType.DMA],
         [mine, low, high, taps, gate, value_weight, out_weight] + firsts + rests,
         4 * block * chans * chans,
+        far_outs=1,
     )
     (out,) = call(
         functools.partial(edge_kernel, frames, rows, cols, len(h_rounds)),
         "edge",
         [shape((block, chans), BF16)],
-        [],
-        [edges, taps, gate, value_weight, out_weight, inner] + ends,
-        4 * frames * cols * chans * chans,
+        [
+            pltpu.VMEM((len(h_rounds) * 2 * frames * cols, chans), BF16),
+            pltpu.SemaphoreType.DMA((len(h_rounds) * frames,)),
+        ],
+        [inner, edges, taps, gate, value_weight, out_weight] + ends,
+        8 * frames * cols * chans * chans,
+        far=1,
+        far_outs=1,
+        aliases={0: 0},
     )
     return out.reshape(latents.shape)
 

time: 17.4 us -> 17.3 us (level)
  waiting for transfers between devices: 4.06 us -> 3.31 us
  Pallas kernels: 4.27 us -> 4.89 us
    pallas_call x7 -> x9, Pallas kernels: 4.27 us -> 4.89 us  [call(): pl.pallas_call(kernel, out_shape=tuple(outs), in_specs=[HBM] * far + [VME...]
    ppermute x1, waiting for transfers between devices: 0.45 us -> 0.01 us  [body(): lax.ppermute(e, 'height', pairs)]
    ppermute x4, waiting for transfers between devices: 3.45 us -> 3.26 us  [the longest x2 1.52 us: body(): columns.append(lax.ppermute(column, ('tm', 'height', 'width'), route))]
  transfers between devices with their start and end apart: 7 -> 7, of which waited for: 5 -> 3; matrix products, arithmetic and copies ran while one was open for 0% -> 0% of each run, Pallas kernels for 15% -> 22%
where the time goes in v10:
time: 17.3 us; the launch traced here: 17 us
  starting transfers between devices  8.59 us (50%)
  Pallas kernels  4.89 us (28%)
  waiting for transfers between devices  3.31 us (19%)
    pallas_call x9, Pallas kernels, call(): pl.pallas_call(kernel, out_shape=tuple(outs), in_specs=[HBM] * far + [VME...  4.89 us
    ppermute x2, starting transfers between devices, body(): columns.append(lax.ppermute(column, ('tm', 'height', 'width'), route))  4.42 us
    ppermute x1, starting transfers between devices, body(): rests.append(lax.ppermute(sent[2 * d - 1], 'tm', route))  1.83 us
    ppermute x1, starting transfers between devices, body(): lax.ppermute(e, 'height', pairs)  1.56 us
    ppermute x2, waiting for transfers between devices, body(): columns.append(lax.ppermute(column, ('tm', 'height', 'width'), route))  1.52 us
    ppermute x1, waiting for transfers between devices, body(): firsts.append(lax.ppermute(sent[2 * d - 2], 'tm', route))  1.05 us
    ppermute x1, waiting for transfers between devices, body(): rests.append(lax.ppermute(sent[2 * d - 1], 'tm', route))  0.7 us
    ppermute x1, starting transfers between devices, body(): partner = lax.ppermute(x, 'tm', [(i, i ^ 1) for i in range(n_t)])  0.45 us
  transfers between devices with their start and end apart: 7, of which 3 were waited for; matrix products, arithmetic and copies ran while one was open for 0% of the time, Pallas kernels for 22%

profile of v10, /device:TPU:0, one launch (start us, length us, event | category | flops | bytes accessed | tf_op | source)
XLA Modules:
  0.0 17.0 jit_solution(5549164048867411841)
XLA Ops:
  0.0 0.5 %collective-permute-start = (bf16[256,512]{1,0:T(8,128)(2,1)}, bf16[256,512]{1,0:T(8,128)(2,1)S(1)}, u32[]{:S(2)}, u32[]{:S(2)}) collective-permute-start(bf16[256,512]{1,0:T(8,128)(2,1)} %bitcast.3), channel_id=1, source_target_pairs={{0,8},{8,0},{16,24},{24,16},{1,9},{9,1},{17,25},{25,17},{2,10},{10... | collective-permute-start | bytes 786440 | tf_op jit(solution)/shard_map/ppermute | solution.py:304
  0.5 1.3 %early.1 = (f32[24,8,512]{2,1,0:T(8,128)S(1)}, f32[32,512]{1,0:T(8,128)S(1)}, f32[256,512]{1,0:T(8,128)S(1)}, f32[256,512]{1,0:T(8,128)S(1)}) custom-call(bf16[16,512]{1,0:T(8,128)(2,1)} %refs_0_.1, f32[1,512]{1,0:T(1,128)} %bitcast.6, bf16[256,512]{1,0:T(8,128)(2,1)} %bitcast.4), custom_call_target="tpu_custom_call" | custom-call | flops 2097152 | bytes 1787904 | tf_op jit(solution)/shard_map/early/pallas_call | solution.py:20
  1.8 0.0 collective-permute-done.partner_ref
  1.8 0.1 column.1
  1.9 4.0 %collective-permute-start.1 = (bf16[64,512]{1,0:T(8,128)(2,1)S(1)}, bf16[64,512]{1,0:T(8,128)(2,1)S(1)}, u32[]{:S(2)}, u32[]{:S(2)}) collective-permute-start(bf16[64,512]{1,0:T(8,128)(2,1)S(1)} %column.1), channel_id=1, source_target_pairs={{0,17},{1,16},{2,19},{3,18},{4,21},{5,20},{6,23},{7,22},{8,28},{9,... | collective-permute-start | bytes 196616 | tf_op jit(solution)/shard_map/ppermute | solution.py:357
  5.9 0.4 %collective-permute-start.2 = (bf16[64,512]{1,0:T(8,128)(2,1)S(1)}, bf16[64,512]{1,0:T(8,128)(2,1)S(1)}, u32[]{:S(2)}, u32[]{:S(2)}) collective-permute-start(bf16[64,512]{1,0:T(8,128)(2,1)S(1)} %column.1), channel_id=1, source_target_pairs={{0,1},{1,0},{2,3},{3,2},{4,5},{5,4},{6,7},{7,6},{8,12},{9,10},{10,... | collective-permute-start | bytes 196616 | tf_op jit(solution)/shard_map/ppermute | solution.py:357
  6.3 0.2 %later.1 = (bf16[64,512]{1,0:T(8,128)(2,1)S(1)}, bf16[192,512]{1,0:T(8,128)(2,1)S(1)}) custom-call(bf16[256,512]{1,0:T(8,128)(2,1)S(1)} %collective-permute-done.partner_ref, f32[24,8,512]{2,1,0:T(8,128)S(1)} %get-tuple-element.18.table_ref, f32[256,512]{1,0:T(8,128)S(1)} %get-tuple-element.23.refs_0_), custom_call_target="tpu_custom_call" | custom-call | flops 1048576 | bytes 1441792 | tf_op jit(solution)/shard_map/later/pallas_call | solution.py:20
  6.5 0.3 %collective-permute-start.4 = (bf16[64,512]{1,0:T(8,128)(2,1)S(1)}, bf16[64,512]{1,0:T(8,128)(2,1)S(1)}, u32[]{:S(2)}, u32[]{:S(2)}) collective-permute-start(bf16[64,512]{1,0:T(8,128)(2,1)S(1)} %get-tuple-element.24), channel_id=1, source_target_pairs={{0,16},{8,24},{16,0},{24,8},{1,17},{9,25},{17,1},{25,9},{2,18},{10... | collective-permute-start | bytes 196616 | tf_op jit(solution)/shard_map/ppermute | solution.py:360
  6.8 1.8 %collective-permute-start.5 = (bf16[192,512]{1,0:T(8,128)(2,1)S(1)}, bf16[192,512]{1,0:T(8,128)(2,1)S(1)}, u32[]{:S(2)}, u32[]{:S(2)}) collective-permute-start(bf16[192,512]{1,0:T(8,128)(2,1)S(1)} %get-tuple-element.27), channel_id=1, source_target_pairs={{0,16},{8,24},{16,0},{24,8},{1,17},{9,25},{17,1},{25,9},{2,18},{10... | collective-permute-start | bytes 589832 | tf_op jit(solution)/shard_map/ppermute | solution.py:361
  8.6 0.0 collective-permute-done.1.refs_0_
  8.6 1.5 %collective-permute-done.2.refs_1_ = bf16[64,512]{1,0:T(8,128)(2,1)S(1)} collective-permute-done((bf16[64,512]{1,0:T(8,128)(2,1)S(1)}, bf16[64,512]{1,0:T(8,128)(2,1)S(1)}, u32[]{:S(2)}, u32[]{:S(2)}) %collective-permute-start.2) | collective-permute-done | bytes 65568 | tf_op jit(solution)/shard_map/ppermute | solution.py:357
  10.1 0.2 side.1
  10.3 0.1 collective-permute-start.3
  10.4 0.0 copy-start.3
  10.4 0.2 own.1.mine_ref
  10.5 1.0 %collective-permute-done.4.refs_0_ = bf16[64,512]{1,0:T(8,128)(2,1)S(1)} collective-permute-done((bf16[64,512]{1,0:T(8,128)(2,1)S(1)}, bf16[64,512]{1,0:T(8,128)(2,1)S(1)}, u32[]{:S(2)}, u32[]{:S(2)}) %collective-permute-start.4) | collective-permute-done | bytes 65568 | tf_op jit(solution)/shard_map/ppermute | solution.py:360
  11.6 0.0 collective-permute-done.3.other_ref
  11.6 0.0 copy-start.4
  11.6 0.0 copy-start.2
  11.6 1.6 %collective-permute-start.6 = (bf16[40,512]{1,0:T(8,128)(2,1)S(1)}, bf16[40,512]{1,0:T(8,128)(2,1)S(1)}, u32[]{:S(2)}, u32[]{:S(2)}) collective-permute-start(bf16[40,512]{1,0:T(8,128)(2,1)S(1)} %get-tuple-element.30), channel_id=1, source_target_pairs={{0,4},{4,0},{1,5},{5,1},{2,6},{6,2},{3,7},{7,3},{8,12},{12,8},{9,1... | collective-permute-start | bytes 122888 | tf_op jit(solution)/shard_map/ppermute | solution.py:380
  13.2 0.0 copy-done.4
  13.2 0.0 copy-done.3
  13.2 0.0 copy-done.2
  13.2 0.0 copy-start
  13.3 0.0 copy-start.1
  13.3 0.4 %gate.1.gate_ref = f32[256,512]{1,0:T(8,128)S(1)} custom-call(bf16[256,512]{1,0:T(8,128)(2,1)S(1)} %bitcast.5, bf16[512,512]{1,0:T(8,128)(2,1)S(1)} %copy-done.3), custom_call_target="tpu_custom_call" | custom-call | flops 134217728 | bytes 1310720 | tf_op jit(solution)/shard_map/gate/pallas_call | solution.py:20
  13.7 0.7 %collective-permute-done.5.refs_1_ = bf16[192,512]{1,0:T(8,128)(2,1)S(1)} collective-permute-done((bf16[192,512]{1,0:T(8,128)(2,1)S(1)}, bf16[192,512]{1,0:T(8,128)(2,1)S(1)}, u32[]{:S(2)}, u32[]{:S(2)}) %collective-permute-start.5) | collective-permute-done | bytes 196640 | tf_op jit(solution)/shard_map/ppermute | solution.py:361
  14.4 0.0 copy-done
  14.4 0.1 copy-done.1
  14.5 1.5 %inner.1 = (bf16[256,512]{1,0:T(8,128)(2,1)}, f32[128,512]{1,0:T(8,128)S(1)}) custom-call(f32[256,512]{1,0:T(8,128)S(1)} %own.1.mine_ref, f32[32,512]{1,0:T(8,128)S(1)} %get-tuple-element.25.low_ref, f32[32,512]{1,0:T(8,128)S(1)} %get-tuple-element.26.high_ref, f32[9,512]{1,0:T(8,128)S(1)} %reshape.14.taps_ref, f32[256,512]{1,0:T(8,128)S(1)} %gate.1.gate_ref, ...), custom_call_target="tpu_custom_call" | custom-call | flops 268435456 | bytes 3033088 | tf_op jit(solution)/shard_map/inner/pallas_call | solution.py:20
  16.0 0.0 collective-permute-done.6.refs_0_
  16.0 1.0 %edge.1 = bf16[256,512]{1,0:T(8,128)(2,1)} custom-call(bf16[256,512]{1,0:T(8,128)(2,1)} %get-tuple-element.28.inner_ref, f32[128,512]{1,0:T(8,128)S(1)} %get-tuple-element.29.edges_ref, f32[9,512]{1,0:T(8,128)S(1)} %reshape.14.taps_ref, f32[256,512]{1,0:T(8,128)S(1)} %gate.1.gate_ref, bf16[512,512]{1,0:T(8,128)(2,1)S(1)} %copy-done, ...), custom_call_target="tpu_custom_call", output_to_operand_aliasing={{}: (0, {})} | custom-call | flops 67108864 | bytes 2418688 | tf_op jit(solution)/shard_map/edge/pallas_call | solution.py:20
  (2 shorter events, 0.1 us)
Async XLA Ops:
  0.0 1.8 %collective-permute-start = (bf16[256,512]{1,0:T(8,128)(2,1)}, bf16[256,512]{1,0:T(8,128)(2,1)S(1)}, u32[]{:S(2)}, u32[]{:S(2)}) collective-permute-start(bf16[256,512]{1,0:T(8,128)(2,1)} %bitcast.3), channel_id=1, source_target_pairs={{0,8},{8,0},{16,24},{24,16},{1,9},{9,1},{17,25},{25,17},{2,10},{10... | collective-permute-start | bytes 786440 | tf_op jit(solution)/shard_map/ppermute | solution.py:304
  1.9 6.7 %collective-permute-start.1 = (bf16[64,512]{1,0:T(8,128)(2,1)S(1)}, bf16[64,512]{1,0:T(8,128)(2,1)S(1)}, u32[]{:S(2)}, u32[]{:S(2)}) collective-permute-start(bf16[64,512]{1,0:T(8,128)(2,1)S(1)} %column.1), channel_id=1, source_target_pairs={{0,17},{1,16},{2,19},{3,18},{4,21},{5,20},{6,23},{7,22},{8,28},{9,... | collective-permute-start | bytes 196616 | tf_op jit(solution)/shard_map/ppermute | solution.py:357
  5.9 4.3 %collective-permute-start.2 = (bf16[64,512]{1,0:T(8,128)(2,1)S(1)}, bf16[64,512]{1,0:T(8,128)(2,1)S(1)}, u32[]{:S(2)}, u32[]{:S(2)}) collective-permute-start(bf16[64,512]{1,0:T(8,128)(2,1)S(1)} %column.1), channel_id=1, source_target_pairs={{0,1},{1,0},{2,3},{3,2},{4,5},{5,4},{6,7},{7,6},{8,12},{9,10},{10,... | collective-permute-start | bytes 196616 | tf_op jit(solution)/shard_map/ppermute | solution.py:357
  6.5 5.1 %collective-permute-start.4 = (bf16[64,512]{1,0:T(8,128)(2,1)S(1)}, bf16[64,512]{1,0:T(8,128)(2,1)S(1)}, u32[]{:S(2)}, u32[]{:S(2)}) collective-permute-start(bf16[64,512]{1,0:T(8,128)(2,1)S(1)} %get-tuple-element.24), channel_id=1, source_target_pairs={{0,16},{8,24},{16,0},{24,8},{1,17},{9,25},{17,1},{25,9},{2,18},{10... | collective-permute-start | bytes 196616 | tf_op jit(solution)/shard_map/ppermute | solution.py:360
  6.8 7.6 %collective-permute-start.5 = (bf16[192,512]{1,0:T(8,128)(2,1)S(1)}, bf16[192,512]{1,0:T(8,128)(2,1)S(1)}, u32[]{:S(2)}, u32[]{:S(2)}) collective-permute-start(bf16[192,512]{1,0:T(8,128)(2,1)S(1)} %get-tuple-element.27), channel_id=1, source_target_pairs={{0,16},{8,24},{16,0},{24,8},{1,17},{9,25},{17,1},{25,9},{2,18},{10... | collective-permute-start | bytes 589832 | tf_op jit(solution)/shard_map/ppermute | solution.py:361
  10.3 1.3 %collective-permute-start.3 = (bf16[32,512]{1,0:T(8,128)(2,1)S(1)}, bf16[32,512]{1,0:T(8,128)(2,1)S(1)}, u32[]{:S(2)}, u32[]{:S(2)}) collective-permute-start(bf16[32,512]{1,0:T(8,128)(2,1)S(1)} %get-tuple-element.22), channel_id=1, source_target_pairs={{0,8},{8,0},{16,24},{24,16},{1,9},{9,1},{17,25},{25,17},{2,10},{10... | collective-permute-start | bytes 98312 | tf_op jit(solution)/shard_map/ppermute | solution.py:371
  10.4 2.9 %copy-start.3 = (bf16[512,512]{1,0:T(8,128)(2,1)S(1)}, bf16[512,512]{1,0:T(8,128)(2,1)}, u32[]{:S(2)}) copy-start(bf16[512,512]{1,0:T(8,128)(2,1)} %w_ref.1) | copy-start | bytes 1572868
  11.6 1.6 %copy-start.4 = (f32[3,3,512]{2,1,0:T(4,128)S(1)}, f32[3,3,512]{2,1,0:T(4,128)}, u32[]{:S(2)}) copy-start(f32[3,3,512]{2,1,0:T(4,128)} %param.8) | copy-start | bytes 55300
  11.6 1.6 %copy-start.2 = (bf16[4,8,8,512]{3,2,1,0:T(8,128)(2,1)S(1)}, bf16[4,8,8,512]{3,2,1,0:T(8,128)(2,1)}, u32[]{:S(2)}) copy-start(bf16[4,8,8,512]{3,2,1,0:T(8,128)(2,1)} %param.7) | copy-start | bytes 786436
  11.6 4.3 %collective-permute-start.6 = (bf16[40,512]{1,0:T(8,128)(2,1)S(1)}, bf16[40,512]{1,0:T(8,128)(2,1)S(1)}, u32[]{:S(2)}, u32[]{:S(2)}) collective-permute-start(bf16[40,512]{1,0:T(8,128)(2,1)S(1)} %get-tuple-element.30), channel_id=1, source_target_pairs={{0,4},{4,0},{1,5},{5,1},{2,6},{6,2},{3,7},{7,3},{8,12},{12,8},{9,1... | collective-permute-start | bytes 122888 | tf_op jit(solution)/shard_map/ppermute | solution.py:380
  13.2 1.1 %copy-start = (bf16[512,512]{1,0:T(8,128)(2,1)S(1)}, bf16[512,512]{1,0:T(8,128)(2,1)}, u32[]{:S(2)}) copy-start(bf16[512,512]{1,0:T(8,128)(2,1)} %wv_ref.3) | copy-start | bytes 1572868
  13.3 1.2 %copy-start.1 = (bf16[512,512]{1,0:T(8,128)(2,1)S(1)}, bf16[512,512]{1,0:T(8,128)(2,1)}, u32[]{:S(2)}) copy-start(bf16[512,512]{1,0:T(8,128)(2,1)} %wo_ref.3) | copy-start | bytes 1572868

commit v11 on v10

--- a/solution.py
+++ b/solution.py
@@ -14,16 +14,15 @@
 HBM = pl.BlockSpec(memory_space=pltpu.HBM)
 
 
-def call(kernel, name, outs, scratch, operands, flops=0, exps=0, far=0, far_outs=0, aliases={}):
+def call(kernel, name, outs, scratch, operands, flops=0, exps=0, far=0):
     operands = [pltpu.with_memory_space_constraint(a, pltpu.HBM) for a in operands[:far]] + list(operands[far:])
     moved = sum(a.size * a.dtype.itemsize for a in operands) + sum(a.size * a.dtype.itemsize for a in outs)
     return pl.pallas_call(
         kernel,
         out_shape=tuple(outs),
         in_specs=[HBM] * far + [VMEM] * (len(operands) - far),
-        out_specs=(HBM,) * far_outs + (VMEM,) * (len(outs) - far_outs),
+        out_specs=(VMEM,) * len(outs),
         scratch_shapes=scratch,
-        input_output_aliases=aliases,
         compiler_params=pltpu.CompilerParams(vmem_limit_bytes=24 * 1024 * 1024),
         cost_estimate=pl.CostEstimate(flops=flops, bytes_accessed=moved, transcendentals=exps),
         name=name,
@@ -137,8 +136,8 @@
             span = slice(lane, lane + LANES)
             totals = with_partner(frames, rows, cols, d, field, partner_ref, table_ref, span)
             tiles = reordered([jnp.concatenate([t[r] for t in totals]) for r in range(rows)], rounds_h)
-            outs[2 * d - 2][:, span] = jnp.concatenate(tiles[:2]).astype(BF16)
-            outs[2 * d - 1][:, span] = jnp.concatenate(tiles[2:]).astype(BF16)
+            outs[2 * d - 2][:, span] = jnp.concatenate(tiles[:rounds_h]).astype(BF16)
+            outs[2 * d - 1][:, span] = jnp.concatenate(tiles[rounds_h:]).astype(BF16)
 
 
 def own_kernel(frames, rows, cols, partner_ref, table_ref, field_ref, mine_ref):
@@ -219,7 +218,7 @@
 def inner_kernel(
     frames, rows, cols, rounds_h, mine_ref, low_ref, high_ref, taps_ref, gate_ref, wv_ref, wo_ref, *refs
 ):
-    *parts, out_ref, edges_ref, mixed, held, done = refs
+    *parts, out_ref, edges_ref, mixed = refs
     firsts, rests = parts[: len(parts) // 2], parts[len(parts) // 2 :]
     chans = mine_ref.shape[1]
     sites = rows * cols
@@ -233,8 +232,8 @@
             for r in range(rows)
         ]
         for d, (first, rest) in enumerate(zip(firsts, rests), 1):
-            more = [first[i * size : (i + 1) * size, span].astype(F32) for i in range(2)]
-            more += [rest[i * size : (i + 1) * size, span].astype(F32) for i in range(rows - 2)]
+            more = [first[i * size : (i + 1) * size, span].astype(F32) for i in range(rounds_h)]
+            more += [rest[i * size : (i + 1) * size, span].astype(F32) for i in range(rows - rounds_h)]
             more = reordered(more, rounds_h, back=True)
             lines = [line + later(d, other) for line, other in zip(lines, more)]
         for t in range(frames):
@@ -249,47 +248,39 @@
                         term = near[0] * taps[a][0] + near[1] * taps[a][1] + near[2] * taps[a][2]
                         totals[to] = term if totals[to] is None else totals[to] + term
             mixed[at : at + sites, span] = jnp.concatenate(totals, axis=0).astype(BF16)
-            for k, edge in enumerate((totals[:2], totals[-2:])):
-                edges_ref[2 * (k * size + t * cols) : 2 * (k * size + (t + 1) * cols), span] = jnp.concatenate(edge)
-    held[...] = projected(mixed[...], gate_ref[...], wv_ref, wo_ref)
-    copy = pltpu.make_async_copy(held, out_ref, done)
-    copy.start()
-    copy.wait()
-
-
-def edge_kernel(frames, rows, cols, rounds_h, inner_ref, edges_ref, taps_ref, gate_ref, wv_ref, wo_ref, *refs):
-    ends, (out_ref, held, done) = refs[:rounds_h], refs[rounds_h:]
+            edges_ref[t * cols : (t + 1) * cols, span] = totals[0]
+            edges_ref[size + t * cols : size + (t + 1) * cols, span] = totals[rows - 1]
+    out_ref[...] = projected(mixed[...], gate_ref[...], wv_ref, wo_ref)
+
+
+def edge_kernel(frames, rows, cols, rounds_h, edges_ref, taps_ref, gate_ref, wv_ref, wo_ref, inner_ref, *refs):
+    ends, out_ref = refs[:rounds_h], refs[rounds_h]
     sites = rows * cols
     size = frames * cols
-    odd, lower, upper = position("height")
+    odd, _, _ = position("height")
+    out_ref[...] = inner_ref[...]
     taps = taps_ref[...]
-    mixed, gate, starts = [], [], []
+    mixed, gate = [], []
     for k, end in enumerate(ends):
         end = end[...].astype(F32)
         first = jnp.logical_not(odd) if k else odd
         lefts, rights = end[size : size + frames], end[size + frames : size + 2 * frames]
+        lower, upper = position("height")[1:]
         exists = jnp.where(first, lower, upper)
         tap = jnp.where(first, taps[0:3], taps[6:9])
-        total = jnp.where(first, edges_ref[: 2 * size], edges_ref[2 * size :])
+        total = jnp.where(first, edges_ref[0:size], edges_ref[size : 2 * size])
         for t in range(frames):
             near = shifted(end[t * cols : (t + 1) * cols], lefts[t : t + 1], rights[t : t + 1])
             more = near[0] * tap[0:1] + near[1] * tap[1:2] + near[2] * tap[2:3]
-            more = jnp.where(exists, more, jnp.zeros_like(more))
-            none = jnp.zeros_like(more)
-            mixed.append(total[2 * t * cols : (2 * t + 1) * cols] + jnp.where(first, more, none))
-            mixed.append(total[(2 * t + 1) * cols : (2 * t + 2) * cols] + jnp.where(first, none, more))
+            mixed.append(total[t * cols : (t + 1) * cols] + jnp.where(exists, more, jnp.zeros_like(more)))
             at = t * sites
-            gate.append(jnp.where(first, gate_ref[at : at + 2 * cols], gate_ref[at + sites - 2 * cols : at + sites]))
-            starts.append(pl.multiple_of(at + jnp.where(first, 0, sites - 2 * cols), 2 * cols))
-    held[...] = projected(jnp.concatenate(mixed).astype(BF16), jnp.concatenate(gate), wv_ref, wo_ref)
-    copies = [
-        pltpu.make_async_copy(held.at[pl.ds(2 * i * cols, 2 * cols)], out_ref.at[pl.ds(at, 2 * cols)], done.at[i])
-        for i, at in enumerate(starts)
-    ]
-    for copy in copies:
-        copy.start()
-    for copy in copies:
-        copy.wait()
+            gate.append(jnp.where(first, gate_ref[at : at + cols], gate_ref[at + sites - cols : at + sites]))
+    out = projected(jnp.concatenate(mixed, axis=0).astype(BF16), jnp.concatenate(gate, axis=0), wv_ref, wo_ref)
+    for t in range(frames):
+        new = [out[k * size + t * cols : k * size + (t + 1) * cols] for k in range(rounds_h)]
+        for at, other in ((t * sites, False), (t * sites + sites - cols, True)):
+            kept = new[1] if rounds_h > 1 else inner_ref[at : at + cols]
+            out_ref[at : at + cols] = jnp.where(odd, kept, new[0]) if other else jnp.where(odd, new[0], kept)
 
 
 def body(latents, spatial_taps, kernel_taps, skip_gain, gate_weight, value_weight, out_weight):
@@ -327,7 +318,7 @@
         [pltpu.VMEM((block, LANES), F32)],
         [partner, side],
     )
-    parts = [shape((n * frames * cols, chans), BF16) for n in (2, rows - 2)]
+    parts = [shape((n * frames * cols, chans), BF16) for n in (len(h_rounds), rows - len(h_rounds))]
     sent = call(
         functools.partial(later_kernel, frames, rows, cols, len(h_rounds)),
         "later",
@@ -383,25 +374,18 @@
     inner, edges = call(
         functools.partial(inner_kernel, frames, rows, cols, len(h_rounds)),
         "inner",
-        [shape((block, chans), BF16), shape((4 * frames * cols, chans), F32)],
-        [pltpu.VMEM((block, chans), BF16)] * 2 + [pltpu.SemaphoreType.DMA],
+        [shape((block, chans), BF16), shape((2 * frames * cols, chans), F32)],
+        [pltpu.VMEM((block, chans), BF16)],
         [mine, low, high, taps, gate, value_weight, out_weight] + firsts + rests,
         4 * block * chans * chans,
-        far_outs=1,
     )
     (out,) = call(
         functools.partial(edge_kernel, frames, rows, cols, len(h_rounds)),
         "edge",
         [shape((block, chans), BF16)],
-        [
-            pltpu.VMEM((len(h_rounds) * 2 * frames * cols, chans), BF16),
-            pltpu.SemaphoreType.DMA((len(h_rounds) * frames,)),
-        ],
-        [inner, edges, taps, gate, value_weight, out_weight] + ends,
-        8 * frames * cols * chans * chans,
-        far=1,
-        far_outs=1,
-        aliases={0: 0},
+        [],
+        [edges, taps, gate, value_weight, out_weight, inner] + ends,
+        4 * frames * cols * chans * chans,
     )
     return out.reshape(latents.shape)
 

time: 17.3 us -> 17 us (0.983)
  Pallas kernels: 4.89 us -> 4.19 us
  waiting for transfers between devices: 3.31 us -> 3.76 us
    ppermute x1, waiting for transfers between devices: 1.05 us -> 0.34 us  [body(): firsts.append(lax.ppermute(sent[2 * d - 2], 'tm', route))]
    pallas_call x9, Pallas kernels: 4.89 us -> 4.19 us  [call(): pl.pallas_call(kernel, out_shape=tuple(outs), in_specs=[HBM] * far + [VME...]
    ppermute x1, waiting for transfers between devices: 0.01 us -> 0.67 us  [body(): other = lax.ppermute(other, 'tm', [(i, i ^ 1) for i in range(n_t)])]
    ppermute x1, waiting for transfers between devices: 0.01 us -> 0.45 us  [body(): lax.ppermute(e, 'height', pairs)]
  transfers between devices with their start and end apart: 7 -> 7, of which waited for: 3 -> 5; matrix products, arithmetic and copies ran while one was open for 0% -> 0% of each run, Pallas kernels for 22% -> 18%
where the time goes in v11:
time: 17 us; the launch traced here: 16.7 us
  starting transfers between devices  8.59 us (51%)
  Pallas kernels  4.19 us (25%)
  waiting for transfers between devices  3.76 us (22%)
    ppermute x2, starting transfers between devices, body(): columns.append(lax.ppermute(column, ('tm', 'height', 'width'), route))  4.42 us
    pallas_call x9, Pallas kernels, call(): pl.pallas_call(kernel, out_shape=tuple(outs), in_specs=[HBM] * far + [VME...  4.19 us
    ppermute x1, starting transfers between devices, body(): rests.append(lax.ppermute(sent[2 * d - 1], 'tm', route))  1.83 us
    ppermute x1, starting transfers between devices, body(): lax.ppermute(e, 'height', pairs)  1.56 us
    ppermute x2, waiting for transfers between devices, body(): columns.append(lax.ppermute(column, ('tm', 'height', 'width'), route))  1.52 us
    ppermute x1, waiting for transfers between devices, body(): rests.append(lax.ppermute(sent[2 * d - 1], 'tm', route))  0.74 us
    ppermute x1, waiting for transfers between devices, body(): other = lax.ppermute(other, 'tm', [(i, i ^ 1) for i in range(n_t)])  0.67 us
    ppermute x1, starting transfers between devices, body(): partner = lax.ppermute(x, 'tm', [(i, i ^ 1) for i in range(n_t)])  0.45 us
  transfers between devices with their start and end apart: 7, of which 5 were waited for; matrix products, arithmetic and copies ran while one was open for 0% of the time, Pallas kernels for 18%

profile of v11, /device:TPU:0, one launch (start us, length us, event | category | flops | bytes accessed | tf_op | source)
XLA Modules:
  0.0 16.7 jit_solution(16091203744089250916)
XLA Ops:
  0.0 0.5 %collective-permute-start = (bf16[256,512]{1,0:T(8,128)(2,1)}, bf16[256,512]{1,0:T(8,128)(2,1)S(1)}, u32[]{:S(2)}, u32[]{:S(2)}) collective-permute-start(bf16[256,512]{1,0:T(8,128)(2,1)} %bitcast.3), channel_id=1, source_target_pairs={{0,8},{8,0},{16,24},{24,16},{1,9},{9,1},{17,25},{25,17},{2,10},{10... | collective-permute-start | bytes 786440 | tf_op jit(solution)/shard_map/ppermute | solution.py:295
  0.5 1.3 %early.1 = (f32[24,8,512]{2,1,0:T(8,128)S(1)}, f32[32,512]{1,0:T(8,128)S(1)}, f32[256,512]{1,0:T(8,128)S(1)}, f32[256,512]{1,0:T(8,128)S(1)}) custom-call(bf16[16,512]{1,0:T(8,128)(2,1)} %refs_0_.1, f32[1,512]{1,0:T(1,128)} %bitcast.6, bf16[256,512]{1,0:T(8,128)(2,1)} %bitcast.4), custom_call_target="tpu_custom_call" | custom-call | flops 2097152 | bytes 1787904 | tf_op jit(solution)/shard_map/early/pallas_call | solution.py:20
  1.8 0.0 collective-permute-done.partner_ref
  1.8 0.1 column.1
  1.9 4.0 %collective-permute-start.1 = (bf16[64,512]{1,0:T(8,128)(2,1)S(1)}, bf16[64,512]{1,0:T(8,128)(2,1)S(1)}, u32[]{:S(2)}, u32[]{:S(2)}) collective-permute-start(bf16[64,512]{1,0:T(8,128)(2,1)S(1)} %column.1), channel_id=1, source_target_pairs={{0,17},{1,16},{2,19},{3,18},{4,21},{5,20},{6,23},{7,22},{8,28},{9,... | collective-permute-start | bytes 196616 | tf_op jit(solution)/shard_map/ppermute | solution.py:348
  5.9 0.4 %collective-permute-start.2 = (bf16[64,512]{1,0:T(8,128)(2,1)S(1)}, bf16[64,512]{1,0:T(8,128)(2,1)S(1)}, u32[]{:S(2)}, u32[]{:S(2)}) collective-permute-start(bf16[64,512]{1,0:T(8,128)(2,1)S(1)} %column.1), channel_id=1, source_target_pairs={{0,1},{1,0},{2,3},{3,2},{4,5},{5,4},{6,7},{7,6},{8,12},{9,10},{10,... | collective-permute-start | bytes 196616 | tf_op jit(solution)/shard_map/ppermute | solution.py:348
  6.3 0.2 %later.1 = (bf16[32,512]{1,0:T(8,128)(2,1)S(1)}, bf16[224,512]{1,0:T(8,128)(2,1)S(1)}) custom-call(bf16[256,512]{1,0:T(8,128)(2,1)S(1)} %collective-permute-done.partner_ref, f32[24,8,512]{2,1,0:T(8,128)S(1)} %get-tuple-element.18.table_ref, f32[256,512]{1,0:T(8,128)S(1)} %get-tuple-element.23.refs_0_), custom_call_target="tpu_custom_call" | custom-call | flops 1048576 | bytes 1441792 | tf_op jit(solution)/shard_map/later/pallas_call | solution.py:20
  6.5 0.3 %collective-permute-start.4 = (bf16[32,512]{1,0:T(8,128)(2,1)S(1)}, bf16[32,512]{1,0:T(8,128)(2,1)S(1)}, u32[]{:S(2)}, u32[]{:S(2)}) collective-permute-start(bf16[32,512]{1,0:T(8,128)(2,1)S(1)} %get-tuple-element.24), channel_id=1, source_target_pairs={{0,16},{8,24},{16,0},{24,8},{1,17},{9,25},{17,1},{25,9},{2,18},{10... | collective-permute-start | bytes 98312 | tf_op jit(solution)/shard_map/ppermute | solution.py:351
  6.8 1.8 %collective-permute-start.5 = (bf16[224,512]{1,0:T(8,128)(2,1)S(1)}, bf16[224,512]{1,0:T(8,128)(2,1)S(1)}, u32[]{:S(2)}, u32[]{:S(2)}) collective-permute-start(bf16[224,512]{1,0:T(8,128)(2,1)S(1)} %get-tuple-element.27), channel_id=1, source_target_pairs={{0,16},{8,24},{16,0},{24,8},{1,17},{9,25},{17,1},{25,9},{2,18},{10... | collective-permute-start | bytes 688136 | tf_op jit(solution)/shard_map/ppermute | solution.py:352
  8.6 0.0 collective-permute-done.1.refs_0_
  8.6 1.5 %collective-permute-done.2.refs_1_ = bf16[64,512]{1,0:T(8,128)(2,1)S(1)} collective-permute-done((bf16[64,512]{1,0:T(8,128)(2,1)S(1)}, bf16[64,512]{1,0:T(8,128)(2,1)S(1)}, u32[]{:S(2)}, u32[]{:S(2)}) %collective-permute-start.2) | collective-permute-done | bytes 65568 | tf_op jit(solution)/shard_map/ppermute | solution.py:348
  10.1 0.2 side.1
  10.3 0.1 collective-permute-start.3
  10.4 0.0 copy-start.3
  10.4 0.2 own.1.mine_ref
  10.5 0.3 %collective-permute-done.4.refs_0_ = bf16[32,512]{1,0:T(8,128)(2,1)S(1)} collective-permute-done((bf16[32,512]{1,0:T(8,128)(2,1)S(1)}, bf16[32,512]{1,0:T(8,128)(2,1)S(1)}, u32[]{:S(2)}, u32[]{:S(2)}) %collective-permute-start.4) | collective-permute-done | bytes 32800 | tf_op jit(solution)/shard_map/ppermute | solution.py:351
  10.9 0.7 %collective-permute-done.3.other_ref = bf16[32,512]{1,0:T(8,128)(2,1)S(1)} collective-permute-done((bf16[32,512]{1,0:T(8,128)(2,1)S(1)}, bf16[32,512]{1,0:T(8,128)(2,1)S(1)}, u32[]{:S(2)}, u32[]{:S(2)}) %collective-permute-start.3) | collective-permute-done | bytes 32800 | tf_op jit(solution)/shard_map/ppermute | solution.py:362
  11.6 0.0 copy-start.4
  11.6 0.0 copy-start.2
  11.6 1.6 %collective-permute-start.6 = (bf16[40,512]{1,0:T(8,128)(2,1)S(1)}, bf16[40,512]{1,0:T(8,128)(2,1)S(1)}, u32[]{:S(2)}, u32[]{:S(2)}) collective-permute-start(bf16[40,512]{1,0:T(8,128)(2,1)S(1)} %get-tuple-element.30), channel_id=1, source_target_pairs={{0,4},{4,0},{1,5},{5,1},{2,6},{6,2},{3,7},{7,3},{8,12},{12,8},{9,1... | collective-permute-start | bytes 122888 | tf_op jit(solution)/shard_map/ppermute | solution.py:371
  13.2 0.0 copy-done.4
  13.2 0.0 copy-done.3
  13.2 0.0 copy-done.2
  13.2 0.0 copy-start
  13.2 0.0 copy-start.1
  13.2 0.4 %gate.1.gate_ref = f32[256,512]{1,0:T(8,128)S(1)} custom-call(bf16[256,512]{1,0:T(8,128)(2,1)S(1)} %bitcast.5, bf16[512,512]{1,0:T(8,128)(2,1)S(1)} %copy-done.3), custom_call_target="tpu_custom_call" | custom-call | flops 134217728 | bytes 1310720 | tf_op jit(solution)/shard_map/gate/pallas_call | solution.py:20
  13.6 0.7 %collective-permute-done.5.refs_1_ = bf16[224,512]{1,0:T(8,128)(2,1)S(1)} collective-permute-done((bf16[224,512]{1,0:T(8,128)(2,1)S(1)}, bf16[224,512]{1,0:T(8,128)(2,1)S(1)}, u32[]{:S(2)}, u32[]{:S(2)}) %collective-permute-start.5) | collective-permute-done | bytes 229408 | tf_op jit(solution)/shard_map/ppermute | solution.py:352
  14.4 0.0 copy-done
  14.4 0.0 copy-done.1
  14.4 0.8 %inner.1 = (bf16[256,512]{1,0:T(8,128)(2,1)S(1)}, f32[64,512]{1,0:T(8,128)S(1)}) custom-call(f32[256,512]{1,0:T(8,128)S(1)} %own.1.mine_ref, f32[32,512]{1,0:T(8,128)S(1)} %get-tuple-element.25.low_ref, f32[32,512]{1,0:T(8,128)S(1)} %get-tuple-element.26.high_ref, f32[9,512]{1,0:T(8,128)S(1)} %reshape.14.taps_ref, f32[256,512]{1,0:T(8,128)S(1)} %gate.1.gate_ref, ...), custom_call_target="tpu_custom_call" | custom-call | flops 268435456 | bytes 2902016 | tf_op jit(solution)/shard_map/inner/pallas_call | solution.py:20
  15.2 0.4 %collective-permute-done.6.refs_0_ = bf16[40,512]{1,0:T(8,128)(2,1)S(1)} collective-permute-done((bf16[40,512]{1,0:T(8,128)(2,1)S(1)}, bf16[40,512]{1,0:T(8,128)(2,1)S(1)}, u32[]{:S(2)}, u32[]{:S(2)}) %collective-permute-start.6) | collective-permute-done | bytes 40992 | tf_op jit(solution)/shard_map/ppermute | solution.py:371
  15.7 1.1 %edge.1 = bf16[256,512]{1,0:T(8,128)(2,1)} custom-call(f32[64,512]{1,0:T(8,128)S(1)} %get-tuple-element.28.edges_ref, f32[9,512]{1,0:T(8,128)S(1)} %reshape.14.taps_ref, f32[256,512]{1,0:T(8,128)S(1)} %gate.1.gate_ref, bf16[512,512]{1,0:T(8,128)(2,1)S(1)} %copy-done, bf16[512,512]{1,0:T(8,128)(2,1)S(1)} %copy-done.1, ...), custom_call_target="tpu_custom_call" | custom-call | flops 33554432 | bytes 2287616 | tf_op jit(solution)/shard_map/edge/pallas_call | solution.py:20
  (2 shorter events, 0.1 us)
Async XLA Ops:
  0.0 1.8 %collective-permute-start = (bf16[256,512]{1,0:T(8,128)(2,1)}, bf16[256,512]{1,0:T(8,128)(2,1)S(1)}, u32[]{:S(2)}, u32[]{:S(2)}) collective-permute-start(bf16[256,512]{1,0:T(8,128)(2,1)} %bitcast.3), channel_id=1, source_target_pairs={{0,8},{8,0},{16,24},{24,16},{1,9},{9,1},{17,25},{25,17},{2,10},{10... | collective-permute-start | bytes 786440 | tf_op jit(solution)/shard_map/ppermute | solution.py:295
  1.9 6.7 %collective-permute-start.1 = (bf16[64,512]{1,0:T(8,128)(2,1)S(1)}, bf16[64,512]{1,0:T(8,128)(2,1)S(1)}, u32[]{:S(2)}, u32[]{:S(2)}) collective-permute-start(bf16[64,512]{1,0:T(8,128)(2,1)S(1)} %column.1), channel_id=1, source_target_pairs={{0,17},{1,16},{2,19},{3,18},{4,21},{5,20},{6,23},{7,22},{8,28},{9,... | collective-permute-start | bytes 196616 | tf_op jit(solution)/shard_map/ppermute | solution.py:348
  5.9 4.3 %collective-permute-start.2 = (bf16[64,512]{1,0:T(8,128)(2,1)S(1)}, bf16[64,512]{1,0:T(8,128)(2,1)S(1)}, u32[]{:S(2)}, u32[]{:S(2)}) collective-permute-start(bf16[64,512]{1,0:T(8,128)(2,1)S(1)} %column.1), channel_id=1, source_target_pairs={{0,1},{1,0},{2,3},{3,2},{4,5},{5,4},{6,7},{7,6},{8,12},{9,10},{10,... | collective-permute-start | bytes 196616 | tf_op jit(solution)/shard_map/ppermute | solution.py:348
  6.5 4.4 %collective-permute-start.4 = (bf16[32,512]{1,0:T(8,128)(2,1)S(1)}, bf16[32,512]{1,0:T(8,128)(2,1)S(1)}, u32[]{:S(2)}, u32[]{:S(2)}) collective-permute-start(bf16[32,512]{1,0:T(8,128)(2,1)S(1)} %get-tuple-element.24), channel_id=1, source_target_pairs={{0,16},{8,24},{16,0},{24,8},{1,17},{9,25},{17,1},{25,9},{2,18},{10... | collective-permute-start | bytes 98312 | tf_op jit(solution)/shard_map/ppermute | solution.py:351
  6.8 7.6 %collective-permute-start.5 = (bf16[224,512]{1,0:T(8,128)(2,1)S(1)}, bf16[224,512]{1,0:T(8,128)(2,1)S(1)}, u32[]{:S(2)}, u32[]{:S(2)}) collective-permute-start(bf16[224,512]{1,0:T(8,128)(2,1)S(1)} %get-tuple-element.27), channel_id=1, source_target_pairs={{0,16},{8,24},{16,0},{24,8},{1,17},{9,25},{17,1},{25,9},{2,18},{10... | collective-permute-start | bytes 688136 | tf_op jit(solution)/shard_map/ppermute | solution.py:352
  10.3 1.3 %collective-permute-start.3 = (bf16[32,512]{1,0:T(8,128)(2,1)S(1)}, bf16[32,512]{1,0:T(8,128)(2,1)S(1)}, u32[]{:S(2)}, u32[]{:S(2)}) collective-permute-start(bf16[32,512]{1,0:T(8,128)(2,1)S(1)} %get-tuple-element.22), channel_id=1, source_target_pairs={{0,8},{8,0},{16,24},{24,16},{1,9},{9,1},{17,25},{25,17},{2,10},{10... | collective-permute-start | bytes 98312 | tf_op jit(solution)/shard_map/ppermute | solution.py:362
  10.4 2.8 %copy-start.3 = (bf16[512,512]{1,0:T(8,128)(2,1)S(1)}, bf16[512,512]{1,0:T(8,128)(2,1)}, u32[]{:S(2)}) copy-start(bf16[512,512]{1,0:T(8,128)(2,1)} %w_ref.1) | copy-start | bytes 1572868
  11.6 1.6 %copy-start.4 = (f32[3,3,512]{2,1,0:T(4,128)S(1)}, f32[3,3,512]{2,1,0:T(4,128)}, u32[]{:S(2)}) copy-start(f32[3,3,512]{2,1,0:T(4,128)} %param.8) | copy-start | bytes 55300
  11.6 1.6 %copy-start.2 = (bf16[4,8,8,512]{3,2,1,0:T(8,128)(2,1)S(1)}, bf16[4,8,8,512]{3,2,1,0:T(8,128)(2,1)}, u32[]{:S(2)}) copy-start(bf16[4,8,8,512]{3,2,1,0:T(8,128)(2,1)} %param.7) | copy-start | bytes 786436
  11.6 4.1 %collective-permute-start.6 = (bf16[40,512]{1,0:T(8,128)(2,1)S(1)}, bf16[40,512]{1,0:T(8,128)(2,1)S(1)}, u32[]{:S(2)}, u32[]{:S(2)}) collective-permute-start(bf16[40,512]{1,0:T(8,128)(2,1)S(1)} %get-tuple-element.30), channel_id=1, source_target_pairs={{0,4},{4,0},{1,5},{5,1},{2,6},{6,2},{3,7},{7,3},{8,12},{12,8},{9,1... | collective-permute-start | bytes 122888 | tf_op jit(solution)/shard_map/ppermute | solution.py:371
  13.2 1.2 %copy-start = (bf16[512,512]{1,0:T(8,128)(2,1)S(1)}, bf16[512,512]{1,0:T(8,128)(2,1)}, u32[]{:S(2)}) copy-start(bf16[512,512]{1,0:T(8,128)(2,1)} %wv_ref.3) | copy-start | bytes 1572868
  13.2 1.2 %copy-start.1 = (bf16[512,512]{1,0:T(8,128)(2,1)S(1)}, bf16[512,512]{1,0:T(8,128)(2,1)}, u32[]{:S(2)}) copy-start(bf16[512,512]{1,0:T(8,128)(2,1)} %wo_ref.3) | copy-start | bytes 1572868

commit v12 on v11

--- a/solution.py
+++ b/solution.py
@@ -158,7 +158,7 @@
     for lane in range(0, own_ref.shape[1], LANES):
         span = slice(lane, lane + LANES)
         totals = [jnp.zeros((rows, LANES), F32)] * (2 * frames)
-        for d, ref in enumerate(arrived[::-1]):
+        for d, ref in enumerate(arrived):
             column = later(d, ref[:, span].astype(F32))
             base = 2 * frames + 2 * d * frames
             for t in range(2 * frames):
@@ -219,6 +219,7 @@
     frames, rows, cols, rounds_h, mine_ref, low_ref, high_ref, taps_ref, gate_ref, wv_ref, wo_ref, *refs
 ):
     *parts, out_ref, edges_ref, mixed = refs
+    value = 0.0
     firsts, rests = parts[: len(parts) // 2], parts[len(parts) // 2 :]
     chans = mine_ref.shape[1]
     sites = rows * cols
@@ -250,7 +251,11 @@
             mixed[at : at + sites, span] = jnp.concatenate(totals, axis=0).astype(BF16)
             edges_ref[t * cols : (t + 1) * cols, span] = totals[0]
             edges_ref[size + t * cols : size + (t + 1) * cols, span] = totals[rows - 1]
-    out_ref[...] = projected(mixed[...], gate_ref[...], wv_ref, wo_ref)
+        if (lane + LANES) % (chans // 2) == 0:
+            half = slice(lane + LANES - chans // 2, lane + LANES)
+            value = value + jnp.dot(mixed[:, half], wv_ref[half], preferred_element_type=F32)
+    hidden = (value * gate_ref[...]).astype(BF16)
+    out_ref[...] = jnp.dot(hidden, wo_ref[...], preferred_element_type=F32).astype(BF16)
 
 
 def edge_kernel(frames, rows, cols, rounds_h, edges_ref, taps_ref, gate_ref, wv_ref, wo_ref, inner_ref, *refs):
@@ -336,7 +341,7 @@
         2 * frames * x.size,
     )
     columns, firsts, rests = [], [], []
-    for d in reversed(range(chips)):
+    for d in range(chips):
         route = []
         for i in range(n_t):
             for h in range(n_h):

time: 17 us -> 17.3 us (1.018)
  waiting for transfers between devices: 3.76 us -> 4.14 us
    ppermute x1, waiting for transfers between devices: 0.74 us -> 1.52 us  [body(): rests.append(lax.ppermute(sent[2 * d - 1], 'tm', route))]
    ppermute x1, waiting for transfers between devices: 0.45 us -> 0.01 us  [body(): lax.ppermute(e, 'height', pairs)]
  transfers between devices with their start and end apart: 7 -> 7, of which waited for: 5 -> 4; matrix products, arithmetic and copies ran while one was open for 0% -> 0% of each run, Pallas kernels for 18% -> 18%
where the time goes in v12:
time: 17.3 us; the launch traced here: 17.1 us
  starting transfers between devices  8.59 us (50%)
  Pallas kernels  4.2 us (24%)
  waiting for transfers between devices  4.14 us (24%)
    ppermute x2, starting transfers between devices, body(): columns.append(lax.ppermute(column, ('tm', 'height', 'width'), route))  4.42 us
    pallas_call x9, Pallas kernels, call(): pl.pallas_call(kernel, out_shape=tuple(outs), in_specs=[HBM] * far + [VME...  4.2 us
    ppermute x1, starting transfers between devices, body(): rests.append(lax.ppermute(sent[2 * d - 1], 'tm', route))  1.89 us
    ppermute x2, waiting for transfers between devices, body(): columns.append(lax.ppermute(column, ('tm', 'height', 'width'), route))  1.57 us
    ppermute x1, starting transfers between devices, body(): lax.ppermute(e, 'height', pairs)  1.56 us
    ppermute x1, waiting for transfers between devices, body(): rests.append(lax.ppermute(sent[2 * d - 1], 'tm', route))  1.52 us
    ppermute x1, waiting for transfers between devices, body(): other = lax.ppermute(other, 'tm', [(i, i ^ 1) for i in range(n_t)])  0.69 us
    ppermute x1, starting transfers between devices, body(): partner = lax.ppermute(x, 'tm', [(i, i ^ 1) for i in range(n_t)])  0.45 us
  transfers between devices with their start and end apart: 7, of which 4 were waited for; matrix products, arithmetic and copies ran while one was open for 0% of the time, Pallas kernels for 18%

profile of v12, /device:TPU:0, one launch (start us, length us, event | category | flops | bytes accessed | tf_op | source)
XLA Modules:
  0.0 17.1 jit_solution(17841186982019886991)
XLA Ops:
  0.0 0.5 %collective-permute-start = (bf16[256,512]{1,0:T(8,128)(2,1)}, bf16[256,512]{1,0:T(8,128)(2,1)S(1)}, u32[]{:S(2)}, u32[]{:S(2)}) collective-permute-start(bf16[256,512]{1,0:T(8,128)(2,1)} %bitcast.3), channel_id=1, source_target_pairs={{0,8},{8,0},{16,24},{24,16},{1,9},{9,1},{17,25},{25,17},{2,10},{10... | collective-permute-start | bytes 786440 | tf_op jit(solution)/shard_map/ppermute | solution.py:300
  0.5 1.3 %early.1 = (f32[24,8,512]{2,1,0:T(8,128)S(1)}, f32[32,512]{1,0:T(8,128)S(1)}, f32[256,512]{1,0:T(8,128)S(1)}, f32[256,512]{1,0:T(8,128)S(1)}) custom-call(bf16[16,512]{1,0:T(8,128)(2,1)} %refs_0_.1, f32[1,512]{1,0:T(1,128)} %bitcast.6, bf16[256,512]{1,0:T(8,128)(2,1)} %bitcast.4), custom_call_target="tpu_custom_call" | custom-call | flops 2097152 | bytes 1787904 | tf_op jit(solution)/shard_map/early/pallas_call | solution.py:20
  1.8 0.0 collective-permute-done.partner_ref
  1.8 0.1 column.1
  1.9 3.0 %collective-permute-start.1 = (bf16[64,512]{1,0:T(8,128)(2,1)S(1)}, bf16[64,512]{1,0:T(8,128)(2,1)S(1)}, u32[]{:S(2)}, u32[]{:S(2)}) collective-permute-start(bf16[64,512]{1,0:T(8,128)(2,1)S(1)} %column.1), channel_id=1, source_target_pairs={{0,1},{1,0},{2,3},{3,2},{4,5},{5,4},{6,7},{7,6},{8,12},{9,10},{10,... | collective-permute-start | bytes 196616 | tf_op jit(solution)/shard_map/ppermute | solution.py:353
  4.9 1.4 %collective-permute-start.2 = (bf16[64,512]{1,0:T(8,128)(2,1)S(1)}, bf16[64,512]{1,0:T(8,128)(2,1)S(1)}, u32[]{:S(2)}, u32[]{:S(2)}) collective-permute-start(bf16[64,512]{1,0:T(8,128)(2,1)S(1)} %column.1), channel_id=1, source_target_pairs={{0,17},{1,16},{2,19},{3,18},{4,21},{5,20},{6,23},{7,22},{8,28},{9,... | collective-permute-start | bytes 196616 | tf_op jit(solution)/shard_map/ppermute | solution.py:353
  6.3 0.2 %later.1 = (bf16[32,512]{1,0:T(8,128)(2,1)S(1)}, bf16[224,512]{1,0:T(8,128)(2,1)S(1)}) custom-call(bf16[256,512]{1,0:T(8,128)(2,1)S(1)} %collective-permute-done.partner_ref, f32[24,8,512]{2,1,0:T(8,128)S(1)} %get-tuple-element.18.table_ref, f32[256,512]{1,0:T(8,128)S(1)} %get-tuple-element.23.refs_0_), custom_call_target="tpu_custom_call" | custom-call | flops 1048576 | bytes 1441792 | tf_op jit(solution)/shard_map/later/pallas_call | solution.py:20
  6.5 0.2 %collective-permute-start.4 = (bf16[32,512]{1,0:T(8,128)(2,1)S(1)}, bf16[32,512]{1,0:T(8,128)(2,1)S(1)}, u32[]{:S(2)}, u32[]{:S(2)}) collective-permute-start(bf16[32,512]{1,0:T(8,128)(2,1)S(1)} %get-tuple-element.24), channel_id=1, source_target_pairs={{0,16},{8,24},{16,0},{24,8},{1,17},{9,25},{17,1},{25,9},{2,18},{10... | collective-permute-start | bytes 98312 | tf_op jit(solution)/shard_map/ppermute | solution.py:356
  6.7 1.9 %collective-permute-start.5 = (bf16[224,512]{1,0:T(8,128)(2,1)S(1)}, bf16[224,512]{1,0:T(8,128)(2,1)S(1)}, u32[]{:S(2)}, u32[]{:S(2)}) collective-permute-start(bf16[224,512]{1,0:T(8,128)(2,1)S(1)} %get-tuple-element.27), channel_id=1, source_target_pairs={{0,16},{8,24},{16,0},{24,8},{1,17},{9,25},{17,1},{25,9},{2,18},{10... | collective-permute-start | bytes 688136 | tf_op jit(solution)/shard_map/ppermute | solution.py:357
  8.6 0.0 collective-permute-done.1.refs_0_
  8.6 1.6 %collective-permute-done.2.refs_1_ = bf16[64,512]{1,0:T(8,128)(2,1)S(1)} collective-permute-done((bf16[64,512]{1,0:T(8,128)(2,1)S(1)}, bf16[64,512]{1,0:T(8,128)(2,1)S(1)}, u32[]{:S(2)}, u32[]{:S(2)}) %collective-permute-start.2) | collective-permute-done | bytes 65568 | tf_op jit(solution)/shard_map/ppermute | solution.py:353
  10.2 0.2 side.1
  10.3 0.1 collective-permute-start.3
  10.4 0.0 copy-start.3
  10.4 0.2 own.1.mine_ref
  10.6 0.3 %collective-permute-done.4.refs_0_ = bf16[32,512]{1,0:T(8,128)(2,1)S(1)} collective-permute-done((bf16[32,512]{1,0:T(8,128)(2,1)S(1)}, bf16[32,512]{1,0:T(8,128)(2,1)S(1)}, u32[]{:S(2)}, u32[]{:S(2)}) %collective-permute-start.4) | collective-permute-done | bytes 32800 | tf_op jit(solution)/shard_map/ppermute | solution.py:356
  10.9 0.7 %collective-permute-done.3.other_ref = bf16[32,512]{1,0:T(8,128)(2,1)S(1)} collective-permute-done((bf16[32,512]{1,0:T(8,128)(2,1)S(1)}, bf16[32,512]{1,0:T(8,128)(2,1)S(1)}, u32[]{:S(2)}, u32[]{:S(2)}) %collective-permute-start.3) | collective-permute-done | bytes 32800 | tf_op jit(solution)/shard_map/ppermute | solution.py:367
  11.6 0.0 copy-start.4
  11.6 0.0 copy-start.2
  11.7 1.6 %collective-permute-start.6 = (bf16[40,512]{1,0:T(8,128)(2,1)S(1)}, bf16[40,512]{1,0:T(8,128)(2,1)S(1)}, u32[]{:S(2)}, u32[]{:S(2)}) collective-permute-start(bf16[40,512]{1,0:T(8,128)(2,1)S(1)} %get-tuple-element.30), channel_id=1, source_target_pairs={{0,4},{4,0},{1,5},{5,1},{2,6},{6,2},{3,7},{7,3},{8,12},{12,8},{9,1... | collective-permute-start | bytes 122888 | tf_op jit(solution)/shard_map/ppermute | solution.py:376
  13.2 0.0 copy-done.4
  13.2 0.0 copy-done.3
  13.2 0.0 copy-done.2
  13.3 0.0 copy-start
  13.3 0.0 copy-start.1
  13.3 0.4 %gate.1.gate_ref = f32[256,512]{1,0:T(8,128)S(1)} custom-call(bf16[256,512]{1,0:T(8,128)(2,1)S(1)} %bitcast.5, bf16[512,512]{1,0:T(8,128)(2,1)S(1)} %copy-done.3), custom_call_target="tpu_custom_call" | custom-call | flops 134217728 | bytes 1310720 | tf_op jit(solution)/shard_map/gate/pallas_call | solution.py:20
  13.7 1.5 %collective-permute-done.5.refs_1_ = bf16[224,512]{1,0:T(8,128)(2,1)S(1)} collective-permute-done((bf16[224,512]{1,0:T(8,128)(2,1)S(1)}, bf16[224,512]{1,0:T(8,128)(2,1)S(1)}, u32[]{:S(2)}, u32[]{:S(2)}) %collective-permute-start.5) | collective-permute-done | bytes 229408 | tf_op jit(solution)/shard_map/ppermute | solution.py:357
  15.2 0.0 copy-done
  15.2 0.0 copy-done.1
  15.2 0.8 %inner.1 = (bf16[256,512]{1,0:T(8,128)(2,1)S(1)}, f32[64,512]{1,0:T(8,128)S(1)}) custom-call(f32[256,512]{1,0:T(8,128)S(1)} %own.1.mine_ref, f32[32,512]{1,0:T(8,128)S(1)} %get-tuple-element.25.low_ref, f32[32,512]{1,0:T(8,128)S(1)} %get-tuple-element.26.high_ref, f32[9,512]{1,0:T(8,128)S(1)} %reshape.14.taps_ref, f32[256,512]{1,0:T(8,128)S(1)} %gate.1.gate_ref, ...), custom_call_target="tpu_custom_call" | custom-call | flops 268435456 | bytes 2902016 | tf_op jit(solution)/shard_map/inner/pallas_call | solution.py:20
  16.0 0.0 collective-permute-done.6.refs_0_
  16.0 1.1 %edge.1 = bf16[256,512]{1,0:T(8,128)(2,1)} custom-call(f32[64,512]{1,0:T(8,128)S(1)} %get-tuple-element.28.edges_ref, f32[9,512]{1,0:T(8,128)S(1)} %reshape.14.taps_ref, f32[256,512]{1,0:T(8,128)S(1)} %gate.1.gate_ref, bf16[512,512]{1,0:T(8,128)(2,1)S(1)} %copy-done, bf16[512,512]{1,0:T(8,128)(2,1)S(1)} %copy-done.1, ...), custom_call_target="tpu_custom_call" | custom-call | flops 33554432 | bytes 2287616 | tf_op jit(solution)/shard_map/edge/pallas_call | solution.py:20
  (2 shorter events, 0.1 us)
Async XLA Ops:
  0.0 1.8 %collective-permute-start = (bf16[256,512]{1,0:T(8,128)(2,1)}, bf16[256,512]{1,0:T(8,128)(2,1)S(1)}, u32[]{:S(2)}, u32[]{:S(2)}) collective-permute-start(bf16[256,512]{1,0:T(8,128)(2,1)} %bitcast.3), channel_id=1, source_target_pairs={{0,8},{8,0},{16,24},{24,16},{1,9},{9,1},{17,25},{25,17},{2,10},{10... | collective-permute-start | bytes 786440 | tf_op jit(solution)/shard_map/ppermute | solution.py:300
  1.9 6.7 %collective-permute-start.1 = (bf16[64,512]{1,0:T(8,128)(2,1)S(1)}, bf16[64,512]{1,0:T(8,128)(2,1)S(1)}, u32[]{:S(2)}, u32[]{:S(2)}) collective-permute-start(bf16[64,512]{1,0:T(8,128)(2,1)S(1)} %column.1), channel_id=1, source_target_pairs={{0,1},{1,0},{2,3},{3,2},{4,5},{5,4},{6,7},{7,6},{8,12},{9,10},{10,... | collective-permute-start | bytes 196616 | tf_op jit(solution)/shard_map/ppermute | solution.py:353
  4.9 5.3 %collective-permute-start.2 = (bf16[64,512]{1,0:T(8,128)(2,1)S(1)}, bf16[64,512]{1,0:T(8,128)(2,1)S(1)}, u32[]{:S(2)}, u32[]{:S(2)}) collective-permute-start(bf16[64,512]{1,0:T(8,128)(2,1)S(1)} %column.1), channel_id=1, source_target_pairs={{0,17},{1,16},{2,19},{3,18},{4,21},{5,20},{6,23},{7,22},{8,28},{9,... | collective-permute-start | bytes 196616 | tf_op jit(solution)/shard_map/ppermute | solution.py:353
  6.5 4.4 %collective-permute-start.4 = (bf16[32,512]{1,0:T(8,128)(2,1)S(1)}, bf16[32,512]{1,0:T(8,128)(2,1)S(1)}, u32[]{:S(2)}, u32[]{:S(2)}) collective-permute-start(bf16[32,512]{1,0:T(8,128)(2,1)S(1)} %get-tuple-element.24), channel_id=1, source_target_pairs={{0,16},{8,24},{16,0},{24,8},{1,17},{9,25},{17,1},{25,9},{2,18},{10... | collective-permute-start | bytes 98312 | tf_op jit(solution)/shard_map/ppermute | solution.py:356
  6.7 8.5 %collective-permute-start.5 = (bf16[224,512]{1,0:T(8,128)(2,1)S(1)}, bf16[224,512]{1,0:T(8,128)(2,1)S(1)}, u32[]{:S(2)}, u32[]{:S(2)}) collective-permute-start(bf16[224,512]{1,0:T(8,128)(2,1)S(1)} %get-tuple-element.27), channel_id=1, source_target_pairs={{0,16},{8,24},{16,0},{24,8},{1,17},{9,25},{17,1},{25,9},{2,18},{10... | collective-permute-start | bytes 688136 | tf_op jit(solution)/shard_map/ppermute | solution.py:357
  10.3 1.3 %collective-permute-start.3 = (bf16[32,512]{1,0:T(8,128)(2,1)S(1)}, bf16[32,512]{1,0:T(8,128)(2,1)S(1)}, u32[]{:S(2)}, u32[]{:S(2)}) collective-permute-start(bf16[32,512]{1,0:T(8,128)(2,1)S(1)} %get-tuple-element.22), channel_id=1, source_target_pairs={{0,8},{8,0},{16,24},{24,16},{1,9},{9,1},{17,25},{25,17},{2,10},{10... | collective-permute-start | bytes 98312 | tf_op jit(solution)/shard_map/ppermute | solution.py:367
  10.4 2.8 %copy-start.3 = (bf16[512,512]{1,0:T(8,128)(2,1)S(1)}, bf16[512,512]{1,0:T(8,128)(2,1)}, u32[]{:S(2)}) copy-start(bf16[512,512]{1,0:T(8,128)(2,1)} %w_ref.1) | copy-start | bytes 1572868
  11.6 1.6 %copy-start.4 = (f32[3,3,512]{2,1,0:T(4,128)S(1)}, f32[3,3,512]{2,1,0:T(4,128)}, u32[]{:S(2)}) copy-start(f32[3,3,512]{2,1,0:T(4,128)} %param.8) | copy-start | bytes 55300
  11.6 1.6 %copy-start.2 = (bf16[4,8,8,512]{3,2,1,0:T(8,128)(2,1)S(1)}, bf16[4,8,8,512]{3,2,1,0:T(8,128)(2,1)}, u32[]{:S(2)}) copy-start(bf16[4,8,8,512]{3,2,1,0:T(8,128)(2,1)} %param.7) | copy-start | bytes 786436
  11.7 4.4 %collective-permute-start.6 = (bf16[40,512]{1,0:T(8,128)(2,1)S(1)}, bf16[40,512]{1,0:T(8,128)(2,1)S(1)}, u32[]{:S(2)}, u32[]{:S(2)}) collective-permute-start(bf16[40,512]{1,0:T(8,128)(2,1)S(1)} %get-tuple-element.30), channel_id=1, source_target_pairs={{0,4},{4,0},{1,5},{5,1},{2,6},{6,2},{3,7},{7,3},{8,12},{12,8},{9,1... | collective-permute-start | bytes 122888 | tf_op jit(solution)/shard_map/ppermute | solution.py:376
  13.3 1.9 %copy-start = (bf16[512,512]{1,0:T(8,128)(2,1)S(1)}, bf16[512,512]{1,0:T(8,128)(2,1)}, u32[]{:S(2)}) copy-start(bf16[512,512]{1,0:T(8,128)(2,1)} %wv_ref.3) | copy-start | bytes 1572868
  13.3 1.9 %copy-start.1 = (bf16[512,512]{1,0:T(8,128)(2,1)S(1)}, bf16[512,512]{1,0:T(8,128)(2,1)}, u32[]{:S(2)}) copy-start(bf16[512,512]{1,0:T(8,128)(2,1)} %wo_ref.3) | copy-start | bytes 1572868

commit v13 on v11

--- a/solution.py
+++ b/solution.py
@@ -215,72 +215,112 @@
     return jnp.dot(hidden, wo_ref[...], preferred_element_type=F32).astype(BF16)
 
 
+def filtered(lines, lefts, rights, taps):
+    totals = [None] * len(lines)
+    for r, line in enumerate(lines):
+        near = shifted(line, lefts[r], rights[r])
+        for a in range(3):
+            to = r + 1 - a
+            if 0 <= to < len(lines):
+                term = near[0] * taps[a][0] + near[1] * taps[a][1] + near[2] * taps[a][2]
+                totals[to] = term if totals[to] is None else totals[to] + term
+    return totals
+
+
+def taps_of(taps_ref, span):
+    return [[taps_ref[3 * a + b : 3 * a + b + 1, span] for b in range(3)] for a in range(3)]
+
+
 def inner_kernel(
-    frames, rows, cols, rounds_h, mine_ref, low_ref, high_ref, taps_ref, gate_ref, wv_ref, wo_ref, *refs
+    frames, rows, cols, mine_ref, low_ref, high_ref, taps_ref, gate_ref, wv_ref, wo_ref, out_ref, totals_ref, mixed
 ):
-    *parts, out_ref, edges_ref, mixed = refs
-    firsts, rests = parts[: len(parts) // 2], parts[len(parts) // 2 :]
-    chans = mine_ref.shape[1]
+    sites = rows * cols
+    for lane in range(0, mine_ref.shape[1], LANES):
+        span = slice(lane, lane + LANES)
+        taps = taps_of(taps_ref, span)
+        low, high = low_ref[:, span], high_ref[:, span]
+        for t in range(frames):
+            at = t * sites
+            lines = [mine_ref[at + r * cols : at + (r + 1) * cols, span] for r in range(rows)]
+            lefts = [low[t * rows + r : t * rows + r + 1] for r in range(rows)]
+            rights = [high[t * rows + r : t * rows + r + 1] for r in range(rows)]
+            total = jnp.concatenate(filtered(lines, lefts, rights, taps))
+            totals_ref[at : at + sites, span] = total
+            mixed[at : at + sites, span] = total.astype(BF16)
+    out_ref[...] = projected(mixed[...], gate_ref[...], wv_ref, wo_ref)
+
+
+def last_kernel(frames, rows, cols, chips, inner_ref, totals_ref, taps_ref, gate_ref, wv_ref, wo_ref, *refs):
+    *parts, out_ref, mixed = refs
+    firsts, rests, ends = parts[: chips - 1], parts[chips - 1 : 2 * chips - 2], parts[2 * chips - 2 :]
+    rounds_h = len(ends)
+    chans = out_ref.shape[1]
     sites = rows * cols
     size = frames * cols
-    for lane in range(0, chans, LANES):
-        span = slice(lane, lane + LANES)
-        taps = [[taps_ref[3 * a + b : 3 * a + b + 1, span] for b in range(3)] for a in range(3)]
-        low, high = low_ref[:, span], high_ref[:, span]
-        lines = [
-            jnp.concatenate([mine_ref[t * sites + r * cols : t * sites + (r + 1) * cols, span] for t in range(frames)])
-            for r in range(rows)
-        ]
-        for d, (first, rest) in enumerate(zip(firsts, rests), 1):
-            more = [first[i * size : (i + 1) * size, span].astype(F32) for i in range(rounds_h)]
-            more += [rest[i * size : (i + 1) * size, span].astype(F32) for i in range(rows - rounds_h)]
-            more = reordered(more, rounds_h, back=True)
-            lines = [line + later(d, other) for line, other in zip(lines, more)]
-        for t in range(frames):
-            at = t * sites
-            totals = [None] * rows
-            for r in range(rows):
-                row = t * rows + r
-                near = shifted(lines[r][t * cols : (t + 1) * cols], low[row : row + 1], high[row : row + 1])
-                for a in range(3):
-                    to = r + 1 - a
-                    if 0 <= to < rows:
-                        term = near[0] * taps[a][0] + near[1] * taps[a][1] + near[2] * taps[a][2]
-                        totals[to] = term if totals[to] is None else totals[to] + term
-            mixed[at : at + sites, span] = jnp.concatenate(totals, axis=0).astype(BF16)
-            edges_ref[t * cols : (t + 1) * cols, span] = totals[0]
-            edges_ref[size + t * cols : size + (t + 1) * cols, span] = totals[rows - 1]
-    out_ref[...] = projected(mixed[...], gate_ref[...], wv_ref, wo_ref)
-
-
-def edge_kernel(frames, rows, cols, rounds_h, edges_ref, taps_ref, gate_ref, wv_ref, wo_ref, inner_ref, *refs):
-    ends, out_ref = refs[:rounds_h], refs[rounds_h]
-    sites = rows * cols
-    size = frames * cols
-    odd, _, _ = position("height")
-    out_ref[...] = inner_ref[...]
-    taps = taps_ref[...]
-    mixed, gate = [], []
+    odd, lower, upper = position("height")
+    earlier = lax.div(lax.axis_index("tm"), 2) > 0
+    none = jnp.zeros((cols, chans), F32)
+    above, below = [none] * frames, [none] * frames
     for k, end in enumerate(ends):
         end = end[...].astype(F32)
         first = jnp.logical_not(odd) if k else odd
         lefts, rights = end[size : size + frames], end[size + frames : size + 2 * frames]
-        lower, upper = position("height")[1:]
         exists = jnp.where(first, lower, upper)
-        tap = jnp.where(first, taps[0:3], taps[6:9])
-        total = jnp.where(first, edges_ref[0:size], edges_ref[size : 2 * size])
+        tap = jnp.where(first, taps_ref[0:3], taps_ref[6:9])
         for t in range(frames):
             near = shifted(end[t * cols : (t + 1) * cols], lefts[t : t + 1], rights[t : t + 1])
             more = near[0] * tap[0:1] + near[1] * tap[1:2] + near[2] * tap[2:3]
-            mixed.append(total[t * cols : (t + 1) * cols] + jnp.where(exists, more, jnp.zeros_like(more)))
-            at = t * sites
-            gate.append(jnp.where(first, gate_ref[at : at + cols], gate_ref[at + sites - cols : at + sites]))
-    out = projected(jnp.concatenate(mixed, axis=0).astype(BF16), jnp.concatenate(gate, axis=0), wv_ref, wo_ref)
-    for t in range(frames):
-        new = [out[k * size + t * cols : k * size + (t + 1) * cols] for k in range(rounds_h)]
-        for at, other in ((t * sites, False), (t * sites + sites - cols, True)):
-            kept = new[1] if rounds_h > 1 else inner_ref[at : at + cols]
-            out_ref[at : at + cols] = jnp.where(odd, kept, new[0]) if other else jnp.where(odd, new[0], kept)
+            more = jnp.where(exists, more, none)
+            above[t] = above[t] + jnp.where(first, more, none)
+            below[t] = below[t] + jnp.where(first, none, more)
+
+    @pl.when(jnp.logical_not(earlier))
+    def _():
+        out_ref[...] = inner_ref[...]
+        rows_at = [t * sites for t in range(frames)], [(t + 1) * sites - cols for t in range(frames)]
+        added = above, below
+        if rounds_h > 1:
+            change, gate = [], []
+            for at, more in zip(rows_at, added):
+                change += [totals_ref[i : i + cols] + m for i, m in zip(at, more)]
+                gate += [gate_ref[i : i + cols] for i in at]
+        else:
+            change = [
+                jnp.where(odd, totals_ref[i : i + cols] + m, totals_ref[j : j + cols] + n)
+                for i, j, m, n in zip(*rows_at, *added)
+            ]
+            gate = [jnp.where(odd, gate_ref[i : i + cols], gate_ref[j : j + cols]) for i, j in zip(*rows_at)]
+        new = projected(jnp.concatenate(change).astype(BF16), jnp.concatenate(gate), wv_ref, wo_ref)
+        for t in range(frames):
+            i, j = rows_at[0][t], rows_at[1][t]
+            line = new[t * cols : (t + 1) * cols]
+            if rounds_h > 1:
+                out_ref[i : i + cols] = line
+                out_ref[j : j + cols] = new[size + t * cols : size + (t + 1) * cols]
+            else:
+                out_ref[i : i + cols] = jnp.where(odd, line, inner_ref[i : i + cols])
+                out_ref[j : j + cols] = jnp.where(odd, inner_ref[j : j + cols], line)
+
+    @pl.when(earlier)
+    def _():
+        for lane in range(0, chans, LANES):
+            span = slice(lane, lane + LANES)
+            taps = taps_of(taps_ref, span)
+            lines = [jnp.zeros((size, LANES), F32)] * rows
+            for d, (first, rest) in enumerate(zip(firsts, rests), 1):
+                more = [first[i * size : (i + 1) * size, span].astype(F32) for i in range(rounds_h)]
+                more += [rest[i * size : (i + 1) * size, span].astype(F32) for i in range(rows - rounds_h)]
+                more = reordered(more, rounds_h, back=True)
+                lines = [line + later(d, other) for line, other in zip(lines, more)]
+            zero = [jnp.zeros((1, LANES), F32)] * rows
+            for t in range(frames):
+                at = t * sites
+                total = filtered([line[t * cols : (t + 1) * cols] for line in lines], zero, zero, taps)
+                total[0] = total[0] + above[t][:, span]
+                total[rows - 1] = total[rows - 1] + below[t][:, span]
+                total = jnp.concatenate(total) + totals_ref[at : at + sites, span]
+                mixed[at : at + sites, span] = total.astype(BF16)
+        out_ref[...] = projected(mixed[...], gate_ref[...], wv_ref, wo_ref)
 
 
 def body(latents, spatial_taps, kernel_taps, skip_gain, gate_weight, value_weight, out_weight):
@@ -341,8 +381,11 @@
         for i in range(n_t):
             for h in range(n_h):
                 for j in range(n_w):
-                    to = facing(i % 2, j, n_w)
-                    beside = h ^ 1 if to == j and n_h % 2 == 0 else h
+                    to, beside = facing(i % 2, j, n_w), h
+                    if i // 2 + d >= chips:
+                        to = j
+                    elif to == j and n_h % 2 == 0:
+                        beside = h ^ 1
                     source = (i * n_h + h) * n_w + j
                     route.append((source, ((i + 2 * d) % n_t * n_h + beside) * n_w + to))
         columns.append(lax.ppermute(column, ("tm", "height", "width"), route))
@@ -371,21 +414,21 @@
     ends = [lax.ppermute(e, "height", pairs) for e, pairs in zip(ends, h_rounds)]
 
     taps = spatial_taps.reshape(9, chans)
-    inner, edges = call(
-        functools.partial(inner_kernel, frames, rows, cols, len(h_rounds)),
+    inner, totals = call(
+        functools.partial(inner_kernel, frames, rows, cols),
         "inner",
-        [shape((block, chans), BF16), shape((2 * frames * cols, chans), F32)],
+        [shape((block, chans), BF16), field],
         [pltpu.VMEM((block, chans), BF16)],
-        [mine, low, high, taps, gate, value_weight, out_weight] + firsts + rests,
+        [mine, low, high, taps, gate, value_weight, out_weight],
         4 * block * chans * chans,
     )
     (out,) = call(
-        functools.partial(edge_kernel, frames, rows, cols, len(h_rounds)),
-        "edge",
+        functools.partial(last_kernel, frames, rows, cols, chips),
+        "last",
         [shape((block, chans), BF16)],
-        [],
-        [edges, taps, gate, value_weight, out_weight, inner] + ends,
-        4 * frames * cols * chans * chans,
+        [pltpu.VMEM((block, chans), BF16)],
+        [inner, totals, taps, gate, value_weight, out_weight] + firsts + rests + ends,
+        4 * block * chans * chans,
     )
     return out.reshape(latents.shape)
 

time: 17 us -> 17 us (level)
  local copies, waits for them, and re-layouts: 0.09 us -> 0.83 us
  waiting for transfers between devices: 3.76 us -> 3.1 us
    unnamed x10, local copies, waits for them, and re-layouts: 0.07 us -> 0.81 us
    ppermute x1, waiting for transfers between devices: 0.74 us -> 0.01 us  [body(): rests.append(lax.ppermute(sent[2 * d - 1], 'tm', route))]
    ppermute x1, starting transfers between devices: 1.83 us -> 1.41 us  [body(): rests.append(lax.ppermute(sent[2 * d - 1], 'tm', route))]
    ppermute x1, starting transfers between devices: 0.26 us -> 0.69 us  [body(): firsts.append(lax.ppermute(sent[2 * d - 2], 'tm', route))]
  transfers between devices with their start and end apart: 7 -> 7, of which waited for: 5 -> 4; matrix products, arithmetic and copies ran while one was open for 0% -> 0% of each run, Pallas kernels for 18% -> 18%
where the time goes in v13:
time: 17 us; the launch traced here: 16.8 us
  starting transfers between devices  8.57 us (50%)
  Pallas kernels  4.17 us (25%)
  waiting for transfers between devices  3.1 us (18%)
  local copies, waits for them, and re-layouts  0.83 us (5%)
    ppermute x2, starting transfers between devices, body(): columns.append(lax.ppermute(column, ('tm', 'height', 'width'), route))  4.4 us
    pallas_call x9, Pallas kernels, call(): pl.pallas_call(kernel, out_shape=tuple(outs), in_specs=[HBM] * far + [VME...  4.17 us
    ppermute x1, starting transfers between devices, body(): lax.ppermute(e, 'height', pairs)  1.56 us
    ppermute x2, waiting for transfers between devices, body(): columns.append(lax.ppermute(column, ('tm', 'height', 'width'), route))  1.52 us
    ppermute x1, starting transfers between devices, body(): rests.append(lax.ppermute(sent[2 * d - 1], 'tm', route))  1.41 us
    unnamed x10, local copies, waits for them, and re-layouts  0.81 us
    ppermute x1, starting transfers between devices, body(): firsts.append(lax.ppermute(sent[2 * d - 2], 'tm', route))  0.69 us
    ppermute x1, waiting for transfers between devices, body(): other = lax.ppermute(other, 'tm', [(i, i ^ 1) for i in range(n_t)])  0.67 us
  transfers between devices with their start and end apart: 7, of which 4 were waited for; matrix products, arithmetic and copies ran while one was open for 0% of the time, Pallas kernels for 18%

profile of v13, /device:TPU:0, one launch (start us, length us, event | category | flops | bytes accessed | tf_op | source)
XLA Modules:
  0.0 16.8 jit_solution(2610339689705568709)
XLA Ops:
  0.0 0.5 %collective-permute-start = (bf16[256,512]{1,0:T(8,128)(2,1)}, bf16[256,512]{1,0:T(8,128)(2,1)S(1)}, u32[]{:S(2)}, u32[]{:S(2)}) collective-permute-start(bf16[256,512]{1,0:T(8,128)(2,1)} %bitcast.3), channel_id=1, source_target_pairs={{0,8},{8,0},{16,24},{24,16},{1,9},{9,1},{17,25},{25,17},{2,10},{10... | collective-permute-start | bytes 786440 | tf_op jit(solution)/shard_map/ppermute | solution.py:335
  0.5 1.3 %early.1 = (f32[24,8,512]{2,1,0:T(8,128)S(1)}, f32[32,512]{1,0:T(8,128)S(1)}, f32[256,512]{1,0:T(8,128)S(1)}, f32[256,512]{1,0:T(8,128)S(1)}) custom-call(bf16[16,512]{1,0:T(8,128)(2,1)} %refs_0_.1, f32[1,512]{1,0:T(1,128)} %bitcast.6, bf16[256,512]{1,0:T(8,128)(2,1)} %bitcast.4), custom_call_target="tpu_custom_call" | custom-call | flops 2097152 | bytes 1787904 | tf_op jit(solution)/shard_map/early/pallas_call | solution.py:20
  1.8 0.0 collective-permute-done.partner_ref
  1.8 0.1 column.1
  1.9 4.0 %collective-permute-start.1 = (bf16[64,512]{1,0:T(8,128)(2,1)S(1)}, bf16[64,512]{1,0:T(8,128)(2,1)S(1)}, u32[]{:S(2)}, u32[]{:S(2)}) collective-permute-start(bf16[64,512]{1,0:T(8,128)(2,1)S(1)} %column.1), channel_id=1, source_target_pairs={{0,17},{1,16},{2,19},{3,18},{4,21},{5,20},{6,23},{7,22},{8,28},{9,... | collective-permute-start | bytes 196616 | tf_op jit(solution)/shard_map/ppermute | solution.py:391
  5.8 0.4 %collective-permute-start.2 = (bf16[64,512]{1,0:T(8,128)(2,1)S(1)}, bf16[64,512]{1,0:T(8,128)(2,1)S(1)}, u32[]{:S(2)}, u32[]{:S(2)}) collective-permute-start(bf16[64,512]{1,0:T(8,128)(2,1)S(1)} %column.1), channel_id=1, source_target_pairs={{0,1},{1,0},{2,3},{3,2},{4,5},{5,4},{6,7},{7,6},{8,12},{9,10},{10,... | collective-permute-start | bytes 196616 | tf_op jit(solution)/shard_map/ppermute | solution.py:391
  6.3 0.2 %later.1 = (bf16[32,512]{1,0:T(8,128)(2,1)S(1)}, bf16[224,512]{1,0:T(8,128)(2,1)S(1)}) custom-call(bf16[256,512]{1,0:T(8,128)(2,1)S(1)} %collective-permute-done.partner_ref, f32[24,8,512]{2,1,0:T(8,128)S(1)} %get-tuple-element.18.table_ref, f32[256,512]{1,0:T(8,128)S(1)} %get-tuple-element.23.refs_0_), custom_call_target="tpu_custom_call" | custom-call | flops 1048576 | bytes 1441792 | tf_op jit(solution)/shard_map/later/pallas_call | solution.py:20
  6.5 0.7 %collective-permute-start.4 = (bf16[32,512]{1,0:T(8,128)(2,1)S(1)}, bf16[32,512]{1,0:T(8,128)(2,1)S(1)}, u32[]{:S(2)}, u32[]{:S(2)}) collective-permute-start(bf16[32,512]{1,0:T(8,128)(2,1)S(1)} %get-tuple-element.24), channel_id=1, source_target_pairs={{0,16},{8,24},{16,0},{24,8},{1,17},{9,25},{17,1},{25,9},{2,18},{10... | collective-permute-start | bytes 98312 | tf_op jit(solution)/shard_map/ppermute | solution.py:394
  7.2 1.4 %collective-permute-start.5 = (bf16[224,512]{1,0:T(8,128)(2,1)S(1)}, bf16[224,512]{1,0:T(8,128)(2,1)S(1)}, u32[]{:S(2)}, u32[]{:S(2)}) collective-permute-start(bf16[224,512]{1,0:T(8,128)(2,1)S(1)} %get-tuple-element.29), channel_id=1, source_target_pairs={{0,16},{8,24},{16,0},{24,8},{1,17},{9,25},{17,1},{25,9},{2,18},{10... | collective-permute-start | bytes 688136 | tf_op jit(solution)/shard_map/ppermute | solution.py:395
  8.6 0.0 collective-permute-done.1.refs_0_
  8.6 1.5 %collective-permute-done.2.refs_1_ = bf16[64,512]{1,0:T(8,128)(2,1)S(1)} collective-permute-done((bf16[64,512]{1,0:T(8,128)(2,1)S(1)}, bf16[64,512]{1,0:T(8,128)(2,1)S(1)}, u32[]{:S(2)}, u32[]{:S(2)}) %collective-permute-start.2) | collective-permute-done | bytes 65568 | tf_op jit(solution)/shard_map/ppermute | solution.py:391
  10.1 0.2 side.1
  10.3 0.1 collective-permute-start.3
  10.3 0.0 copy-start.3
  10.4 0.2 own.1.mine_ref
  10.5 0.3 %collective-permute-done.4.refs_0_ = bf16[32,512]{1,0:T(8,128)(2,1)S(1)} collective-permute-done((bf16[32,512]{1,0:T(8,128)(2,1)S(1)}, bf16[32,512]{1,0:T(8,128)(2,1)S(1)}, u32[]{:S(2)}, u32[]{:S(2)}) %collective-permute-start.4) | collective-permute-done | bytes 32800 | tf_op jit(solution)/shard_map/ppermute | solution.py:394
  10.9 0.7 %collective-permute-done.3.other_ref = bf16[32,512]{1,0:T(8,128)(2,1)S(1)} collective-permute-done((bf16[32,512]{1,0:T(8,128)(2,1)S(1)}, bf16[32,512]{1,0:T(8,128)(2,1)S(1)}, u32[]{:S(2)}, u32[]{:S(2)}) %collective-permute-start.3) | collective-permute-done | bytes 32800 | tf_op jit(solution)/shard_map/ppermute | solution.py:405
  11.5 0.0 copy-start.4
  11.5 0.0 copy-start.2
  11.6 1.6 %collective-permute-start.6 = (bf16[40,512]{1,0:T(8,128)(2,1)S(1)}, bf16[40,512]{1,0:T(8,128)(2,1)S(1)}, u32[]{:S(2)}, u32[]{:S(2)}) collective-permute-start(bf16[40,512]{1,0:T(8,128)(2,1)S(1)} %get-tuple-element.30), channel_id=1, source_target_pairs={{0,4},{4,0},{1,5},{5,1},{2,6},{6,2},{3,7},{7,3},{8,12},{12,8},{9,1... | collective-permute-start | bytes 122888 | tf_op jit(solution)/shard_map/ppermute | solution.py:414
  13.2 0.0 copy-done.4
  13.2 0.0 copy-done.3
  13.2 0.0 copy-done.2
  13.2 0.0 copy-start
  13.2 0.0 copy-start.1
  13.2 0.4 %gate.1.gate_ref = f32[256,512]{1,0:T(8,128)S(1)} custom-call(bf16[256,512]{1,0:T(8,128)(2,1)S(1)} %bitcast.5, bf16[512,512]{1,0:T(8,128)(2,1)S(1)} %copy-done.3), custom_call_target="tpu_custom_call" | custom-call | flops 134217728 | bytes 1310720 | tf_op jit(solution)/shard_map/gate/pallas_call | solution.py:20
  13.6 0.6 %copy-done = bf16[512,512]{1,0:T(8,128)(2,1)S(1)} copy-done((bf16[512,512]{1,0:T(8,128)(2,1)S(1)}, bf16[512,512]{1,0:T(8,128)(2,1)}, u32[]{:S(2)}) %copy-start) | copy-done | bytes 524312
  14.2 0.2 copy-done.1
  14.4 0.7 %inner.1 = (bf16[256,512]{1,0:T(8,128)(2,1)S(1)}, f32[256,512]{1,0:T(8,128)S(1)}) custom-call(f32[256,512]{1,0:T(8,128)S(1)} %own.1.mine_ref, f32[32,512]{1,0:T(8,128)S(1)} %get-tuple-element.25.low_ref, f32[32,512]{1,0:T(8,128)S(1)} %get-tuple-element.26.high_ref, f32[9,512]{1,0:T(8,128)S(1)} %reshape.14.taps_ref, f32[256,512]{1,0:T(8,128)S(1)} %gate.1.gate_ref, ...), custom_call_target="tpu_custom_call" | custom-call | flops 268435456 | bytes 3033088 | tf_op jit(solution)/shard_map/inner/pallas_call | solution.py:20
  15.1 0.5 %collective-permute-done.6.refs_2_ = bf16[40,512]{1,0:T(8,128)(2,1)S(1)} collective-permute-done((bf16[40,512]{1,0:T(8,128)(2,1)S(1)}, bf16[40,512]{1,0:T(8,128)(2,1)S(1)}, u32[]{:S(2)}, u32[]{:S(2)}) %collective-permute-start.6) | collective-permute-done | bytes 40992 | tf_op jit(solution)/shard_map/ppermute | solution.py:414
  15.7 0.0 collective-permute-done.5.refs_1_
  15.7 1.1 %last.1 = bf16[256,512]{1,0:T(8,128)(2,1)} custom-call(bf16[256,512]{1,0:T(8,128)(2,1)S(1)} %get-tuple-element.27.inner_ref, f32[256,512]{1,0:T(8,128)S(1)} %get-tuple-element.28.totals_ref, f32[9,512]{1,0:T(8,128)S(1)} %reshape.14.taps_ref, f32[256,512]{1,0:T(8,128)S(1)} %gate.1.gate_ref, bf16[512,512]{1,0:T(8,128)(2,1)S(1)} %copy-done, ...), custom_call_target="tpu_custom_call" | custom-call | flops 268435456 | bytes 2942976 | tf_op jit(solution)/shard_map/last/pallas_call | solution.py:20
  (2 shorter events, 0.1 us)
Async XLA Ops:
  0.0 1.8 %collective-permute-start = (bf16[256,512]{1,0:T(8,128)(2,1)}, bf16[256,512]{1,0:T(8,128)(2,1)S(1)}, u32[]{:S(2)}, u32[]{:S(2)}) collective-permute-start(bf16[256,512]{1,0:T(8,128)(2,1)} %bitcast.3), channel_id=1, source_target_pairs={{0,8},{8,0},{16,24},{24,16},{1,9},{9,1},{17,25},{25,17},{2,10},{10... | collective-permute-start | bytes 786440 | tf_op jit(solution)/shard_map/ppermute | solution.py:335
  1.9 6.7 %collective-permute-start.1 = (bf16[64,512]{1,0:T(8,128)(2,1)S(1)}, bf16[64,512]{1,0:T(8,128)(2,1)S(1)}, u32[]{:S(2)}, u32[]{:S(2)}) collective-permute-start(bf16[64,512]{1,0:T(8,128)(2,1)S(1)} %column.1), channel_id=1, source_target_pairs={{0,17},{1,16},{2,19},{3,18},{4,21},{5,20},{6,23},{7,22},{8,28},{9,... | collective-permute-start | bytes 196616 | tf_op jit(solution)/shard_map/ppermute | solution.py:391
  5.8 4.3 %collective-permute-start.2 = (bf16[64,512]{1,0:T(8,128)(2,1)S(1)}, bf16[64,512]{1,0:T(8,128)(2,1)S(1)}, u32[]{:S(2)}, u32[]{:S(2)}) collective-permute-start(bf16[64,512]{1,0:T(8,128)(2,1)S(1)} %column.1), channel_id=1, source_target_pairs={{0,1},{1,0},{2,3},{3,2},{4,5},{5,4},{6,7},{7,6},{8,12},{9,10},{10,... | collective-permute-start | bytes 196616 | tf_op jit(solution)/shard_map/ppermute | solution.py:391
  6.5 4.4 %collective-permute-start.4 = (bf16[32,512]{1,0:T(8,128)(2,1)S(1)}, bf16[32,512]{1,0:T(8,128)(2,1)S(1)}, u32[]{:S(2)}, u32[]{:S(2)}) collective-permute-start(bf16[32,512]{1,0:T(8,128)(2,1)S(1)} %get-tuple-element.24), channel_id=1, source_target_pairs={{0,16},{8,24},{16,0},{24,8},{1,17},{9,25},{17,1},{25,9},{2,18},{10... | collective-permute-start | bytes 98312 | tf_op jit(solution)/shard_map/ppermute | solution.py:394
  7.2 8.5 %collective-permute-start.5 = (bf16[224,512]{1,0:T(8,128)(2,1)S(1)}, bf16[224,512]{1,0:T(8,128)(2,1)S(1)}, u32[]{:S(2)}, u32[]{:S(2)}) collective-permute-start(bf16[224,512]{1,0:T(8,128)(2,1)S(1)} %get-tuple-element.29), channel_id=1, source_target_pairs={{0,16},{8,24},{16,0},{24,8},{1,17},{9,25},{17,1},{25,9},{2,18},{10... | collective-permute-start | bytes 688136 | tf_op jit(solution)/shard_map/ppermute | solution.py:395
  10.3 1.3 %collective-permute-start.3 = (bf16[32,512]{1,0:T(8,128)(2,1)S(1)}, bf16[32,512]{1,0:T(8,128)(2,1)S(1)}, u32[]{:S(2)}, u32[]{:S(2)}) collective-permute-start(bf16[32,512]{1,0:T(8,128)(2,1)S(1)} %get-tuple-element.22), channel_id=1, source_target_pairs={{0,8},{8,0},{16,24},{24,16},{1,9},{9,1},{17,25},{25,17},{2,10},{10... | collective-permute-start | bytes 98312 | tf_op jit(solution)/shard_map/ppermute | solution.py:405
  10.3 2.8 %copy-start.3 = (bf16[512,512]{1,0:T(8,128)(2,1)S(1)}, bf16[512,512]{1,0:T(8,128)(2,1)}, u32[]{:S(2)}) copy-start(bf16[512,512]{1,0:T(8,128)(2,1)} %w_ref.1) | copy-start | bytes 1572868
  11.5 1.6 %copy-start.4 = (f32[3,3,512]{2,1,0:T(4,128)S(1)}, f32[3,3,512]{2,1,0:T(4,128)}, u32[]{:S(2)}) copy-start(f32[3,3,512]{2,1,0:T(4,128)} %param.8) | copy-start | bytes 55300
  11.5 1.6 %copy-start.2 = (bf16[4,8,8,512]{3,2,1,0:T(8,128)(2,1)S(1)}, bf16[4,8,8,512]{3,2,1,0:T(8,128)(2,1)}, u32[]{:S(2)}) copy-start(bf16[4,8,8,512]{3,2,1,0:T(8,128)(2,1)} %param.7) | copy-start | bytes 786436
  11.6 4.1 %collective-permute-start.6 = (bf16[40,512]{1,0:T(8,128)(2,1)S(1)}, bf16[40,512]{1,0:T(8,128)(2,1)S(1)}, u32[]{:S(2)}, u32[]{:S(2)}) collective-permute-start(bf16[40,512]{1,0:T(8,128)(2,1)S(1)} %get-tuple-element.30), channel_id=1, source_target_pairs={{0,4},{4,0},{1,5},{5,1},{2,6},{6,2},{3,7},{7,3},{8,12},{12,8},{9,1... | collective-permute-start | bytes 122888 | tf_op jit(solution)/shard_map/ppermute | solution.py:414
  13.2 1.0 %copy-start = (bf16[512,512]{1,0:T(8,128)(2,1)S(1)}, bf16[512,512]{1,0:T(8,128)(2,1)}, u32[]{:S(2)}) copy-start(bf16[512,512]{1,0:T(8,128)(2,1)} %wv_ref.3) | copy-start | bytes 1572868
  13.2 1.2 %copy-start.1 = (bf16[512,512]{1,0:T(8,128)(2,1)S(1)}, bf16[512,512]{1,0:T(8,128)(2,1)}, u32[]{:S(2)}) copy-start(bf16[512,512]{1,0:T(8,128)(2,1)} %wo_ref.3) | copy-start | bytes 1572868

commit v14 on v13

--- a/solution.py
+++ b/solution.py
@@ -8,7 +8,6 @@
 from jax.sharding import PartitionSpec as P
 
 LANES = 128
-LATER = 8 * 10**9
 F32, BF16 = jnp.float32, jnp.bfloat16
 VMEM = pl.BlockSpec(memory_space=pltpu.VMEM)
 HBM = pl.BlockSpec(memory_space=pltpu.HBM)
@@ -99,19 +98,17 @@
                 field[t * sites : (t + 1) * sites, span] = totals[t].reshape(sites, LANES)
 
 
-def reordered(lines, rounds_h, back=False):
-    if rounds_h > 1:
-        return lines[:1] + lines[2:] + lines[1:2] if back else lines[:1] + lines[-1:] + lines[1:-1]
+def column_kernel(frames, rows, cols, partner_ref, side_ref, out_ref, *refs):
+    *corners, held = refs
     odd = position("height")[0]
-    return [jnp.where(odd, a, b) for a, b in zip(lines, lines[::-1])]
-
-
-def column_kernel(frames, rows, cols, partner_ref, side_ref, out_ref, held):
-    lines = frames * rows
     for lane in range(0, out_ref.shape[1], LANES):
         span = slice(lane, lane + LANES)
         held[...] = partner_ref[:, span].astype(F32)
-        out_ref[:, span] = jnp.concatenate([side_ref[:, span], outer_column(held, lines, cols)]).astype(BF16)
+        column = jnp.concatenate([side_ref[:, span], outer_column(held, frames * rows, cols)])
+        out_ref[:, span] = column.astype(BF16)
+        ends = [jnp.concatenate([column[s + r : s + r + 1] for s in range(0, column.shape[0], rows)]) for r in (0, rows - 1)]
+        for k, corner in enumerate(corners):
+            corner[:, span] = jnp.where(odd, *(ends[::-1] if k else ends)).astype(BF16)
 
 
 def shift(frames):
@@ -130,14 +127,18 @@
 
 
 def later_kernel(frames, rows, cols, rounds_h, partner_ref, table_ref, *refs):
-    fields, outs = refs[: len(refs) // 3], refs[len(refs) // 3 :]
+    n = len(refs) // (2 + rounds_h)
+    fields, outs = refs[:n], refs[n:]
+    odd = position("height")[0]
     for d, field in enumerate(fields, 1):
+        whole, *lines = outs[(d - 1) * (1 + rounds_h) : d * (1 + rounds_h)]
         for lane in range(0, field.shape[1], LANES):
             span = slice(lane, lane + LANES)
             totals = with_partner(frames, rows, cols, d, field, partner_ref, table_ref, span)
-            tiles = reordered([jnp.concatenate([t[r] for t in totals]) for r in range(rows)], rounds_h)
-            outs[2 * d - 2][:, span] = jnp.concatenate(tiles[:rounds_h]).astype(BF16)
-            outs[2 * d - 1][:, span] = jnp.concatenate(tiles[rounds_h:]).astype(BF16)
+            whole[:, span] = jnp.concatenate(totals).reshape(whole.shape[0], LANES).astype(BF16)
+            ends = [jnp.concatenate([t[r] for t in totals]) for r in (0, rows - 1)]
+            for k, line in enumerate(lines):
+                line[:, span] = jnp.where(odd, *(ends[::-1] if k else ends)).astype(BF16)
 
 
 def own_kernel(frames, rows, cols, partner_ref, table_ref, field_ref, mine_ref):
@@ -151,54 +152,71 @@
     return jnp.where(lax.div(lax.axis_index("tm"), 2) >= d, value, jnp.zeros_like(value))
 
 
-def side_kernel(frames, rows, table_ref, *refs):
-    *arrived, own_ref, other_ref = refs
+def mixed_columns(frames, rows, d, column, table_ref, span):
+    base = 2 * frames + 2 * d * frames
+    totals = [jnp.zeros((rows, column.shape[1]), F32)] * (2 * frames)
+    for t in range(2 * frames):
+        for s in range(2 * frames):
+            lag = t % frames - s % frames
+            if t // frames == s // frames:
+                if d == 0 and lag < 0:
+                    continue
+            else:
+                lag = lag + (shift(frames) if t < frames else -shift(frames))
+            tap = table_ref[base + lag, :, span][:rows]
+            totals[t] = totals[t] + tap * column[s * rows : (s + 1) * rows]
+    return totals
+
+
+def beside(totals):
     _, lower, upper = position("width")
     exists = jnp.where(on_right(), upper, lower)
+    return [jnp.where(exists, total, jnp.zeros_like(total)) for total in totals]
+
+
+def side_kernel(frames, rows, table_ref, arrived_ref, own_ref, other_ref):
     for lane in range(0, own_ref.shape[1], LANES):
         span = slice(lane, lane + LANES)
-        totals = [jnp.zeros((rows, LANES), F32)] * (2 * frames)
-        for d, ref in enumerate(arrived[::-1]):
-            column = later(d, ref[:, span].astype(F32))
-            base = 2 * frames + 2 * d * frames
-            for t in range(2 * frames):
-                for s in range(2 * frames):
-                    lag = t % frames - s % frames
-                    if t // frames == s // frames:
-                        if d == 0 and lag < 0:
-                            continue
-                    else:
-                        lag = lag + (shift(frames) if t < frames else -shift(frames))
-                    totals[t] = totals[t] + table_ref[base + lag, :, span] * column[s * rows : (s + 1) * rows]
-        totals = [jnp.where(exists, total, jnp.zeros_like(total)) for total in totals]
+        totals = beside(mixed_columns(frames, rows, 0, arrived_ref[:, span].astype(F32), table_ref, span))
         own_ref[:, span] = jnp.concatenate(totals[:frames])
         other_ref[:, span] = jnp.concatenate(totals[frames:]).astype(BF16)
 
 
-def border_kernel(frames, rows, cols, chips, mine_ref, own_ref, other_ref, *refs):
-    arrived, (low_ref, high_ref, *outs) = refs[: chips - 1], refs[chips - 1 :]
+def before_kernel(frames, rows, rounds_h, table_ref, *refs):
+    *arrived, own_ref, other_ref = refs
+    per = 1 + rounds_h
+    for lane in range(0, own_ref.shape[1], LANES):
+        span = slice(lane, lane + LANES)
+        parts = [0.0] * per
+        for d in range(1, len(arrived) // per + 1):
+            for i, ref in enumerate(arrived[(d - 1) * per : d * per]):
+                pixels = rows if i == 0 else 1
+                column = later(d, ref[:, span].astype(F32))
+                totals = beside(mixed_columns(frames, pixels, d, column, table_ref, span))
+                sums = jnp.concatenate(totals[:frames]), jnp.concatenate(totals[frames:])
+                parts[i] = sums if d == 1 else tuple(a + b for a, b in zip(parts[i], sums))
+        own_ref[:, span] = jnp.concatenate([a for a, _ in parts])
+        other_ref[:, span] = jnp.concatenate([b for _, b in parts]).astype(BF16)
+
+
+def both_sides(own, other):
+    right = on_right()
+    return jnp.where(right, other, own), jnp.where(right, own, other)
+
+
+def border_kernel(frames, rows, cols, mine_ref, own_ref, other_ref, low_ref, high_ref, *outs):
     sites = rows * cols
     odd, _, _ = position("height")
-    right, own, other = on_right(), own_ref[...], other_ref[...].astype(F32)
-    low, high = jnp.where(right, other, own), jnp.where(right, own, other)
+    low, high = both_sides(own_ref[...], other_ref[...].astype(F32))
     low_ref[...] = low
     high_ref[...] = high
-    size = frames * cols
-    lines, corners = [], []
+    ends = []
     for r in (0, rows - 1):
-        lines.append(jnp.concatenate([mine_ref[t * sites + r * cols : t * sites + (r + 1) * cols] for t in range(frames)]))
-        ends = [side[t * rows + r : t * rows + r + 1] for side in (low, high) for t in range(frames)]
-        corners.append(jnp.concatenate(ends))
+        line = [mine_ref[t * sites + r * cols : t * sites + (r + 1) * cols] for t in range(frames)]
+        corners = [side[t * rows + r : t * rows + r + 1] for side in (low, high) for t in range(frames)]
+        ends.append(jnp.concatenate(line + corners))
     for k, out in enumerate(outs):
-        line = jnp.where(odd, *(lines[::-1] if k else lines))
-        for d, ref in enumerate(arrived, 1):
-            if len(outs) > 1:
-                ends = [ref[i * size : (i + 1) * size].astype(F32) for i in range(2)]
-                more = jnp.where(odd, *(ends[::-1] if k else ends))
-            else:
-                more = ref[:size].astype(F32)
-            line = line + later(d, more)
-        out[...] = jnp.concatenate([line, jnp.where(odd, *(corners[::-1] if k else corners))]).astype(BF16)
+        out[...] = jnp.where(odd, *(ends[::-1] if k else ends)).astype(BF16)
 
 
 def shifted(line, left, right):
@@ -252,23 +270,33 @@
 
 def last_kernel(frames, rows, cols, chips, inner_ref, totals_ref, taps_ref, gate_ref, wv_ref, wo_ref, *refs):
     *parts, out_ref, mixed = refs
-    firsts, rests, ends = parts[: chips - 1], parts[chips - 1 : 2 * chips - 2], parts[2 * chips - 2 :]
-    rounds_h = len(ends)
     chans = out_ref.shape[1]
     sites = rows * cols
     size = frames * cols
     odd, lower, upper = position("height")
     earlier = lax.div(lax.axis_index("tm"), 2) > 0
+    rounds_h = (len(parts) - (chips + 1 if chips > 1 else 0)) // chips
+    ends, parts = parts[:rounds_h], parts[rounds_h:]
+    lines_before, parts = parts[: rounds_h * (chips - 1)], parts[rounds_h * (chips - 1) :]
+    wholes, sides = parts[: chips - 1], parts[chips - 1 :]
     none = jnp.zeros((cols, chans), F32)
     above, below = [none] * frames, [none] * frames
+    low = high = None
+    if sides:
+        low, high = both_sides(sides[0][...], sides[1][...].astype(F32))
     for k, end in enumerate(ends):
         end = end[...].astype(F32)
         first = jnp.logical_not(odd) if k else odd
-        lefts, rights = end[size : size + frames], end[size + frames : size + 2 * frames]
+        line, lefts, rights = end[:size], end[size : size + frames], end[size + frames : size + 2 * frames]
+        for d in range(1, chips):
+            line = line + later(d, lines_before[(d - 1) * rounds_h + k][...].astype(F32))
+        if sides:
+            at = frames * rows + k * frames
+            lefts, rights = lefts + low[at : at + frames], rights + high[at : at + frames]
         exists = jnp.where(first, lower, upper)
         tap = jnp.where(first, taps_ref[0:3], taps_ref[6:9])
         for t in range(frames):
-            near = shifted(end[t * cols : (t + 1) * cols], lefts[t : t + 1], rights[t : t + 1])
+            near = shifted(line[t * cols : (t + 1) * cols], lefts[t : t + 1], rights[t : t + 1])
             more = near[0] * tap[0:1] + near[1] * tap[1:2] + near[2] * tap[2:3]
             more = jnp.where(exists, more, none)
             above[t] = above[t] + jnp.where(first, more, none)
@@ -301,21 +329,23 @@
                 out_ref[i : i + cols] = jnp.where(odd, line, inner_ref[i : i + cols])
                 out_ref[j : j + cols] = jnp.where(odd, inner_ref[j : j + cols], line)
 
+    if chips == 1:
+        return
+
     @pl.when(earlier)
     def _():
         for lane in range(0, chans, LANES):
             span = slice(lane, lane + LANES)
             taps = taps_of(taps_ref, span)
-            lines = [jnp.zeros((size, LANES), F32)] * rows
-            for d, (first, rest) in enumerate(zip(firsts, rests), 1):
-                more = [first[i * size : (i + 1) * size, span].astype(F32) for i in range(rounds_h)]
-                more += [rest[i * size : (i + 1) * size, span].astype(F32) for i in range(rows - rounds_h)]
-                more = reordered(more, rounds_h, back=True)
-                lines = [line + later(d, other) for line, other in zip(lines, more)]
-            zero = [jnp.zeros((1, LANES), F32)] * rows
             for t in range(frames):
                 at = t * sites
-                total = filtered([line[t * cols : (t + 1) * cols] for line in lines], zero, zero, taps)
+                tile = 0.0
+                for d, ref in enumerate(wholes, 1):
+                    tile = tile + later(d, ref[at : at + sites, span].astype(F32))
+                lines = [tile[r * cols : (r + 1) * cols] for r in range(rows)]
+                lefts = [low[t * rows + r : t * rows + r + 1, span] for r in range(rows)]
+                rights = [high[t * rows + r : t * rows + r + 1, span] for r in range(rows)]
+                total = filtered(lines, lefts, rights, taps)
                 total[0] = total[0] + above[t][:, span]
                 total[rows - 1] = total[rows - 1] + below[t][:, span]
                 total = jnp.concatenate(total) + totals_ref[at : at + sites, span]
@@ -351,18 +381,18 @@
     )
 
     h_rounds = swaps("height")
-    (column,) = call(
+    rounds = len(h_rounds)
+    column, *corners = call(
         functools.partial(column_kernel, frames, rows, cols),
         "column",
-        [shape((2 * lines, chans), BF16)],
+        [shape((2 * lines, chans), BF16)] + [shape((2 * frames, chans), BF16)] * rounds,
         [pltpu.VMEM((block, LANES), F32)],
         [partner, side],
     )
-    parts = [shape((n * frames * cols, chans), BF16) for n in (len(h_rounds), rows - len(h_rounds))]
     sent = call(
-        functools.partial(later_kernel, frames, rows, cols, len(h_rounds)),
+        functools.partial(later_kernel, frames, rows, cols, rounds),
         "later",
-        parts * (chips - 1),
+        ([shape((block, chans), BF16)] + [shape((frames * cols, chans), BF16)] * rounds) * (chips - 1),
         [],
         [partner, table] + fields[1:],
         2 * (chips - 1) * frames * x.size,
@@ -375,41 +405,54 @@
         [partner, table, fields[0]],
         2 * frames * x.size,
     )
-    columns, firsts, rests = [], [], []
-    for d in reversed(range(chips)):
+
+    def move(data, d, across_w, pairs=None):
         route = []
         for i in range(n_t):
             for h in range(n_h):
                 for j in range(n_w):
-                    to, beside = facing(i % 2, j, n_w), h
-                    if i // 2 + d >= chips:
-                        to = j
-                    elif to == j and n_h % 2 == 0:
-                        beside = h ^ 1
-                    source = (i * n_h + h) * n_w + j
-                    route.append((source, ((i + 2 * d) % n_t * n_h + beside) * n_w + to))
-        columns.append(lax.ppermute(column, ("tm", "height", "width"), route))
+                    real = i // 2 + d < chips
+                    to = facing(i % 2, j, n_w) if across_w and real else j
+                    at = pairs[h][1] if pairs and real else h
+                    if d == 0 and to == j and n_h % 2 == 0:
+                        at = h ^ 1
+                    route.append(((i * n_h + h) * n_w + j, ((i + 2 * d) % n_t * n_h + at) * n_w + to))
+        return lax.ppermute(data, ("tm", "height", "width"), route)
+
+    wholes, before, rows_before = [], [], []
     for d in range(1, chips):
-        route = [(i, (i + 2 * d) % n_t) for i in range(n_t)]
-        firsts.append(lax.ppermute(sent[2 * d - 2], "tm", route))
-        rests.append(lax.ppermute(sent[2 * d - 1], "tm", route))
-
+        whole, *edges = sent[(d - 1) * (1 + rounds) : d * (1 + rounds)]
+        wholes.append(move(whole, d, False))
+        before.append(move(column, d, True))
+        rows_before += [move(edge, d, False, pairs) for edge, pairs in zip(edges, h_rounds)]
+        before += [move(corner, d, True, pairs) for corner, pairs in zip(corners, h_rounds)]
+    swap = [(i, i ^ 1) for i in range(n_t)]
     own, other = call(
         functools.partial(side_kernel, frames, rows),
         "side",
         [shape((lines, chans), F32), shape((lines, chans), BF16)],
         [],
-        [table] + columns,
-        LATER,
-    )
-    other = lax.ppermute(other, "tm", [(i, i ^ 1) for i in range(n_t)])
+        [table, move(column, 0, True)],
+    )
+    other = lax.ppermute(other, "tm", swap)
+    sides = []
+    if chips > 1:
+        many = lines + rounds * frames
+        mine_before, other_before = call(
+            functools.partial(before_kernel, frames, rows, rounds),
+            "before",
+            [shape((many, chans), F32), shape((many, chans), BF16)],
+            [],
+            [table] + before,
+        )
+        sides = [mine_before, lax.ppermute(other_before, "tm", swap)]
     size = frames * cols + 2 * frames
     low, high, *ends = call(
-        functools.partial(border_kernel, frames, rows, cols, chips),
+        functools.partial(border_kernel, frames, rows, cols),
         "border",
         [shape((lines, chans), F32)] * 2 + [shape((size, chans), BF16)] * len(h_rounds),
         [],
-        [mine, own, other] + firsts,
+        [mine, own, other],
     )
     ends = [lax.ppermute(e, "height", pairs) for e, pairs in zip(ends, h_rounds)]
 
@@ -427,7 +470,7 @@
         "last",
         [shape((block, chans), BF16)],
         [pltpu.VMEM((block, chans), BF16)],
-        [inner, totals, taps, gate, value_weight, out_weight] + firsts + rests + ends,
+        [inner, totals, taps, gate, value_weight, out_weight] + ends + rows_before + wholes + sides,
         4 * block * chans * chans,
     )
     return out.reshape(latents.shape)

time: 17 us -> 18.3 us (1.076)
  waiting for transfers between devices: 3.1 us -> 4 us
  starting transfers between devices: 8.57 us -> 8.86 us
    ppermute x5 -> x7, waiting for transfers between devices: 2.54 us -> 3.96 us  [the longest x5 3.95 us: move(): return lax.ppermute(data, ('tm', 'height', 'width'), route)]
    ppermute x5 -> x7, starting transfers between devices: 6.56 us -> 7.8 us  [the longest x5 7.66 us: move(): return lax.ppermute(data, ('tm', 'height', 'width'), route)]
    ppermute x1, starting transfers between devices: 1.56 us -> 0.6 us  [body(): lax.ppermute(e, 'height', pairs)]
    ppermute x1, waiting for transfers between devices: 0.52 us -> 0.01 us  [body(): lax.ppermute(e, 'height', pairs)]
    pallas_call x9 -> x10, Pallas kernels: 4.17 us -> 4.29 us  [call(): pl.pallas_call(kernel, out_shape=tuple(outs), in_specs=[HBM] * far + [VME...]
  transfers between devices with their start and end apart: 7 -> 9, of which waited for: 4 -> 2; matrix products, arithmetic and copies ran while one was open for 0% -> 0% of each run, Pallas kernels for 18% -> 16%
where the time goes in v14:
time: 18.3 us; the launch traced here: 18.1 us
  starting transfers between devices  8.86 us (48%)
  Pallas kernels  4.29 us (23%)
  waiting for transfers between devices  4 us (22%)
  local copies, waits for them, and re-layouts  0.78 us (4%)
    ppermute x5, starting transfers between devices, move(): return lax.ppermute(data, ('tm', 'height', 'width'), route)  7.66 us
    pallas_call x10, Pallas kernels, call(): pl.pallas_call(kernel, out_shape=tuple(outs), in_specs=[HBM] * far + [VME...  4.29 us
    ppermute x5, waiting for transfers between devices, move(): return lax.ppermute(data, ('tm', 'height', 'width'), route)  3.95 us
    unnamed x10, local copies, waits for them, and re-layouts  0.77 us
    ppermute x1, starting transfers between devices, body(): lax.ppermute(e, 'height', pairs)  0.6 us
    ppermute x1, starting transfers between devices, body(): partner = lax.ppermute(x, 'tm', [(i, i ^ 1) for i in range(n_t)])  0.45 us
  transfers between devices with their start and end apart: 9, of which 2 were waited for; matrix products, arithmetic and copies ran while one was open for 0% of the time, Pallas kernels for 16%

profile of v14, /device:TPU:0, one launch (start us, length us, event | category | flops | bytes accessed | tf_op | source)
XLA Modules:
  0.0 18.1 jit_solution(1868599821169058396)
XLA Ops:
  0.0 0.5 %collective-permute-start = (bf16[256,512]{1,0:T(8,128)(2,1)}, bf16[256,512]{1,0:T(8,128)(2,1)S(1)}, u32[]{:S(2)}, u32[]{:S(2)}) collective-permute-start(bf16[256,512]{1,0:T(8,128)(2,1)} %bitcast.3), channel_id=1, source_target_pairs={{0,8},{8,0},{16,24},{24,16},{1,9},{9,1},{17,25},{25,17},{2,10},{10... | collective-permute-start | bytes 786440 | tf_op jit(solution)/shard_map/ppermute | solution.py:365
  0.5 1.3 %early.1 = (f32[24,8,512]{2,1,0:T(8,128)S(1)}, f32[32,512]{1,0:T(8,128)S(1)}, f32[256,512]{1,0:T(8,128)S(1)}, f32[256,512]{1,0:T(8,128)S(1)}) custom-call(bf16[16,512]{1,0:T(8,128)(2,1)} %refs_0_.1, f32[1,512]{1,0:T(1,128)} %bitcast.6, bf16[256,512]{1,0:T(8,128)(2,1)} %bitcast.4), custom_call_target="tpu_custom_call" | custom-call | flops 2097152 | bytes 1787904 | tf_op jit(solution)/shard_map/early/pallas_call | solution.py:19
  1.8 0.0 collective-permute-done.partner_ref
  1.8 0.2 %later.1 = (bf16[256,512]{1,0:T(8,128)(2,1)S(1)}, bf16[32,512]{1,0:T(8,128)(2,1)S(1)}) custom-call(bf16[256,512]{1,0:T(8,128)(2,1)S(1)} %collective-permute-done.partner_ref, f32[24,8,512]{2,1,0:T(8,128)S(1)} %get-tuple-element.22.table_ref, f32[256,512]{1,0:T(8,128)S(1)} %get-tuple-element.33.refs_0_), custom_call_target="tpu_custom_call" | custom-call | flops 1048576 | bytes 1474560 | tf_op jit(solution)/shard_map/later/pallas_call | solution.py:19
  2.0 3.0 %collective-permute-start.5 = (bf16[256,512]{1,0:T(8,128)(2,1)S(1)}, bf16[256,512]{1,0:T(8,128)(2,1)S(1)}, u32[]{:S(2)}, u32[]{:S(2)}) collective-permute-start(bf16[256,512]{1,0:T(8,128)(2,1)S(1)} %get-tuple-element.35), channel_id=1, source_target_pairs={{0,16},{1,17},{2,18},{3,19},{4,20},{5,21},{6,22},{7,23},{8,24},{9,... | collective-permute-start | bytes 786440 | tf_op jit(solution)/shard_map/ppermute | solution.py:420
  5.0 0.1 column.1
  5.0 1.6 %collective-permute-start.1 = (bf16[64,512]{1,0:T(8,128)(2,1)S(1)}, bf16[64,512]{1,0:T(8,128)(2,1)S(1)}, u32[]{:S(2)}, u32[]{:S(2)}) collective-permute-start(bf16[64,512]{1,0:T(8,128)(2,1)S(1)} %get-tuple-element.25), channel_id=1, source_target_pairs={{0,1},{1,0},{2,3},{3,2},{4,5},{5,4},{6,7},{7,6},{8,12},{9,10},{10,... | collective-permute-start | bytes 196616 | tf_op jit(solution)/shard_map/ppermute | solution.py:420
  6.7 0.0 collective-permute-start.6
  6.7 2.7 %collective-permute-done.1.arrived_ref = bf16[64,512]{1,0:T(8,128)(2,1)S(1)} collective-permute-done((bf16[64,512]{1,0:T(8,128)(2,1)S(1)}, bf16[64,512]{1,0:T(8,128)(2,1)S(1)}, u32[]{:S(2)}, u32[]{:S(2)}) %collective-permute-start.1) | collective-permute-done | bytes 65568 | tf_op jit(solution)/shard_map/ppermute | solution.py:420
  9.4 0.1 side.1
  9.4 0.1 collective-permute-start.2
  9.5 2.5 %collective-permute-start.7 = (bf16[8,512]{1,0:T(8,128)(2,1)S(1)}, bf16[8,512]{1,0:T(8,128)(2,1)S(1)}, u32[]{:S(2)}, u32[]{:S(2)}) collective-permute-start(bf16[8,512]{1,0:T(8,128)(2,1)S(1)} %get-tuple-element.36), channel_id=1, source_target_pairs={{0,21},{1,20},{2,23},{3,22},{4,17},{5,16},{6,19},{7,18},{8,28},{9,... | collective-permute-start | bytes 24584 | tf_op jit(solution)/shard_map/ppermute | solution.py:420
  12.0 0.2 own.1.mine_ref
  12.2 0.0 collective-permute-done.2.other_ref
  12.2 0.0 copy-start.4
  12.2 0.0 copy-start.3
  12.3 0.0 copy-start.2
  12.3 0.6 %collective-permute-start.3 = (bf16[40,512]{1,0:T(8,128)(2,1)S(1)}, bf16[40,512]{1,0:T(8,128)(2,1)S(1)}, u32[]{:S(2)}, u32[]{:S(2)}) collective-permute-start(bf16[40,512]{1,0:T(8,128)(2,1)S(1)} %get-tuple-element.32), channel_id=1, source_target_pairs={{0,4},{4,0},{1,5},{5,1},{2,6},{6,2},{3,7},{7,3},{8,12},{12,8},{9,1... | collective-permute-start | bytes 122888 | tf_op jit(solution)/shard_map/ppermute | solution.py:457
  12.9 0.1 copy-done.4
  13.0 0.6 %collective-permute-start.4 = (bf16[32,512]{1,0:T(8,128)(2,1)S(1)}, bf16[32,512]{1,0:T(8,128)(2,1)S(1)}, u32[]{:S(2)}, u32[]{:S(2)}) collective-permute-start(bf16[32,512]{1,0:T(8,128)(2,1)S(1)} %get-tuple-element.34), channel_id=1, source_target_pairs={{0,20},{1,21},{2,22},{3,23},{4,16},{5,17},{6,18},{7,19},{8,28},{9,... | collective-permute-start | bytes 98312 | tf_op jit(solution)/shard_map/ppermute | solution.py:420
  13.5 0.0 collective-permute-done.7.refs_1_
  13.5 0.0 collective-permute-done.6.refs_0_
  13.5 0.2 before.1
  13.7 0.0 copy-start
  13.7 0.0 copy-start.1
  13.7 0.1 collective-permute-start.8
  13.8 0.0 copy-done.3
  13.8 0.0 copy-done.2
  13.8 0.4 %gate.1.gate_ref = f32[256,512]{1,0:T(8,128)S(1)} custom-call(bf16[256,512]{1,0:T(8,128)(2,1)S(1)} %bitcast.5, bf16[512,512]{1,0:T(8,128)(2,1)S(1)} %copy-done.3), custom_call_target="tpu_custom_call" | custom-call | flops 134217728 | bytes 1310720 | tf_op jit(solution)/shard_map/gate/pallas_call | solution.py:19
  14.2 0.5 %copy-done = bf16[512,512]{1,0:T(8,128)(2,1)S(1)} copy-done((bf16[512,512]{1,0:T(8,128)(2,1)S(1)}, bf16[512,512]{1,0:T(8,128)(2,1)}, u32[]{:S(2)}) %copy-start) | copy-done | bytes 524312
  14.7 0.2 copy-done.1
  14.9 0.7 %inner.1 = (bf16[256,512]{1,0:T(8,128)(2,1)S(1)}, f32[256,512]{1,0:T(8,128)S(1)}) custom-call(f32[256,512]{1,0:T(8,128)S(1)} %own.1.mine_ref, f32[32,512]{1,0:T(8,128)S(1)} %get-tuple-element.28.low_ref, f32[32,512]{1,0:T(8,128)S(1)} %get-tuple-element.29.high_ref, f32[9,512]{1,0:T(8,128)S(1)} %reshape.14.taps_ref, f32[256,512]{1,0:T(8,128)S(1)} %gate.1.gate_ref, ...), custom_call_target="tpu_custom_call" | custom-call | flops 268435456 | bytes 3033088 | tf_op jit(solution)/shard_map/inner/pallas_call | solution.py:19
  15.7 1.3 %collective-permute-done.4.refs_1_ = bf16[32,512]{1,0:T(8,128)(2,1)S(1)} collective-permute-done((bf16[32,512]{1,0:T(8,128)(2,1)S(1)}, bf16[32,512]{1,0:T(8,128)(2,1)S(1)}, u32[]{:S(2)}, u32[]{:S(2)}) %collective-permute-start.4) | collective-permute-done | bytes 32800 | tf_op jit(solution)/shard_map/ppermute | solution.py:420
  16.9 0.0 collective-permute-done.8.refs_4_
  16.9 0.0 collective-permute-done.3.refs_0_
  16.9 0.0 collective-permute-done.5.refs_2_
  16.9 1.1 %last.1 = bf16[256,512]{1,0:T(8,128)(2,1)} custom-call(bf16[256,512]{1,0:T(8,128)(2,1)S(1)} %get-tuple-element.30.inner_ref, f32[256,512]{1,0:T(8,128)S(1)} %get-tuple-element.31.totals_ref, f32[9,512]{1,0:T(8,128)S(1)} %reshape.14.taps_ref, f32[256,512]{1,0:T(8,128)S(1)} %gate.1.gate_ref, bf16[512,512]{1,0:T(8,128)(2,1)S(1)} %copy-done, ...), custom_call_target="tpu_custom_call" | custom-call | flops 268435456 | bytes 3086336 | tf_op jit(solution)/shard_map/last/pallas_call | solution.py:19
  (2 shorter events, 0.1 us)
Async XLA Ops:
  0.0 1.8 %collective-permute-start = (bf16[256,512]{1,0:T(8,128)(2,1)}, bf16[256,512]{1,0:T(8,128)(2,1)S(1)}, u32[]{:S(2)}, u32[]{:S(2)}) collective-permute-start(bf16[256,512]{1,0:T(8,128)(2,1)} %bitcast.3), channel_id=1, source_target_pairs={{0,8},{8,0},{16,24},{24,16},{1,9},{9,1},{17,25},{25,17},{2,10},{10... | collective-permute-start | bytes 786440 | tf_op jit(solution)/shard_map/ppermute | solution.py:365
  2.0 14.9 %collective-permute-start.5 = (bf16[256,512]{1,0:T(8,128)(2,1)S(1)}, bf16[256,512]{1,0:T(8,128)(2,1)S(1)}, u32[]{:S(2)}, u32[]{:S(2)}) collective-permute-start(bf16[256,512]{1,0:T(8,128)(2,1)S(1)} %get-tuple-element.35), channel_id=1, source_target_pairs={{0,16},{1,17},{2,18},{3,19},{4,20},{5,21},{6,22},{7,23},{8,24},{9,... | collective-permute-start | bytes 786440 | tf_op jit(solution)/shard_map/ppermute | solution.py:420
  5.0 4.3 %collective-permute-start.1 = (bf16[64,512]{1,0:T(8,128)(2,1)S(1)}, bf16[64,512]{1,0:T(8,128)(2,1)S(1)}, u32[]{:S(2)}, u32[]{:S(2)}) collective-permute-start(bf16[64,512]{1,0:T(8,128)(2,1)S(1)} %get-tuple-element.25), channel_id=1, source_target_pairs={{0,1},{1,0},{2,3},{3,2},{4,5},{5,4},{6,7},{7,6},{8,12},{9,10},{10,... | collective-permute-start | bytes 196616 | tf_op jit(solution)/shard_map/ppermute | solution.py:420
  6.7 6.8 %collective-permute-start.6 = (bf16[64,512]{1,0:T(8,128)(2,1)S(1)}, bf16[64,512]{1,0:T(8,128)(2,1)S(1)}, u32[]{:S(2)}, u32[]{:S(2)}) collective-permute-start(bf16[64,512]{1,0:T(8,128)(2,1)S(1)} %get-tuple-element.25), channel_id=1, source_target_pairs={{0,17},{1,16},{2,19},{3,18},{4,21},{5,20},{6,23},{7,22},{8,24},{9,... | collective-permute-start | bytes 196616 | tf_op jit(solution)/shard_map/ppermute | solution.py:420
  9.4 2.7 %collective-permute-start.2 = (bf16[32,512]{1,0:T(8,128)(2,1)S(1)}, bf16[32,512]{1,0:T(8,128)(2,1)S(1)}, u32[]{:S(2)}, u32[]{:S(2)}) collective-permute-start(bf16[32,512]{1,0:T(8,128)(2,1)S(1)} %get-tuple-element.27), channel_id=1, source_target_pairs={{0,8},{8,0},{16,24},{24,16},{1,9},{9,1},{17,25},{25,17},{2,10},{10... | collective-permute-start | bytes 98312 | tf_op jit(solution)/shard_map/ppermute | solution.py:437
  9.5 4.0 %collective-permute-start.7 = (bf16[8,512]{1,0:T(8,128)(2,1)S(1)}, bf16[8,512]{1,0:T(8,128)(2,1)S(1)}, u32[]{:S(2)}, u32[]{:S(2)}) collective-permute-start(bf16[8,512]{1,0:T(8,128)(2,1)S(1)} %get-tuple-element.36), channel_id=1, source_target_pairs={{0,21},{1,20},{2,23},{3,22},{4,17},{5,16},{6,19},{7,18},{8,28},{9,... | collective-permute-start | bytes 24584 | tf_op jit(solution)/shard_map/ppermute | solution.py:420
  12.2 0.7 %copy-start.4 = (f32[3,3,512]{2,1,0:T(4,128)S(1)}, f32[3,3,512]{2,1,0:T(4,128)}, u32[]{:S(2)}) copy-start(f32[3,3,512]{2,1,0:T(4,128)} %param.8) | copy-start | bytes 55300
  12.2 1.6 %copy-start.3 = (bf16[512,512]{1,0:T(8,128)(2,1)S(1)}, bf16[512,512]{1,0:T(8,128)(2,1)}, u32[]{:S(2)}) copy-start(bf16[512,512]{1,0:T(8,128)(2,1)} %w_ref.1) | copy-start | bytes 1572868
  12.3 1.5 %copy-start.2 = (bf16[4,8,8,512]{3,2,1,0:T(8,128)(2,1)S(1)}, bf16[4,8,8,512]{3,2,1,0:T(8,128)(2,1)}, u32[]{:S(2)}) copy-start(bf16[4,8,8,512]{3,2,1,0:T(8,128)(2,1)} %param.7) | copy-start | bytes 786436
  12.3 4.6 %collective-permute-start.3 = (bf16[40,512]{1,0:T(8,128)(2,1)S(1)}, bf16[40,512]{1,0:T(8,128)(2,1)S(1)}, u32[]{:S(2)}, u32[]{:S(2)}) collective-permute-start(bf16[40,512]{1,0:T(8,128)(2,1)S(1)} %get-tuple-element.32), channel_id=1, source_target_pairs={{0,4},{4,0},{1,5},{5,1},{2,6},{6,2},{3,7},{7,3},{8,12},{12,8},{9,1... | collective-permute-start | bytes 122888 | tf_op jit(solution)/shard_map/ppermute | solution.py:457
  13.0 4.0 %collective-permute-start.4 = (bf16[32,512]{1,0:T(8,128)(2,1)S(1)}, bf16[32,512]{1,0:T(8,128)(2,1)S(1)}, u32[]{:S(2)}, u32[]{:S(2)}) collective-permute-start(bf16[32,512]{1,0:T(8,128)(2,1)S(1)} %get-tuple-element.34), channel_id=1, source_target_pairs={{0,20},{1,21},{2,22},{3,23},{4,16},{5,17},{6,18},{7,19},{8,28},{9,... | collective-permute-start | bytes 98312 | tf_op jit(solution)/shard_map/ppermute | solution.py:420
  13.7 1.0 %copy-start = (bf16[512,512]{1,0:T(8,128)(2,1)S(1)}, bf16[512,512]{1,0:T(8,128)(2,1)}, u32[]{:S(2)}) copy-start(bf16[512,512]{1,0:T(8,128)(2,1)} %wv_ref.3) | copy-start | bytes 1572868
  13.7 1.2 %copy-start.1 = (bf16[512,512]{1,0:T(8,128)(2,1)S(1)}, bf16[512,512]{1,0:T(8,128)(2,1)}, u32[]{:S(2)}) copy-start(bf16[512,512]{1,0:T(8,128)(2,1)} %wo_ref.3) | copy-start | bytes 1572868
  13.7 3.2 %collective-permute-start.8 = (bf16[36,512]{1,0:T(8,128)(2,1)S(1)}, bf16[36,512]{1,0:T(8,128)(2,1)S(1)}, u32[]{:S(2)}, u32[]{:S(2)}) collective-permute-start(bf16[36,512]{1,0:T(8,128)(2,1)S(1)} %get-tuple-element.38), channel_id=1, source_target_pairs={{0,8},{8,0},{16,24},{24,16},{1,9},{9,1},{17,25},{25,17},{2,10},{10... | collective-permute-start | bytes 110600 | tf_op jit(solution)/shard_map/ppermute | solution.py:448

commit v15 on v14

--- a/solution.py
+++ b/solution.py
@@ -13,9 +13,8 @@
 HBM = pl.BlockSpec(memory_space=pltpu.HBM)
 
 
-def call(kernel, name, outs, scratch, operands, flops=0, exps=0, far=0):
+def call(kernel, name, outs, scratch, operands, far=0):
     operands = [pltpu.with_memory_space_constraint(a, pltpu.HBM) for a in operands[:far]] + list(operands[far:])
-    moved = sum(a.size * a.dtype.itemsize for a in operands) + sum(a.size * a.dtype.itemsize for a in outs)
     return pl.pallas_call(
         kernel,
         out_shape=tuple(outs),
@@ -23,7 +22,7 @@
         out_specs=(VMEM,) * len(outs),
         scratch_shapes=scratch,
         compiler_params=pltpu.CompilerParams(vmem_limit_bytes=24 * 1024 * 1024),
-        cost_estimate=pl.CostEstimate(flops=flops, bytes_accessed=moved, transcendentals=exps),
+        cost_estimate=pl.CostEstimate(flops=0, bytes_accessed=0, transcendentals=0),
         name=name,
     )(*operands)
 
@@ -66,12 +65,14 @@
     gate_ref[...] = v / (1.0 + jnp.exp(-v))
 
 
-def early_kernel(frames, rows, cols, *refs):
-    far, (table_ref, side_ref, *fields), near, (arrived, held) = refs[:3], refs[3:-5], refs[-5:-2], refs[-2:]
+def early_kernel(frames, rows, cols, count, *refs):
+    far, kept, rest = refs[:count], refs[count : 2 * count - 2], refs[2 * count - 2 :]
+    table_ref, side_ref, *fields, taps_ref, skip_ref, arrived, held = rest
+    near = (taps_ref, skip_ref) + kept
+    x_ref = near[2]
     copies = [pltpu.make_async_copy(a, b, arrived.at[i]) for i, (a, b) in enumerate(zip(far, near))]
     for copy in copies:
         copy.start()
-    taps_ref, skip_ref, x_ref = near
     lags, chans = taps_ref.shape
     copies[0].wait()
     copies[1].wait()
@@ -96,6 +97,8 @@
                     totals[t] = term if totals[t] is None else totals[t] + term
             for t in range(frames):
                 field[t * sites : (t + 1) * sites, span] = totals[t].reshape(sites, LANES)
+    for copy in copies[3:]:
+        copy.wait()
 
 
 def column_kernel(frames, rows, cols, partner_ref, side_ref, out_ref, *refs):
@@ -174,21 +177,33 @@
     return [jnp.where(exists, total, jnp.zeros_like(total)) for total in totals]
 
 
-def side_kernel(frames, rows, table_ref, arrived_ref, own_ref, other_ref):
+def side_kernel(frames, rows, table_ref, arrived_ref, own_ref, other_ref, *corners):
+    odd = position("height")[0]
     for lane in range(0, own_ref.shape[1], LANES):
         span = slice(lane, lane + LANES)
         totals = beside(mixed_columns(frames, rows, 0, arrived_ref[:, span].astype(F32), table_ref, span))
         own_ref[:, span] = jnp.concatenate(totals[:frames])
         other_ref[:, span] = jnp.concatenate(totals[frames:]).astype(BF16)
+        ends = [jnp.concatenate([total[r : r + 1] for total in totals]) for r in (0, rows - 1)]
+        for k, corner in enumerate(corners):
+            corner[:, span] = jnp.where(odd, *(ends[::-1] if k else ends)).astype(BF16)
 
 
 def before_kernel(frames, rows, rounds_h, table_ref, *refs):
-    *arrived, own_ref, other_ref = refs
+    *arrived, own_ref, other_ref, line_ref = refs
     per = 1 + rounds_h
+    chips = len(arrived) // (per + rounds_h)
+    arrived, lines = arrived[: chips * per], arrived[chips * per :]
+    size = line_ref.shape[0] // rounds_h
+    for k in range(rounds_h):
+        line = 0.0
+        for d in range(1, chips + 1):
+            line = line + later(d, lines[(d - 1) * rounds_h + k][...].astype(F32))
+        line_ref[k * size : (k + 1) * size] = line
     for lane in range(0, own_ref.shape[1], LANES):
         span = slice(lane, lane + LANES)
         parts = [0.0] * per
-        for d in range(1, len(arrived) // per + 1):
+        for d in range(1, chips + 1):
             for i, ref in enumerate(arrived[(d - 1) * per : d * per]):
                 pixels = rows if i == 0 else 1
                 column = later(d, ref[:, span].astype(F32))
@@ -204,19 +219,17 @@
     return jnp.where(right, other, own), jnp.where(right, own, other)
 
 
-def border_kernel(frames, rows, cols, mine_ref, own_ref, other_ref, low_ref, high_ref, *outs):
+def border_kernel(frames, rows, cols, mine_ref, *refs):
+    n = len(refs) // 3
     sites = rows * cols
     odd, _, _ = position("height")
-    low, high = both_sides(own_ref[...], other_ref[...].astype(F32))
-    low_ref[...] = low
-    high_ref[...] = high
     ends = []
     for r in (0, rows - 1):
         line = [mine_ref[t * sites + r * cols : t * sites + (r + 1) * cols] for t in range(frames)]
-        corners = [side[t * rows + r : t * rows + r + 1] for side in (low, high) for t in range(frames)]
-        ends.append(jnp.concatenate(line + corners))
-    for k, out in enumerate(outs):
-        out[...] = jnp.where(odd, *(ends[::-1] if k else ends)).astype(BF16)
+        ends.append(jnp.concatenate(line))
+    for k, (own, other, out) in enumerate(zip(refs[:n], refs[n : 2 * n], refs[2 * n :])):
+        corners = both_sides(own[...].astype(F32)[:frames], other[...].astype(F32)[frames:])
+        out[...] = jnp.concatenate([jnp.where(odd, *(ends[::-1] if k else ends)), *corners]).astype(BF16)
 
 
 def shifted(line, left, right):
@@ -246,17 +259,17 @@
 
 
 def taps_of(taps_ref, span):
-    return [[taps_ref[3 * a + b : 3 * a + b + 1, span] for b in range(3)] for a in range(3)]
+    return [[taps_ref[a, b : b + 1, span] for b in range(3)] for a in range(3)]
 
 
 def inner_kernel(
-    frames, rows, cols, mine_ref, low_ref, high_ref, taps_ref, gate_ref, wv_ref, wo_ref, out_ref, totals_ref, mixed
+    frames, rows, cols, mine_ref, own_ref, other_ref, taps_ref, gate_ref, wv_ref, wo_ref, out_ref, totals_ref, mixed
 ):
     sites = rows * cols
     for lane in range(0, mine_ref.shape[1], LANES):
         span = slice(lane, lane + LANES)
         taps = taps_of(taps_ref, span)
-        low, high = low_ref[:, span], high_ref[:, span]
+        low, high = both_sides(own_ref[:, span], other_ref[:, span].astype(F32))
         for t in range(frames):
             at = t * sites
             lines = [mine_ref[at + r * cols : at + (r + 1) * cols, span] for r in range(rows)]
@@ -275,10 +288,8 @@
     size = frames * cols
     odd, lower, upper = position("height")
     earlier = lax.div(lax.axis_index("tm"), 2) > 0
-    rounds_h = (len(parts) - (chips + 1 if chips > 1 else 0)) // chips
-    ends, parts = parts[:rounds_h], parts[rounds_h:]
-    lines_before, parts = parts[: rounds_h * (chips - 1)], parts[rounds_h * (chips - 1) :]
-    wholes, sides = parts[: chips - 1], parts[chips - 1 :]
+    rounds_h = len(parts) - (chips + 2 if chips > 1 else 0)
+    ends, wholes, sides = parts[:rounds_h], parts[rounds_h : rounds_h + chips - 1], parts[rounds_h + chips - 1 :]
     none = jnp.zeros((cols, chans), F32)
     above, below = [none] * frames, [none] * frames
     low = high = None
@@ -288,13 +299,12 @@
         end = end[...].astype(F32)
         first = jnp.logical_not(odd) if k else odd
         line, lefts, rights = end[:size], end[size : size + frames], end[size + frames : size + 2 * frames]
-        for d in range(1, chips):
-            line = line + later(d, lines_before[(d - 1) * rounds_h + k][...].astype(F32))
         if sides:
+            line = line + sides[2][k * size : (k + 1) * size]
             at = frames * rows + k * frames
             lefts, rights = lefts + low[at : at + frames], rights + high[at : at + frames]
         exists = jnp.where(first, lower, upper)
-        tap = jnp.where(first, taps_ref[0:3], taps_ref[6:9])
+        tap = jnp.where(first, taps_ref[0], taps_ref[2])
         for t in range(frames):
             near = shifted(line[t * cols : (t + 1) * cols], lefts[t : t + 1], rights[t : t + 1])
             more = near[0] * tap[0:1] + near[1] * tap[1:2] + near[2] * tap[2:3]
@@ -363,22 +373,21 @@
     x = latents.reshape(block, chans)
 
     partner = lax.ppermute(x, "tm", [(i, i ^ 1) for i in range(n_t)])
-    inputs = [kernel_taps, skip_gain.reshape(1, chans), x]
     lines = frames * rows
     field = shape((block, chans), F32)
-    table, side, *fields = call(
-        functools.partial(early_kernel, frames, rows, cols),
+    inputs = [kernel_taps, skip_gain.reshape(1, chans), x, gate_weight, spatial_taps, value_weight, out_weight]
+    near_x, near_gate, taps, value_weight, out_weight, table, side, *fields = call(
+        functools.partial(early_kernel, frames, rows, cols, len(inputs)),
         "early",
-        [shape((lags + 2 * frames, cols, chans), F32), shape((lines, chans), F32)] + [field] * chips,
-        [pltpu.VMEM(a.shape, a.dtype) for a in inputs]
+        [shape(a.shape, a.dtype) for a in inputs[2:]]
+        + [shape((lags + 2 * frames, cols, chans), F32), shape((lines, chans), F32)]
+        + [field] * chips,
+        [pltpu.VMEM(a.shape, a.dtype) for a in inputs[:2]]
         + [pltpu.SemaphoreType.DMA((len(inputs),)), pltpu.VMEM((block, LANES), F32)],
         inputs,
-        2 * chips * frames * x.size,
         far=len(inputs),
     )
-    (gate,) = call(
-        gate_kernel, "gate", [shape((block, chans), F32)], [], [x, gate_weight], 2 * block * chans * chans, x.size
-    )
+    (gate,) = call(gate_kernel, "gate", [field], [], [near_x, near_gate])
 
     h_rounds = swaps("height")
     rounds = len(h_rounds)
@@ -395,7 +404,6 @@
         ([shape((block, chans), BF16)] + [shape((frames * cols, chans), BF16)] * rounds) * (chips - 1),
         [],
         [partner, table] + fields[1:],
-        2 * (chips - 1) * frames * x.size,
     )
     (mine,) = call(
         functools.partial(own_kernel, frames, rows, cols),
@@ -403,7 +411,6 @@
         [field],
         [],
         [partner, table, fields[0]],
-        2 * frames * x.size,
     )
 
     def move(data, d, across_w, pairs=None):
@@ -427,51 +434,49 @@
         rows_before += [move(edge, d, False, pairs) for edge, pairs in zip(edges, h_rounds)]
         before += [move(corner, d, True, pairs) for corner, pairs in zip(corners, h_rounds)]
     swap = [(i, i ^ 1) for i in range(n_t)]
-    own, other = call(
+    own, other, *own_corners = call(
         functools.partial(side_kernel, frames, rows),
         "side",
-        [shape((lines, chans), F32), shape((lines, chans), BF16)],
+        [shape((lines, chans), F32), shape((lines, chans), BF16)] + [shape((2 * frames, chans), BF16)] * rounds,
         [],
         [table, move(column, 0, True)],
     )
+    other_corners = [lax.ppermute(corner, "tm", swap) for corner in own_corners]
     other = lax.ppermute(other, "tm", swap)
     sides = []
     if chips > 1:
         many = lines + rounds * frames
-        mine_before, other_before = call(
+        mine_before, other_before, line = call(
             functools.partial(before_kernel, frames, rows, rounds),
             "before",
-            [shape((many, chans), F32), shape((many, chans), BF16)],
+            [shape((many, chans), F32), shape((many, chans), BF16), shape((rounds * frames * cols, chans), F32)],
             [],
-            [table] + before,
+            [table] + before + rows_before,
         )
-        sides = [mine_before, lax.ppermute(other_before, "tm", swap)]
+        sides = [mine_before, lax.ppermute(other_before, "tm", swap), line]
     size = frames * cols + 2 * frames
-    low, high, *ends = call(
+    ends = call(
         functools.partial(border_kernel, frames, rows, cols),
         "border",
-        [shape((lines, chans), F32)] * 2 + [shape((size, chans), BF16)] * len(h_rounds),
+        [shape((size, chans), BF16)] * rounds,
         [],
-        [mine, own, other],
+        [mine] + own_corners + other_corners,
     )
     ends = [lax.ppermute(e, "height", pairs) for e, pairs in zip(ends, h_rounds)]
 
-    taps = spatial_taps.reshape(9, chans)
     inner, totals = call(
         functools.partial(inner_kernel, frames, rows, cols),
         "inner",
         [shape((block, chans), BF16), field],
         [pltpu.VMEM((block, chans), BF16)],
-        [mine, low, high, taps, gate, value_weight, out_weight],
-        4 * block * chans * chans,
+        [mine, own, other, taps, gate, value_weight, out_weight],
     )
     (out,) = call(
         functools.partial(last_kernel, frames, rows, cols, chips),
         "last",
         [shape((block, chans), BF16)],
         [pltpu.VMEM((block, chans), BF16)],
-        [inner, totals, taps, gate, value_weight, out_weight] + ends + rows_before + wholes + sides,
-        4 * block * chans * chans,
+        [inner, totals, taps, gate, value_weight, out_weight] + ends + wholes + sides,
     )
     return out.reshape(latents.shape)
 

time: 18.3 us -> 17.9 us (0.978)
  starting transfers between devices: 8.86 us -> 11.3 us
  waiting for transfers between devices: 4 us -> 1.69 us
  local copies, waits for them, and re-layouts: 0.78 us -> 0 us
  Pallas kernels: 4.29 us -> 4.57 us
    ppermute x5, waiting for transfers between devices: 3.95 us -> 1.21 us  [move(): return lax.ppermute(data, ('tm', 'height', 'width'), route)]
    ppermute x5, starting transfers between devices: 7.66 us -> 9.58 us  [move(): return lax.ppermute(data, ('tm', 'height', 'width'), route)]
    unnamed x10 -> x0, local copies, waits for them, and re-layouts: 0.77 us -> none
    ppermute x1, waiting for transfers between devices: 0.01 us -> 0.47 us  [body(): other = lax.ppermute(other, 'tm', swap)]
    ppermute x1, starting transfers between devices: 0.07 us -> 0.5 us  [body(): other = lax.ppermute(other, 'tm', swap)]
    pallas_call x10, Pallas kernels: 4.29 us -> 4.57 us  [call(): pl.pallas_call(kernel, out_shape=tuple(outs), in_specs=[HBM] * far + [VME...]
  transfers between devices with their start and end apart: 9 -> 10, of which waited for: 2 -> 2; matrix products, arithmetic and copies ran while one was open for 0% -> 0% of each run, Pallas kernels for 16% -> 18%
where the time goes in v15:
time: 17.9 us; the launch traced here: 17.6 us
  starting transfers between devices  11.3 us (63%)
  Pallas kernels  4.57 us (26%)
  waiting for transfers between devices  1.69 us (9%)
    ppermute x5, starting transfers between devices, move(): return lax.ppermute(data, ('tm', 'height', 'width'), route)  9.58 us
    pallas_call x10, Pallas kernels, call(): pl.pallas_call(kernel, out_shape=tuple(outs), in_specs=[HBM] * far + [VME...  4.57 us
    ppermute x5, waiting for transfers between devices, move(): return lax.ppermute(data, ('tm', 'height', 'width'), route)  1.21 us
    ppermute x1, starting transfers between devices, body(): lax.ppermute(e, 'height', pairs)  0.6 us
    ppermute x1, starting transfers between devices, body(): other = lax.ppermute(other, 'tm', swap)  0.5 us
    ppermute x1, waiting for transfers between devices, body(): other = lax.ppermute(other, 'tm', swap)  0.47 us
    ppermute x1, starting transfers between devices, body(): partner = lax.ppermute(x, 'tm', [(i, i ^ 1) for i in range(n_t)])  0.45 us
  transfers between devices with their start and end apart: 10, of which 2 were waited for; matrix products, arithmetic and copies ran while one was open for 0% of the time, Pallas kernels for 18%

profile of v15, /device:TPU:0, one launch (start us, length us, event | category | flops | bytes accessed | tf_op | source)
XLA Modules:
  0.0 17.6 jit_solution(14899860636033086031)
XLA Ops:
  0.0 0.5 %collective-permute-start = (bf16[256,512]{1,0:T(8,128)(2,1)}, bf16[256,512]{1,0:T(8,128)(2,1)S(1)}, u32[]{:S(2)}, u32[]{:S(2)}) collective-permute-start(bf16[256,512]{1,0:T(8,128)(2,1)} %bitcast.3), channel_id=1, source_target_pairs={{0,8},{8,0},{16,24},{24,16},{1,9},{9,1},{17,25},{25,17},{2,10},{10... | collective-permute-start | bytes 786440 | tf_op jit(solution)/shard_map/ppermute | solution.py:375
  0.5 1.5 %early.1 = (bf16[256,512]{1,0:T(8,128)(2,1)S(1)}, bf16[512,512]{1,0:T(8,128)(2,1)S(1)}, f32[3,3,512]{2,1,0:T(4,128)S(1)}, bf16[512,512]{1,0:T(8,128)(2,1)S(1)}, ...) custom-call(bf16[16,512]{1,0:T(8,128)(2,1)} %refs_0_.1, ...), custom_call_target="tpu_custom_call" | custom-call | tf_op jit(solution)/shard_map/early/pallas_call | solution.py:18
  2.0 0.0 collective-permute-done.partner_ref
  2.0 0.2 %later.1 = (bf16[256,512]{1,0:T(8,128)(2,1)S(1)}, bf16[32,512]{1,0:T(8,128)(2,1)S(1)}) custom-call(bf16[256,512]{1,0:T(8,128)(2,1)S(1)} %collective-permute-done.partner_ref, f32[24,8,512]{2,1,0:T(8,128)S(1)} %get-tuple-element.26.table_ref, f32[256,512]{1,0:T(8,128)S(1)} %get-tuple-element.40.refs_0_), custom_call_target="tpu_custom_call" | custom-call | tf_op jit(solution)/shard_map/later/pallas_call | solution.py:18
  2.2 2.8 %collective-permute-start.5 = (bf16[256,512]{1,0:T(8,128)(2,1)S(1)}, bf16[256,512]{1,0:T(8,128)(2,1)S(1)}, u32[]{:S(2)}, u32[]{:S(2)}) collective-permute-start(bf16[256,512]{1,0:T(8,128)(2,1)S(1)} %get-tuple-element.41), channel_id=1, source_target_pairs={{0,16},{1,17},{2,18},{3,19},{4,20},{5,21},{6,22},{7,23},{8,24},{9,... | collective-permute-start | bytes 786440 | tf_op jit(solution)/shard_map/ppermute | solution.py:427
  5.0 0.1 column.1
  5.0 1.6 %collective-permute-start.1 = (bf16[64,512]{1,0:T(8,128)(2,1)S(1)}, bf16[64,512]{1,0:T(8,128)(2,1)S(1)}, u32[]{:S(2)}, u32[]{:S(2)}) collective-permute-start(bf16[64,512]{1,0:T(8,128)(2,1)S(1)} %get-tuple-element.29), channel_id=1, source_target_pairs={{0,1},{1,0},{2,3},{3,2},{4,5},{5,4},{6,7},{7,6},{8,12},{9,10},{10,... | collective-permute-start | bytes 196616 | tf_op jit(solution)/shard_map/ppermute | solution.py:427
  6.7 0.0 collective-permute-start.6
  6.7 2.9 %collective-permute-start.8 = (bf16[32,512]{1,0:T(8,128)(2,1)S(1)}, bf16[32,512]{1,0:T(8,128)(2,1)S(1)}, u32[]{:S(2)}, u32[]{:S(2)}) collective-permute-start(bf16[32,512]{1,0:T(8,128)(2,1)S(1)} %get-tuple-element.43), channel_id=1, source_target_pairs={{0,20},{1,21},{2,22},{3,23},{4,16},{5,17},{6,18},{7,19},{8,28},{9,... | collective-permute-start | bytes 98312 | tf_op jit(solution)/shard_map/ppermute | solution.py:427
  9.6 0.0 collective-permute-done.1.arrived_ref
  9.6 0.1 side.1
  9.7 0.1 collective-permute-start.3
  9.8 2.2 %collective-permute-start.7 = (bf16[8,512]{1,0:T(8,128)(2,1)S(1)}, bf16[8,512]{1,0:T(8,128)(2,1)S(1)}, u32[]{:S(2)}, u32[]{:S(2)}) collective-permute-start(bf16[8,512]{1,0:T(8,128)(2,1)S(1)} %get-tuple-element.42), channel_id=1, source_target_pairs={{0,21},{1,20},{2,23},{3,22},{4,17},{5,16},{6,19},{7,18},{8,28},{9,... | collective-permute-start | bytes 24584 | tf_op jit(solution)/shard_map/ppermute | solution.py:427
  12.0 0.2 own.1.mine_ref
  12.2 0.0 collective-permute-done.3.refs_1_
  12.3 0.6 %collective-permute-start.4 = (bf16[40,512]{1,0:T(8,128)(2,1)S(1)}, bf16[40,512]{1,0:T(8,128)(2,1)S(1)}, u32[]{:S(2)}, u32[]{:S(2)}) collective-permute-start(bf16[40,512]{1,0:T(8,128)(2,1)S(1)} %border.1), channel_id=1, source_target_pairs={{0,4},{4,0},{1,5},{5,1},{2,6},{6,2},{3,7},{7,3},{8,12},{12,8},{9,1... | collective-permute-start | bytes 122888 | tf_op jit(solution)/shard_map/ppermute | solution.py:465
  12.9 1.2 %collective-permute-done.7.refs_1_ = bf16[8,512]{1,0:T(8,128)(2,1)S(1)} collective-permute-done((bf16[8,512]{1,0:T(8,128)(2,1)S(1)}, bf16[8,512]{1,0:T(8,128)(2,1)S(1)}, u32[]{:S(2)}, u32[]{:S(2)}) %collective-permute-start.7) | collective-permute-done | bytes 8224 | tf_op jit(solution)/shard_map/ppermute | solution.py:427
  14.1 0.0 collective-permute-done.8.refs_2_
  14.1 0.0 collective-permute-done.6.refs_0_
  14.1 0.2 %before.1 = (f32[36,512]{1,0:T(8,128)S(1)}, bf16[36,512]{1,0:T(8,128)(2,1)S(1)}, f32[32,512]{1,0:T(8,128)S(1)}) custom-call(f32[24,8,512]{2,1,0:T(8,128)S(1)} %get-tuple-element.26.table_ref, bf16[64,512]{1,0:T(8,128)(2,1)S(1)} %collective-permute-done.6.refs_0_, bf16[8,512]{1,0:T(8,128)(2,1)S(1)} %collective-permute-done.7.refs_1_, ...), custom_call_target="tpu_custom_call" | custom-call | tf_op jit(solution)/shard_map/before/pallas_call | solution.py:18
  14.2 0.1 collective-permute-start.9
  14.3 0.5 %collective-permute-start.2 = (bf16[32,512]{1,0:T(8,128)(2,1)S(1)}, bf16[32,512]{1,0:T(8,128)(2,1)S(1)}, u32[]{:S(2)}, u32[]{:S(2)}) collective-permute-start(bf16[32,512]{1,0:T(8,128)(2,1)S(1)} %get-tuple-element.31), channel_id=1, source_target_pairs={{0,8},{8,0},{16,24},{24,16},{1,9},{9,1},{17,25},{25,17},{2,10},{10... | collective-permute-start | bytes 98312 | tf_op jit(solution)/shard_map/ppermute | solution.py:445
  14.8 0.4 %gate.1.gate_ref = f32[256,512]{1,0:T(8,128)S(1)} custom-call(bf16[256,512]{1,0:T(8,128)(2,1)S(1)} %get-tuple-element.33.x_ref, bf16[512,512]{1,0:T(8,128)(2,1)S(1)} %get-tuple-element.34.w_ref), custom_call_target="tpu_custom_call" | custom-call | tf_op jit(solution)/shard_map/gate/pallas_call | solution.py:18
  15.2 0.5 %collective-permute-done.2.other_ref = bf16[32,512]{1,0:T(8,128)(2,1)S(1)} collective-permute-done((bf16[32,512]{1,0:T(8,128)(2,1)S(1)}, bf16[32,512]{1,0:T(8,128)(2,1)S(1)}, u32[]{:S(2)}, u32[]{:S(2)}) %collective-permute-start.2) | collective-permute-done | bytes 32800 | tf_op jit(solution)/shard_map/ppermute | solution.py:445
  15.7 0.8 %inner.1 = (bf16[256,512]{1,0:T(8,128)(2,1)S(1)}, f32[256,512]{1,0:T(8,128)S(1)}) custom-call(f32[256,512]{1,0:T(8,128)S(1)} %own.1.mine_ref, f32[32,512]{1,0:T(8,128)S(1)} %get-tuple-element.30.own_ref, bf16[32,512]{1,0:T(8,128)(2,1)S(1)} %collective-permute-done.2.other_ref, f32[3,3,512]{2,1,0:T(4,128)S(1)} %get-tuple-element.32.taps_ref, ...), custom_call_target="tpu_custom_call" | custom-call | tf_op jit(solution)/shard_map/inner/pallas_call | solution.py:18
  16.5 0.0 collective-permute-done.9.refs_3_
  16.5 0.0 collective-permute-done.4.refs_0_
  16.5 0.0 collective-permute-done.5.refs_1_
  16.5 1.1 %last.1 = bf16[256,512]{1,0:T(8,128)(2,1)} custom-call(bf16[256,512]{1,0:T(8,128)(2,1)S(1)} %get-tuple-element.37.inner_ref, f32[256,512]{1,0:T(8,128)S(1)} %get-tuple-element.38.totals_ref, f32[3,3,512]{2,1,0:T(4,128)S(1)} %get-tuple-element.32.taps_ref, f32[256,512]{1,0:T(8,128)S(1)} %gate.1.gate_ref, bf16[512,512]{1,0:T(8,128)(2,1)S(1)} %get-tuple-element.35.wv_ref, ...), custom_call_target="tpu_custom_call" | custom-call | tf_op jit(solution)/shard_map/last/pallas_call | solution.py:18
  (1 shorter events, 0.0 us)
Async XLA Ops:
  0.0 2.0 %collective-permute-start = (bf16[256,512]{1,0:T(8,128)(2,1)}, bf16[256,512]{1,0:T(8,128)(2,1)S(1)}, u32[]{:S(2)}, u32[]{:S(2)}) collective-permute-start(bf16[256,512]{1,0:T(8,128)(2,1)} %bitcast.3), channel_id=1, source_target_pairs={{0,8},{8,0},{16,24},{24,16},{1,9},{9,1},{17,25},{25,17},{2,10},{10... | collective-permute-start | bytes 786440 | tf_op jit(solution)/shard_map/ppermute | solution.py:375
  2.2 14.3 %collective-permute-start.5 = (bf16[256,512]{1,0:T(8,128)(2,1)S(1)}, bf16[256,512]{1,0:T(8,128)(2,1)S(1)}, u32[]{:S(2)}, u32[]{:S(2)}) collective-permute-start(bf16[256,512]{1,0:T(8,128)(2,1)S(1)} %get-tuple-element.41), channel_id=1, source_target_pairs={{0,16},{1,17},{2,18},{3,19},{4,20},{5,21},{6,22},{7,23},{8,24},{9,... | collective-permute-start | bytes 786440 | tf_op jit(solution)/shard_map/ppermute | solution.py:427
  5.0 4.6 %collective-permute-start.1 = (bf16[64,512]{1,0:T(8,128)(2,1)S(1)}, bf16[64,512]{1,0:T(8,128)(2,1)S(1)}, u32[]{:S(2)}, u32[]{:S(2)}) collective-permute-start(bf16[64,512]{1,0:T(8,128)(2,1)S(1)} %get-tuple-element.29), channel_id=1, source_target_pairs={{0,1},{1,0},{2,3},{3,2},{4,5},{5,4},{6,7},{7,6},{8,12},{9,10},{10,... | collective-permute-start | bytes 196616 | tf_op jit(solution)/shard_map/ppermute | solution.py:427
  6.7 7.4 %collective-permute-start.6 = (bf16[64,512]{1,0:T(8,128)(2,1)S(1)}, bf16[64,512]{1,0:T(8,128)(2,1)S(1)}, u32[]{:S(2)}, u32[]{:S(2)}) collective-permute-start(bf16[64,512]{1,0:T(8,128)(2,1)S(1)} %get-tuple-element.29), channel_id=1, source_target_pairs={{0,17},{1,16},{2,19},{3,18},{4,21},{5,20},{6,23},{7,22},{8,24},{9,... | collective-permute-start | bytes 196616 | tf_op jit(solution)/shard_map/ppermute | solution.py:427
  6.7 7.4 %collective-permute-start.8 = (bf16[32,512]{1,0:T(8,128)(2,1)S(1)}, bf16[32,512]{1,0:T(8,128)(2,1)S(1)}, u32[]{:S(2)}, u32[]{:S(2)}) collective-permute-start(bf16[32,512]{1,0:T(8,128)(2,1)S(1)} %get-tuple-element.43), channel_id=1, source_target_pairs={{0,20},{1,21},{2,22},{3,23},{4,16},{5,17},{6,18},{7,19},{8,28},{9,... | collective-permute-start | bytes 98312 | tf_op jit(solution)/shard_map/ppermute | solution.py:427
  9.7 2.5 %collective-permute-start.3 = (bf16[8,512]{1,0:T(8,128)(2,1)S(1)}, bf16[8,512]{1,0:T(8,128)(2,1)S(1)}, u32[]{:S(2)}, u32[]{:S(2)}) collective-permute-start(bf16[8,512]{1,0:T(8,128)(2,1)S(1)} %get-tuple-element.39.refs_0_), channel_id=1, source_target_pairs={{0,8},{8,0},{16,24},{24,16},{1,9},{9,1},{17,25},{25,17},{2,10},{10... | collective-permute-start | bytes 24584 | tf_op jit(solution)/shard_map/ppermute | solution.py:444
  9.8 4.2 %collective-permute-start.7 = (bf16[8,512]{1,0:T(8,128)(2,1)S(1)}, bf16[8,512]{1,0:T(8,128)(2,1)S(1)}, u32[]{:S(2)}, u32[]{:S(2)}) collective-permute-start(bf16[8,512]{1,0:T(8,128)(2,1)S(1)} %get-tuple-element.42), channel_id=1, source_target_pairs={{0,21},{1,20},{2,23},{3,22},{4,17},{5,16},{6,19},{7,18},{8,28},{9,... | collective-permute-start | bytes 24584 | tf_op jit(solution)/shard_map/ppermute | solution.py:427
  12.3 4.2 %collective-permute-start.4 = (bf16[40,512]{1,0:T(8,128)(2,1)S(1)}, bf16[40,512]{1,0:T(8,128)(2,1)S(1)}, u32[]{:S(2)}, u32[]{:S(2)}) collective-permute-start(bf16[40,512]{1,0:T(8,128)(2,1)S(1)} %border.1), channel_id=1, source_target_pairs={{0,4},{4,0},{1,5},{5,1},{2,6},{6,2},{3,7},{7,3},{8,12},{12,8},{9,1... | collective-permute-start | bytes 122888 | tf_op jit(solution)/shard_map/ppermute | solution.py:465
  14.2 2.2 %collective-permute-start.9 = (bf16[36,512]{1,0:T(8,128)(2,1)S(1)}, bf16[36,512]{1,0:T(8,128)(2,1)S(1)}, u32[]{:S(2)}, u32[]{:S(2)}) collective-permute-start(bf16[36,512]{1,0:T(8,128)(2,1)S(1)} %get-tuple-element.45), channel_id=1, source_target_pairs={{0,8},{8,0},{16,24},{24,16},{1,9},{9,1},{17,25},{25,17},{2,10},{10... | collective-permute-start | bytes 110600 | tf_op jit(solution)/shard_map/ppermute | solution.py:456
  14.3 1.4 %collective-permute-start.2 = (bf16[32,512]{1,0:T(8,128)(2,1)S(1)}, bf16[32,512]{1,0:T(8,128)(2,1)S(1)}, u32[]{:S(2)}, u32[]{:S(2)}) collective-permute-start(bf16[32,512]{1,0:T(8,128)(2,1)S(1)} %get-tuple-element.31), channel_id=1, source_target_pairs={{0,8},{8,0},{16,24},{24,16},{1,9},{9,1},{17,25},{25,17},{2,10},{10... | collective-permute-start | bytes 98312 | tf_op jit(solution)/shard_map/ppermute | solution.py:445

commit v16 on v13

--- a/solution.py
+++ b/solution.py
@@ -67,12 +67,14 @@
     gate_ref[...] = v / (1.0 + jnp.exp(-v))
 
 
-def early_kernel(frames, rows, cols, *refs):
-    far, (table_ref, side_ref, *fields), near, (arrived, held) = refs[:3], refs[3:-5], refs[-5:-2], refs[-2:]
+def early_kernel(frames, rows, cols, count, *refs):
+    far, kept, rest = refs[:count], refs[count : 2 * count - 2], refs[2 * count - 2 :]
+    table_ref, side_ref, *fields, taps_ref, skip_ref, arrived, held = rest
+    near = (taps_ref, skip_ref) + kept
+    x_ref = near[2]
     copies = [pltpu.make_async_copy(a, b, arrived.at[i]) for i, (a, b) in enumerate(zip(far, near))]
     for copy in copies:
         copy.start()
-    taps_ref, skip_ref, x_ref = near
     lags, chans = taps_ref.shape
     copies[0].wait()
     copies[1].wait()
@@ -97,6 +99,8 @@
                     totals[t] = term if totals[t] is None else totals[t] + term
             for t in range(frames):
                 field[t * sites : (t + 1) * sites, span] = totals[t].reshape(sites, LANES)
+    for copy in copies[3:]:
+        copy.wait()
 
 
 def reordered(lines, rounds_h, back=False):
@@ -158,7 +162,7 @@
     for lane in range(0, own_ref.shape[1], LANES):
         span = slice(lane, lane + LANES)
         totals = [jnp.zeros((rows, LANES), F32)] * (2 * frames)
-        for d, ref in enumerate(arrived[::-1]):
+        for d, ref in enumerate(arrived):
             column = later(d, ref[:, span].astype(F32))
             base = 2 * frames + 2 * d * frames
             for t in range(2 * frames):
@@ -228,7 +232,7 @@
 
 
 def taps_of(taps_ref, span):
-    return [[taps_ref[3 * a + b : 3 * a + b + 1, span] for b in range(3)] for a in range(3)]
+    return [[taps_ref[a, b : b + 1, span] for b in range(3)] for a in range(3)]
 
 
 def inner_kernel(
@@ -266,7 +270,7 @@
         first = jnp.logical_not(odd) if k else odd
         lefts, rights = end[size : size + frames], end[size + frames : size + 2 * frames]
         exists = jnp.where(first, lower, upper)
-        tap = jnp.where(first, taps_ref[0:3], taps_ref[6:9])
+        tap = jnp.where(first, taps_ref[0], taps_ref[2])
         for t in range(frames):
             near = shifted(end[t * cols : (t + 1) * cols], lefts[t : t + 1], rights[t : t + 1])
             more = near[0] * tap[0:1] + near[1] * tap[1:2] + near[2] * tap[2:3]
@@ -333,22 +337,21 @@
     x = latents.reshape(block, chans)
 
     partner = lax.ppermute(x, "tm", [(i, i ^ 1) for i in range(n_t)])
-    inputs = [kernel_taps, skip_gain.reshape(1, chans), x]
     lines = frames * rows
     field = shape((block, chans), F32)
-    table, side, *fields = call(
-        functools.partial(early_kernel, frames, rows, cols),
+    inputs = [kernel_taps, skip_gain.reshape(1, chans), x, gate_weight, spatial_taps, value_weight, out_weight]
+    near_x, near_gate, taps, value_weight, out_weight, table, side, *fields = call(
+        functools.partial(early_kernel, frames, rows, cols, len(inputs)),
         "early",
-        [shape((lags + 2 * frames, cols, chans), F32), shape((lines, chans), F32)] + [field] * chips,
-        [pltpu.VMEM(a.shape, a.dtype) for a in inputs]
+        [shape(a.shape, a.dtype) for a in inputs[2:]]
+        + [shape((lags + 2 * frames, cols, chans), F32), shape((lines, chans), F32)]
+        + [field] * chips,
+        [pltpu.VMEM(a.shape, a.dtype) for a in inputs[:2]]
         + [pltpu.SemaphoreType.DMA((len(inputs),)), pltpu.VMEM((block, LANES), F32)],
         inputs,
-        2 * chips * frames * x.size,
         far=len(inputs),
     )
-    (gate,) = call(
-        gate_kernel, "gate", [shape((block, chans), F32)], [], [x, gate_weight], 2 * block * chans * chans, x.size
-    )
+    (gate,) = call(gate_kernel, "gate", [field], [], [near_x, near_gate])
 
     h_rounds = swaps("height")
     (column,) = call(
@@ -376,7 +379,7 @@
         2 * frames * x.size,
     )
     columns, firsts, rests = [], [], []
-    for d in reversed(range(chips)):
+    for d in range(chips):
         route = []
         for i in range(n_t):
             for h in range(n_h):
@@ -413,7 +416,6 @@
     )
     ends = [lax.ppermute(e, "height", pairs) for e, pairs in zip(ends, h_rounds)]
 
-    taps = spatial_taps.reshape(9, chans)
     inner, totals = call(
         functools.partial(inner_kernel, frames, rows, cols),
         "inner",

time: 17 us -> 16.4 us (0.965)
  local copies, waits for them, and re-layouts: 0.83 us -> 0 us
  Pallas kernels: 4.17 us -> 4.4 us
  starting transfers between devices: 8.57 us -> 8.39 us
    ppermute x1, waiting for transfers between devices: 0.52 us -> 1.37 us  [body(): lax.ppermute(e, 'height', pairs)]
    unnamed x10 -> x0, local copies, waits for them, and re-layouts: 0.81 us -> none
    ppermute x2, waiting for transfers between devices: 1.52 us -> 0.87 us  [body(): columns.append(lax.ppermute(column, ('tm', 'height', 'width'), route))]
    ppermute x1, waiting for transfers between devices: 0.34 us -> 0.98 us  [body(): firsts.append(lax.ppermute(sent[2 * d - 2], 'tm', route))]
    ppermute x1, waiting for transfers between devices: 0.67 us -> 0.04 us  [body(): other = lax.ppermute(other, 'tm', [(i, i ^ 1) for i in range(n_t)])]
    pallas_call x9, Pallas kernels: 4.17 us -> 4.4 us  [call(): pl.pallas_call(kernel, out_shape=tuple(outs), in_specs=[HBM] * far + [VME...]
    ppermute x2, starting transfers between devices: 4.4 us -> 4.22 us  [body(): columns.append(lax.ppermute(column, ('tm', 'height', 'width'), route))]
  transfers between devices with their start and end apart: 7 -> 7, of which waited for: 4 -> 3; matrix products, arithmetic and copies ran while one was open for 0% -> 0% of each run, Pallas kernels for 18% -> 20%
where the time goes in v16:
time: 16.4 us; the launch traced here: 16.1 us
  starting transfers between devices  8.39 us (51%)
  Pallas kernels  4.4 us (27%)
  waiting for transfers between devices  3.27 us (20%)
    pallas_call x9, Pallas kernels, call(): pl.pallas_call(kernel, out_shape=tuple(outs), in_specs=[HBM] * far + [VME...  4.4 us
    ppermute x2, starting transfers between devices, body(): columns.append(lax.ppermute(column, ('tm', 'height', 'width'), route))  4.22 us
    ppermute x1, starting transfers between devices, body(): lax.ppermute(e, 'height', pairs)  1.56 us
    ppermute x1, starting transfers between devices, body(): rests.append(lax.ppermute(sent[2 * d - 1], 'tm', route))  1.41 us
    ppermute x1, waiting for transfers between devices, body(): lax.ppermute(e, 'height', pairs)  1.37 us
    ppermute x1, waiting for transfers between devices, body(): firsts.append(lax.ppermute(sent[2 * d - 2], 'tm', route))  0.98 us
    ppermute x2, waiting for transfers between devices, body(): columns.append(lax.ppermute(column, ('tm', 'height', 'width'), route))  0.87 us
    ppermute x1, starting transfers between devices, body(): firsts.append(lax.ppermute(sent[2 * d - 2], 'tm', route))  0.69 us
  transfers between devices with their start and end apart: 7, of which 3 were waited for; matrix products, arithmetic and copies ran while one was open for 0% of the time, Pallas kernels for 20%

profile of v16, /device:TPU:0, one launch (start us, length us, event | category | flops | bytes accessed | tf_op | source)
XLA Modules:
  0.0 16.1 jit_solution(13310550583732389232)
XLA Ops:
  0.0 0.5 %collective-permute-start = (bf16[256,512]{1,0:T(8,128)(2,1)}, bf16[256,512]{1,0:T(8,128)(2,1)S(1)}, u32[]{:S(2)}, u32[]{:S(2)}) collective-permute-start(bf16[256,512]{1,0:T(8,128)(2,1)} %bitcast.3), channel_id=1, source_target_pairs={{0,8},{8,0},{16,24},{24,16},{1,9},{9,1},{17,25},{25,17},{2,10},{10... | collective-permute-start | bytes 786440 | tf_op jit(solution)/shard_map/ppermute | solution.py:339
  0.5 1.5 %early.1 = (bf16[256,512]{1,0:T(8,128)(2,1)S(1)}, bf16[512,512]{1,0:T(8,128)(2,1)S(1)}, f32[3,3,512]{2,1,0:T(4,128)S(1)}, bf16[512,512]{1,0:T(8,128)(2,1)S(1)}, ...) custom-call(bf16[16,512]{1,0:T(8,128)(2,1)} %refs_0_.1, ...), custom_call_target="tpu_custom_call" | custom-call | bytes 5232640 | tf_op jit(solution)/shard_map/early/pallas_call | solution.py:20
  2.0 0.0 collective-permute-done.partner_ref
  2.0 0.1 column.1
  2.1 2.8 %collective-permute-start.1 = (bf16[64,512]{1,0:T(8,128)(2,1)S(1)}, bf16[64,512]{1,0:T(8,128)(2,1)S(1)}, u32[]{:S(2)}, u32[]{:S(2)}) collective-permute-start(bf16[64,512]{1,0:T(8,128)(2,1)S(1)} %column.1), channel_id=1, source_target_pairs={{0,1},{1,0},{2,3},{3,2},{4,5},{5,4},{6,7},{7,6},{8,12},{9,10},{10,... | collective-permute-start | bytes 196616 | tf_op jit(solution)/shard_map/ppermute | solution.py:394
  4.9 1.4 %collective-permute-start.2 = (bf16[64,512]{1,0:T(8,128)(2,1)S(1)}, bf16[64,512]{1,0:T(8,128)(2,1)S(1)}, u32[]{:S(2)}, u32[]{:S(2)}) collective-permute-start(bf16[64,512]{1,0:T(8,128)(2,1)S(1)} %column.1), channel_id=1, source_target_pairs={{0,17},{1,16},{2,19},{3,18},{4,21},{5,20},{6,23},{7,22},{8,28},{9,... | collective-permute-start | bytes 196616 | tf_op jit(solution)/shard_map/ppermute | solution.py:394
  6.3 0.2 %later.1 = (bf16[32,512]{1,0:T(8,128)(2,1)S(1)}, bf16[224,512]{1,0:T(8,128)(2,1)S(1)}) custom-call(bf16[256,512]{1,0:T(8,128)(2,1)S(1)} %collective-permute-done.partner_ref, f32[24,8,512]{2,1,0:T(8,128)S(1)} %get-tuple-element.23.table_ref, f32[256,512]{1,0:T(8,128)S(1)} %get-tuple-element.28.refs_0_), custom_call_target="tpu_custom_call" | custom-call | flops 1048576 | bytes 1441792 | tf_op jit(solution)/shard_map/later/pallas_call | solution.py:20
  6.5 0.7 %collective-permute-start.4 = (bf16[32,512]{1,0:T(8,128)(2,1)S(1)}, bf16[32,512]{1,0:T(8,128)(2,1)S(1)}, u32[]{:S(2)}, u32[]{:S(2)}) collective-permute-start(bf16[32,512]{1,0:T(8,128)(2,1)S(1)} %get-tuple-element.29), channel_id=1, source_target_pairs={{0,16},{8,24},{16,0},{24,8},{1,17},{9,25},{17,1},{25,9},{2,18},{10... | collective-permute-start | bytes 98312 | tf_op jit(solution)/shard_map/ppermute | solution.py:397
  7.2 1.4 %collective-permute-start.5 = (bf16[224,512]{1,0:T(8,128)(2,1)S(1)}, bf16[224,512]{1,0:T(8,128)(2,1)S(1)}, u32[]{:S(2)}, u32[]{:S(2)}) collective-permute-start(bf16[224,512]{1,0:T(8,128)(2,1)S(1)} %get-tuple-element.39), channel_id=1, source_target_pairs={{0,16},{8,24},{16,0},{24,8},{1,17},{9,25},{17,1},{25,9},{2,18},{10... | collective-permute-start | bytes 688136 | tf_op jit(solution)/shard_map/ppermute | solution.py:398
  8.6 0.0 collective-permute-done.1.refs_0_
  8.6 0.9 %collective-permute-done.2.refs_1_ = bf16[64,512]{1,0:T(8,128)(2,1)S(1)} collective-permute-done((bf16[64,512]{1,0:T(8,128)(2,1)S(1)}, bf16[64,512]{1,0:T(8,128)(2,1)S(1)}, u32[]{:S(2)}, u32[]{:S(2)}) %collective-permute-start.2) | collective-permute-done | bytes 65568 | tf_op jit(solution)/shard_map/ppermute | solution.py:394
  9.5 0.2 side.1
  9.6 0.1 collective-permute-start.3
  9.7 0.2 %own.1.mine_ref = f32[256,512]{1,0:T(8,128)S(1)} custom-call(bf16[256,512]{1,0:T(8,128)(2,1)S(1)} %collective-permute-done.partner_ref, f32[24,8,512]{2,1,0:T(8,128)S(1)} %get-tuple-element.23.table_ref, f32[256,512]{1,0:T(8,128)S(1)} %get-tuple-element.24.field_ref), custom_call_target="tpu_custom_call" | custom-call | flops 1048576 | bytes 1703936 | tf_op jit(solution)/shard_map/own/pallas_call | solution.py:20
  9.9 1.0 %collective-permute-done.4.refs_0_ = bf16[32,512]{1,0:T(8,128)(2,1)S(1)} collective-permute-done((bf16[32,512]{1,0:T(8,128)(2,1)S(1)}, bf16[32,512]{1,0:T(8,128)(2,1)S(1)}, u32[]{:S(2)}, u32[]{:S(2)}) %collective-permute-start.4) | collective-permute-done | bytes 32800 | tf_op jit(solution)/shard_map/ppermute | solution.py:397
  10.9 0.0 collective-permute-done.3.other_ref
  10.9 1.6 %collective-permute-start.6 = (bf16[40,512]{1,0:T(8,128)(2,1)S(1)}, bf16[40,512]{1,0:T(8,128)(2,1)S(1)}, u32[]{:S(2)}, u32[]{:S(2)}) collective-permute-start(bf16[40,512]{1,0:T(8,128)(2,1)S(1)} %get-tuple-element.40), channel_id=1, source_target_pairs={{0,4},{4,0},{1,5},{5,1},{2,6},{6,2},{3,7},{7,3},{8,12},{12,8},{9,1... | collective-permute-start | bytes 122888 | tf_op jit(solution)/shard_map/ppermute | solution.py:417
  12.5 0.4 %gate.1.gate_ref = f32[256,512]{1,0:T(8,128)S(1)} custom-call(bf16[256,512]{1,0:T(8,128)(2,1)S(1)} %get-tuple-element.33.x_ref, bf16[512,512]{1,0:T(8,128)(2,1)S(1)} %get-tuple-element.34.w_ref), custom_call_target="tpu_custom_call" | custom-call | bytes 1310720 | tf_op jit(solution)/shard_map/gate/pallas_call | solution.py:20
  12.9 0.7 %inner.1 = (bf16[256,512]{1,0:T(8,128)(2,1)S(1)}, f32[256,512]{1,0:T(8,128)S(1)}) custom-call(f32[256,512]{1,0:T(8,128)S(1)} %own.1.mine_ref, f32[32,512]{1,0:T(8,128)S(1)} %get-tuple-element.30.low_ref, f32[32,512]{1,0:T(8,128)S(1)} %get-tuple-element.31.high_ref, f32[3,3,512]{2,1,0:T(4,128)S(1)} %get-tuple-element.32.taps_ref, ...), custom_call_target="tpu_custom_call" | custom-call | flops 268435456 | bytes 3033088 | tf_op jit(solution)/shard_map/inner/pallas_call | solution.py:20
  13.6 1.4 %collective-permute-done.6.refs_2_ = bf16[40,512]{1,0:T(8,128)(2,1)S(1)} collective-permute-done((bf16[40,512]{1,0:T(8,128)(2,1)S(1)}, bf16[40,512]{1,0:T(8,128)(2,1)S(1)}, u32[]{:S(2)}, u32[]{:S(2)}) %collective-permute-start.6) | collective-permute-done | bytes 40992 | tf_op jit(solution)/shard_map/ppermute | solution.py:417
  15.0 0.0 collective-permute-done.5.refs_1_
  15.0 1.1 %last.1 = bf16[256,512]{1,0:T(8,128)(2,1)} custom-call(bf16[256,512]{1,0:T(8,128)(2,1)S(1)} %get-tuple-element.37.inner_ref, f32[256,512]{1,0:T(8,128)S(1)} %get-tuple-element.38.totals_ref, f32[3,3,512]{2,1,0:T(4,128)S(1)} %get-tuple-element.32.taps_ref, f32[256,512]{1,0:T(8,128)S(1)} %gate.1.gate_ref, bf16[512,512]{1,0:T(8,128)(2,1)S(1)} %get-tuple-element.35.wv_ref, ...), custom_call_target="tpu_custom_call" | custom-call | flops 268435456 | bytes 2942976 | tf_op jit(solution)/shard_map/last/pallas_call | solution.py:20
  (1 shorter events, 0.0 us)
Async XLA Ops:
  0.0 2.0 %collective-permute-start = (bf16[256,512]{1,0:T(8,128)(2,1)}, bf16[256,512]{1,0:T(8,128)(2,1)S(1)}, u32[]{:S(2)}, u32[]{:S(2)}) collective-permute-start(bf16[256,512]{1,0:T(8,128)(2,1)} %bitcast.3), channel_id=1, source_target_pairs={{0,8},{8,0},{16,24},{24,16},{1,9},{9,1},{17,25},{25,17},{2,10},{10... | collective-permute-start | bytes 786440 | tf_op jit(solution)/shard_map/ppermute | solution.py:339
  2.1 6.5 %collective-permute-start.1 = (bf16[64,512]{1,0:T(8,128)(2,1)S(1)}, bf16[64,512]{1,0:T(8,128)(2,1)S(1)}, u32[]{:S(2)}, u32[]{:S(2)}) collective-permute-start(bf16[64,512]{1,0:T(8,128)(2,1)S(1)} %column.1), channel_id=1, source_target_pairs={{0,1},{1,0},{2,3},{3,2},{4,5},{5,4},{6,7},{7,6},{8,12},{9,10},{10,... | collective-permute-start | bytes 196616 | tf_op jit(solution)/shard_map/ppermute | solution.py:394
  4.9 4.6 %collective-permute-start.2 = (bf16[64,512]{1,0:T(8,128)(2,1)S(1)}, bf16[64,512]{1,0:T(8,128)(2,1)S(1)}, u32[]{:S(2)}, u32[]{:S(2)}) collective-permute-start(bf16[64,512]{1,0:T(8,128)(2,1)S(1)} %column.1), channel_id=1, source_target_pairs={{0,17},{1,16},{2,19},{3,18},{4,21},{5,20},{6,23},{7,22},{8,28},{9,... | collective-permute-start | bytes 196616 | tf_op jit(solution)/shard_map/ppermute | solution.py:394
  6.5 4.4 %collective-permute-start.4 = (bf16[32,512]{1,0:T(8,128)(2,1)S(1)}, bf16[32,512]{1,0:T(8,128)(2,1)S(1)}, u32[]{:S(2)}, u32[]{:S(2)}) collective-permute-start(bf16[32,512]{1,0:T(8,128)(2,1)S(1)} %get-tuple-element.29), channel_id=1, source_target_pairs={{0,16},{8,24},{16,0},{24,8},{1,17},{9,25},{17,1},{25,9},{2,18},{10... | collective-permute-start | bytes 98312 | tf_op jit(solution)/shard_map/ppermute | solution.py:397
  7.2 7.8 %collective-permute-start.5 = (bf16[224,512]{1,0:T(8,128)(2,1)S(1)}, bf16[224,512]{1,0:T(8,128)(2,1)S(1)}, u32[]{:S(2)}, u32[]{:S(2)}) collective-permute-start(bf16[224,512]{1,0:T(8,128)(2,1)S(1)} %get-tuple-element.39), channel_id=1, source_target_pairs={{0,16},{8,24},{16,0},{24,8},{1,17},{9,25},{17,1},{25,9},{2,18},{10... | collective-permute-start | bytes 688136 | tf_op jit(solution)/shard_map/ppermute | solution.py:398
  9.6 1.3 %collective-permute-start.3 = (bf16[32,512]{1,0:T(8,128)(2,1)S(1)}, bf16[32,512]{1,0:T(8,128)(2,1)S(1)}, u32[]{:S(2)}, u32[]{:S(2)}) collective-permute-start(bf16[32,512]{1,0:T(8,128)(2,1)S(1)} %get-tuple-element.27), channel_id=1, source_target_pairs={{0,8},{8,0},{16,24},{24,16},{1,9},{9,1},{17,25},{25,17},{2,10},{10... | collective-permute-start | bytes 98312 | tf_op jit(solution)/shard_map/ppermute | solution.py:408
  10.9 4.1 %collective-permute-start.6 = (bf16[40,512]{1,0:T(8,128)(2,1)S(1)}, bf16[40,512]{1,0:T(8,128)(2,1)S(1)}, u32[]{:S(2)}, u32[]{:S(2)}) collective-permute-start(bf16[40,512]{1,0:T(8,128)(2,1)S(1)} %get-tuple-element.40), channel_id=1, source_target_pairs={{0,4},{4,0},{1,5},{5,1},{2,6},{6,2},{3,7},{7,3},{8,12},{12,8},{9,1... | collective-permute-start | bytes 122888 | tf_op jit(solution)/shard_map/ppermute | solution.py:417

commit v17 on v15

--- a/solution.py
+++ b/solution.py
@@ -8,21 +8,24 @@
 from jax.sharding import PartitionSpec as P
 
 LANES = 128
+SIDE = 4 * 10**9
+PAD = 16
 F32, BF16 = jnp.float32, jnp.bfloat16
 VMEM = pl.BlockSpec(memory_space=pltpu.VMEM)
 HBM = pl.BlockSpec(memory_space=pltpu.HBM)
 
 
-def call(kernel, name, outs, scratch, operands, far=0):
+def call(kernel, name, outs, scratch, operands, far=0, far_outs=0, aliases={}, flops=0):
     operands = [pltpu.with_memory_space_constraint(a, pltpu.HBM) for a in operands[:far]] + list(operands[far:])
     return pl.pallas_call(
         kernel,
         out_shape=tuple(outs),
         in_specs=[HBM] * far + [VMEM] * (len(operands) - far),
-        out_specs=(VMEM,) * len(outs),
+        out_specs=(HBM,) * far_outs + (VMEM,) * (len(outs) - far_outs),
         scratch_shapes=scratch,
+        input_output_aliases=aliases,
         compiler_params=pltpu.CompilerParams(vmem_limit_bytes=24 * 1024 * 1024),
-        cost_estimate=pl.CostEstimate(flops=0, bytes_accessed=0, transcendentals=0),
+        cost_estimate=pl.CostEstimate(flops=flops, bytes_accessed=0, transcendentals=0),
         name=name,
     )(*operands)
 
@@ -101,17 +104,12 @@
         copy.wait()
 
 
-def column_kernel(frames, rows, cols, partner_ref, side_ref, out_ref, *refs):
-    *corners, held = refs
-    odd = position("height")[0]
+def column_kernel(frames, rows, cols, partner_ref, side_ref, out_ref, held):
     for lane in range(0, out_ref.shape[1], LANES):
         span = slice(lane, lane + LANES)
         held[...] = partner_ref[:, span].astype(F32)
         column = jnp.concatenate([side_ref[:, span], outer_column(held, frames * rows, cols)])
         out_ref[:, span] = column.astype(BF16)
-        ends = [jnp.concatenate([column[s + r : s + r + 1] for s in range(0, column.shape[0], rows)]) for r in (0, rows - 1)]
-        for k, corner in enumerate(corners):
-            corner[:, span] = jnp.where(odd, *(ends[::-1] if k else ends)).astype(BF16)
 
 
 def shift(frames):
@@ -177,41 +175,44 @@
     return [jnp.where(exists, total, jnp.zeros_like(total)) for total in totals]
 
 
-def side_kernel(frames, rows, table_ref, arrived_ref, own_ref, other_ref, *corners):
+def side_kernel(frames, rows, rounds_h, table_ref, arrived_ref, *refs):
+    n = (len(refs) - 2) // 2
+    lines, (own_ref, other_ref, *outs) = refs[:n], refs[n:]
     odd = position("height")[0]
+    other_ref[frames * rows :] = jnp.zeros((PAD, other_ref.shape[1]), BF16)
     for lane in range(0, own_ref.shape[1], LANES):
         span = slice(lane, lane + LANES)
-        totals = beside(mixed_columns(frames, rows, 0, arrived_ref[:, span].astype(F32), table_ref, span))
+        column = arrived_ref[:, span].astype(F32)
+        totals = beside(mixed_columns(frames, rows, 0, column, table_ref, span))
         own_ref[:, span] = jnp.concatenate(totals[:frames])
-        other_ref[:, span] = jnp.concatenate(totals[frames:]).astype(BF16)
-        ends = [jnp.concatenate([total[r : r + 1] for total in totals]) for r in (0, rows - 1)]
-        for k, corner in enumerate(corners):
-            corner[:, span] = jnp.where(odd, *(ends[::-1] if k else ends)).astype(BF16)
-
-
-def before_kernel(frames, rows, rounds_h, table_ref, *refs):
+        other_ref[: frames * rows, span] = jnp.concatenate(totals[frames:]).astype(BF16)
+        if n:
+            ends = [jnp.concatenate([column[s + r : s + r + 1] for s in range(0, column.shape[0], rows)]) for r in (0, rows - 1)]
+        for i, (line, out) in enumerate(zip(lines, outs)):
+            d, k = i // rounds_h + 1, i % rounds_h
+            pixels = jnp.where(odd, *(ends[::-1] if k else ends))
+            corners = beside(mixed_columns(frames, 1, d, pixels, table_ref, span))
+            out[:, span] = jnp.concatenate([line[:, span].astype(F32)] + corners).astype(BF16)
+
+
+def before_kernel(frames, rows, cols, rounds_h, after_ref, table_ref, *refs):
     *arrived, own_ref, other_ref, line_ref = refs
     per = 1 + rounds_h
-    chips = len(arrived) // (per + rounds_h)
-    arrived, lines = arrived[: chips * per], arrived[chips * per :]
-    size = line_ref.shape[0] // rounds_h
-    for k in range(rounds_h):
-        line = 0.0
-        for d in range(1, chips + 1):
-            line = line + later(d, lines[(d - 1) * rounds_h + k][...].astype(F32))
-        line_ref[k * size : (k + 1) * size] = line
+    size = frames * cols
     for lane in range(0, own_ref.shape[1], LANES):
         span = slice(lane, lane + LANES)
-        parts = [0.0] * per
-        for d in range(1, chips + 1):
-            for i, ref in enumerate(arrived[(d - 1) * per : d * per]):
-                pixels = rows if i == 0 else 1
-                column = later(d, ref[:, span].astype(F32))
-                totals = beside(mixed_columns(frames, pixels, d, column, table_ref, span))
-                sums = jnp.concatenate(totals[:frames]), jnp.concatenate(totals[frames:])
-                parts[i] = sums if d == 1 else tuple(a + b for a, b in zip(parts[i], sums))
-        own_ref[:, span] = jnp.concatenate([a for a, _ in parts])
-        other_ref[:, span] = jnp.concatenate([b for _, b in parts]).astype(BF16)
+        own = other = lines = 0.0
+        for d in range(1, len(arrived) // per + 1):
+            column, *ends = arrived[(d - 1) * per : d * per]
+            column = later(d, column[:, span].astype(F32))
+            totals = beside(mixed_columns(frames, rows, d, column, table_ref, span))
+            ends = [later(d, end[:, span].astype(F32)) for end in ends]
+            own = own + jnp.concatenate(totals[:frames] + [end[size : size + frames] for end in ends])
+            other = other + jnp.concatenate(totals[frames:] + [end[size + frames :] for end in ends])
+            lines = lines + jnp.concatenate([end[:size] for end in ends])
+        own_ref[:, span] = own
+        other_ref[: other.shape[0], span] = other.astype(BF16)
+        line_ref[:, span] = lines
 
 
 def both_sides(own, other):
@@ -219,17 +220,17 @@
     return jnp.where(right, other, own), jnp.where(right, own, other)
 
 
-def border_kernel(frames, rows, cols, mine_ref, *refs):
-    n = len(refs) // 3
+def border_kernel(frames, rows, cols, mine_ref, own_ref, other_ref, *outs):
     sites = rows * cols
     odd, _, _ = position("height")
+    sides = both_sides(own_ref[...], other_ref[: own_ref.shape[0]].astype(F32))
     ends = []
     for r in (0, rows - 1):
         line = [mine_ref[t * sites + r * cols : t * sites + (r + 1) * cols] for t in range(frames)]
-        ends.append(jnp.concatenate(line))
-    for k, (own, other, out) in enumerate(zip(refs[:n], refs[n : 2 * n], refs[2 * n :])):
-        corners = both_sides(own[...].astype(F32)[:frames], other[...].astype(F32)[frames:])
-        out[...] = jnp.concatenate([jnp.where(odd, *(ends[::-1] if k else ends)), *corners]).astype(BF16)
+        corners = [side[t * rows + r : t * rows + r + 1] for side in sides for t in range(frames)]
+        ends.append(jnp.concatenate(line + corners))
+    for k, out in enumerate(outs):
+        out[...] = jnp.where(odd, *(ends[::-1] if k else ends)).astype(BF16)
 
 
 def shifted(line, left, right):
@@ -269,7 +270,7 @@
     for lane in range(0, mine_ref.shape[1], LANES):
         span = slice(lane, lane + LANES)
         taps = taps_of(taps_ref, span)
-        low, high = both_sides(own_ref[:, span], other_ref[:, span].astype(F32))
+        low, high = both_sides(own_ref[:, span], other_ref[: own_ref.shape[0], span].astype(F32))
         for t in range(frames):
             at = t * sites
             lines = [mine_ref[at + r * cols : at + (r + 1) * cols, span] for r in range(rows)]
@@ -281,27 +282,19 @@
     out_ref[...] = projected(mixed[...], gate_ref[...], wv_ref, wo_ref)
 
 
-def last_kernel(frames, rows, cols, chips, inner_ref, totals_ref, taps_ref, gate_ref, wv_ref, wo_ref, *refs):
-    *parts, out_ref, mixed = refs
-    chans = out_ref.shape[1]
-    sites = rows * cols
+def from_ends(frames, cols, ends, taps_ref, sides):
     size = frames * cols
     odd, lower, upper = position("height")
-    earlier = lax.div(lax.axis_index("tm"), 2) > 0
-    rounds_h = len(parts) - (chips + 2 if chips > 1 else 0)
-    ends, wholes, sides = parts[:rounds_h], parts[rounds_h : rounds_h + chips - 1], parts[rounds_h + chips - 1 :]
-    none = jnp.zeros((cols, chans), F32)
+    none = jnp.zeros((cols, taps_ref.shape[2]), F32)
     above, below = [none] * frames, [none] * frames
-    low = high = None
-    if sides:
-        low, high = both_sides(sides[0][...], sides[1][...].astype(F32))
     for k, end in enumerate(ends):
         end = end[...].astype(F32)
         first = jnp.logical_not(odd) if k else odd
         line, lefts, rights = end[:size], end[size : size + frames], end[size + frames : size + 2 * frames]
         if sides:
-            line = line + sides[2][k * size : (k + 1) * size]
-            at = frames * rows + k * frames
+            low, high, lines = sides
+            at = low.shape[0] - (len(ends) - k) * frames
+            line = line + lines[k * size : (k + 1) * size]
             lefts, rights = lefts + low[at : at + frames], rights + high[at : at + frames]
         exists = jnp.where(first, lower, upper)
         tap = jnp.where(first, taps_ref[0], taps_ref[2])
@@ -311,10 +304,24 @@
             more = jnp.where(exists, more, none)
             above[t] = above[t] + jnp.where(first, more, none)
             below[t] = below[t] + jnp.where(first, none, more)
-
-    @pl.when(jnp.logical_not(earlier))
+    return above, below
+
+
+def has_earlier():
+    return lax.div(lax.axis_index("tm"), 2) > 0
+
+
+def edge_kernel(frames, rows, cols, inner_ref, totals_ref, taps_ref, gate_ref, wv_ref, wo_ref, *refs):
+    *ends, out_ref, held, done = refs
+    rounds_h = len(ends)
+    sites = rows * cols
+    size = frames * cols
+    odd = position("height")[0]
+
+    @pl.when(jnp.logical_not(has_earlier()))
     def _():
-        out_ref[...] = inner_ref[...]
+        above, below = from_ends(frames, cols, ends, taps_ref, None)
+        held[...] = inner_ref[...]
         rows_at = [t * sites for t in range(frames)], [(t + 1) * sites - cols for t in range(frames)]
         added = above, below
         if rounds_h > 1:
@@ -333,17 +340,28 @@
             i, j = rows_at[0][t], rows_at[1][t]
             line = new[t * cols : (t + 1) * cols]
             if rounds_h > 1:
-                out_ref[i : i + cols] = line
-                out_ref[j : j + cols] = new[size + t * cols : size + (t + 1) * cols]
+                held[i : i + cols] = line
+                held[j : j + cols] = new[size + t * cols : size + (t + 1) * cols]
             else:
-                out_ref[i : i + cols] = jnp.where(odd, line, inner_ref[i : i + cols])
-                out_ref[j : j + cols] = jnp.where(odd, inner_ref[j : j + cols], line)
-
-    if chips == 1:
-        return
-
-    @pl.when(earlier)
+                held[i : i + cols] = jnp.where(odd, line, inner_ref[i : i + cols])
+                held[j : j + cols] = jnp.where(odd, inner_ref[j : j + cols], line)
+        copy = pltpu.make_async_copy(held, out_ref, done)
+        copy.start()
+        copy.wait()
+
+
+def last_kernel(
+    frames, rows, cols, rounds_h, before_ref, totals_ref, taps_ref, gate_ref, wv_ref, wo_ref, *refs
+):
+    *parts, out_ref, mixed, held, done = refs
+    ends, wholes, (own_ref, other_ref, line_ref) = parts[:rounds_h], parts[rounds_h:-3], parts[-3:]
+    chans = held.shape[1]
+    sites = rows * cols
+
+    @pl.when(has_earlier())
     def _():
+        low, high = both_sides(own_ref[...], other_ref[: own_ref.shape[0]].astype(F32))
+        above, below = from_ends(frames, cols, ends, taps_ref, (low, high, line_ref[...]))
         for lane in range(0, chans, LANES):
             span = slice(lane, lane + LANES)
             taps = taps_of(taps_ref, span)
@@ -360,7 +378,10 @@
                 total[rows - 1] = total[rows - 1] + below[t][:, span]
                 total = jnp.concatenate(total) + totals_ref[at : at + sites, span]
                 mixed[at : at + sites, span] = total.astype(BF16)
-        out_ref[...] = projected(mixed[...], gate_ref[...], wv_ref, wo_ref)
+        held[...] = projected(mixed[...], gate_ref[...], wv_ref, wo_ref)
+        copy = pltpu.make_async_copy(held, out_ref, done)
+        copy.start()
+        copy.wait()
 
 
 def body(latents, spatial_taps, kernel_taps, skip_gain, gate_weight, value_weight, out_weight):
@@ -391,10 +412,10 @@
 
     h_rounds = swaps("height")
     rounds = len(h_rounds)
-    column, *corners = call(
+    (column,) = call(
         functools.partial(column_kernel, frames, rows, cols),
         "column",
-        [shape((2 * lines, chans), BF16)] + [shape((2 * frames, chans), BF16)] * rounds,
+        [shape((2 * lines, chans), BF16)],
         [pltpu.VMEM((block, LANES), F32)],
         [partner, side],
     )
@@ -426,41 +447,30 @@
                     route.append(((i * n_h + h) * n_w + j, ((i + 2 * d) % n_t * n_h + at) * n_w + to))
         return lax.ppermute(data, ("tm", "height", "width"), route)
 
-    wholes, before, rows_before = [], [], []
+    wholes, before, edges = [], [], []
     for d in range(1, chips):
-        whole, *edges = sent[(d - 1) * (1 + rounds) : d * (1 + rounds)]
+        whole, *lines_later = sent[(d - 1) * (1 + rounds) : d * (1 + rounds)]
         wholes.append(move(whole, d, False))
-        before.append(move(column, d, True))
-        rows_before += [move(edge, d, False, pairs) for edge, pairs in zip(edges, h_rounds)]
-        before += [move(corner, d, True, pairs) for corner, pairs in zip(corners, h_rounds)]
+        before.append([move(column, d, True)])
+        edges += lines_later
     swap = [(i, i ^ 1) for i in range(n_t)]
-    own, other, *own_corners = call(
-        functools.partial(side_kernel, frames, rows),
+    with_corners = shape((frames * cols + 2 * frames, chans), BF16)
+    own, other, *edges = call(
+        functools.partial(side_kernel, frames, rows, rounds),
         "side",
-        [shape((lines, chans), F32), shape((lines, chans), BF16)] + [shape((2 * frames, chans), BF16)] * rounds,
+        [shape((lines, chans), F32), shape((lines + PAD, chans), BF16)] + [with_corners] * len(edges),
         [],
-        [table, move(column, 0, True)],
-    )
-    other_corners = [lax.ppermute(corner, "tm", swap) for corner in own_corners]
+        [table, move(column, 0, True)] + edges,
+        flops=SIDE,
+    )
     other = lax.ppermute(other, "tm", swap)
-    sides = []
-    if chips > 1:
-        many = lines + rounds * frames
-        mine_before, other_before, line = call(
-            functools.partial(before_kernel, frames, rows, rounds),
-            "before",
-            [shape((many, chans), F32), shape((many, chans), BF16), shape((rounds * frames * cols, chans), F32)],
-            [],
-            [table] + before + rows_before,
-        )
-        sides = [mine_before, lax.ppermute(other_before, "tm", swap), line]
     size = frames * cols + 2 * frames
     ends = call(
         functools.partial(border_kernel, frames, rows, cols),
         "border",
         [shape((size, chans), BF16)] * rounds,
         [],
-        [mine] + own_corners + other_corners,
+        [mine, own, other],
     )
     ends = [lax.ppermute(e, "height", pairs) for e, pairs in zip(ends, h_rounds)]
 
@@ -471,13 +481,38 @@
         [pltpu.VMEM((block, chans), BF16)],
         [mine, own, other, taps, gate, value_weight, out_weight],
     )
+    sides = []
+    if chips > 1:
+        for i, edge in enumerate(edges):
+            before[i // rounds].append(move(edge, i // rounds + 1, False, h_rounds[i % rounds]))
+        many = lines + rounds * frames
+        mine_before, other_before, line = call(
+            functools.partial(before_kernel, frames, rows, cols, rounds),
+            "before",
+            [shape((many, chans), F32), shape((many, chans), BF16), shape((rounds * frames * cols, chans), F32)],
+            [],
+            [totals, table] + sum(before, []),
+        )
+        sides = [mine_before, lax.ppermute(other_before, "tm", swap), line]
     (out,) = call(
-        functools.partial(last_kernel, frames, rows, cols, chips),
-        "last",
+        functools.partial(edge_kernel, frames, rows, cols),
+        "edge",
         [shape((block, chans), BF16)],
-        [pltpu.VMEM((block, chans), BF16)],
-        [inner, totals, taps, gate, value_weight, out_weight] + ends + wholes + sides,
-    )
+        [pltpu.VMEM((block, chans), BF16), pltpu.SemaphoreType.DMA],
+        [inner, totals, taps, gate, value_weight, out_weight] + ends,
+        far_outs=1,
+    )
+    if chips > 1:
+        (out,) = call(
+            functools.partial(last_kernel, frames, rows, cols, rounds),
+            "last",
+            [shape((block, chans), BF16)],
+            [pltpu.VMEM((block, chans), BF16), pltpu.VMEM((block, chans), BF16), pltpu.SemaphoreType.DMA],
+            [out, totals, taps, gate, value_weight, out_weight] + ends + wholes + sides,
+            far=1,
+            far_outs=1,
+            aliases={0: 0},
+        )
     return out.reshape(latents.shape)
 
 

time: 17.9 us -> 17.3 us (0.966)
  starting transfers between devices: 11.3 us -> 9.01 us
  waiting for transfers between devices: 1.69 us -> 3.43 us
    ppermute x5 -> x4, waiting for transfers between devices: 1.21 us -> 3.32 us  [move(): return lax.ppermute(data, ('tm', 'height', 'width'), route)]
    ppermute x5 -> x4, starting transfers between devices: 9.58 us -> 7.81 us  [move(): return lax.ppermute(data, ('tm', 'height', 'width'), route)]
    ppermute x1, waiting for transfers between devices: 0.47 us -> 0.01 us  [body(): other = lax.ppermute(other, 'tm', swap)]
    ppermute x1, starting transfers between devices: 0.5 us -> 0.07 us  [body(): other = lax.ppermute(other, 'tm', swap)]
    pallas_call x10 -> x11, Pallas kernels: 4.57 us -> 4.51 us  [call(): pl.pallas_call(kernel, out_shape=tuple(outs), in_specs=[HBM] * far + [VME...]
  transfers between devices with their start and end apart: 10 -> 8, of which waited for: 2 -> 2; matrix products, arithmetic and copies ran while one was open for 0% -> 0% of each run, Pallas kernels for 18% -> 26%
where the time goes in v17:
time: 17.3 us; the launch traced here: 17.1 us
  starting transfers between devices  9.01 us (52%)
  Pallas kernels  4.51 us (26%)
  waiting for transfers between devices  3.43 us (20%)
    ppermute x4, starting transfers between devices, move(): return lax.ppermute(data, ('tm', 'height', 'width'), route)  7.81 us
    pallas_call x11, Pallas kernels, call(): pl.pallas_call(kernel, out_shape=tuple(outs), in_specs=[HBM] * far + [VME...  4.51 us
    ppermute x4, waiting for transfers between devices, move(): return lax.ppermute(data, ('tm', 'height', 'width'), route)  3.32 us
    ppermute x1, starting transfers between devices, body(): lax.ppermute(e, 'height', pairs)  0.6 us
    ppermute x1, starting transfers between devices, body(): partner = lax.ppermute(x, 'tm', [(i, i ^ 1) for i in range(n_t)])  0.45 us
  transfers between devices with their start and end apart: 8, of which 2 were waited for; matrix products, arithmetic and copies ran while one was open for 0% of the time, Pallas kernels for 26%

profile of v17, /device:TPU:0, one launch (start us, length us, event | category | flops | bytes accessed | tf_op | source)
XLA Modules:
  0.0 17.1 jit_solution(7340647379391072773)
XLA Ops:
  0.0 0.5 %collective-permute-start = (bf16[256,512]{1,0:T(8,128)(2,1)}, bf16[256,512]{1,0:T(8,128)(2,1)S(1)}, u32[]{:S(2)}, u32[]{:S(2)}) collective-permute-start(bf16[256,512]{1,0:T(8,128)(2,1)} %bitcast.3), channel_id=1, source_target_pairs={{0,8},{8,0},{16,24},{24,16},{1,9},{9,1},{17,25},{25,17},{2,10},{10... | collective-permute-start | bytes 786440 | tf_op jit(solution)/shard_map/ppermute | solution.py:396
  0.5 1.5 %early.1 = (bf16[256,512]{1,0:T(8,128)(2,1)S(1)}, bf16[512,512]{1,0:T(8,128)(2,1)S(1)}, f32[3,3,512]{2,1,0:T(4,128)S(1)}, bf16[512,512]{1,0:T(8,128)(2,1)S(1)}, ...) custom-call(bf16[16,512]{1,0:T(8,128)(2,1)} %refs_0_.1, ...), custom_call_target="tpu_custom_call" | custom-call | tf_op jit(solution)/shard_map/early/pallas_call | solution.py:20
  2.0 0.0 collective-permute-done.partner_ref
  2.0 0.1 column.1
  2.1 2.8 %collective-permute-start.1 = (bf16[64,512]{1,0:T(8,128)(2,1)S(1)}, bf16[64,512]{1,0:T(8,128)(2,1)S(1)}, u32[]{:S(2)}, u32[]{:S(2)}) collective-permute-start(bf16[64,512]{1,0:T(8,128)(2,1)S(1)} %column.1), channel_id=1, source_target_pairs={{0,1},{1,0},{2,3},{3,2},{4,5},{5,4},{6,7},{7,6},{8,12},{9,10},{10,... | collective-permute-start | bytes 196616 | tf_op jit(solution)/shard_map/ppermute | solution.py:448
  4.9 1.4 %collective-permute-start.5 = (bf16[64,512]{1,0:T(8,128)(2,1)S(1)}, bf16[64,512]{1,0:T(8,128)(2,1)S(1)}, u32[]{:S(2)}, u32[]{:S(2)}) collective-permute-start(bf16[64,512]{1,0:T(8,128)(2,1)S(1)} %column.1), channel_id=1, source_target_pairs={{0,17},{1,16},{2,19},{3,18},{4,21},{5,20},{6,23},{7,22},{8,24},{9,... | collective-permute-start | bytes 196616 | tf_op jit(solution)/shard_map/ppermute | solution.py:448
  6.3 0.2 %later.1 = (bf16[256,512]{1,0:T(8,128)(2,1)S(1)}, bf16[32,512]{1,0:T(8,128)(2,1)S(1)}) custom-call(bf16[256,512]{1,0:T(8,128)(2,1)S(1)} %collective-permute-done.partner_ref, f32[24,8,512]{2,1,0:T(8,128)S(1)} %get-tuple-element.24.table_ref, f32[256,512]{1,0:T(8,128)S(1)} %get-tuple-element.27.refs_0_), custom_call_target="tpu_custom_call" | custom-call | tf_op jit(solution)/shard_map/later/pallas_call | solution.py:20
  6.5 0.7 %collective-permute-start.4 = (bf16[256,512]{1,0:T(8,128)(2,1)S(1)}, bf16[256,512]{1,0:T(8,128)(2,1)S(1)}, u32[]{:S(2)}, u32[]{:S(2)}) collective-permute-start(bf16[256,512]{1,0:T(8,128)(2,1)S(1)} %get-tuple-element.38), channel_id=1, source_target_pairs={{0,16},{1,17},{2,18},{3,19},{4,20},{5,21},{6,22},{7,23},{8,24},{9,... | collective-permute-start | bytes 786440 | tf_op jit(solution)/shard_map/ppermute | solution.py:448
  7.2 0.0 collective-permute-done.1.arrived_ref
  7.2 0.2 side.1
  7.3 0.1 collective-permute-start.2
  7.4 2.9 %collective-permute-start.6 = (bf16[40,512]{1,0:T(8,128)(2,1)S(1)}, bf16[40,512]{1,0:T(8,128)(2,1)S(1)}, u32[]{:S(2)}, u32[]{:S(2)}) collective-permute-start(bf16[40,512]{1,0:T(8,128)(2,1)S(1)} %get-tuple-element.39), channel_id=1, source_target_pairs={{0,20},{1,21},{2,22},{3,23},{4,16},{5,17},{6,18},{7,19},{8,28},{9,... | collective-permute-start | bytes 122888 | tf_op jit(solution)/shard_map/ppermute | solution.py:448
  10.3 0.2 own.1.mine_ref
  10.5 0.0 collective-permute-done.2.other_ref
  10.6 0.6 %collective-permute-start.3 = (bf16[40,512]{1,0:T(8,128)(2,1)S(1)}, bf16[40,512]{1,0:T(8,128)(2,1)S(1)}, u32[]{:S(2)}, u32[]{:S(2)}) collective-permute-start(bf16[40,512]{1,0:T(8,128)(2,1)S(1)} %border.1), channel_id=1, source_target_pairs={{0,4},{4,0},{1,5},{5,1},{2,6},{6,2},{3,7},{7,3},{8,12},{12,8},{9,1... | collective-permute-start | bytes 122888 | tf_op jit(solution)/shard_map/ppermute | solution.py:475
  11.2 0.4 %gate.1.gate_ref = f32[256,512]{1,0:T(8,128)S(1)} custom-call(bf16[256,512]{1,0:T(8,128)(2,1)S(1)} %get-tuple-element.32.x_ref, bf16[512,512]{1,0:T(8,128)(2,1)S(1)} %get-tuple-element.33.w_ref), custom_call_target="tpu_custom_call" | custom-call | tf_op jit(solution)/shard_map/gate/pallas_call | solution.py:20
  11.5 0.8 %inner.1 = (bf16[256,512]{1,0:T(8,128)(2,1)S(1)}, f32[256,512]{1,0:T(8,128)S(1)}) custom-call(f32[256,512]{1,0:T(8,128)S(1)} %own.1.mine_ref, f32[32,512]{1,0:T(8,128)S(1)} %get-tuple-element.29.own_ref, bf16[48,512]{1,0:T(8,128)(2,1)S(1)} %collective-permute-done.2.other_ref, f32[3,3,512]{2,1,0:T(4,128)S(1)} %get-tuple-element.31.taps_ref, ...), custom_call_target="tpu_custom_call" | custom-call | tf_op jit(solution)/shard_map/inner/pallas_call | solution.py:20
  12.3 0.0 collective-permute-done.5.refs_0_
  12.3 3.3 %collective-permute-done.6.refs_1_ = bf16[40,512]{1,0:T(8,128)(2,1)S(1)} collective-permute-done((bf16[40,512]{1,0:T(8,128)(2,1)S(1)}, bf16[40,512]{1,0:T(8,128)(2,1)S(1)}, u32[]{:S(2)}, u32[]{:S(2)}) %collective-permute-start.6) | collective-permute-done | bytes 40992 | tf_op jit(solution)/shard_map/ppermute | solution.py:448
  15.7 0.1 before.1
  15.8 0.1 collective-permute-start.7
  15.8 0.0 collective-permute-done.3.refs_0_
  15.9 1.1 %edge.1.before_ref = bf16[256,512]{1,0:T(8,128)(2,1)} custom-call(bf16[256,512]{1,0:T(8,128)(2,1)S(1)} %get-tuple-element.36.inner_ref, f32[256,512]{1,0:T(8,128)S(1)} %get-tuple-element.37.totals_ref.after_ref, f32[3,3,512]{2,1,0:T(4,128)S(1)} %get-tuple-element.31.taps_ref, f32[256,512]{1,0:T(8,128)S(1)} %gate.1.gate_ref, ...), custom_call_target="tpu_custom_call" | custom-call | tf_op jit(solution)/shard_map/edge/pallas_call | solution.py:20
  16.9 0.1 collective-permute-done.7.refs_3_
  17.1 0.0 collective-permute-done.4.refs_1_
  (2 shorter events, 0.1 us)
Async XLA Ops:
  0.0 2.0 %collective-permute-start = (bf16[256,512]{1,0:T(8,128)(2,1)}, bf16[256,512]{1,0:T(8,128)(2,1)S(1)}, u32[]{:S(2)}, u32[]{:S(2)}) collective-permute-start(bf16[256,512]{1,0:T(8,128)(2,1)} %bitcast.3), channel_id=1, source_target_pairs={{0,8},{8,0},{16,24},{24,16},{1,9},{9,1},{17,25},{25,17},{2,10},{10... | collective-permute-start | bytes 786440 | tf_op jit(solution)/shard_map/ppermute | solution.py:396
  2.1 5.1 %collective-permute-start.1 = (bf16[64,512]{1,0:T(8,128)(2,1)S(1)}, bf16[64,512]{1,0:T(8,128)(2,1)S(1)}, u32[]{:S(2)}, u32[]{:S(2)}) collective-permute-start(bf16[64,512]{1,0:T(8,128)(2,1)S(1)} %column.1), channel_id=1, source_target_pairs={{0,1},{1,0},{2,3},{3,2},{4,5},{5,4},{6,7},{7,6},{8,12},{9,10},{10,... | collective-permute-start | bytes 196616 | tf_op jit(solution)/shard_map/ppermute | solution.py:448
  4.9 7.4 %collective-permute-start.5 = (bf16[64,512]{1,0:T(8,128)(2,1)S(1)}, bf16[64,512]{1,0:T(8,128)(2,1)S(1)}, u32[]{:S(2)}, u32[]{:S(2)}) collective-permute-start(bf16[64,512]{1,0:T(8,128)(2,1)S(1)} %column.1), channel_id=1, source_target_pairs={{0,17},{1,16},{2,19},{3,18},{4,21},{5,20},{6,23},{7,22},{8,24},{9,... | collective-permute-start | bytes 196616 | tf_op jit(solution)/shard_map/ppermute | solution.py:448
  6.5 10.6 %collective-permute-start.4 = (bf16[256,512]{1,0:T(8,128)(2,1)S(1)}, bf16[256,512]{1,0:T(8,128)(2,1)S(1)}, u32[]{:S(2)}, u32[]{:S(2)}) collective-permute-start(bf16[256,512]{1,0:T(8,128)(2,1)S(1)} %get-tuple-element.38), channel_id=1, source_target_pairs={{0,16},{1,17},{2,18},{3,19},{4,20},{5,21},{6,22},{7,23},{8,24},{9,... | collective-permute-start | bytes 786440 | tf_op jit(solution)/shard_map/ppermute | solution.py:448
  7.3 3.2 %collective-permute-start.2 = (bf16[48,512]{1,0:T(8,128)(2,1)S(1)}, bf16[48,512]{1,0:T(8,128)(2,1)S(1)}, u32[]{:S(2)}, u32[]{:S(2)}) collective-permute-start(bf16[48,512]{1,0:T(8,128)(2,1)S(1)} %get-tuple-element.30), channel_id=1, source_target_pairs={{0,8},{8,0},{16,24},{24,16},{1,9},{9,1},{17,25},{25,17},{2,10},{10... | collective-permute-start | bytes 147464 | tf_op jit(solution)/shard_map/ppermute | solution.py:466
  7.4 8.2 %collective-permute-start.6 = (bf16[40,512]{1,0:T(8,128)(2,1)S(1)}, bf16[40,512]{1,0:T(8,128)(2,1)S(1)}, u32[]{:S(2)}, u32[]{:S(2)}) collective-permute-start(bf16[40,512]{1,0:T(8,128)(2,1)S(1)} %get-tuple-element.39), channel_id=1, source_target_pairs={{0,20},{1,21},{2,22},{3,23},{4,16},{5,17},{6,18},{7,19},{8,28},{9,... | collective-permute-start | bytes 122888 | tf_op jit(solution)/shard_map/ppermute | solution.py:448
  10.6 5.3 %collective-permute-start.3 = (bf16[40,512]{1,0:T(8,128)(2,1)S(1)}, bf16[40,512]{1,0:T(8,128)(2,1)S(1)}, u32[]{:S(2)}, u32[]{:S(2)}) collective-permute-start(bf16[40,512]{1,0:T(8,128)(2,1)S(1)} %border.1), channel_id=1, source_target_pairs={{0,4},{4,0},{1,5},{5,1},{2,6},{6,2},{3,7},{7,3},{8,12},{12,8},{9,1... | collective-permute-start | bytes 122888 | tf_op jit(solution)/shard_map/ppermute | solution.py:475
  15.8 1.3 %collective-permute-start.7 = (bf16[36,512]{1,0:T(8,128)(2,1)S(1)}, bf16[36,512]{1,0:T(8,128)(2,1)S(1)}, u32[]{:S(2)}, u32[]{:S(2)}) collective-permute-start(bf16[36,512]{1,0:T(8,128)(2,1)S(1)} %get-tuple-element.41), channel_id=1, source_target_pairs={{0,8},{8,0},{16,24},{24,16},{1,9},{9,1},{17,25},{25,17},{2,10},{10... | collective-permute-start | bytes 110600 | tf_op jit(solution)/shard_map/ppermute | solution.py:496

commit v18 on v16

--- a/solution.py
+++ b/solution.py
@@ -14,7 +14,7 @@
 HBM = pl.BlockSpec(memory_space=pltpu.HBM)
 
 
-def call(kernel, name, outs, scratch, operands, flops=0, exps=0, far=0):
+def call(kernel, name, outs, scratch, operands, flops=0, exps=0, far=0, aliases={}):
     operands = [pltpu.with_memory_space_constraint(a, pltpu.HBM) for a in operands[:far]] + list(operands[far:])
     moved = sum(a.size * a.dtype.itemsize for a in operands) + sum(a.size * a.dtype.itemsize for a in outs)
     return pl.pallas_call(
@@ -23,6 +23,7 @@
         in_specs=[HBM] * far + [VMEM] * (len(operands) - far),
         out_specs=(VMEM,) * len(outs),
         scratch_shapes=scratch,
+        input_output_aliases=aliases,
         compiler_params=pltpu.CompilerParams(vmem_limit_bytes=24 * 1024 * 1024),
         cost_estimate=pl.CostEstimate(flops=flops, bytes_accessed=moved, transcendentals=exps),
         name=name,
@@ -254,60 +255,15 @@
     out_ref[...] = projected(mixed[...], gate_ref[...], wv_ref, wo_ref)
 
 
-def last_kernel(frames, rows, cols, chips, inner_ref, totals_ref, taps_ref, gate_ref, wv_ref, wo_ref, *refs):
-    *parts, out_ref, mixed = refs
-    firsts, rests, ends = parts[: chips - 1], parts[chips - 1 : 2 * chips - 2], parts[2 * chips - 2 :]
-    rounds_h = len(ends)
-    chans = out_ref.shape[1]
+def block_kernel(frames, rows, cols, rounds_h, inner_ref, totals_ref, taps_ref, gate_ref, wv_ref, wo_ref, *refs):
+    *parts, out_ref, sums_ref, mixed = refs
+    firsts, rests = parts[: len(parts) // 2], parts[len(parts) // 2 :]
     sites = rows * cols
     size = frames * cols
-    odd, lower, upper = position("height")
-    earlier = lax.div(lax.axis_index("tm"), 2) > 0
-    none = jnp.zeros((cols, chans), F32)
-    above, below = [none] * frames, [none] * frames
-    for k, end in enumerate(ends):
-        end = end[...].astype(F32)
-        first = jnp.logical_not(odd) if k else odd
-        lefts, rights = end[size : size + frames], end[size + frames : size + 2 * frames]
-        exists = jnp.where(first, lower, upper)
-        tap = jnp.where(first, taps_ref[0], taps_ref[2])
-        for t in range(frames):
-            near = shifted(end[t * cols : (t + 1) * cols], lefts[t : t + 1], rights[t : t + 1])
-            more = near[0] * tap[0:1] + near[1] * tap[1:2] + near[2] * tap[2:3]
-            more = jnp.where(exists, more, none)
-            above[t] = above[t] + jnp.where(first, more, none)
-            below[t] = below[t] + jnp.where(first, none, more)
-
-    @pl.when(jnp.logical_not(earlier))
+
+    @pl.when(lax.div(lax.axis_index("tm"), 2) > 0)
     def _():
-        out_ref[...] = inner_ref[...]
-        rows_at = [t * sites for t in range(frames)], [(t + 1) * sites - cols for t in range(frames)]
-        added = above, below
-        if rounds_h > 1:
-            change, gate = [], []
-            for at, more in zip(rows_at, added):
-                change += [totals_ref[i : i + cols] + m for i, m in zip(at, more)]
-                gate += [gate_ref[i : i + cols] for i in at]
-        else:
-            change = [
-                jnp.where(odd, totals_ref[i : i + cols] + m, totals_ref[j : j + cols] + n)
-                for i, j, m, n in zip(*rows_at, *added)
-            ]
-            gate = [jnp.where(odd, gate_ref[i : i + cols], gate_ref[j : j + cols]) for i, j in zip(*rows_at)]
-        new = projected(jnp.concatenate(change).astype(BF16), jnp.concatenate(gate), wv_ref, wo_ref)
-        for t in range(frames):
-            i, j = rows_at[0][t], rows_at[1][t]
-            line = new[t * cols : (t + 1) * cols]
-            if rounds_h > 1:
-                out_ref[i : i + cols] = line
-                out_ref[j : j + cols] = new[size + t * cols : size + (t + 1) * cols]
-            else:
-                out_ref[i : i + cols] = jnp.where(odd, line, inner_ref[i : i + cols])
-                out_ref[j : j + cols] = jnp.where(odd, inner_ref[j : j + cols], line)
-
-    @pl.when(earlier)
-    def _():
-        for lane in range(0, chans, LANES):
+        for lane in range(0, out_ref.shape[1], LANES):
             span = slice(lane, lane + LANES)
             taps = taps_of(taps_ref, span)
             lines = [jnp.zeros((size, LANES), F32)] * rows
@@ -320,11 +276,38 @@
             for t in range(frames):
                 at = t * sites
                 total = filtered([line[t * cols : (t + 1) * cols] for line in lines], zero, zero, taps)
-                total[0] = total[0] + above[t][:, span]
-                total[rows - 1] = total[rows - 1] + below[t][:, span]
                 total = jnp.concatenate(total) + totals_ref[at : at + sites, span]
+                sums_ref[at : at + sites, span] = total
                 mixed[at : at + sites, span] = total.astype(BF16)
         out_ref[...] = projected(mixed[...], gate_ref[...], wv_ref, wo_ref)
+
+
+def last_kernel(frames, rows, cols, inner_ref, totals_ref, taps_ref, gate_ref, wv_ref, wo_ref, *refs):
+    *ends, out_ref = refs
+    sites = rows * cols
+    size = frames * cols
+    odd, lower, upper = position("height")
+    out_ref[...] = inner_ref[...]
+    mixed, gate = [], []
+    for k, end in enumerate(ends):
+        end = end[...].astype(F32)
+        first = jnp.logical_not(odd) if k else odd
+        lefts, rights = end[size : size + frames], end[size + frames : size + 2 * frames]
+        exists = jnp.where(first, lower, upper)
+        tap = jnp.where(first, taps_ref[0], taps_ref[2])
+        for t in range(frames):
+            near = shifted(end[t * cols : (t + 1) * cols], lefts[t : t + 1], rights[t : t + 1])
+            more = near[0] * tap[0:1] + near[1] * tap[1:2] + near[2] * tap[2:3]
+            i, j = t * sites, (t + 1) * sites - cols
+            total = jnp.where(first, totals_ref[i : i + cols], totals_ref[j : j + cols])
+            mixed.append(total + jnp.where(exists, more, jnp.zeros_like(more)))
+            gate.append(jnp.where(first, gate_ref[i : i + cols], gate_ref[j : j + cols]))
+    out = projected(jnp.concatenate(mixed).astype(BF16), jnp.concatenate(gate), wv_ref, wo_ref)
+    for t in range(frames):
+        new = [out[k * size + t * cols : k * size + (t + 1) * cols] for k in range(len(ends))]
+        for at, is_last in ((t * sites, False), ((t + 1) * sites - cols, True)):
+            kept = new[1] if len(new) > 1 else inner_ref[at : at + cols]
+            out_ref[at : at + cols] = jnp.where(odd, kept, new[0]) if is_last else jnp.where(odd, new[0], kept)
 
 
 def body(latents, spatial_taps, kernel_taps, skip_gain, gate_weight, value_weight, out_weight):
@@ -424,13 +407,21 @@
         [mine, low, high, taps, gate, value_weight, out_weight],
         4 * block * chans * chans,
     )
+    if chips > 1:
+        inner, totals = call(
+            functools.partial(block_kernel, frames, rows, cols, len(h_rounds)),
+            "block",
+            [shape((block, chans), BF16), field],
+            [pltpu.VMEM((block, chans), BF16)],
+            [inner, totals, taps, gate, value_weight, out_weight] + firsts + rests,
+            aliases={0: 0, 1: 1},
+        )
     (out,) = call(
-        functools.partial(last_kernel, frames, rows, cols, chips),
+        functools.partial(last_kernel, frames, rows, cols),
         "last",
         [shape((block, chans), BF16)],
-        [pltpu.VMEM((block, chans), BF16)],
-        [inner, totals, taps, gate, value_weight, out_weight] + firsts + rests + ends,
-        4 * block * chans * chans,
+        [],
+        [inner, totals, taps, gate, value_weight, out_weight] + ends,
     )
     return out.reshape(latents.shape)
 

time: 16.4 us -> 16.3 us (level)
    ppermute x1, waiting for transfers between devices: 1.37 us -> 0.24 us  [body(): lax.ppermute(e, 'height', pairs)]
    ppermute x1, waiting for transfers between devices: 0.01 us -> 1.14 us  [body(): rests.append(lax.ppermute(sent[2 * d - 1], 'tm', route))]
    pallas_call x9 -> x10, Pallas kernels: 4.4 us -> 4.35 us  [call(): pl.pallas_call(kernel, out_shape=tuple(outs), in_specs=[HBM] * far + [VME...]
  transfers between devices with their start and end apart: 7 -> 7, of which waited for: 3 -> 4; matrix products, arithmetic and copies ran while one was open for 0% -> 0% of each run, Pallas kernels for 20% -> 20%
where the time goes in v18:
time: 16.3 us; the launch traced here: 16.1 us
  starting transfers between devices  8.39 us (51%)
  Pallas kernels  4.35 us (27%)
  waiting for transfers between devices  3.27 us (20%)
    pallas_call x10, Pallas kernels, call(): pl.pallas_call(kernel, out_shape=tuple(outs), in_specs=[HBM] * far + [VME...  4.35 us
    ppermute x2, starting transfers between devices, body(): columns.append(lax.ppermute(column, ('tm', 'height', 'width'), route))  4.22 us
    ppermute x1, starting transfers between devices, body(): lax.ppermute(e, 'height', pairs)  1.56 us
    ppermute x1, starting transfers between devices, body(): rests.append(lax.ppermute(sent[2 * d - 1], 'tm', route))  1.41 us
    ppermute x1, waiting for transfers between devices, body(): rests.append(lax.ppermute(sent[2 * d - 1], 'tm', route))  1.14 us
    ppermute x1, waiting for transfers between devices, body(): firsts.append(lax.ppermute(sent[2 * d - 2], 'tm', route))  0.98 us
    ppermute x2, waiting for transfers between devices, body(): columns.append(lax.ppermute(column, ('tm', 'height', 'width'), route))  0.87 us
    ppermute x1, starting transfers between devices, body(): firsts.append(lax.ppermute(sent[2 * d - 2], 'tm', route))  0.69 us
  transfers between devices with their start and end apart: 7, of which 4 were waited for; matrix products, arithmetic and copies ran while one was open for 0% of the time, Pallas kernels for 20%

profile of v18, /device:TPU:0, one launch (start us, length us, event | category | flops | bytes accessed | tf_op | source)
XLA Modules:
  0.0 16.1 jit_solution(5445702498554856296)
XLA Ops:
  0.0 0.5 %collective-permute-start = (bf16[256,512]{1,0:T(8,128)(2,1)}, bf16[256,512]{1,0:T(8,128)(2,1)S(1)}, u32[]{:S(2)}, u32[]{:S(2)}) collective-permute-start(bf16[256,512]{1,0:T(8,128)(2,1)} %bitcast.3), channel_id=1, source_target_pairs={{0,8},{8,0},{16,24},{24,16},{1,9},{9,1},{17,25},{25,17},{2,10},{10... | collective-permute-start | bytes 786440 | tf_op jit(solution)/shard_map/ppermute | solution.py:322
  0.5 1.5 %early.1 = (bf16[256,512]{1,0:T(8,128)(2,1)S(1)}, bf16[512,512]{1,0:T(8,128)(2,1)S(1)}, f32[3,3,512]{2,1,0:T(4,128)S(1)}, bf16[512,512]{1,0:T(8,128)(2,1)S(1)}, ...) custom-call(bf16[16,512]{1,0:T(8,128)(2,1)} %refs_0_.1, ...), custom_call_target="tpu_custom_call" | custom-call | bytes 5232640 | tf_op jit(solution)/shard_map/early/pallas_call | solution.py:20
  2.0 0.0 collective-permute-done.partner_ref
  2.0 0.1 column.1
  2.1 2.8 %collective-permute-start.1 = (bf16[64,512]{1,0:T(8,128)(2,1)S(1)}, bf16[64,512]{1,0:T(8,128)(2,1)S(1)}, u32[]{:S(2)}, u32[]{:S(2)}) collective-permute-start(bf16[64,512]{1,0:T(8,128)(2,1)S(1)} %column.1), channel_id=1, source_target_pairs={{0,1},{1,0},{2,3},{3,2},{4,5},{5,4},{6,7},{7,6},{8,12},{9,10},{10,... | collective-permute-start | bytes 196616 | tf_op jit(solution)/shard_map/ppermute | solution.py:377
  4.9 1.4 %collective-permute-start.2 = (bf16[64,512]{1,0:T(8,128)(2,1)S(1)}, bf16[64,512]{1,0:T(8,128)(2,1)S(1)}, u32[]{:S(2)}, u32[]{:S(2)}) collective-permute-start(bf16[64,512]{1,0:T(8,128)(2,1)S(1)} %column.1), channel_id=1, source_target_pairs={{0,17},{1,16},{2,19},{3,18},{4,21},{5,20},{6,23},{7,22},{8,28},{9,... | collective-permute-start | bytes 196616 | tf_op jit(solution)/shard_map/ppermute | solution.py:377
  6.3 0.2 %later.1 = (bf16[32,512]{1,0:T(8,128)(2,1)S(1)}, bf16[224,512]{1,0:T(8,128)(2,1)S(1)}) custom-call(bf16[256,512]{1,0:T(8,128)(2,1)S(1)} %collective-permute-done.partner_ref, f32[24,8,512]{2,1,0:T(8,128)S(1)} %get-tuple-element.25.table_ref, f32[256,512]{1,0:T(8,128)S(1)} %get-tuple-element.30.refs_0_), custom_call_target="tpu_custom_call" | custom-call | flops 1048576 | bytes 1441792 | tf_op jit(solution)/shard_map/later/pallas_call | solution.py:20
  6.5 0.7 %collective-permute-start.4 = (bf16[32,512]{1,0:T(8,128)(2,1)S(1)}, bf16[32,512]{1,0:T(8,128)(2,1)S(1)}, u32[]{:S(2)}, u32[]{:S(2)}) collective-permute-start(bf16[32,512]{1,0:T(8,128)(2,1)S(1)} %get-tuple-element.31), channel_id=1, source_target_pairs={{0,16},{8,24},{16,0},{24,8},{1,17},{9,25},{17,1},{25,9},{2,18},{10... | collective-permute-start | bytes 98312 | tf_op jit(solution)/shard_map/ppermute | solution.py:380
  7.2 1.4 %collective-permute-start.5 = (bf16[224,512]{1,0:T(8,128)(2,1)S(1)}, bf16[224,512]{1,0:T(8,128)(2,1)S(1)}, u32[]{:S(2)}, u32[]{:S(2)}) collective-permute-start(bf16[224,512]{1,0:T(8,128)(2,1)S(1)} %get-tuple-element.41), channel_id=1, source_target_pairs={{0,16},{8,24},{16,0},{24,8},{1,17},{9,25},{17,1},{25,9},{2,18},{10... | collective-permute-start | bytes 688136 | tf_op jit(solution)/shard_map/ppermute | solution.py:381
  8.6 0.0 collective-permute-done.1.refs_0_
  8.6 0.9 %collective-permute-done.2.refs_1_ = bf16[64,512]{1,0:T(8,128)(2,1)S(1)} collective-permute-done((bf16[64,512]{1,0:T(8,128)(2,1)S(1)}, bf16[64,512]{1,0:T(8,128)(2,1)S(1)}, u32[]{:S(2)}, u32[]{:S(2)}) %collective-permute-start.2) | collective-permute-done | bytes 65568 | tf_op jit(solution)/shard_map/ppermute | solution.py:377
  9.5 0.2 %side.1 = (f32[32,512]{1,0:T(8,128)S(1)}, bf16[32,512]{1,0:T(8,128)(2,1)S(1)}) custom-call(f32[24,8,512]{2,1,0:T(8,128)S(1)} %get-tuple-element.25.table_ref, bf16[64,512]{1,0:T(8,128)(2,1)S(1)} %collective-permute-done.1.refs_0_, bf16[64,512]{1,0:T(8,128)(2,1)S(1)} %collective-permute-done.2.refs_1_), custom_call_target="tpu_custom_call" | custom-call | flops 8000000000 | bytes 622592 | tf_op jit(solution)/shard_map/side/pallas_call | solution.py:20
  9.6 0.1 collective-permute-start.3
  9.7 0.2 %own.1.mine_ref = f32[256,512]{1,0:T(8,128)S(1)} custom-call(bf16[256,512]{1,0:T(8,128)(2,1)S(1)} %collective-permute-done.partner_ref, f32[24,8,512]{2,1,0:T(8,128)S(1)} %get-tuple-element.25.table_ref, f32[256,512]{1,0:T(8,128)S(1)} %get-tuple-element.26.field_ref), custom_call_target="tpu_custom_call" | custom-call | flops 1048576 | bytes 1703936 | tf_op jit(solution)/shard_map/own/pallas_call | solution.py:20
  9.9 1.0 %collective-permute-done.4.refs_0_ = bf16[32,512]{1,0:T(8,128)(2,1)S(1)} collective-permute-done((bf16[32,512]{1,0:T(8,128)(2,1)S(1)}, bf16[32,512]{1,0:T(8,128)(2,1)S(1)}, u32[]{:S(2)}, u32[]{:S(2)}) %collective-permute-start.4) | collective-permute-done | bytes 32800 | tf_op jit(solution)/shard_map/ppermute | solution.py:380
  10.9 0.0 collective-permute-done.3.other_ref
  10.9 1.6 %collective-permute-start.6 = (bf16[40,512]{1,0:T(8,128)(2,1)S(1)}, bf16[40,512]{1,0:T(8,128)(2,1)S(1)}, u32[]{:S(2)}, u32[]{:S(2)}) collective-permute-start(bf16[40,512]{1,0:T(8,128)(2,1)S(1)} %get-tuple-element.44), channel_id=1, source_target_pairs={{0,4},{4,0},{1,5},{5,1},{2,6},{6,2},{3,7},{7,3},{8,12},{12,8},{9,1... | collective-permute-start | bytes 122888 | tf_op jit(solution)/shard_map/ppermute | solution.py:400
  12.5 0.4 %gate.1.gate_ref = f32[256,512]{1,0:T(8,128)S(1)} custom-call(bf16[256,512]{1,0:T(8,128)(2,1)S(1)} %get-tuple-element.35.x_ref, bf16[512,512]{1,0:T(8,128)(2,1)S(1)} %get-tuple-element.36.w_ref), custom_call_target="tpu_custom_call" | custom-call | bytes 1310720 | tf_op jit(solution)/shard_map/gate/pallas_call | solution.py:20
  12.9 0.7 %inner.1 = (bf16[256,512]{1,0:T(8,128)(2,1)S(1)}, f32[256,512]{1,0:T(8,128)S(1)}) custom-call(f32[256,512]{1,0:T(8,128)S(1)} %own.1.mine_ref, f32[32,512]{1,0:T(8,128)S(1)} %get-tuple-element.32.low_ref, f32[32,512]{1,0:T(8,128)S(1)} %get-tuple-element.33.high_ref, f32[3,3,512]{2,1,0:T(4,128)S(1)} %get-tuple-element.34.taps_ref, ...), custom_call_target="tpu_custom_call" | custom-call | flops 268435456 | bytes 3033088 | tf_op jit(solution)/shard_map/inner/pallas_call | solution.py:20
  13.6 1.1 %collective-permute-done.5.refs_1_ = bf16[224,512]{1,0:T(8,128)(2,1)S(1)} collective-permute-done((bf16[224,512]{1,0:T(8,128)(2,1)S(1)}, bf16[224,512]{1,0:T(8,128)(2,1)S(1)}, u32[]{:S(2)}, u32[]{:S(2)}) %collective-permute-start.5) | collective-permute-done | bytes 229408 | tf_op jit(solution)/shard_map/ppermute | solution.py:381
  14.8 0.2 %collective-permute-done.6.refs_0_ = bf16[40,512]{1,0:T(8,128)(2,1)S(1)} collective-permute-done((bf16[40,512]{1,0:T(8,128)(2,1)S(1)}, bf16[40,512]{1,0:T(8,128)(2,1)S(1)}, u32[]{:S(2)}, u32[]{:S(2)}) %collective-permute-start.6) | collective-permute-done | bytes 40992 | tf_op jit(solution)/shard_map/ppermute | solution.py:400
  15.0 1.1 %last.1 = bf16[256,512]{1,0:T(8,128)(2,1)} custom-call(bf16[256,512]{1,0:T(8,128)(2,1)S(1)} %get-tuple-element.42.inner_ref, f32[256,512]{1,0:T(8,128)S(1)} %get-tuple-element.43.totals_ref, f32[3,3,512]{2,1,0:T(4,128)S(1)} %get-tuple-element.34.taps_ref, f32[256,512]{1,0:T(8,128)S(1)} %gate.1.gate_ref, bf16[512,512]{1,0:T(8,128)(2,1)S(1)} %get-tuple-element.37.wv_ref, ...), custom_call_target="tpu_custom_call" | custom-call | bytes 2680832 | tf_op jit(solution)/shard_map/last/pallas_call | solution.py:20
  (2 shorter events, 0.0 us)
Async XLA Ops:
  0.0 2.0 %collective-permute-start = (bf16[256,512]{1,0:T(8,128)(2,1)}, bf16[256,512]{1,0:T(8,128)(2,1)S(1)}, u32[]{:S(2)}, u32[]{:S(2)}) collective-permute-start(bf16[256,512]{1,0:T(8,128)(2,1)} %bitcast.3), channel_id=1, source_target_pairs={{0,8},{8,0},{16,24},{24,16},{1,9},{9,1},{17,25},{25,17},{2,10},{10... | collective-permute-start | bytes 786440 | tf_op jit(solution)/shard_map/ppermute | solution.py:322
  2.1 6.5 %collective-permute-start.1 = (bf16[64,512]{1,0:T(8,128)(2,1)S(1)}, bf16[64,512]{1,0:T(8,128)(2,1)S(1)}, u32[]{:S(2)}, u32[]{:S(2)}) collective-permute-start(bf16[64,512]{1,0:T(8,128)(2,1)S(1)} %column.1), channel_id=1, source_target_pairs={{0,1},{1,0},{2,3},{3,2},{4,5},{5,4},{6,7},{7,6},{8,12},{9,10},{10,... | collective-permute-start | bytes 196616 | tf_op jit(solution)/shard_map/ppermute | solution.py:377
  4.9 4.6 %collective-permute-start.2 = (bf16[64,512]{1,0:T(8,128)(2,1)S(1)}, bf16[64,512]{1,0:T(8,128)(2,1)S(1)}, u32[]{:S(2)}, u32[]{:S(2)}) collective-permute-start(bf16[64,512]{1,0:T(8,128)(2,1)S(1)} %column.1), channel_id=1, source_target_pairs={{0,17},{1,16},{2,19},{3,18},{4,21},{5,20},{6,23},{7,22},{8,28},{9,... | collective-permute-start | bytes 196616 | tf_op jit(solution)/shard_map/ppermute | solution.py:377
  6.5 4.4 %collective-permute-start.4 = (bf16[32,512]{1,0:T(8,128)(2,1)S(1)}, bf16[32,512]{1,0:T(8,128)(2,1)S(1)}, u32[]{:S(2)}, u32[]{:S(2)}) collective-permute-start(bf16[32,512]{1,0:T(8,128)(2,1)S(1)} %get-tuple-element.31), channel_id=1, source_target_pairs={{0,16},{8,24},{16,0},{24,8},{1,17},{9,25},{17,1},{25,9},{2,18},{10... | collective-permute-start | bytes 98312 | tf_op jit(solution)/shard_map/ppermute | solution.py:380
  7.2 7.6 %collective-permute-start.5 = (bf16[224,512]{1,0:T(8,128)(2,1)S(1)}, bf16[224,512]{1,0:T(8,128)(2,1)S(1)}, u32[]{:S(2)}, u32[]{:S(2)}) collective-permute-start(bf16[224,512]{1,0:T(8,128)(2,1)S(1)} %get-tuple-element.41), channel_id=1, source_target_pairs={{0,16},{8,24},{16,0},{24,8},{1,17},{9,25},{17,1},{25,9},{2,18},{10... | collective-permute-start | bytes 688136 | tf_op jit(solution)/shard_map/ppermute | solution.py:381
  9.6 1.3 %collective-permute-start.3 = (bf16[32,512]{1,0:T(8,128)(2,1)S(1)}, bf16[32,512]{1,0:T(8,128)(2,1)S(1)}, u32[]{:S(2)}, u32[]{:S(2)}) collective-permute-start(bf16[32,512]{1,0:T(8,128)(2,1)S(1)} %get-tuple-element.29), channel_id=1, source_target_pairs={{0,8},{8,0},{16,24},{24,16},{1,9},{9,1},{17,25},{25,17},{2,10},{10... | collective-permute-start | bytes 98312 | tf_op jit(solution)/shard_map/ppermute | solution.py:391
  10.9 4.1 %collective-permute-start.6 = (bf16[40,512]{1,0:T(8,128)(2,1)S(1)}, bf16[40,512]{1,0:T(8,128)(2,1)S(1)}, u32[]{:S(2)}, u32[]{:S(2)}) collective-permute-start(bf16[40,512]{1,0:T(8,128)(2,1)S(1)} %get-tuple-element.44), channel_id=1, source_target_pairs={{0,4},{4,0},{1,5},{5,1},{2,6},{6,2},{3,7},{7,3},{8,12},{12,8},{9,1... | collective-permute-start | bytes 122888 | tf_op jit(solution)/shard_map/ppermute | solution.py:400

commit v19 on v18

--- a/solution.py
+++ b/solution.py
@@ -156,25 +156,37 @@
     return jnp.where(lax.div(lax.axis_index("tm"), 2) >= d, value, jnp.zeros_like(value))
 
 
-def side_kernel(frames, rows, table_ref, *refs):
+def add_column(frames, rows, d, totals, column, table_ref, span):
+    base = 2 * frames + 2 * d * frames
+    for t in range(2 * frames):
+        for s in range(2 * frames):
+            lag = t % frames - s % frames
+            if t // frames == s // frames:
+                if d == 0 and lag < 0:
+                    continue
+            else:
+                lag = lag + (shift(frames) if t < frames else -shift(frames))
+            totals[t] = totals[t] + table_ref[base + lag, :, span] * column[s * rows : (s + 1) * rows]
+    return totals
+
+
+def width_kernel(frames, rows, table_ref, arrived_ref, sums_ref):
+    for lane in range(0, sums_ref.shape[1], LANES):
+        span = slice(lane, lane + LANES)
+        totals = [jnp.zeros((rows, LANES), F32)] * (2 * frames)
+        totals = add_column(frames, rows, 0, totals, arrived_ref[:, span].astype(F32), table_ref, span)
+        sums_ref[:, span] = jnp.concatenate(totals)
+
+
+def side_kernel(frames, rows, table_ref, sums_ref, *refs):
     *arrived, own_ref, other_ref = refs
     _, lower, upper = position("width")
     exists = jnp.where(on_right(), upper, lower)
     for lane in range(0, own_ref.shape[1], LANES):
         span = slice(lane, lane + LANES)
-        totals = [jnp.zeros((rows, LANES), F32)] * (2 * frames)
-        for d, ref in enumerate(arrived):
-            column = later(d, ref[:, span].astype(F32))
-            base = 2 * frames + 2 * d * frames
-            for t in range(2 * frames):
-                for s in range(2 * frames):
-                    lag = t % frames - s % frames
-                    if t // frames == s // frames:
-                        if d == 0 and lag < 0:
-                            continue
-                    else:
-                        lag = lag + (shift(frames) if t < frames else -shift(frames))
-                    totals[t] = totals[t] + table_ref[base + lag, :, span] * column[s * rows : (s + 1) * rows]
+        totals = [sums_ref[t * rows : (t + 1) * rows, span] for t in range(2 * frames)]
+        for d, ref in enumerate(arrived, 1):
+            totals = add_column(frames, rows, d, totals, later(d, ref[:, span].astype(F32)), table_ref, span)
         totals = [jnp.where(exists, total, jnp.zeros_like(total)) for total in totals]
         own_ref[:, span] = jnp.concatenate(totals[:frames])
         other_ref[:, span] = jnp.concatenate(totals[frames:]).astype(BF16)
@@ -304,10 +316,15 @@
             gate.append(jnp.where(first, gate_ref[i : i + cols], gate_ref[j : j + cols]))
     out = projected(jnp.concatenate(mixed).astype(BF16), jnp.concatenate(gate), wv_ref, wo_ref)
     for t in range(frames):
-        new = [out[k * size + t * cols : k * size + (t + 1) * cols] for k in range(len(ends))]
-        for at, is_last in ((t * sites, False), ((t + 1) * sites - cols, True)):
-            kept = new[1] if len(new) > 1 else inner_ref[at : at + cols]
-            out_ref[at : at + cols] = jnp.where(odd, kept, new[0]) if is_last else jnp.where(odd, new[0], kept)
+        new = [out[k * size + t * cols : k * size + (t + 1) * cols].astype(F32) for k in range(len(ends))]
+        first, final = t * sites, (t + 1) * sites - 2 * cols
+        top = inner_ref[first : first + 2 * cols].astype(F32)
+        bottom = inner_ref[final : final + 2 * cols].astype(F32)
+        other = new[1] if len(new) > 1 else None
+        row = jnp.where(odd, new[0], top[:cols] if other is None else other)
+        out_ref[first : first + 2 * cols] = jnp.concatenate([row, top[cols:]]).astype(BF16)
+        row = jnp.where(odd, bottom[cols:] if other is None else other, new[0])
+        out_ref[final : final + 2 * cols] = jnp.concatenate([bottom[:cols], row]).astype(BF16)
 
 
 def body(latents, spatial_taps, kernel_taps, skip_gain, gate_weight, value_weight, out_weight):
@@ -380,12 +397,19 @@
         firsts.append(lax.ppermute(sent[2 * d - 2], "tm", route))
         rests.append(lax.ppermute(sent[2 * d - 1], "tm", route))
 
+    (sums,) = call(
+        functools.partial(width_kernel, frames, rows),
+        "width",
+        [shape((2 * lines, chans), F32)],
+        [],
+        [table, columns[0]],
+    )
     own, other = call(
         functools.partial(side_kernel, frames, rows),
         "side",
         [shape((lines, chans), F32), shape((lines, chans), BF16)],
         [],
-        [table] + columns,
+        [table, sums] + columns[1:],
         LATER,
     )
     other = lax.ppermute(other, "tm", [(i, i ^ 1) for i in range(n_t)])

time: 16.3 us -> 16.3 us (level)
    pallas_call x10 -> x11, Pallas kernels: 4.35 us -> 4.35 us  [call(): pl.pallas_call(kernel, out_shape=tuple(outs), in_specs=[HBM] * far + [VME...]
where the time goes in v19:
time: 16.3 us; the launch traced here: 16 us
  starting transfers between devices  8.39 us (51%)
  Pallas kernels  4.35 us (27%)
  waiting for transfers between devices  3.22 us (20%)
    pallas_call x11, Pallas kernels, call(): pl.pallas_call(kernel, out_shape=tuple(outs), in_specs=[HBM] * far + [VME...  4.35 us
    ppermute x2, starting transfers between devices, body(): columns.append(lax.ppermute(column, ('tm', 'height', 'width'), route))  4.22 us
    ppermute x1, starting transfers between devices, body(): lax.ppermute(e, 'height', pairs)  1.56 us
    ppermute x1, starting transfers between devices, body(): rests.append(lax.ppermute(sent[2 * d - 1], 'tm', route))  1.41 us
    ppermute x1, waiting for transfers between devices, body(): rests.append(lax.ppermute(sent[2 * d - 1], 'tm', route))  1.17 us
    ppermute x1, waiting for transfers between devices, body(): firsts.append(lax.ppermute(sent[2 * d - 2], 'tm', route))  1.04 us
    ppermute x2, waiting for transfers between devices, body(): columns.append(lax.ppermute(column, ('tm', 'height', 'width'), route))  0.8 us
    ppermute x1, starting transfers between devices, body(): firsts.append(lax.ppermute(sent[2 * d - 2], 'tm', route))  0.69 us
  transfers between devices with their start and end apart: 7, of which 4 were waited for; matrix products, arithmetic and copies ran while one was open for 0% of the time, Pallas kernels for 20%

profile of v19, /device:TPU:0, one launch (start us, length us, event | category | flops | bytes accessed | tf_op | source)
XLA Modules:
  0.0 16.0 jit_solution(12912360346890318732)
XLA Ops:
  0.0 0.5 %collective-permute-start = (bf16[256,512]{1,0:T(8,128)(2,1)}, bf16[256,512]{1,0:T(8,128)(2,1)S(1)}, u32[]{:S(2)}, u32[]{:S(2)}) collective-permute-start(bf16[256,512]{1,0:T(8,128)(2,1)} %bitcast.3), channel_id=1, source_target_pairs={{0,8},{8,0},{16,24},{24,16},{1,9},{9,1},{17,25},{25,17},{2,10},{10... | collective-permute-start | bytes 786440 | tf_op jit(solution)/shard_map/ppermute | solution.py:339
  0.5 1.5 %early.1 = (bf16[256,512]{1,0:T(8,128)(2,1)S(1)}, bf16[512,512]{1,0:T(8,128)(2,1)S(1)}, f32[3,3,512]{2,1,0:T(4,128)S(1)}, bf16[512,512]{1,0:T(8,128)(2,1)S(1)}, ...) custom-call(bf16[16,512]{1,0:T(8,128)(2,1)} %refs_0_.1, ...), custom_call_target="tpu_custom_call" | custom-call | bytes 5232640 | tf_op jit(solution)/shard_map/early/pallas_call | solution.py:20
  2.0 0.0 collective-permute-done.partner_ref
  2.0 0.1 column.1
  2.1 2.8 %collective-permute-start.1 = (bf16[64,512]{1,0:T(8,128)(2,1)S(1)}, bf16[64,512]{1,0:T(8,128)(2,1)S(1)}, u32[]{:S(2)}, u32[]{:S(2)}) collective-permute-start(bf16[64,512]{1,0:T(8,128)(2,1)S(1)} %column.1), channel_id=1, source_target_pairs={{0,1},{1,0},{2,3},{3,2},{4,5},{5,4},{6,7},{7,6},{8,12},{9,10},{10,... | collective-permute-start | bytes 196616 | tf_op jit(solution)/shard_map/ppermute | solution.py:394
  4.9 1.4 %collective-permute-start.2 = (bf16[64,512]{1,0:T(8,128)(2,1)S(1)}, bf16[64,512]{1,0:T(8,128)(2,1)S(1)}, u32[]{:S(2)}, u32[]{:S(2)}) collective-permute-start(bf16[64,512]{1,0:T(8,128)(2,1)S(1)} %column.1), channel_id=1, source_target_pairs={{0,17},{1,16},{2,19},{3,18},{4,21},{5,20},{6,23},{7,22},{8,28},{9,... | collective-permute-start | bytes 196616 | tf_op jit(solution)/shard_map/ppermute | solution.py:394
  6.3 0.2 %later.1 = (bf16[32,512]{1,0:T(8,128)(2,1)S(1)}, bf16[224,512]{1,0:T(8,128)(2,1)S(1)}) custom-call(bf16[256,512]{1,0:T(8,128)(2,1)S(1)} %collective-permute-done.partner_ref, f32[24,8,512]{2,1,0:T(8,128)S(1)} %get-tuple-element.25.table_ref, f32[256,512]{1,0:T(8,128)S(1)} %get-tuple-element.30.refs_0_), custom_call_target="tpu_custom_call" | custom-call | flops 1048576 | bytes 1441792 | tf_op jit(solution)/shard_map/later/pallas_call | solution.py:20
  6.5 0.7 %collective-permute-start.4 = (bf16[32,512]{1,0:T(8,128)(2,1)S(1)}, bf16[32,512]{1,0:T(8,128)(2,1)S(1)}, u32[]{:S(2)}, u32[]{:S(2)}) collective-permute-start(bf16[32,512]{1,0:T(8,128)(2,1)S(1)} %get-tuple-element.31), channel_id=1, source_target_pairs={{0,16},{8,24},{16,0},{24,8},{1,17},{9,25},{17,1},{25,9},{2,18},{10... | collective-permute-start | bytes 98312 | tf_op jit(solution)/shard_map/ppermute | solution.py:397
  7.2 1.4 %collective-permute-start.5 = (bf16[224,512]{1,0:T(8,128)(2,1)S(1)}, bf16[224,512]{1,0:T(8,128)(2,1)S(1)}, u32[]{:S(2)}, u32[]{:S(2)}) collective-permute-start(bf16[224,512]{1,0:T(8,128)(2,1)S(1)} %get-tuple-element.41), channel_id=1, source_target_pairs={{0,16},{8,24},{16,0},{24,8},{1,17},{9,25},{17,1},{25,9},{2,18},{10... | collective-permute-start | bytes 688136 | tf_op jit(solution)/shard_map/ppermute | solution.py:398
  8.6 0.0 collective-permute-done.1.arrived_ref
  8.6 0.1 width.1.sums_ref
  8.7 0.8 %collective-permute-done.2.refs_0_ = bf16[64,512]{1,0:T(8,128)(2,1)S(1)} collective-permute-done((bf16[64,512]{1,0:T(8,128)(2,1)S(1)}, bf16[64,512]{1,0:T(8,128)(2,1)S(1)}, u32[]{:S(2)}, u32[]{:S(2)}) %collective-permute-start.2) | collective-permute-done | bytes 65568 | tf_op jit(solution)/shard_map/ppermute | solution.py:394
  9.5 0.1 side.1
  9.6 0.1 collective-permute-start.3
  9.6 0.2 %own.1.mine_ref = f32[256,512]{1,0:T(8,128)S(1)} custom-call(bf16[256,512]{1,0:T(8,128)(2,1)S(1)} %collective-permute-done.partner_ref, f32[24,8,512]{2,1,0:T(8,128)S(1)} %get-tuple-element.25.table_ref, f32[256,512]{1,0:T(8,128)S(1)} %get-tuple-element.26.field_ref), custom_call_target="tpu_custom_call" | custom-call | flops 1048576 | bytes 1703936 | tf_op jit(solution)/shard_map/own/pallas_call | solution.py:20
  9.8 1.0 %collective-permute-done.4.refs_0_ = bf16[32,512]{1,0:T(8,128)(2,1)S(1)} collective-permute-done((bf16[32,512]{1,0:T(8,128)(2,1)S(1)}, bf16[32,512]{1,0:T(8,128)(2,1)S(1)}, u32[]{:S(2)}, u32[]{:S(2)}) %collective-permute-start.4) | collective-permute-done | bytes 32800 | tf_op jit(solution)/shard_map/ppermute | solution.py:397
  10.9 0.0 collective-permute-done.3.other_ref
  10.9 1.6 %collective-permute-start.6 = (bf16[40,512]{1,0:T(8,128)(2,1)S(1)}, bf16[40,512]{1,0:T(8,128)(2,1)S(1)}, u32[]{:S(2)}, u32[]{:S(2)}) collective-permute-start(bf16[40,512]{1,0:T(8,128)(2,1)S(1)} %get-tuple-element.44), channel_id=1, source_target_pairs={{0,4},{4,0},{1,5},{5,1},{2,6},{6,2},{3,7},{7,3},{8,12},{12,8},{9,1... | collective-permute-start | bytes 122888 | tf_op jit(solution)/shard_map/ppermute | solution.py:424
  12.5 0.4 %gate.1.gate_ref = f32[256,512]{1,0:T(8,128)S(1)} custom-call(bf16[256,512]{1,0:T(8,128)(2,1)S(1)} %get-tuple-element.35.x_ref, bf16[512,512]{1,0:T(8,128)(2,1)S(1)} %get-tuple-element.36.w_ref), custom_call_target="tpu_custom_call" | custom-call | bytes 1310720 | tf_op jit(solution)/shard_map/gate/pallas_call | solution.py:20
  12.9 0.7 %inner.1 = (bf16[256,512]{1,0:T(8,128)(2,1)S(1)}, f32[256,512]{1,0:T(8,128)S(1)}) custom-call(f32[256,512]{1,0:T(8,128)S(1)} %own.1.mine_ref, f32[32,512]{1,0:T(8,128)S(1)} %get-tuple-element.32.low_ref, f32[32,512]{1,0:T(8,128)S(1)} %get-tuple-element.33.high_ref, f32[3,3,512]{2,1,0:T(4,128)S(1)} %get-tuple-element.34.taps_ref, ...), custom_call_target="tpu_custom_call" | custom-call | flops 268435456 | bytes 3033088 | tf_op jit(solution)/shard_map/inner/pallas_call | solution.py:20
  13.6 1.2 %collective-permute-done.5.refs_1_ = bf16[224,512]{1,0:T(8,128)(2,1)S(1)} collective-permute-done((bf16[224,512]{1,0:T(8,128)(2,1)S(1)}, bf16[224,512]{1,0:T(8,128)(2,1)S(1)}, u32[]{:S(2)}, u32[]{:S(2)}) %collective-permute-start.5) | collective-permute-done | bytes 229408 | tf_op jit(solution)/shard_map/ppermute | solution.py:398
  14.8 0.2 %collective-permute-done.6.refs_0_ = bf16[40,512]{1,0:T(8,128)(2,1)S(1)} collective-permute-done((bf16[40,512]{1,0:T(8,128)(2,1)S(1)}, bf16[40,512]{1,0:T(8,128)(2,1)S(1)}, u32[]{:S(2)}, u32[]{:S(2)}) %collective-permute-start.6) | collective-permute-done | bytes 40992 | tf_op jit(solution)/shard_map/ppermute | solution.py:424
  15.0 1.1 %last.1 = bf16[256,512]{1,0:T(8,128)(2,1)} custom-call(bf16[256,512]{1,0:T(8,128)(2,1)S(1)} %get-tuple-element.42.inner_ref, f32[256,512]{1,0:T(8,128)S(1)} %get-tuple-element.43.totals_ref, f32[3,3,512]{2,1,0:T(4,128)S(1)} %get-tuple-element.34.taps_ref, f32[256,512]{1,0:T(8,128)S(1)} %gate.1.gate_ref, bf16[512,512]{1,0:T(8,128)(2,1)S(1)} %get-tuple-element.37.wv_ref, ...), custom_call_target="tpu_custom_call" | custom-call | bytes 2680832 | tf_op jit(solution)/shard_map/last/pallas_call | solution.py:20
  (2 shorter events, 0.0 us)
Async XLA Ops:
  0.0 2.0 %collective-permute-start = (bf16[256,512]{1,0:T(8,128)(2,1)}, bf16[256,512]{1,0:T(8,128)(2,1)S(1)}, u32[]{:S(2)}, u32[]{:S(2)}) collective-permute-start(bf16[256,512]{1,0:T(8,128)(2,1)} %bitcast.3), channel_id=1, source_target_pairs={{0,8},{8,0},{16,24},{24,16},{1,9},{9,1},{17,25},{25,17},{2,10},{10... | collective-permute-start | bytes 786440 | tf_op jit(solution)/shard_map/ppermute | solution.py:339
  2.1 6.5 %collective-permute-start.1 = (bf16[64,512]{1,0:T(8,128)(2,1)S(1)}, bf16[64,512]{1,0:T(8,128)(2,1)S(1)}, u32[]{:S(2)}, u32[]{:S(2)}) collective-permute-start(bf16[64,512]{1,0:T(8,128)(2,1)S(1)} %column.1), channel_id=1, source_target_pairs={{0,1},{1,0},{2,3},{3,2},{4,5},{5,4},{6,7},{7,6},{8,12},{9,10},{10,... | collective-permute-start | bytes 196616 | tf_op jit(solution)/shard_map/ppermute | solution.py:394
  4.9 4.6 %collective-permute-start.2 = (bf16[64,512]{1,0:T(8,128)(2,1)S(1)}, bf16[64,512]{1,0:T(8,128)(2,1)S(1)}, u32[]{:S(2)}, u32[]{:S(2)}) collective-permute-start(bf16[64,512]{1,0:T(8,128)(2,1)S(1)} %column.1), channel_id=1, source_target_pairs={{0,17},{1,16},{2,19},{3,18},{4,21},{5,20},{6,23},{7,22},{8,28},{9,... | collective-permute-start | bytes 196616 | tf_op jit(solution)/shard_map/ppermute | solution.py:394
  6.5 4.4 %collective-permute-start.4 = (bf16[32,512]{1,0:T(8,128)(2,1)S(1)}, bf16[32,512]{1,0:T(8,128)(2,1)S(1)}, u32[]{:S(2)}, u32[]{:S(2)}) collective-permute-start(bf16[32,512]{1,0:T(8,128)(2,1)S(1)} %get-tuple-element.31), channel_id=1, source_target_pairs={{0,16},{8,24},{16,0},{24,8},{1,17},{9,25},{17,1},{25,9},{2,18},{10... | collective-permute-start | bytes 98312 | tf_op jit(solution)/shard_map/ppermute | solution.py:397
  7.2 7.6 %collective-permute-start.5 = (bf16[224,512]{1,0:T(8,128)(2,1)S(1)}, bf16[224,512]{1,0:T(8,128)(2,1)S(1)}, u32[]{:S(2)}, u32[]{:S(2)}) collective-permute-start(bf16[224,512]{1,0:T(8,128)(2,1)S(1)} %get-tuple-element.41), channel_id=1, source_target_pairs={{0,16},{8,24},{16,0},{24,8},{1,17},{9,25},{17,1},{25,9},{2,18},{10... | collective-permute-start | bytes 688136 | tf_op jit(solution)/shard_map/ppermute | solution.py:398
  9.6 1.3 %collective-permute-start.3 = (bf16[32,512]{1,0:T(8,128)(2,1)S(1)}, bf16[32,512]{1,0:T(8,128)(2,1)S(1)}, u32[]{:S(2)}, u32[]{:S(2)}) collective-permute-start(bf16[32,512]{1,0:T(8,128)(2,1)S(1)} %get-tuple-element.29), channel_id=1, source_target_pairs={{0,8},{8,0},{16,24},{24,16},{1,9},{9,1},{17,25},{25,17},{2,10},{10... | collective-permute-start | bytes 98312 | tf_op jit(solution)/shard_map/ppermute | solution.py:415
  10.9 4.1 %collective-permute-start.6 = (bf16[40,512]{1,0:T(8,128)(2,1)S(1)}, bf16[40,512]{1,0:T(8,128)(2,1)S(1)}, u32[]{:S(2)}, u32[]{:S(2)}) collective-permute-start(bf16[40,512]{1,0:T(8,128)(2,1)S(1)} %get-tuple-element.44), channel_id=1, source_target_pairs={{0,4},{4,0},{1,5},{5,1},{2,6},{6,2},{3,7},{7,3},{8,12},{12,8},{9,1... | collective-permute-start | bytes 122888 | tf_op jit(solution)/shard_map/ppermute | solution.py:424

commit v20 on v19

--- a/solution.py
+++ b/solution.py
@@ -14,14 +14,14 @@
 HBM = pl.BlockSpec(memory_space=pltpu.HBM)
 
 
-def call(kernel, name, outs, scratch, operands, flops=0, exps=0, far=0, aliases={}):
+def call(kernel, name, outs, scratch, operands, flops=0, exps=0, far=0, far_outs=0, aliases={}):
     operands = [pltpu.with_memory_space_constraint(a, pltpu.HBM) for a in operands[:far]] + list(operands[far:])
     moved = sum(a.size * a.dtype.itemsize for a in operands) + sum(a.size * a.dtype.itemsize for a in outs)
     return pl.pallas_call(
         kernel,
         out_shape=tuple(outs),
         in_specs=[HBM] * far + [VMEM] * (len(operands) - far),
-        out_specs=(VMEM,) * len(outs),
+        out_specs=(HBM,) * far_outs + (VMEM,) * (len(outs) - far_outs),
         scratch_shapes=scratch,
         input_output_aliases=aliases,
         compiler_params=pltpu.CompilerParams(vmem_limit_bytes=24 * 1024 * 1024),
@@ -170,52 +170,59 @@
     return totals
 
 
-def width_kernel(frames, rows, table_ref, arrived_ref, sums_ref):
-    for lane in range(0, sums_ref.shape[1], LANES):
-        span = slice(lane, lane + LANES)
-        totals = [jnp.zeros((rows, LANES), F32)] * (2 * frames)
-        totals = add_column(frames, rows, 0, totals, arrived_ref[:, span].astype(F32), table_ref, span)
-        sums_ref[:, span] = jnp.concatenate(totals)
-
-
-def side_kernel(frames, rows, table_ref, sums_ref, *refs):
+def side_kernel(frames, rows, first, table_ref, *refs):
     *arrived, own_ref, other_ref = refs
     _, lower, upper = position("width")
     exists = jnp.where(on_right(), upper, lower)
     for lane in range(0, own_ref.shape[1], LANES):
         span = slice(lane, lane + LANES)
-        totals = [sums_ref[t * rows : (t + 1) * rows, span] for t in range(2 * frames)]
-        for d, ref in enumerate(arrived, 1):
+        totals = [jnp.zeros((rows, LANES), F32)] * (2 * frames)
+        for d, ref in enumerate(arrived, first):
             totals = add_column(frames, rows, d, totals, later(d, ref[:, span].astype(F32)), table_ref, span)
         totals = [jnp.where(exists, total, jnp.zeros_like(total)) for total in totals]
         own_ref[:, span] = jnp.concatenate(totals[:frames])
         other_ref[:, span] = jnp.concatenate(totals[frames:]).astype(BF16)
 
 
-def border_kernel(frames, rows, cols, chips, mine_ref, own_ref, other_ref, *refs):
-    arrived, (low_ref, high_ref, *outs) = refs[: chips - 1], refs[chips - 1 :]
+def both_sides(own, other):
+    right = on_right()
+    return jnp.where(right, other, own), jnp.where(right, own, other)
+
+
+def end_corners(frames, rows, own_ref, other_ref):
+    sides = both_sides(own_ref[...], other_ref[...].astype(F32))
+    pick = lambda r: [side[t * rows + r : t * rows + r + 1] for side in sides for t in range(frames)]
+    return [jnp.concatenate(pick(r)) for r in (0, rows - 1)]
+
+
+def border_kernel(frames, rows, cols, mine_ref, own_ref, other_ref, *outs):
     sites = rows * cols
     odd, _, _ = position("height")
-    right, own, other = on_right(), own_ref[...], other_ref[...].astype(F32)
-    low, high = jnp.where(right, other, own), jnp.where(right, own, other)
-    low_ref[...] = low
-    high_ref[...] = high
-    size = frames * cols
-    lines, corners = [], []
+    corners = end_corners(frames, rows, own_ref, other_ref)
+    lines = []
     for r in (0, rows - 1):
         lines.append(jnp.concatenate([mine_ref[t * sites + r * cols : t * sites + (r + 1) * cols] for t in range(frames)]))
-        ends = [side[t * rows + r : t * rows + r + 1] for side in (low, high) for t in range(frames)]
-        corners.append(jnp.concatenate(ends))
+    ends = [jnp.concatenate(pair) for pair in zip(lines, corners)]
     for k, out in enumerate(outs):
-        line = jnp.where(odd, *(lines[::-1] if k else lines))
-        for d, ref in enumerate(arrived, 1):
-            if len(outs) > 1:
-                ends = [ref[i * size : (i + 1) * size].astype(F32) for i in range(2)]
-                more = jnp.where(odd, *(ends[::-1] if k else ends))
-            else:
-                more = ref[:size].astype(F32)
-            line = line + later(d, more)
-        out[...] = jnp.concatenate([line, jnp.where(odd, *(corners[::-1] if k else corners))]).astype(BF16)
+        out[...] = jnp.where(odd, *(ends[::-1] if k else ends)).astype(BF16)
+
+
+def before_kernel(frames, rows, cols, own_ref, other_ref, *refs):
+    rounds_h = refs[0].shape[0] // (frames * cols)
+    firsts, outs = refs[:-rounds_h], refs[-rounds_h:]
+    size = frames * cols
+    odd, _, _ = position("height")
+    corners = end_corners(frames, rows, own_ref, other_ref)
+    line = 0.0
+    for d, ref in enumerate(firsts, 1):
+        line = line + later(d, ref[...].astype(F32))
+    for k, out in enumerate(outs):
+        if rounds_h > 1:
+            pair = line[:size], line[size:]
+            row = jnp.where(odd, *(pair[::-1] if k else pair))
+        else:
+            row = line
+        out[...] = jnp.concatenate([row, jnp.where(odd, *(corners[::-1] if k else corners))]).astype(BF16)
 
 
 def shifted(line, left, right):
@@ -249,13 +256,13 @@
 
 
 def inner_kernel(
-    frames, rows, cols, mine_ref, low_ref, high_ref, taps_ref, gate_ref, wv_ref, wo_ref, out_ref, totals_ref, mixed
+    frames, rows, cols, mine_ref, own_ref, other_ref, taps_ref, gate_ref, wv_ref, wo_ref, out_ref, totals_ref, mixed
 ):
     sites = rows * cols
     for lane in range(0, mine_ref.shape[1], LANES):
         span = slice(lane, lane + LANES)
         taps = taps_of(taps_ref, span)
-        low, high = low_ref[:, span], high_ref[:, span]
+        low, high = both_sides(own_ref[:, span], other_ref[:, span].astype(F32))
         for t in range(frames):
             at = t * sites
             lines = [mine_ref[at + r * cols : at + (r + 1) * cols, span] for r in range(rows)]
@@ -267,42 +274,46 @@
     out_ref[...] = projected(mixed[...], gate_ref[...], wv_ref, wo_ref)
 
 
+def has_earlier():
+    return lax.div(lax.axis_index("tm"), 2) > 0
+
+
 def block_kernel(frames, rows, cols, rounds_h, inner_ref, totals_ref, taps_ref, gate_ref, wv_ref, wo_ref, *refs):
-    *parts, out_ref, sums_ref, mixed = refs
+    own_ref, other_ref, *parts, out_ref, sums_ref, mixed = refs
     firsts, rests = parts[: len(parts) // 2], parts[len(parts) // 2 :]
     sites = rows * cols
     size = frames * cols
 
-    @pl.when(lax.div(lax.axis_index("tm"), 2) > 0)
+    @pl.when(has_earlier())
     def _():
         for lane in range(0, out_ref.shape[1], LANES):
             span = slice(lane, lane + LANES)
             taps = taps_of(taps_ref, span)
+            low, high = both_sides(own_ref[:, span], other_ref[:, span].astype(F32))
             lines = [jnp.zeros((size, LANES), F32)] * rows
             for d, (first, rest) in enumerate(zip(firsts, rests), 1):
                 more = [first[i * size : (i + 1) * size, span].astype(F32) for i in range(rounds_h)]
                 more += [rest[i * size : (i + 1) * size, span].astype(F32) for i in range(rows - rounds_h)]
                 more = reordered(more, rounds_h, back=True)
                 lines = [line + later(d, other) for line, other in zip(lines, more)]
-            zero = [jnp.zeros((1, LANES), F32)] * rows
             for t in range(frames):
                 at = t * sites
-                total = filtered([line[t * cols : (t + 1) * cols] for line in lines], zero, zero, taps)
+                lefts = [low[t * rows + r : t * rows + r + 1] for r in range(rows)]
+                rights = [high[t * rows + r : t * rows + r + 1] for r in range(rows)]
+                total = filtered([line[t * cols : (t + 1) * cols] for line in lines], lefts, rights, taps)
                 total = jnp.concatenate(total) + totals_ref[at : at + sites, span]
                 sums_ref[at : at + sites, span] = total
                 mixed[at : at + sites, span] = total.astype(BF16)
         out_ref[...] = projected(mixed[...], gate_ref[...], wv_ref, wo_ref)
 
 
-def last_kernel(frames, rows, cols, inner_ref, totals_ref, taps_ref, gate_ref, wv_ref, wo_ref, *refs):
-    *ends, out_ref = refs
+def complete(frames, rows, cols, inner_ref, totals_ref, taps_ref, gate_ref, wv_ref, wo_ref, ends, out_ref, held, done):
     sites = rows * cols
     size = frames * cols
     odd, lower, upper = position("height")
-    out_ref[...] = inner_ref[...]
+    held[...] = inner_ref[...]
     mixed, gate = [], []
     for k, end in enumerate(ends):
-        end = end[...].astype(F32)
         first = jnp.logical_not(odd) if k else odd
         lefts, rights = end[size : size + frames], end[size + frames : size + 2 * frames]
         exists = jnp.where(first, lower, upper)
@@ -322,9 +333,35 @@
         bottom = inner_ref[final : final + 2 * cols].astype(F32)
         other = new[1] if len(new) > 1 else None
         row = jnp.where(odd, new[0], top[:cols] if other is None else other)
-        out_ref[first : first + 2 * cols] = jnp.concatenate([row, top[cols:]]).astype(BF16)
+        held[first : first + 2 * cols] = jnp.concatenate([row, top[cols:]]).astype(BF16)
         row = jnp.where(odd, bottom[cols:] if other is None else other, new[0])
-        out_ref[final : final + 2 * cols] = jnp.concatenate([bottom[:cols], row]).astype(BF16)
+        held[final : final + 2 * cols] = jnp.concatenate([bottom[:cols], row]).astype(BF16)
+    copy = pltpu.make_async_copy(held, out_ref, done)
+    copy.start()
+    copy.wait()
+
+
+def first_kernel(frames, rows, cols, inner_ref, totals_ref, taps_ref, gate_ref, wv_ref, wo_ref, *refs):
+    *ends, out_ref, held, done = refs
+
+    @pl.when(jnp.logical_not(has_earlier()))
+    def _():
+        values = [end[...].astype(F32) for end in ends]
+        complete(
+            frames, rows, cols, inner_ref, totals_ref, taps_ref, gate_ref, wv_ref, wo_ref, values, out_ref, held, done
+        )
+
+
+def last_kernel(frames, rows, cols, before_ref, inner_ref, totals_ref, taps_ref, gate_ref, wv_ref, wo_ref, *refs):
+    *ends, out_ref, held, done = refs
+    own, earlier = ends[: len(ends) // 2], ends[len(ends) // 2 :]
+
+    @pl.when(has_earlier())
+    def _():
+        values = [a[...].astype(F32) + b[...].astype(F32) for a, b in zip(own, earlier)]
+        complete(
+            frames, rows, cols, inner_ref, totals_ref, taps_ref, gate_ref, wv_ref, wo_ref, values, out_ref, held, done
+        )
 
 
 def body(latents, spatial_taps, kernel_taps, skip_gain, gate_weight, value_weight, out_weight):
@@ -397,57 +434,60 @@
         firsts.append(lax.ppermute(sent[2 * d - 2], "tm", route))
         rests.append(lax.ppermute(sent[2 * d - 1], "tm", route))
 
-    (sums,) = call(
-        functools.partial(width_kernel, frames, rows),
-        "width",
-        [shape((2 * lines, chans), F32)],
-        [],
-        [table, columns[0]],
-    )
-    own, other = call(
-        functools.partial(side_kernel, frames, rows),
-        "side",
-        [shape((lines, chans), F32), shape((lines, chans), BF16)],
-        [],
-        [table, sums] + columns[1:],
-        LATER,
-    )
-    other = lax.ppermute(other, "tm", [(i, i ^ 1) for i in range(n_t)])
-    size = frames * cols + 2 * frames
-    low, high, *ends = call(
-        functools.partial(border_kernel, frames, rows, cols, chips),
-        "border",
-        [shape((lines, chans), F32)] * 2 + [shape((size, chans), BF16)] * len(h_rounds),
-        [],
-        [mine, own, other] + firsts,
-    )
+    swap = [(i, i ^ 1) for i in range(n_t)]
+    both = [shape((lines, chans), F32), shape((lines, chans), BF16)]
+    own, other = call(functools.partial(side_kernel, frames, rows, 0), "side", both, [], [table, columns[0]], LATER)
+    other = lax.ppermute(other, "tm", swap)
+    end = [shape((frames * cols + 2 * frames, chans), BF16)] * len(h_rounds)
+    ends = call(functools.partial(border_kernel, frames, rows, cols), "border", end, [], [mine, own, other])
     ends = [lax.ppermute(e, "height", pairs) for e, pairs in zip(ends, h_rounds)]
+    if chips > 1:
+        own_d, other_d = call(
+            functools.partial(side_kernel, frames, rows, 1), "beside", both, [], [table] + columns[1:], LATER
+        )
+        other_d = lax.ppermute(other_d, "tm", swap)
+        earlier = call(functools.partial(before_kernel, frames, rows, cols), "before", end, [], [own_d, other_d] + firsts)
+        earlier = [lax.ppermute(e, "height", pairs) for e, pairs in zip(earlier, h_rounds)]
 
     inner, totals = call(
         functools.partial(inner_kernel, frames, rows, cols),
         "inner",
         [shape((block, chans), BF16), field],
         [pltpu.VMEM((block, chans), BF16)],
-        [mine, low, high, taps, gate, value_weight, out_weight],
+        [mine, own, other, taps, gate, value_weight, out_weight],
         4 * block * chans * chans,
+    )
+    held = [pltpu.VMEM((block, chans), BF16), pltpu.SemaphoreType.DMA]
+    weights = [taps, gate, value_weight, out_weight]
+    out = shape((block, chans), BF16)
+    (first,) = call(
+        functools.partial(first_kernel, frames, rows, cols),
+        "first",
+        [out],
+        held,
+        [inner, totals] + weights + ends,
+        far_outs=1,
     )
     if chips > 1:
         inner, totals = call(
             functools.partial(block_kernel, frames, rows, cols, len(h_rounds)),
             "block",
-            [shape((block, chans), BF16), field],
-            [pltpu.VMEM((block, chans), BF16)],
-            [inner, totals, taps, gate, value_weight, out_weight] + firsts + rests,
+            [out, field],
+            held[:1],
+            [inner, totals] + weights + [own_d, other_d] + firsts + rests,
             aliases={0: 0, 1: 1},
         )
-    (out,) = call(
-        functools.partial(last_kernel, frames, rows, cols),
-        "last",
-        [shape((block, chans), BF16)],
-        [],
-        [inner, totals, taps, gate, value_weight, out_weight] + ends,
-    )
-    return out.reshape(latents.shape)
+        (first,) = call(
+            functools.partial(last_kernel, frames, rows, cols),
+            "last",
+            [out],
+            held,
+            [first, inner, totals] + weights + ends + earlier,
+            far=1,
+            far_outs=1,
+            aliases={0: 0},
+        )
+    return first.reshape(latents.shape)
 
 
 def solution(mesh):

time: 16.3 us -> 16.1 us (0.988)
  the two profiles are of different devices: /device:TPU:0 before, /device:TPU:4 now
where the time goes in v20:
time: 16.1 us; the launch traced here: 15.9 us
  starting transfers between devices  6.89 us (43%)
  Pallas kernels  5.31 us (33%)
  waiting for transfers between devices  3.56 us (22%)
    pallas_call x13, Pallas kernels, call(): pl.pallas_call(kernel, out_shape=tuple(outs), in_specs=[HBM] * far + [VME...  5.31 us
    ppermute x2, starting transfers between devices, body(): lax.ppermute(e, 'height', pairs)  2.5 us
    ppermute x2, waiting for transfers between devices, body(): columns.append(lax.ppermute(column, ('tm', 'height', 'width'), route))  2.31 us
    ppermute x2, starting transfers between devices, body(): columns.append(lax.ppermute(column, ('tm', 'height', 'width'), route))  2.15 us
    ppermute x1, starting transfers between devices, body(): firsts.append(lax.ppermute(sent[2 * d - 2], 'tm', route))  1.47 us
    ppermute x1, starting transfers between devices, body(): rests.append(lax.ppermute(sent[2 * d - 1], 'tm', route))  0.62 us
    ppermute x2, waiting for transfers between devices, body(): lax.ppermute(e, 'height', pairs)  0.58 us
    ppermute x1, waiting for transfers between devices, body(): rests.append(lax.ppermute(sent[2 * d - 1], 'tm', route))  0.47 us
  transfers between devices with their start and end apart: 9, of which 5 were waited for; matrix products, arithmetic and copies ran while one was open for 0% of the time, Pallas kernels for 26%

profile of v20, /device:TPU:4, one launch (start us, length us, event | category | flops | bytes accessed | tf_op | source)
XLA Modules:
  0.0 15.9 jit_solution(17510729886024128325)
XLA Ops:
  0.0 0.0 collective-permute-start
  0.0 1.5 %early.1 = (bf16[256,512]{1,0:T(8,128)(2,1)S(1)}, bf16[512,512]{1,0:T(8,128)(2,1)S(1)}, f32[3,3,512]{2,1,0:T(4,128)S(1)}, bf16[512,512]{1,0:T(8,128)(2,1)S(1)}, ...) custom-call(bf16[16,512]{1,0:T(8,128)(2,1)} %refs_0_.1, ...), custom_call_target="tpu_custom_call" | custom-call | bytes 5232640 | tf_op jit(solution)/shard_map/early/pallas_call | solution.py:20
  1.6 0.2 %collective-permute-done.partner_ref = bf16[256,512]{1,0:T(8,128)(2,1)S(1)} collective-permute-done((bf16[256,512]{1,0:T(8,128)(2,1)}, bf16[256,512]{1,0:T(8,128)(2,1)S(1)}, u32[]{:S(2)}, u32[]{:S(2)}) %collective-permute-start) | collective-permute-done | bytes 262176 | tf_op jit(solution)/shard_map/ppermute | solution.py:376
  1.7 0.1 column.1
  1.8 1.6 %collective-permute-start.1 = (bf16[64,512]{1,0:T(8,128)(2,1)S(1)}, bf16[64,512]{1,0:T(8,128)(2,1)S(1)}, u32[]{:S(2)}, u32[]{:S(2)}) collective-permute-start(bf16[64,512]{1,0:T(8,128)(2,1)S(1)} %column.1), channel_id=1, source_target_pairs={{0,1},{1,0},{2,3},{3,2},{4,5},{5,4},{6,7},{7,6},{8,12},{9,10},{10,... | collective-permute-start | bytes 196616 | tf_op jit(solution)/shard_map/ppermute | solution.py:431
  3.5 0.5 %collective-permute-start.4 = (bf16[64,512]{1,0:T(8,128)(2,1)S(1)}, bf16[64,512]{1,0:T(8,128)(2,1)S(1)}, u32[]{:S(2)}, u32[]{:S(2)}) collective-permute-start(bf16[64,512]{1,0:T(8,128)(2,1)S(1)} %column.1), channel_id=1, source_target_pairs={{0,17},{1,16},{2,19},{3,18},{4,21},{5,20},{6,23},{7,22},{8,28},{9,... | collective-permute-start | bytes 196616 | tf_op jit(solution)/shard_map/ppermute | solution.py:431
  4.0 0.2 %later.1 = (bf16[32,512]{1,0:T(8,128)(2,1)S(1)}, bf16[224,512]{1,0:T(8,128)(2,1)S(1)}) custom-call(bf16[256,512]{1,0:T(8,128)(2,1)S(1)} %collective-permute-done.partner_ref, f32[24,8,512]{2,1,0:T(8,128)S(1)} %get-tuple-element.24.table_ref, f32[256,512]{1,0:T(8,128)S(1)} %get-tuple-element.38.refs_0_), custom_call_target="tpu_custom_call" | custom-call | flops 1048576 | bytes 1441792 | tf_op jit(solution)/shard_map/later/pallas_call | solution.py:20
  4.2 1.5 %collective-permute-start.6 = (bf16[32,512]{1,0:T(8,128)(2,1)S(1)}, bf16[32,512]{1,0:T(8,128)(2,1)S(1)}, u32[]{:S(2)}, u32[]{:S(2)}) collective-permute-start(bf16[32,512]{1,0:T(8,128)(2,1)S(1)} %get-tuple-element.39), channel_id=1, source_target_pairs={{0,16},{8,24},{16,0},{24,8},{1,17},{9,25},{17,1},{25,9},{2,18},{10... | collective-permute-start | bytes 98312 | tf_op jit(solution)/shard_map/ppermute | solution.py:434
  5.6 0.6 %collective-permute-start.7 = (bf16[224,512]{1,0:T(8,128)(2,1)S(1)}, bf16[224,512]{1,0:T(8,128)(2,1)S(1)}, u32[]{:S(2)}, u32[]{:S(2)}) collective-permute-start(bf16[224,512]{1,0:T(8,128)(2,1)S(1)} %get-tuple-element.40), channel_id=1, source_target_pairs={{0,16},{8,24},{16,0},{24,8},{1,17},{9,25},{17,1},{25,9},{2,18},{10... | collective-permute-start | bytes 688136 | tf_op jit(solution)/shard_map/ppermute | solution.py:435
  6.2 0.0 collective-permute-done.1.refs_0_
  6.3 0.1 side.1
  6.3 0.1 collective-permute-start.2
  6.4 2.3 %collective-permute-done.4.refs_0_ = bf16[64,512]{1,0:T(8,128)(2,1)S(1)} collective-permute-done((bf16[64,512]{1,0:T(8,128)(2,1)S(1)}, bf16[64,512]{1,0:T(8,128)(2,1)S(1)}, u32[]{:S(2)}, u32[]{:S(2)}) %collective-permute-start.4) | collective-permute-done | bytes 65568 | tf_op jit(solution)/shard_map/ppermute | solution.py:431
  8.7 0.1 beside.1
  8.8 0.1 collective-permute-start.5
  8.9 0.2 %own.1.mine_ref = f32[256,512]{1,0:T(8,128)S(1)} custom-call(bf16[256,512]{1,0:T(8,128)(2,1)S(1)} %collective-permute-done.partner_ref, f32[24,8,512]{2,1,0:T(8,128)S(1)} %get-tuple-element.24.table_ref, f32[256,512]{1,0:T(8,128)S(1)} %get-tuple-element.25.field_ref), custom_call_target="tpu_custom_call" | custom-call | flops 1048576 | bytes 1703936 | tf_op jit(solution)/shard_map/own/pallas_call | solution.py:20
  9.1 0.0 collective-permute-done.2.other_ref
  9.1 1.6 %collective-permute-start.3 = (bf16[40,512]{1,0:T(8,128)(2,1)S(1)}, bf16[40,512]{1,0:T(8,128)(2,1)S(1)}, u32[]{:S(2)}, u32[]{:S(2)}) collective-permute-start(bf16[40,512]{1,0:T(8,128)(2,1)S(1)} %border.1), channel_id=1, source_target_pairs={{0,4},{4,0},{1,5},{5,1},{2,6},{6,2},{3,7},{7,3},{8,12},{12,8},{9,1... | collective-permute-start | bytes 122888 | tf_op jit(solution)/shard_map/ppermute | solution.py:443
  10.7 0.0 collective-permute-done.6.refs_2_.refs_0_
  10.7 0.0 collective-permute-done.5.refs_1_.other_ref
  10.7 0.9 %collective-permute-start.8 = (bf16[40,512]{1,0:T(8,128)(2,1)S(1)}, bf16[40,512]{1,0:T(8,128)(2,1)S(1)}, u32[]{:S(2)}, u32[]{:S(2)}) collective-permute-start(bf16[40,512]{1,0:T(8,128)(2,1)S(1)} %before.1), channel_id=1, source_target_pairs={{0,4},{4,0},{1,5},{5,1},{2,6},{6,2},{3,7},{7,3},{8,12},{12,8},{9,1... | collective-permute-start | bytes 122888 | tf_op jit(solution)/shard_map/ppermute | solution.py:450
  11.7 0.4 %gate.1.gate_ref = f32[256,512]{1,0:T(8,128)S(1)} custom-call(bf16[256,512]{1,0:T(8,128)(2,1)S(1)} %get-tuple-element.30.x_ref, bf16[512,512]{1,0:T(8,128)(2,1)S(1)} %get-tuple-element.31.w_ref), custom_call_target="tpu_custom_call" | custom-call | bytes 1310720 | tf_op jit(solution)/shard_map/gate/pallas_call | solution.py:20
  12.1 0.8 %inner.1 = (bf16[256,512]{1,0:T(8,128)(2,1)S(1)}, f32[256,512]{1,0:T(8,128)S(1)}) custom-call(f32[256,512]{1,0:T(8,128)S(1)} %own.1.mine_ref, f32[32,512]{1,0:T(8,128)S(1)} %get-tuple-element.27.own_ref, bf16[32,512]{1,0:T(8,128)(2,1)S(1)} %collective-permute-done.2.other_ref, f32[3,3,512]{2,1,0:T(4,128)S(1)} %get-tuple-element.29.taps_ref, ...), custom_call_target="tpu_custom_call" | custom-call | flops 268435456 | bytes 3000320 | tf_op jit(solution)/shard_map/inner/pallas_call | solution.py:20
  12.9 0.3 %collective-permute-done.3.refs_0_ = bf16[40,512]{1,0:T(8,128)(2,1)S(1)} collective-permute-done((bf16[40,512]{1,0:T(8,128)(2,1)S(1)}, bf16[40,512]{1,0:T(8,128)(2,1)S(1)}, u32[]{:S(2)}, u32[]{:S(2)}) %collective-permute-start.3) | collective-permute-done | bytes 40992 | tf_op jit(solution)/shard_map/ppermute | solution.py:443
  13.2 0.5 %collective-permute-done.7.refs_3_ = bf16[224,512]{1,0:T(8,128)(2,1)S(1)} collective-permute-done((bf16[224,512]{1,0:T(8,128)(2,1)S(1)}, bf16[224,512]{1,0:T(8,128)(2,1)S(1)}, u32[]{:S(2)}, u32[]{:S(2)}) %collective-permute-start.7) | collective-permute-done | bytes 229408 | tf_op jit(solution)/shard_map/ppermute | solution.py:435
  13.7 0.9 %block.1 = (bf16[256,512]{1,0:T(8,128)(2,1)S(1)}, f32[256,512]{1,0:T(8,128)S(1)}) custom-call(bf16[256,512]{1,0:T(8,128)(2,1)S(1)} %get-tuple-element.34.inner_ref, f32[256,512]{1,0:T(8,128)S(1)} %get-tuple-element.35.totals_ref, f32[3,3,512]{2,1,0:T(4,128)S(1)} %get-tuple-element.29.taps_ref, ...), custom_call_target="tpu_custom_call", output_to_operand_aliasing={{0}: (0, {}), {1}: (1, {})} | custom-call | bytes 3524608 | tf_op jit(solution)/shard_map/block/pallas_call | solution.py:20
  14.6 0.3 %collective-permute-done.8.refs_1_ = bf16[40,512]{1,0:T(8,128)(2,1)S(1)} collective-permute-done((bf16[40,512]{1,0:T(8,128)(2,1)S(1)}, bf16[40,512]{1,0:T(8,128)(2,1)S(1)}, u32[]{:S(2)}, u32[]{:S(2)}) %collective-permute-start.8) | collective-permute-done | bytes 40992 | tf_op jit(solution)/shard_map/ppermute | solution.py:450
  14.8 1.1 %last.1 = bf16[256,512]{1,0:T(8,128)(2,1)} custom-call(bf16[256,512]{1,0:T(8,128)(2,1)} %first.1.before_ref, bf16[256,512]{1,0:T(8,128)(2,1)S(1)} %get-tuple-element.41.inner_ref, f32[256,512]{1,0:T(8,128)S(1)} %get-tuple-element.42.totals_ref, f32[3,3,512]{2,1,0:T(4,128)S(1)} %get-tuple-element.29.taps_ref, ...), custom_call_target="tpu_custom_call", output_to_operand_aliasing={{}: (0, {})} | custom-call | bytes 2983936 | tf_op jit(solution)/shard_map/last/pallas_call | solution.py:20
  (3 shorter events, 0.1 us)
Async XLA Ops:
  0.0 1.7 %collective-permute-start = (bf16[256,512]{1,0:T(8,128)(2,1)}, bf16[256,512]{1,0:T(8,128)(2,1)S(1)}, u32[]{:S(2)}, u32[]{:S(2)}) collective-permute-start(bf16[256,512]{1,0:T(8,128)(2,1)} %bitcast.3), channel_id=1, source_target_pairs={{0,8},{8,0},{16,24},{24,16},{1,9},{9,1},{17,25},{25,17},{2,10},{10... | collective-permute-start | bytes 786440 | tf_op jit(solution)/shard_map/ppermute | solution.py:376
  1.8 4.4 %collective-permute-start.1 = (bf16[64,512]{1,0:T(8,128)(2,1)S(1)}, bf16[64,512]{1,0:T(8,128)(2,1)S(1)}, u32[]{:S(2)}, u32[]{:S(2)}) collective-permute-start(bf16[64,512]{1,0:T(8,128)(2,1)S(1)} %column.1), channel_id=1, source_target_pairs={{0,1},{1,0},{2,3},{3,2},{4,5},{5,4},{6,7},{7,6},{8,12},{9,10},{10,... | collective-permute-start | bytes 196616 | tf_op jit(solution)/shard_map/ppermute | solution.py:431
  3.5 5.3 %collective-permute-start.4 = (bf16[64,512]{1,0:T(8,128)(2,1)S(1)}, bf16[64,512]{1,0:T(8,128)(2,1)S(1)}, u32[]{:S(2)}, u32[]{:S(2)}) collective-permute-start(bf16[64,512]{1,0:T(8,128)(2,1)S(1)} %column.1), channel_id=1, source_target_pairs={{0,17},{1,16},{2,19},{3,18},{4,21},{5,20},{6,23},{7,22},{8,28},{9,... | collective-permute-start | bytes 196616 | tf_op jit(solution)/shard_map/ppermute | solution.py:431
  4.2 6.5 %collective-permute-start.6 = (bf16[32,512]{1,0:T(8,128)(2,1)S(1)}, bf16[32,512]{1,0:T(8,128)(2,1)S(1)}, u32[]{:S(2)}, u32[]{:S(2)}) collective-permute-start(bf16[32,512]{1,0:T(8,128)(2,1)S(1)} %get-tuple-element.39), channel_id=1, source_target_pairs={{0,16},{8,24},{16,0},{24,8},{1,17},{9,25},{17,1},{25,9},{2,18},{10... | collective-permute-start | bytes 98312 | tf_op jit(solution)/shard_map/ppermute | solution.py:434
  5.6 8.1 %collective-permute-start.7 = (bf16[224,512]{1,0:T(8,128)(2,1)S(1)}, bf16[224,512]{1,0:T(8,128)(2,1)S(1)}, u32[]{:S(2)}, u32[]{:S(2)}) collective-permute-start(bf16[224,512]{1,0:T(8,128)(2,1)S(1)} %get-tuple-element.40), channel_id=1, source_target_pairs={{0,16},{8,24},{16,0},{24,8},{1,17},{9,25},{17,1},{25,9},{2,18},{10... | collective-permute-start | bytes 688136 | tf_op jit(solution)/shard_map/ppermute | solution.py:435
  6.3 2.7 %collective-permute-start.2 = (bf16[32,512]{1,0:T(8,128)(2,1)S(1)}, bf16[32,512]{1,0:T(8,128)(2,1)S(1)}, u32[]{:S(2)}, u32[]{:S(2)}) collective-permute-start(bf16[32,512]{1,0:T(8,128)(2,1)S(1)} %get-tuple-element.28), channel_id=1, source_target_pairs={{0,8},{8,0},{16,24},{24,16},{1,9},{9,1},{17,25},{25,17},{2,10},{10... | collective-permute-start | bytes 98312 | tf_op jit(solution)/shard_map/ppermute | solution.py:440
  8.8 1.9 %collective-permute-start.5 = (bf16[32,512]{1,0:T(8,128)(2,1)S(1)}, bf16[32,512]{1,0:T(8,128)(2,1)S(1)}, u32[]{:S(2)}, u32[]{:S(2)}) collective-permute-start(bf16[32,512]{1,0:T(8,128)(2,1)S(1)} %get-tuple-element.37), channel_id=1, source_target_pairs={{0,8},{8,0},{16,24},{24,16},{1,9},{9,1},{17,25},{25,17},{2,10},{10... | collective-permute-start | bytes 98312 | tf_op jit(solution)/shard_map/ppermute | solution.py:448
  9.1 4.1 %collective-permute-start.3 = (bf16[40,512]{1,0:T(8,128)(2,1)S(1)}, bf16[40,512]{1,0:T(8,128)(2,1)S(1)}, u32[]{:S(2)}, u32[]{:S(2)}) collective-permute-start(bf16[40,512]{1,0:T(8,128)(2,1)S(1)} %border.1), channel_id=1, source_target_pairs={{0,4},{4,0},{1,5},{5,1},{2,6},{6,2},{3,7},{7,3},{8,12},{12,8},{9,1... | collective-permute-start | bytes 122888 | tf_op jit(solution)/shard_map/ppermute | solution.py:443
  10.7 4.1 %collective-permute-start.8 = (bf16[40,512]{1,0:T(8,128)(2,1)S(1)}, bf16[40,512]{1,0:T(8,128)(2,1)S(1)}, u32[]{:S(2)}, u32[]{:S(2)}) collective-permute-start(bf16[40,512]{1,0:T(8,128)(2,1)S(1)} %before.1), channel_id=1, source_target_pairs={{0,4},{4,0},{1,5},{5,1},{2,6},{6,2},{3,7},{7,3},{8,12},{12,8},{9,1... | collective-permute-start | bytes 122888 | tf_op jit(solution)/shard_map/ppermute | solution.py:450

commit v21 on v20

--- a/solution.py
+++ b/solution.py
@@ -145,7 +145,7 @@
             outs[2 * d - 1][:, span] = jnp.concatenate(tiles[rounds_h:]).astype(BF16)
 
 
-def own_kernel(frames, rows, cols, partner_ref, table_ref, field_ref, mine_ref):
+def own_kernel(frames, rows, cols, after_ref, partner_ref, table_ref, field_ref, mine_ref):
     for lane in range(0, mine_ref.shape[1], LANES):
         span = slice(lane, lane + LANES)
         totals = with_partner(frames, rows, cols, 0, field_ref, partner_ref, table_ref, span)
@@ -170,8 +170,8 @@
     return totals
 
 
-def side_kernel(frames, rows, first, table_ref, *refs):
-    *arrived, own_ref, other_ref = refs
+def side_kernel(frames, rows, first, count, table_ref, *refs):
+    arrived, (own_ref, other_ref) = refs[:count], refs[-2:]
     _, lower, upper = position("width")
     exists = jnp.where(on_right(), upper, lower)
     for lane in range(0, own_ref.shape[1], LANES):
@@ -407,14 +407,6 @@
         [partner, table] + fields[1:],
         2 * (chips - 1) * frames * x.size,
     )
-    (mine,) = call(
-        functools.partial(own_kernel, frames, rows, cols),
-        "own",
-        [field],
-        [],
-        [partner, table, fields[0]],
-        2 * frames * x.size,
-    )
     columns, firsts, rests = [], [], []
     for d in range(chips):
         route = []
@@ -436,14 +428,27 @@
 
     swap = [(i, i ^ 1) for i in range(n_t)]
     both = [shape((lines, chans), F32), shape((lines, chans), BF16)]
-    own, other = call(functools.partial(side_kernel, frames, rows, 0), "side", both, [], [table, columns[0]], LATER)
+    own, other = call(functools.partial(side_kernel, frames, rows, 0, 1), "side", both, [], [table, columns[0]], LATER)
+    (mine,) = call(
+        functools.partial(own_kernel, frames, rows, cols),
+        "own",
+        [field],
+        [],
+        [own, partner, table, fields[0]],
+        2 * frames * x.size,
+    )
     other = lax.ppermute(other, "tm", swap)
     end = [shape((frames * cols + 2 * frames, chans), BF16)] * len(h_rounds)
     ends = call(functools.partial(border_kernel, frames, rows, cols), "border", end, [], [mine, own, other])
     ends = [lax.ppermute(e, "height", pairs) for e, pairs in zip(ends, h_rounds)]
     if chips > 1:
         own_d, other_d = call(
-            functools.partial(side_kernel, frames, rows, 1), "beside", both, [], [table] + columns[1:], LATER
+            functools.partial(side_kernel, frames, rows, 1, chips - 1),
+            "beside",
+            both,
+            [],
+            [table] + columns[1:] + [mine],
+            LATER,
         )
         other_d = lax.ppermute(other_d, "tm", swap)
         earlier = call(functools.partial(before_kernel, frames, rows, cols), "before", end, [], [own_d, other_d] + firsts)

time: 16.1 us -> 15.9 us (0.988)
  the two profiles are of different devices: /device:TPU:4 before, /device:TPU:0 now
where the time goes in v21:
time: 15.9 us; the launch traced here: 15.7 us
  starting transfers between devices  9.32 us (59%)
  Pallas kernels  4.47 us (28%)
  waiting for transfers between devices  1.78 us (11%)
    pallas_call x13, Pallas kernels, call(): pl.pallas_call(kernel, out_shape=tuple(outs), in_specs=[HBM] * far + [VME...  4.47 us
    ppermute x2, starting transfers between devices, body(): columns.append(lax.ppermute(column, ('tm', 'height', 'width'), route))  4.22 us
    ppermute x2, starting transfers between devices, body(): lax.ppermute(e, 'height', pairs)  2.41 us
    ppermute x1, starting transfers between devices, body(): rests.append(lax.ppermute(sent[2 * d - 1], 'tm', route))  1.41 us
    ppermute x2, waiting for transfers between devices, body(): lax.ppermute(e, 'height', pairs)  0.92 us
    ppermute x1, starting transfers between devices, body(): firsts.append(lax.ppermute(sent[2 * d - 2], 'tm', route))  0.69 us
    ppermute x2, waiting for transfers between devices, body(): columns.append(lax.ppermute(column, ('tm', 'height', 'width'), route))  0.54 us
    ppermute x1, starting transfers between devices, body(): partner = lax.ppermute(x, 'tm', [(i, i ^ 1) for i in range(n_t)])  0.45 us
  transfers between devices with their start and end apart: 9, of which 4 were waited for; matrix products, arithmetic and copies ran while one was open for 0% of the time, Pallas kernels for 28%

profile of v21, /device:TPU:0, one launch (start us, length us, event | category | flops | bytes accessed | tf_op | source)
XLA Modules:
  0.0 15.7 jit_solution(13506488873147901320)
XLA Ops:
  0.0 0.5 %collective-permute-start = (bf16[256,512]{1,0:T(8,128)(2,1)}, bf16[256,512]{1,0:T(8,128)(2,1)S(1)}, u32[]{:S(2)}, u32[]{:S(2)}) collective-permute-start(bf16[256,512]{1,0:T(8,128)(2,1)} %bitcast.3), channel_id=1, source_target_pairs={{0,8},{8,0},{16,24},{24,16},{1,9},{9,1},{17,25},{25,17},{2,10},{10... | collective-permute-start | bytes 786440 | tf_op jit(solution)/shard_map/ppermute | solution.py:376
  0.5 1.5 %early.1 = (bf16[256,512]{1,0:T(8,128)(2,1)S(1)}, bf16[512,512]{1,0:T(8,128)(2,1)S(1)}, f32[3,3,512]{2,1,0:T(4,128)S(1)}, bf16[512,512]{1,0:T(8,128)(2,1)S(1)}, ...) custom-call(bf16[16,512]{1,0:T(8,128)(2,1)} %refs_0_.1, ...), custom_call_target="tpu_custom_call" | custom-call | bytes 5232640 | tf_op jit(solution)/shard_map/early/pallas_call | solution.py:20
  2.0 0.0 collective-permute-done.partner_ref
  2.0 0.1 column.1
  2.1 2.8 %collective-permute-start.1 = (bf16[64,512]{1,0:T(8,128)(2,1)S(1)}, bf16[64,512]{1,0:T(8,128)(2,1)S(1)}, u32[]{:S(2)}, u32[]{:S(2)}) collective-permute-start(bf16[64,512]{1,0:T(8,128)(2,1)S(1)} %column.1), channel_id=1, source_target_pairs={{0,1},{1,0},{2,3},{3,2},{4,5},{5,4},{6,7},{7,6},{8,12},{9,10},{10,... | collective-permute-start | bytes 196616 | tf_op jit(solution)/shard_map/ppermute | solution.py:423
  4.9 1.4 %collective-permute-start.4 = (bf16[64,512]{1,0:T(8,128)(2,1)S(1)}, bf16[64,512]{1,0:T(8,128)(2,1)S(1)}, u32[]{:S(2)}, u32[]{:S(2)}) collective-permute-start(bf16[64,512]{1,0:T(8,128)(2,1)S(1)} %column.1), channel_id=1, source_target_pairs={{0,17},{1,16},{2,19},{3,18},{4,21},{5,20},{6,23},{7,22},{8,28},{9,... | collective-permute-start | bytes 196616 | tf_op jit(solution)/shard_map/ppermute | solution.py:423
  6.3 0.2 %later.1 = (bf16[32,512]{1,0:T(8,128)(2,1)S(1)}, bf16[224,512]{1,0:T(8,128)(2,1)S(1)}) custom-call(bf16[256,512]{1,0:T(8,128)(2,1)S(1)} %collective-permute-done.partner_ref, f32[24,8,512]{2,1,0:T(8,128)S(1)} %get-tuple-element.24.table_ref, f32[256,512]{1,0:T(8,128)S(1)} %get-tuple-element.38.refs_0_), custom_call_target="tpu_custom_call" | custom-call | flops 1048576 | bytes 1441792 | tf_op jit(solution)/shard_map/later/pallas_call | solution.py:20
  6.5 0.7 %collective-permute-start.6 = (bf16[32,512]{1,0:T(8,128)(2,1)S(1)}, bf16[32,512]{1,0:T(8,128)(2,1)S(1)}, u32[]{:S(2)}, u32[]{:S(2)}) collective-permute-start(bf16[32,512]{1,0:T(8,128)(2,1)S(1)} %get-tuple-element.39), channel_id=1, source_target_pairs={{0,16},{8,24},{16,0},{24,8},{1,17},{9,25},{17,1},{25,9},{2,18},{10... | collective-permute-start | bytes 98312 | tf_op jit(solution)/shard_map/ppermute | solution.py:426
  7.2 1.4 %collective-permute-start.7 = (bf16[224,512]{1,0:T(8,128)(2,1)S(1)}, bf16[224,512]{1,0:T(8,128)(2,1)S(1)}, u32[]{:S(2)}, u32[]{:S(2)}) collective-permute-start(bf16[224,512]{1,0:T(8,128)(2,1)S(1)} %get-tuple-element.40), channel_id=1, source_target_pairs={{0,16},{8,24},{16,0},{24,8},{1,17},{9,25},{17,1},{25,9},{2,18},{10... | collective-permute-start | bytes 688136 | tf_op jit(solution)/shard_map/ppermute | solution.py:427
  8.6 0.0 collective-permute-done.1.refs_0_
  8.6 0.1 side.1
  8.7 0.1 collective-permute-start.2
  8.8 0.2 %own.1.mine_ref.refs_1_ = f32[256,512]{1,0:T(8,128)S(1)} custom-call(f32[32,512]{1,0:T(8,128)S(1)} %get-tuple-element.26.after_ref.own_ref, bf16[256,512]{1,0:T(8,128)(2,1)S(1)} %collective-permute-done.partner_ref, f32[24,8,512]{2,1,0:T(8,128)S(1)} %get-tuple-element.24.table_ref, f32[256,512]{1,0:T(8,128)S(1)} %get-tuple-element.27.field_ref), custom_call_target="tpu_custom_call" | custom-call | flops 1048576 | bytes 1769472 | tf_op jit(solution)/shard_map/own/pallas_call | solution.py:20
  8.9 0.5 %collective-permute-done.4.refs_0_ = bf16[64,512]{1,0:T(8,128)(2,1)S(1)} collective-permute-done((bf16[64,512]{1,0:T(8,128)(2,1)S(1)}, bf16[64,512]{1,0:T(8,128)(2,1)S(1)}, u32[]{:S(2)}, u32[]{:S(2)}) %collective-permute-start.4) | collective-permute-done | bytes 65568 | tf_op jit(solution)/shard_map/ppermute | solution.py:423
  9.5 0.1 beside.1
  9.6 0.1 collective-permute-start.5
  9.6 0.3 %collective-permute-done.2.other_ref = bf16[32,512]{1,0:T(8,128)(2,1)S(1)} collective-permute-done((bf16[32,512]{1,0:T(8,128)(2,1)S(1)}, bf16[32,512]{1,0:T(8,128)(2,1)S(1)}, u32[]{:S(2)}, u32[]{:S(2)}) %collective-permute-start.2) | collective-permute-done | bytes 32800 | tf_op jit(solution)/shard_map/ppermute | solution.py:440
  10.0 1.6 %collective-permute-start.3 = (bf16[40,512]{1,0:T(8,128)(2,1)S(1)}, bf16[40,512]{1,0:T(8,128)(2,1)S(1)}, u32[]{:S(2)}, u32[]{:S(2)}) collective-permute-start(bf16[40,512]{1,0:T(8,128)(2,1)S(1)} %border.1), channel_id=1, source_target_pairs={{0,4},{4,0},{1,5},{5,1},{2,6},{6,2},{3,7},{7,3},{8,12},{12,8},{9,1... | collective-permute-start | bytes 122888 | tf_op jit(solution)/shard_map/ppermute | solution.py:443
  11.6 0.0 collective-permute-done.6.refs_2_.refs_0_
  11.6 0.0 collective-permute-done.5.refs_1_.other_ref
  11.6 0.9 %collective-permute-start.8 = (bf16[40,512]{1,0:T(8,128)(2,1)S(1)}, bf16[40,512]{1,0:T(8,128)(2,1)S(1)}, u32[]{:S(2)}, u32[]{:S(2)}) collective-permute-start(bf16[40,512]{1,0:T(8,128)(2,1)S(1)} %before.1), channel_id=1, source_target_pairs={{0,4},{4,0},{1,5},{5,1},{2,6},{6,2},{3,7},{7,3},{8,12},{12,8},{9,1... | collective-permute-start | bytes 122888 | tf_op jit(solution)/shard_map/ppermute | solution.py:455
  12.5 0.4 %gate.1.gate_ref = f32[256,512]{1,0:T(8,128)S(1)} custom-call(bf16[256,512]{1,0:T(8,128)(2,1)S(1)} %get-tuple-element.30.x_ref, bf16[512,512]{1,0:T(8,128)(2,1)S(1)} %get-tuple-element.31.w_ref), custom_call_target="tpu_custom_call" | custom-call | bytes 1310720 | tf_op jit(solution)/shard_map/gate/pallas_call | solution.py:20
  12.9 0.8 %inner.1 = (bf16[256,512]{1,0:T(8,128)(2,1)S(1)}, f32[256,512]{1,0:T(8,128)S(1)}) custom-call(f32[256,512]{1,0:T(8,128)S(1)} %own.1.mine_ref.refs_1_, f32[32,512]{1,0:T(8,128)S(1)} %get-tuple-element.26.after_ref.own_ref, bf16[32,512]{1,0:T(8,128)(2,1)S(1)} %collective-permute-done.2.other_ref, f32[3,3,512]{2,1,0:T(4,128)S(1)} %get-tuple-element.29.taps_ref, ...), custom_call_target="tpu_custom_call" | custom-call | flops 268435456 | bytes 3000320 | tf_op jit(solution)/shard_map/inner/pallas_call | solution.py:20
  13.6 0.4 %collective-permute-done.3.refs_0_ = bf16[40,512]{1,0:T(8,128)(2,1)S(1)} collective-permute-done((bf16[40,512]{1,0:T(8,128)(2,1)S(1)}, bf16[40,512]{1,0:T(8,128)(2,1)S(1)}, u32[]{:S(2)}, u32[]{:S(2)}) %collective-permute-start.3) | collective-permute-done | bytes 40992 | tf_op jit(solution)/shard_map/ppermute | solution.py:443
  14.1 1.1 %first.1.before_ref = bf16[256,512]{1,0:T(8,128)(2,1)} custom-call(bf16[256,512]{1,0:T(8,128)(2,1)S(1)} %get-tuple-element.34.inner_ref, f32[256,512]{1,0:T(8,128)S(1)} %get-tuple-element.35.totals_ref, f32[3,3,512]{2,1,0:T(4,128)S(1)} %get-tuple-element.29.taps_ref, f32[256,512]{1,0:T(8,128)S(1)} %gate.1.gate_ref, ...), custom_call_target="tpu_custom_call" | custom-call | bytes 2680832 | tf_op jit(solution)/shard_map/first/pallas_call | solution.py:20
  15.1 0.0 collective-permute-done.7.refs_3_
  15.2 0.5 %collective-permute-done.8.refs_1_ = bf16[40,512]{1,0:T(8,128)(2,1)S(1)} collective-permute-done((bf16[40,512]{1,0:T(8,128)(2,1)S(1)}, bf16[40,512]{1,0:T(8,128)(2,1)S(1)}, u32[]{:S(2)}, u32[]{:S(2)}) %collective-permute-start.8) | collective-permute-done | bytes 40992 | tf_op jit(solution)/shard_map/ppermute | solution.py:455
  (4 shorter events, 0.1 us)
Async XLA Ops:
  0.0 2.0 %collective-permute-start = (bf16[256,512]{1,0:T(8,128)(2,1)}, bf16[256,512]{1,0:T(8,128)(2,1)S(1)}, u32[]{:S(2)}, u32[]{:S(2)}) collective-permute-start(bf16[256,512]{1,0:T(8,128)(2,1)} %bitcast.3), channel_id=1, source_target_pairs={{0,8},{8,0},{16,24},{24,16},{1,9},{9,1},{17,25},{25,17},{2,10},{10... | collective-permute-start | bytes 786440 | tf_op jit(solution)/shard_map/ppermute | solution.py:376
  2.1 6.5 %collective-permute-start.1 = (bf16[64,512]{1,0:T(8,128)(2,1)S(1)}, bf16[64,512]{1,0:T(8,128)(2,1)S(1)}, u32[]{:S(2)}, u32[]{:S(2)}) collective-permute-start(bf16[64,512]{1,0:T(8,128)(2,1)S(1)} %column.1), channel_id=1, source_target_pairs={{0,1},{1,0},{2,3},{3,2},{4,5},{5,4},{6,7},{7,6},{8,12},{9,10},{10,... | collective-permute-start | bytes 196616 | tf_op jit(solution)/shard_map/ppermute | solution.py:423
  4.9 4.6 %collective-permute-start.4 = (bf16[64,512]{1,0:T(8,128)(2,1)S(1)}, bf16[64,512]{1,0:T(8,128)(2,1)S(1)}, u32[]{:S(2)}, u32[]{:S(2)}) collective-permute-start(bf16[64,512]{1,0:T(8,128)(2,1)S(1)} %column.1), channel_id=1, source_target_pairs={{0,17},{1,16},{2,19},{3,18},{4,21},{5,20},{6,23},{7,22},{8,28},{9,... | collective-permute-start | bytes 196616 | tf_op jit(solution)/shard_map/ppermute | solution.py:423
  6.5 5.1 %collective-permute-start.6 = (bf16[32,512]{1,0:T(8,128)(2,1)S(1)}, bf16[32,512]{1,0:T(8,128)(2,1)S(1)}, u32[]{:S(2)}, u32[]{:S(2)}) collective-permute-start(bf16[32,512]{1,0:T(8,128)(2,1)S(1)} %get-tuple-element.39), channel_id=1, source_target_pairs={{0,16},{8,24},{16,0},{24,8},{1,17},{9,25},{17,1},{25,9},{2,18},{10... | collective-permute-start | bytes 98312 | tf_op jit(solution)/shard_map/ppermute | solution.py:426
  7.2 8.0 %collective-permute-start.7 = (bf16[224,512]{1,0:T(8,128)(2,1)S(1)}, bf16[224,512]{1,0:T(8,128)(2,1)S(1)}, u32[]{:S(2)}, u32[]{:S(2)}) collective-permute-start(bf16[224,512]{1,0:T(8,128)(2,1)S(1)} %get-tuple-element.40), channel_id=1, source_target_pairs={{0,16},{8,24},{16,0},{24,8},{1,17},{9,25},{17,1},{25,9},{2,18},{10... | collective-permute-start | bytes 688136 | tf_op jit(solution)/shard_map/ppermute | solution.py:427
  8.7 1.3 %collective-permute-start.2 = (bf16[32,512]{1,0:T(8,128)(2,1)S(1)}, bf16[32,512]{1,0:T(8,128)(2,1)S(1)}, u32[]{:S(2)}, u32[]{:S(2)}) collective-permute-start(bf16[32,512]{1,0:T(8,128)(2,1)S(1)} %get-tuple-element.28), channel_id=1, source_target_pairs={{0,8},{8,0},{16,24},{24,16},{1,9},{9,1},{17,25},{25,17},{2,10},{10... | collective-permute-start | bytes 98312 | tf_op jit(solution)/shard_map/ppermute | solution.py:440
  9.6 2.0 %collective-permute-start.5 = (bf16[32,512]{1,0:T(8,128)(2,1)S(1)}, bf16[32,512]{1,0:T(8,128)(2,1)S(1)}, u32[]{:S(2)}, u32[]{:S(2)}) collective-permute-start(bf16[32,512]{1,0:T(8,128)(2,1)S(1)} %get-tuple-element.37), channel_id=1, source_target_pairs={{0,8},{8,0},{16,24},{24,16},{1,9},{9,1},{17,25},{25,17},{2,10},{10... | collective-permute-start | bytes 98312 | tf_op jit(solution)/shard_map/ppermute | solution.py:453
  10.0 4.1 %collective-permute-start.3 = (bf16[40,512]{1,0:T(8,128)(2,1)S(1)}, bf16[40,512]{1,0:T(8,128)(2,1)S(1)}, u32[]{:S(2)}, u32[]{:S(2)}) collective-permute-start(bf16[40,512]{1,0:T(8,128)(2,1)S(1)} %border.1), channel_id=1, source_target_pairs={{0,4},{4,0},{1,5},{5,1},{2,6},{6,2},{3,7},{7,3},{8,12},{12,8},{9,1... | collective-permute-start | bytes 122888 | tf_op jit(solution)/shard_map/ppermute | solution.py:443
  11.6 4.1 %collective-permute-start.8 = (bf16[40,512]{1,0:T(8,128)(2,1)S(1)}, bf16[40,512]{1,0:T(8,128)(2,1)S(1)}, u32[]{:S(2)}, u32[]{:S(2)}) collective-permute-start(bf16[40,512]{1,0:T(8,128)(2,1)S(1)} %before.1), channel_id=1, source_target_pairs={{0,4},{4,0},{1,5},{5,1},{2,6},{6,2},{3,7},{7,3},{8,12},{12,8},{9,1... | collective-permute-start | bytes 122888 | tf_op jit(solution)/shard_map/ppermute | solution.py:455

commit v22 on v21

--- a/solution.py
+++ b/solution.py
@@ -141,8 +141,8 @@
             span = slice(lane, lane + LANES)
             totals = with_partner(frames, rows, cols, d, field, partner_ref, table_ref, span)
             tiles = reordered([jnp.concatenate([t[r] for t in totals]) for r in range(rows)], rounds_h)
-            outs[2 * d - 2][:, span] = jnp.concatenate(tiles[:rounds_h]).astype(BF16)
-            outs[2 * d - 1][:, span] = jnp.concatenate(tiles[rounds_h:]).astype(BF16)
+            outs[2 * d - 2][:, span] = jnp.concatenate(tiles[: rounds_h + 1]).astype(BF16)
+            outs[2 * d - 1][:, span] = jnp.concatenate(tiles[rounds_h + 1 :]).astype(BF16)
 
 
 def own_kernel(frames, rows, cols, after_ref, partner_ref, table_ref, field_ref, mine_ref):
@@ -208,14 +208,14 @@
 
 
 def before_kernel(frames, rows, cols, own_ref, other_ref, *refs):
-    rounds_h = refs[0].shape[0] // (frames * cols)
+    rounds_h = refs[0].shape[0] // (frames * cols) - 1
     firsts, outs = refs[:-rounds_h], refs[-rounds_h:]
     size = frames * cols
     odd, _, _ = position("height")
     corners = end_corners(frames, rows, own_ref, other_ref)
     line = 0.0
     for d, ref in enumerate(firsts, 1):
-        line = line + later(d, ref[...].astype(F32))
+        line = line + later(d, ref[: rounds_h * size].astype(F32))
     for k, out in enumerate(outs):
         if rounds_h > 1:
             pair = line[:size], line[size:]
@@ -292,8 +292,8 @@
             low, high = both_sides(own_ref[:, span], other_ref[:, span].astype(F32))
             lines = [jnp.zeros((size, LANES), F32)] * rows
             for d, (first, rest) in enumerate(zip(firsts, rests), 1):
-                more = [first[i * size : (i + 1) * size, span].astype(F32) for i in range(rounds_h)]
-                more += [rest[i * size : (i + 1) * size, span].astype(F32) for i in range(rows - rounds_h)]
+                more = [first[i * size : (i + 1) * size, span].astype(F32) for i in range(rounds_h + 1)]
+                more += [rest[i * size : (i + 1) * size, span].astype(F32) for i in range(rows - rounds_h - 1)]
                 more = reordered(more, rounds_h, back=True)
                 lines = [line + later(d, other) for line, other in zip(lines, more)]
             for t in range(frames):
@@ -398,7 +398,7 @@
         [pltpu.VMEM((block, LANES), F32)],
         [partner, side],
     )
-    parts = [shape((n * frames * cols, chans), BF16) for n in (len(h_rounds), rows - len(h_rounds))]
+    parts = [shape((n * frames * cols, chans), BF16) for n in (len(h_rounds) + 1, rows - len(h_rounds) - 1)]
     sent = call(
         functools.partial(later_kernel, frames, rows, cols, len(h_rounds)),
         "later",

time: 15.9 us -> 15.9 us (level)
  waiting for transfers between devices: 1.78 us -> 1.07 us
  starting transfers between devices: 9.32 us -> 10 us
    ppermute x2, waiting for transfers between devices: 0.92 us -> 0.2 us  [body(): lax.ppermute(e, 'height', pairs)]
    ppermute x2, starting transfers between devices: 2.41 us -> 3.11 us  [body(): lax.ppermute(e, 'height', pairs)]
  transfers between devices with their start and end apart: 9 -> 9, of which waited for: 4 -> 3; matrix products, arithmetic and copies ran while one was open for 0% -> 0% of each run, Pallas kernels for 28% -> 28%
where the time goes in v22:
time: 15.9 us; the launch traced here: 15.7 us
  starting transfers between devices  10 us (63%)
  Pallas kernels  4.48 us (28%)
  waiting for transfers between devices  1.07 us (7%)
    pallas_call x13, Pallas kernels, call(): pl.pallas_call(kernel, out_shape=tuple(outs), in_specs=[HBM] * far + [VME...  4.48 us
    ppermute x2, starting transfers between devices, body(): columns.append(lax.ppermute(column, ('tm', 'height', 'width'), route))  4.22 us
    ppermute x2, starting transfers between devices, body(): lax.ppermute(e, 'height', pairs)  3.11 us
    ppermute x1, starting transfers between devices, body(): rests.append(lax.ppermute(sent[2 * d - 1], 'tm', route))  1.41 us
    ppermute x1, starting transfers between devices, body(): firsts.append(lax.ppermute(sent[2 * d - 2], 'tm', route))  0.69 us
    ppermute x2, waiting for transfers between devices, body(): columns.append(lax.ppermute(column, ('tm', 'height', 'width'), route))  0.54 us
    ppermute x1, starting transfers between devices, body(): partner = lax.ppermute(x, 'tm', [(i, i ^ 1) for i in range(n_t)])  0.45 us
  transfers between devices with their start and end apart: 9, of which 3 were waited for; matrix products, arithmetic and copies ran while one was open for 0% of the time, Pallas kernels for 28%

profile of v22, /device:TPU:0, one launch (start us, length us, event | category | flops | bytes accessed | tf_op | source)
XLA Modules:
  0.0 15.7 jit_solution(15368368224116431109)
XLA Ops:
  0.0 0.5 %collective-permute-start = (bf16[256,512]{1,0:T(8,128)(2,1)}, bf16[256,512]{1,0:T(8,128)(2,1)S(1)}, u32[]{:S(2)}, u32[]{:S(2)}) collective-permute-start(bf16[256,512]{1,0:T(8,128)(2,1)} %bitcast.3), channel_id=1, source_target_pairs={{0,8},{8,0},{16,24},{24,16},{1,9},{9,1},{17,25},{25,17},{2,10},{10... | collective-permute-start | bytes 786440 | tf_op jit(solution)/shard_map/ppermute | solution.py:376
  0.5 1.5 %early.1 = (bf16[256,512]{1,0:T(8,128)(2,1)S(1)}, bf16[512,512]{1,0:T(8,128)(2,1)S(1)}, f32[3,3,512]{2,1,0:T(4,128)S(1)}, bf16[512,512]{1,0:T(8,128)(2,1)S(1)}, ...) custom-call(bf16[16,512]{1,0:T(8,128)(2,1)} %refs_0_.1, ...), custom_call_target="tpu_custom_call" | custom-call | bytes 5232640 | tf_op jit(solution)/shard_map/early/pallas_call | solution.py:20
  2.0 0.0 collective-permute-done.partner_ref
  2.0 0.1 column.1
  2.1 2.8 %collective-permute-start.1 = (bf16[64,512]{1,0:T(8,128)(2,1)S(1)}, bf16[64,512]{1,0:T(8,128)(2,1)S(1)}, u32[]{:S(2)}, u32[]{:S(2)}) collective-permute-start(bf16[64,512]{1,0:T(8,128)(2,1)S(1)} %column.1), channel_id=1, source_target_pairs={{0,1},{1,0},{2,3},{3,2},{4,5},{5,4},{6,7},{7,6},{8,12},{9,10},{10,... | collective-permute-start | bytes 196616 | tf_op jit(solution)/shard_map/ppermute | solution.py:423
  4.9 1.4 %collective-permute-start.4 = (bf16[64,512]{1,0:T(8,128)(2,1)S(1)}, bf16[64,512]{1,0:T(8,128)(2,1)S(1)}, u32[]{:S(2)}, u32[]{:S(2)}) collective-permute-start(bf16[64,512]{1,0:T(8,128)(2,1)S(1)} %column.1), channel_id=1, source_target_pairs={{0,17},{1,16},{2,19},{3,18},{4,21},{5,20},{6,23},{7,22},{8,28},{9,... | collective-permute-start | bytes 196616 | tf_op jit(solution)/shard_map/ppermute | solution.py:423
  6.3 0.2 %later.1 = (bf16[64,512]{1,0:T(8,128)(2,1)S(1)}, bf16[192,512]{1,0:T(8,128)(2,1)S(1)}) custom-call(bf16[256,512]{1,0:T(8,128)(2,1)S(1)} %collective-permute-done.partner_ref, f32[24,8,512]{2,1,0:T(8,128)S(1)} %get-tuple-element.24.table_ref, f32[256,512]{1,0:T(8,128)S(1)} %get-tuple-element.38.refs_0_), custom_call_target="tpu_custom_call" | custom-call | flops 1048576 | bytes 1441792 | tf_op jit(solution)/shard_map/later/pallas_call | solution.py:20
  6.5 0.7 %collective-permute-start.6 = (bf16[64,512]{1,0:T(8,128)(2,1)S(1)}, bf16[64,512]{1,0:T(8,128)(2,1)S(1)}, u32[]{:S(2)}, u32[]{:S(2)}) collective-permute-start(bf16[64,512]{1,0:T(8,128)(2,1)S(1)} %get-tuple-element.39), channel_id=1, source_target_pairs={{0,16},{8,24},{16,0},{24,8},{1,17},{9,25},{17,1},{25,9},{2,18},{10... | collective-permute-start | bytes 196616 | tf_op jit(solution)/shard_map/ppermute | solution.py:426
  7.2 1.4 %collective-permute-start.7 = (bf16[192,512]{1,0:T(8,128)(2,1)S(1)}, bf16[192,512]{1,0:T(8,128)(2,1)S(1)}, u32[]{:S(2)}, u32[]{:S(2)}) collective-permute-start(bf16[192,512]{1,0:T(8,128)(2,1)S(1)} %get-tuple-element.40), channel_id=1, source_target_pairs={{0,16},{8,24},{16,0},{24,8},{1,17},{9,25},{17,1},{25,9},{2,18},{10... | collective-permute-start | bytes 589832 | tf_op jit(solution)/shard_map/ppermute | solution.py:427
  8.6 0.0 collective-permute-done.1.refs_0_
  8.6 0.1 side.1
  8.7 0.1 collective-permute-start.2
  8.8 0.2 %own.1.mine_ref.refs_1_ = f32[256,512]{1,0:T(8,128)S(1)} custom-call(f32[32,512]{1,0:T(8,128)S(1)} %get-tuple-element.26.after_ref.own_ref, bf16[256,512]{1,0:T(8,128)(2,1)S(1)} %collective-permute-done.partner_ref, f32[24,8,512]{2,1,0:T(8,128)S(1)} %get-tuple-element.24.table_ref, f32[256,512]{1,0:T(8,128)S(1)} %get-tuple-element.27.field_ref), custom_call_target="tpu_custom_call" | custom-call | flops 1048576 | bytes 1769472 | tf_op jit(solution)/shard_map/own/pallas_call | solution.py:20
  8.9 0.5 %collective-permute-done.4.refs_0_ = bf16[64,512]{1,0:T(8,128)(2,1)S(1)} collective-permute-done((bf16[64,512]{1,0:T(8,128)(2,1)S(1)}, bf16[64,512]{1,0:T(8,128)(2,1)S(1)}, u32[]{:S(2)}, u32[]{:S(2)}) %collective-permute-start.4) | collective-permute-done | bytes 65568 | tf_op jit(solution)/shard_map/ppermute | solution.py:423
  9.5 0.1 beside.1
  9.6 0.1 collective-permute-start.5
  9.6 0.3 %collective-permute-done.2.other_ref = bf16[32,512]{1,0:T(8,128)(2,1)S(1)} collective-permute-done((bf16[32,512]{1,0:T(8,128)(2,1)S(1)}, bf16[32,512]{1,0:T(8,128)(2,1)S(1)}, u32[]{:S(2)}, u32[]{:S(2)}) %collective-permute-start.2) | collective-permute-done | bytes 32800 | tf_op jit(solution)/shard_map/ppermute | solution.py:440
  10.0 1.6 %collective-permute-start.3 = (bf16[40,512]{1,0:T(8,128)(2,1)S(1)}, bf16[40,512]{1,0:T(8,128)(2,1)S(1)}, u32[]{:S(2)}, u32[]{:S(2)}) collective-permute-start(bf16[40,512]{1,0:T(8,128)(2,1)S(1)} %border.1), channel_id=1, source_target_pairs={{0,4},{4,0},{1,5},{5,1},{2,6},{6,2},{3,7},{7,3},{8,12},{12,8},{9,1... | collective-permute-start | bytes 122888 | tf_op jit(solution)/shard_map/ppermute | solution.py:443
  11.6 0.0 collective-permute-done.6.refs_2_.refs_0_
  11.6 0.0 collective-permute-done.5.refs_1_.other_ref
  11.6 1.6 %collective-permute-start.8 = (bf16[40,512]{1,0:T(8,128)(2,1)S(1)}, bf16[40,512]{1,0:T(8,128)(2,1)S(1)}, u32[]{:S(2)}, u32[]{:S(2)}) collective-permute-start(bf16[40,512]{1,0:T(8,128)(2,1)S(1)} %before.1), channel_id=1, source_target_pairs={{0,4},{4,0},{1,5},{5,1},{2,6},{6,2},{3,7},{7,3},{8,12},{12,8},{9,1... | collective-permute-start | bytes 122888 | tf_op jit(solution)/shard_map/ppermute | solution.py:455
  13.2 0.4 %gate.1.gate_ref = f32[256,512]{1,0:T(8,128)S(1)} custom-call(bf16[256,512]{1,0:T(8,128)(2,1)S(1)} %get-tuple-element.30.x_ref, bf16[512,512]{1,0:T(8,128)(2,1)S(1)} %get-tuple-element.31.w_ref), custom_call_target="tpu_custom_call" | custom-call | bytes 1310720 | tf_op jit(solution)/shard_map/gate/pallas_call | solution.py:20
  13.6 0.8 %inner.1 = (bf16[256,512]{1,0:T(8,128)(2,1)S(1)}, f32[256,512]{1,0:T(8,128)S(1)}) custom-call(f32[256,512]{1,0:T(8,128)S(1)} %own.1.mine_ref.refs_1_, f32[32,512]{1,0:T(8,128)S(1)} %get-tuple-element.26.after_ref.own_ref, bf16[32,512]{1,0:T(8,128)(2,1)S(1)} %collective-permute-done.2.other_ref, f32[3,3,512]{2,1,0:T(4,128)S(1)} %get-tuple-element.29.taps_ref, ...), custom_call_target="tpu_custom_call" | custom-call | flops 268435456 | bytes 3000320 | tf_op jit(solution)/shard_map/inner/pallas_call | solution.py:20
  14.3 0.0 collective-permute-done.3.refs_0_
  14.4 1.1 %first.1.before_ref = bf16[256,512]{1,0:T(8,128)(2,1)} custom-call(bf16[256,512]{1,0:T(8,128)(2,1)S(1)} %get-tuple-element.34.inner_ref, f32[256,512]{1,0:T(8,128)S(1)} %get-tuple-element.35.totals_ref, f32[3,3,512]{2,1,0:T(4,128)S(1)} %get-tuple-element.29.taps_ref, f32[256,512]{1,0:T(8,128)S(1)} %gate.1.gate_ref, ...), custom_call_target="tpu_custom_call" | custom-call | bytes 2680832 | tf_op jit(solution)/shard_map/first/pallas_call | solution.py:20
  15.4 0.0 collective-permute-done.7.refs_3_
  15.5 0.2 %collective-permute-done.8.refs_1_ = bf16[40,512]{1,0:T(8,128)(2,1)S(1)} collective-permute-done((bf16[40,512]{1,0:T(8,128)(2,1)S(1)}, bf16[40,512]{1,0:T(8,128)(2,1)S(1)}, u32[]{:S(2)}, u32[]{:S(2)}) %collective-permute-start.8) | collective-permute-done | bytes 40992 | tf_op jit(solution)/shard_map/ppermute | solution.py:455
  (4 shorter events, 0.1 us)
Async XLA Ops:
  0.0 2.0 %collective-permute-start = (bf16[256,512]{1,0:T(8,128)(2,1)}, bf16[256,512]{1,0:T(8,128)(2,1)S(1)}, u32[]{:S(2)}, u32[]{:S(2)}) collective-permute-start(bf16[256,512]{1,0:T(8,128)(2,1)} %bitcast.3), channel_id=1, source_target_pairs={{0,8},{8,0},{16,24},{24,16},{1,9},{9,1},{17,25},{25,17},{2,10},{10... | collective-permute-start | bytes 786440 | tf_op jit(solution)/shard_map/ppermute | solution.py:376
  2.1 6.5 %collective-permute-start.1 = (bf16[64,512]{1,0:T(8,128)(2,1)S(1)}, bf16[64,512]{1,0:T(8,128)(2,1)S(1)}, u32[]{:S(2)}, u32[]{:S(2)}) collective-permute-start(bf16[64,512]{1,0:T(8,128)(2,1)S(1)} %column.1), channel_id=1, source_target_pairs={{0,1},{1,0},{2,3},{3,2},{4,5},{5,4},{6,7},{7,6},{8,12},{9,10},{10,... | collective-permute-start | bytes 196616 | tf_op jit(solution)/shard_map/ppermute | solution.py:423
  4.9 4.6 %collective-permute-start.4 = (bf16[64,512]{1,0:T(8,128)(2,1)S(1)}, bf16[64,512]{1,0:T(8,128)(2,1)S(1)}, u32[]{:S(2)}, u32[]{:S(2)}) collective-permute-start(bf16[64,512]{1,0:T(8,128)(2,1)S(1)} %column.1), channel_id=1, source_target_pairs={{0,17},{1,16},{2,19},{3,18},{4,21},{5,20},{6,23},{7,22},{8,28},{9,... | collective-permute-start | bytes 196616 | tf_op jit(solution)/shard_map/ppermute | solution.py:423
  6.5 5.1 %collective-permute-start.6 = (bf16[64,512]{1,0:T(8,128)(2,1)S(1)}, bf16[64,512]{1,0:T(8,128)(2,1)S(1)}, u32[]{:S(2)}, u32[]{:S(2)}) collective-permute-start(bf16[64,512]{1,0:T(8,128)(2,1)S(1)} %get-tuple-element.39), channel_id=1, source_target_pairs={{0,16},{8,24},{16,0},{24,8},{1,17},{9,25},{17,1},{25,9},{2,18},{10... | collective-permute-start | bytes 196616 | tf_op jit(solution)/shard_map/ppermute | solution.py:426
  7.2 8.3 %collective-permute-start.7 = (bf16[192,512]{1,0:T(8,128)(2,1)S(1)}, bf16[192,512]{1,0:T(8,128)(2,1)S(1)}, u32[]{:S(2)}, u32[]{:S(2)}) collective-permute-start(bf16[192,512]{1,0:T(8,128)(2,1)S(1)} %get-tuple-element.40), channel_id=1, source_target_pairs={{0,16},{8,24},{16,0},{24,8},{1,17},{9,25},{17,1},{25,9},{2,18},{10... | collective-permute-start | bytes 589832 | tf_op jit(solution)/shard_map/ppermute | solution.py:427
  8.7 1.3 %collective-permute-start.2 = (bf16[32,512]{1,0:T(8,128)(2,1)S(1)}, bf16[32,512]{1,0:T(8,128)(2,1)S(1)}, u32[]{:S(2)}, u32[]{:S(2)}) collective-permute-start(bf16[32,512]{1,0:T(8,128)(2,1)S(1)} %get-tuple-element.28), channel_id=1, source_target_pairs={{0,8},{8,0},{16,24},{24,16},{1,9},{9,1},{17,25},{25,17},{2,10},{10... | collective-permute-start | bytes 98312 | tf_op jit(solution)/shard_map/ppermute | solution.py:440
  9.6 2.0 %collective-permute-start.5 = (bf16[32,512]{1,0:T(8,128)(2,1)S(1)}, bf16[32,512]{1,0:T(8,128)(2,1)S(1)}, u32[]{:S(2)}, u32[]{:S(2)}) collective-permute-start(bf16[32,512]{1,0:T(8,128)(2,1)S(1)} %get-tuple-element.37), channel_id=1, source_target_pairs={{0,8},{8,0},{16,24},{24,16},{1,9},{9,1},{17,25},{25,17},{2,10},{10... | collective-permute-start | bytes 98312 | tf_op jit(solution)/shard_map/ppermute | solution.py:453
  10.0 4.3 %collective-permute-start.3 = (bf16[40,512]{1,0:T(8,128)(2,1)S(1)}, bf16[40,512]{1,0:T(8,128)(2,1)S(1)}, u32[]{:S(2)}, u32[]{:S(2)}) collective-permute-start(bf16[40,512]{1,0:T(8,128)(2,1)S(1)} %border.1), channel_id=1, source_target_pairs={{0,4},{4,0},{1,5},{5,1},{2,6},{6,2},{3,7},{7,3},{8,12},{12,8},{9,1... | collective-permute-start | bytes 122888 | tf_op jit(solution)/shard_map/ppermute | solution.py:443
  11.6 4.1 %collective-permute-start.8 = (bf16[40,512]{1,0:T(8,128)(2,1)S(1)}, bf16[40,512]{1,0:T(8,128)(2,1)S(1)}, u32[]{:S(2)}, u32[]{:S(2)}) collective-permute-start(bf16[40,512]{1,0:T(8,128)(2,1)S(1)} %before.1), channel_id=1, source_target_pairs={{0,4},{4,0},{1,5},{5,1},{2,6},{6,2},{3,7},{7,3},{8,12},{12,8},{9,1... | collective-permute-start | bytes 122888 | tf_op jit(solution)/shard_map/ppermute | solution.py:455

commit v23 on v22

--- a/solution.py
+++ b/solution.py
@@ -63,7 +63,7 @@
     return jnp.where(on_right(), ref[pl.ds(cols - 1, lines, stride=cols), :], ref[pl.ds(0, lines, stride=cols), :])
 
 
-def gate_kernel(x_ref, w_ref, gate_ref):
+def gate_kernel(after_ref, x_ref, w_ref, gate_ref):
     v = jnp.dot(x_ref[...], w_ref[...], preferred_element_type=F32)
     gate_ref[...] = v / (1.0 + jnp.exp(-v))
 
@@ -310,8 +310,21 @@
 def complete(frames, rows, cols, inner_ref, totals_ref, taps_ref, gate_ref, wv_ref, wo_ref, ends, out_ref, held, done):
     sites = rows * cols
     size = frames * cols
+    group = 2 * cols
     odd, lower, upper = position("height")
-    held[...] = inner_ref[...]
+    copies = []
+
+    def send(source, start, count):
+        copy = pltpu.make_async_copy(source, out_ref.at[pl.ds(start, count)], done.at[len(copies)])
+        copy.start()
+        copies.append(copy)
+
+    for t in range(frames):
+        inside = t * sites + group
+        send(inner_ref.at[pl.ds(inside, sites - 2 * group)], inside, sites - 2 * group)
+        if len(ends) == 1:
+            kept = pl.multiple_of(t * sites + jnp.where(odd, sites - group, 0), group)
+            send(inner_ref.at[pl.ds(kept, group)], kept, group)
     mixed, gate = [], []
     for k, end in enumerate(ends):
         first = jnp.logical_not(odd) if k else odd
@@ -326,19 +339,19 @@
             mixed.append(total + jnp.where(exists, more, jnp.zeros_like(more)))
             gate.append(jnp.where(first, gate_ref[i : i + cols], gate_ref[j : j + cols]))
     out = projected(jnp.concatenate(mixed).astype(BF16), jnp.concatenate(gate), wv_ref, wo_ref)
-    for t in range(frames):
-        new = [out[k * size + t * cols : k * size + (t + 1) * cols].astype(F32) for k in range(len(ends))]
-        first, final = t * sites, (t + 1) * sites - 2 * cols
-        top = inner_ref[first : first + 2 * cols].astype(F32)
-        bottom = inner_ref[final : final + 2 * cols].astype(F32)
-        other = new[1] if len(new) > 1 else None
-        row = jnp.where(odd, new[0], top[:cols] if other is None else other)
-        held[first : first + 2 * cols] = jnp.concatenate([row, top[cols:]]).astype(BF16)
-        row = jnp.where(odd, bottom[cols:] if other is None else other, new[0])
-        held[final : final + 2 * cols] = jnp.concatenate([bottom[:cols], row]).astype(BF16)
-    copy = pltpu.make_async_copy(held, out_ref, done)
-    copy.start()
-    copy.wait()
+    for k in range(len(ends)):
+        first = jnp.logical_not(odd) if k else odd
+        for t in range(frames):
+            row = k * size + t * cols
+            new = out[row : row + cols].astype(F32)
+            top = inner_ref[t * sites : t * sites + group].astype(F32)
+            bottom = inner_ref[(t + 1) * sites - group : (t + 1) * sites].astype(F32)
+            lines = jnp.where(first, new, bottom[:cols]), jnp.where(first, top[cols:], new)
+            held[2 * row : 2 * row + group] = jnp.concatenate(lines).astype(BF16)
+            start = pl.multiple_of(t * sites + jnp.where(first, 0, sites - group), group)
+            send(held.at[pl.ds(2 * row, group)], start, group)
+    for copy in copies:
+        copy.wait()
 
 
 def first_kernel(frames, rows, cols, inner_ref, totals_ref, taps_ref, gate_ref, wv_ref, wo_ref, *refs):
@@ -388,8 +401,6 @@
         inputs,
         far=len(inputs),
     )
-    (gate,) = call(gate_kernel, "gate", [field], [], [near_x, near_gate])
-
     h_rounds = swaps("height")
     (column,) = call(
         functools.partial(column_kernel, frames, rows, cols),
@@ -437,6 +448,7 @@
         [own, partner, table, fields[0]],
         2 * frames * x.size,
     )
+    (gate,) = call(gate_kernel, "gate", [field], [], [own, near_x, near_gate])
     other = lax.ppermute(other, "tm", swap)
     end = [shape((frames * cols + 2 * frames, chans), BF16)] * len(h_rounds)
     ends = call(functools.partial(border_kernel, frames, rows, cols), "border", end, [], [mine, own, other])
@@ -447,7 +459,7 @@
             "beside",
             both,
             [],
-            [table] + columns[1:] + [mine],
+            [table] + columns[1:] + [mine, gate],
             LATER,
         )
         other_d = lax.ppermute(other_d, "tm", swap)
@@ -462,7 +474,7 @@
         [mine, own, other, taps, gate, value_weight, out_weight],
         4 * block * chans * chans,
     )
-    held = [pltpu.VMEM((block, chans), BF16), pltpu.SemaphoreType.DMA]
+    held = [pltpu.VMEM((2 * len(h_rounds) * frames * cols, chans), BF16), pltpu.SemaphoreType.DMA((3 * frames,))]
     weights = [taps, gate, value_weight, out_weight]
     out = shape((block, chans), BF16)
     (first,) = call(
@@ -478,7 +490,7 @@
             functools.partial(block_kernel, frames, rows, cols, len(h_rounds)),
             "block",
             [out, field],
-            held[:1],
+            [pltpu.VMEM((block, chans), BF16)],
             [inner, totals] + weights + [own_d, other_d] + firsts + rests,
             aliases={0: 0, 1: 1},
         )

time: 15.9 us -> 16.1 us (1.013)
  starting transfers between devices: 10 us -> 10.3 us
  waiting for transfers between devices: 1.07 us -> 0.82 us
    ppermute x2, waiting for transfers between devices: 0.2 us -> 0.65 us  [body(): lax.ppermute(e, 'height', pairs)]
    ppermute x2, waiting for transfers between devices: 0.54 us -> 0.16 us  [body(): columns.append(lax.ppermute(column, ('tm', 'height', 'width'), route))]
    ppermute x1, starting transfers between devices: 0.07 us -> 0.43 us  [body(): other_d = lax.ppermute(other_d, 'tm', swap)]
    ppermute x1, waiting for transfers between devices: 0.31 us -> 0.01 us  [body(): other = lax.ppermute(other, 'tm', swap)]
where the time goes in v23:
time: 16.1 us; the launch traced here: 15.8 us
  starting transfers between devices  10.3 us (64%)
  Pallas kernels  4.57 us (28%)
  waiting for transfers between devices  0.82 us (5%)
    pallas_call x13, Pallas kernels, call(): pl.pallas_call(kernel, out_shape=tuple(outs), in_specs=[HBM] * far + [VME...  4.57 us
    ppermute x2, starting transfers between devices, body(): columns.append(lax.ppermute(column, ('tm', 'height', 'width'), route))  4.22 us
    ppermute x2, starting transfers between devices, body(): lax.ppermute(e, 'height', pairs)  3.07 us
    ppermute x1, starting transfers between devices, body(): rests.append(lax.ppermute(sent[2 * d - 1], 'tm', route))  1.41 us
    ppermute x1, starting transfers between devices, body(): firsts.append(lax.ppermute(sent[2 * d - 2], 'tm', route))  0.69 us
    ppermute x2, waiting for transfers between devices, body(): lax.ppermute(e, 'height', pairs)  0.65 us
    ppermute x1, starting transfers between devices, body(): partner = lax.ppermute(x, 'tm', [(i, i ^ 1) for i in range(n_t)])  0.45 us
    ppermute x1, starting transfers between devices, body(): other_d = lax.ppermute(other_d, 'tm', swap)  0.43 us
  transfers between devices with their start and end apart: 9, of which 3 were waited for; matrix products, arithmetic and copies ran while one was open for 0% of the time, Pallas kernels for 28%

profile of v23, /device:TPU:0, one launch (start us, length us, event | category | flops | bytes accessed | tf_op | source)
XLA Modules:
  0.0 15.8 jit_solution(5069615910767704712)
XLA Ops:
  0.0 0.5 %collective-permute-start = (bf16[256,512]{1,0:T(8,128)(2,1)}, bf16[256,512]{1,0:T(8,128)(2,1)S(1)}, u32[]{:S(2)}, u32[]{:S(2)}) collective-permute-start(bf16[256,512]{1,0:T(8,128)(2,1)} %bitcast.3), channel_id=1, source_target_pairs={{0,8},{8,0},{16,24},{24,16},{1,9},{9,1},{17,25},{25,17},{2,10},{10... | collective-permute-start | bytes 786440 | tf_op jit(solution)/shard_map/ppermute | solution.py:389
  0.5 1.5 %early.1 = (bf16[256,512]{1,0:T(8,128)(2,1)S(1)}, bf16[512,512]{1,0:T(8,128)(2,1)S(1)}, f32[3,3,512]{2,1,0:T(4,128)S(1)}, bf16[512,512]{1,0:T(8,128)(2,1)S(1)}, ...) custom-call(bf16[16,512]{1,0:T(8,128)(2,1)} %refs_0_.1, ...), custom_call_target="tpu_custom_call" | custom-call | bytes 5232640 | tf_op jit(solution)/shard_map/early/pallas_call | solution.py:20
  2.0 0.0 collective-permute-done.partner_ref
  2.0 0.1 column.1
  2.1 2.8 %collective-permute-start.1 = (bf16[64,512]{1,0:T(8,128)(2,1)S(1)}, bf16[64,512]{1,0:T(8,128)(2,1)S(1)}, u32[]{:S(2)}, u32[]{:S(2)}) collective-permute-start(bf16[64,512]{1,0:T(8,128)(2,1)S(1)} %column.1), channel_id=1, source_target_pairs={{0,1},{1,0},{2,3},{3,2},{4,5},{5,4},{6,7},{7,6},{8,12},{9,10},{10,... | collective-permute-start | bytes 196616 | tf_op jit(solution)/shard_map/ppermute | solution.py:434
  4.9 1.4 %collective-permute-start.4 = (bf16[64,512]{1,0:T(8,128)(2,1)S(1)}, bf16[64,512]{1,0:T(8,128)(2,1)S(1)}, u32[]{:S(2)}, u32[]{:S(2)}) collective-permute-start(bf16[64,512]{1,0:T(8,128)(2,1)S(1)} %column.1), channel_id=1, source_target_pairs={{0,17},{1,16},{2,19},{3,18},{4,21},{5,20},{6,23},{7,22},{8,28},{9,... | collective-permute-start | bytes 196616 | tf_op jit(solution)/shard_map/ppermute | solution.py:434
  6.3 0.2 %later.1 = (bf16[64,512]{1,0:T(8,128)(2,1)S(1)}, bf16[192,512]{1,0:T(8,128)(2,1)S(1)}) custom-call(bf16[256,512]{1,0:T(8,128)(2,1)S(1)} %collective-permute-done.partner_ref, f32[24,8,512]{2,1,0:T(8,128)S(1)} %get-tuple-element.24.table_ref, f32[256,512]{1,0:T(8,128)S(1)} %get-tuple-element.38.refs_0_), custom_call_target="tpu_custom_call" | custom-call | flops 1048576 | bytes 1441792 | tf_op jit(solution)/shard_map/later/pallas_call | solution.py:20
  6.5 0.7 %collective-permute-start.6 = (bf16[64,512]{1,0:T(8,128)(2,1)S(1)}, bf16[64,512]{1,0:T(8,128)(2,1)S(1)}, u32[]{:S(2)}, u32[]{:S(2)}) collective-permute-start(bf16[64,512]{1,0:T(8,128)(2,1)S(1)} %get-tuple-element.39), channel_id=1, source_target_pairs={{0,16},{8,24},{16,0},{24,8},{1,17},{9,25},{17,1},{25,9},{2,18},{10... | collective-permute-start | bytes 196616 | tf_op jit(solution)/shard_map/ppermute | solution.py:437
  7.2 1.4 %collective-permute-start.7 = (bf16[192,512]{1,0:T(8,128)(2,1)S(1)}, bf16[192,512]{1,0:T(8,128)(2,1)S(1)}, u32[]{:S(2)}, u32[]{:S(2)}) collective-permute-start(bf16[192,512]{1,0:T(8,128)(2,1)S(1)} %get-tuple-element.40), channel_id=1, source_target_pairs={{0,16},{8,24},{16,0},{24,8},{1,17},{9,25},{17,1},{25,9},{2,18},{10... | collective-permute-start | bytes 589832 | tf_op jit(solution)/shard_map/ppermute | solution.py:438
  8.6 0.0 collective-permute-done.1.refs_0_
  8.6 0.1 side.1
  8.7 0.1 collective-permute-start.2
  8.8 0.4 %gate.1.gate_ref.refs_2_ = f32[256,512]{1,0:T(8,128)S(1)} custom-call(f32[32,512]{1,0:T(8,128)S(1)} %get-tuple-element.26.after_ref.own_ref, bf16[256,512]{1,0:T(8,128)(2,1)S(1)} %get-tuple-element.30.x_ref, bf16[512,512]{1,0:T(8,128)(2,1)S(1)} %get-tuple-element.31.w_ref), custom_call_target="tpu_custom_call" | custom-call | bytes 1376256 | tf_op jit(solution)/shard_map/gate/pallas_call | solution.py:20
  9.1 0.2 %own.1.mine_ref.refs_1_ = f32[256,512]{1,0:T(8,128)S(1)} custom-call(f32[32,512]{1,0:T(8,128)S(1)} %get-tuple-element.26.after_ref.own_ref, bf16[256,512]{1,0:T(8,128)(2,1)S(1)} %collective-permute-done.partner_ref, f32[24,8,512]{2,1,0:T(8,128)S(1)} %get-tuple-element.24.table_ref, f32[256,512]{1,0:T(8,128)S(1)} %get-tuple-element.27.field_ref), custom_call_target="tpu_custom_call" | custom-call | flops 1048576 | bytes 1769472 | tf_op jit(solution)/shard_map/own/pallas_call | solution.py:20
  9.3 0.2 collective-permute-done.4.refs_0_
  9.5 0.1 beside.1
  9.6 0.4 %collective-permute-start.5 = (bf16[32,512]{1,0:T(8,128)(2,1)S(1)}, bf16[32,512]{1,0:T(8,128)(2,1)S(1)}, u32[]{:S(2)}, u32[]{:S(2)}) collective-permute-start(bf16[32,512]{1,0:T(8,128)(2,1)S(1)} %get-tuple-element.37), channel_id=1, source_target_pairs={{0,8},{8,0},{16,24},{24,16},{1,9},{9,1},{17,25},{25,17},{2,10},{10... | collective-permute-start | bytes 98312 | tf_op jit(solution)/shard_map/ppermute | solution.py:465
  10.0 0.0 collective-permute-done.2.other_ref
  10.0 1.6 %collective-permute-start.3 = (bf16[40,512]{1,0:T(8,128)(2,1)S(1)}, bf16[40,512]{1,0:T(8,128)(2,1)S(1)}, u32[]{:S(2)}, u32[]{:S(2)}) collective-permute-start(bf16[40,512]{1,0:T(8,128)(2,1)S(1)} %border.1), channel_id=1, source_target_pairs={{0,4},{4,0},{1,5},{5,1},{2,6},{6,2},{3,7},{7,3},{8,12},{12,8},{9,1... | collective-permute-start | bytes 122888 | tf_op jit(solution)/shard_map/ppermute | solution.py:455
  11.6 0.0 collective-permute-done.6.refs_2_.refs_0_
  11.6 0.0 collective-permute-done.5.refs_1_.other_ref
  11.7 1.5 %collective-permute-start.8 = (bf16[40,512]{1,0:T(8,128)(2,1)S(1)}, bf16[40,512]{1,0:T(8,128)(2,1)S(1)}, u32[]{:S(2)}, u32[]{:S(2)}) collective-permute-start(bf16[40,512]{1,0:T(8,128)(2,1)S(1)} %before.1), channel_id=1, source_target_pairs={{0,4},{4,0},{1,5},{5,1},{2,6},{6,2},{3,7},{7,3},{8,12},{12,8},{9,1... | collective-permute-start | bytes 122888 | tf_op jit(solution)/shard_map/ppermute | solution.py:467
  13.2 0.8 %inner.1 = (bf16[256,512]{1,0:T(8,128)(2,1)S(1)}, f32[256,512]{1,0:T(8,128)S(1)}) custom-call(f32[256,512]{1,0:T(8,128)S(1)} %own.1.mine_ref.refs_1_, f32[32,512]{1,0:T(8,128)S(1)} %get-tuple-element.26.after_ref.own_ref, bf16[32,512]{1,0:T(8,128)(2,1)S(1)} %collective-permute-done.2.other_ref, f32[3,3,512]{2,1,0:T(4,128)S(1)} %get-tuple-element.29.taps_ref, ...), custom_call_target="tpu_custom_call" | custom-call | flops 268435456 | bytes 3000320 | tf_op jit(solution)/shard_map/inner/pallas_call | solution.py:20
  14.0 0.2 %collective-permute-done.3.refs_0_ = bf16[40,512]{1,0:T(8,128)(2,1)S(1)} collective-permute-done((bf16[40,512]{1,0:T(8,128)(2,1)S(1)}, bf16[40,512]{1,0:T(8,128)(2,1)S(1)}, u32[]{:S(2)}, u32[]{:S(2)}) %collective-permute-start.3) | collective-permute-done | bytes 40992 | tf_op jit(solution)/shard_map/ppermute | solution.py:455
  14.1 1.1 %first.1.before_ref = bf16[256,512]{1,0:T(8,128)(2,1)} custom-call(bf16[256,512]{1,0:T(8,128)(2,1)S(1)} %get-tuple-element.34.inner_ref, f32[256,512]{1,0:T(8,128)S(1)} %get-tuple-element.35.totals_ref, f32[3,3,512]{2,1,0:T(4,128)S(1)} %get-tuple-element.29.taps_ref, f32[256,512]{1,0:T(8,128)S(1)} %gate.1.gate_ref.refs_2_, ...), custom_call_target="tpu_custom_call" | custom-call | bytes 2680832 | tf_op jit(solution)/shard_map/first/pallas_call | solution.py:20
  15.2 0.0 collective-permute-done.7.refs_3_
  15.2 0.5 %collective-permute-done.8.refs_1_ = bf16[40,512]{1,0:T(8,128)(2,1)S(1)} collective-permute-done((bf16[40,512]{1,0:T(8,128)(2,1)S(1)}, bf16[40,512]{1,0:T(8,128)(2,1)S(1)}, u32[]{:S(2)}, u32[]{:S(2)}) %collective-permute-start.8) | collective-permute-done | bytes 40992 | tf_op jit(solution)/shard_map/ppermute | solution.py:467
  15.7 0.1 last.1
  (3 shorter events, 0.1 us)
Async XLA Ops:
  0.0 2.0 %collective-permute-start = (bf16[256,512]{1,0:T(8,128)(2,1)}, bf16[256,512]{1,0:T(8,128)(2,1)S(1)}, u32[]{:S(2)}, u32[]{:S(2)}) collective-permute-start(bf16[256,512]{1,0:T(8,128)(2,1)} %bitcast.3), channel_id=1, source_target_pairs={{0,8},{8,0},{16,24},{24,16},{1,9},{9,1},{17,25},{25,17},{2,10},{10... | collective-permute-start | bytes 786440 | tf_op jit(solution)/shard_map/ppermute | solution.py:389
  2.1 6.5 %collective-permute-start.1 = (bf16[64,512]{1,0:T(8,128)(2,1)S(1)}, bf16[64,512]{1,0:T(8,128)(2,1)S(1)}, u32[]{:S(2)}, u32[]{:S(2)}) collective-permute-start(bf16[64,512]{1,0:T(8,128)(2,1)S(1)} %column.1), channel_id=1, source_target_pairs={{0,1},{1,0},{2,3},{3,2},{4,5},{5,4},{6,7},{7,6},{8,12},{9,10},{10,... | collective-permute-start | bytes 196616 | tf_op jit(solution)/shard_map/ppermute | solution.py:434
  4.9 4.6 %collective-permute-start.4 = (bf16[64,512]{1,0:T(8,128)(2,1)S(1)}, bf16[64,512]{1,0:T(8,128)(2,1)S(1)}, u32[]{:S(2)}, u32[]{:S(2)}) collective-permute-start(bf16[64,512]{1,0:T(8,128)(2,1)S(1)} %column.1), channel_id=1, source_target_pairs={{0,17},{1,16},{2,19},{3,18},{4,21},{5,20},{6,23},{7,22},{8,28},{9,... | collective-permute-start | bytes 196616 | tf_op jit(solution)/shard_map/ppermute | solution.py:434
  6.5 5.1 %collective-permute-start.6 = (bf16[64,512]{1,0:T(8,128)(2,1)S(1)}, bf16[64,512]{1,0:T(8,128)(2,1)S(1)}, u32[]{:S(2)}, u32[]{:S(2)}) collective-permute-start(bf16[64,512]{1,0:T(8,128)(2,1)S(1)} %get-tuple-element.39), channel_id=1, source_target_pairs={{0,16},{8,24},{16,0},{24,8},{1,17},{9,25},{17,1},{25,9},{2,18},{10... | collective-permute-start | bytes 196616 | tf_op jit(solution)/shard_map/ppermute | solution.py:437
  7.2 8.0 %collective-permute-start.7 = (bf16[192,512]{1,0:T(8,128)(2,1)S(1)}, bf16[192,512]{1,0:T(8,128)(2,1)S(1)}, u32[]{:S(2)}, u32[]{:S(2)}) collective-permute-start(bf16[192,512]{1,0:T(8,128)(2,1)S(1)} %get-tuple-element.40), channel_id=1, source_target_pairs={{0,16},{8,24},{16,0},{24,8},{1,17},{9,25},{17,1},{25,9},{2,18},{10... | collective-permute-start | bytes 589832 | tf_op jit(solution)/shard_map/ppermute | solution.py:438
  8.7 1.3 %collective-permute-start.2 = (bf16[32,512]{1,0:T(8,128)(2,1)S(1)}, bf16[32,512]{1,0:T(8,128)(2,1)S(1)}, u32[]{:S(2)}, u32[]{:S(2)}) collective-permute-start(bf16[32,512]{1,0:T(8,128)(2,1)S(1)} %get-tuple-element.28), channel_id=1, source_target_pairs={{0,8},{8,0},{16,24},{24,16},{1,9},{9,1},{17,25},{25,17},{2,10},{10... | collective-permute-start | bytes 98312 | tf_op jit(solution)/shard_map/ppermute | solution.py:452
  9.6 2.0 %collective-permute-start.5 = (bf16[32,512]{1,0:T(8,128)(2,1)S(1)}, bf16[32,512]{1,0:T(8,128)(2,1)S(1)}, u32[]{:S(2)}, u32[]{:S(2)}) collective-permute-start(bf16[32,512]{1,0:T(8,128)(2,1)S(1)} %get-tuple-element.37), channel_id=1, source_target_pairs={{0,8},{8,0},{16,24},{24,16},{1,9},{9,1},{17,25},{25,17},{2,10},{10... | collective-permute-start | bytes 98312 | tf_op jit(solution)/shard_map/ppermute | solution.py:465
  10.0 4.1 %collective-permute-start.3 = (bf16[40,512]{1,0:T(8,128)(2,1)S(1)}, bf16[40,512]{1,0:T(8,128)(2,1)S(1)}, u32[]{:S(2)}, u32[]{:S(2)}) collective-permute-start(bf16[40,512]{1,0:T(8,128)(2,1)S(1)} %border.1), channel_id=1, source_target_pairs={{0,4},{4,0},{1,5},{5,1},{2,6},{6,2},{3,7},{7,3},{8,12},{12,8},{9,1... | collective-permute-start | bytes 122888 | tf_op jit(solution)/shard_map/ppermute | solution.py:455
  11.7 4.1 %collective-permute-start.8 = (bf16[40,512]{1,0:T(8,128)(2,1)S(1)}, bf16[40,512]{1,0:T(8,128)(2,1)S(1)}, u32[]{:S(2)}, u32[]{:S(2)}) collective-permute-start(bf16[40,512]{1,0:T(8,128)(2,1)S(1)} %before.1), channel_id=1, source_target_pairs={{0,4},{4,0},{1,5},{5,1},{2,6},{6,2},{3,7},{7,3},{8,12},{12,8},{9,1... | collective-permute-start | bytes 122888 | tf_op jit(solution)/shard_map/ppermute | solution.py:467

commit v24 on v22

--- a/solution.py
+++ b/solution.py
@@ -63,7 +63,7 @@
     return jnp.where(on_right(), ref[pl.ds(cols - 1, lines, stride=cols), :], ref[pl.ds(0, lines, stride=cols), :])
 
 
-def gate_kernel(x_ref, w_ref, gate_ref):
+def gate_kernel(after_ref, x_ref, w_ref, gate_ref):
     v = jnp.dot(x_ref[...], w_ref[...], preferred_element_type=F32)
     gate_ref[...] = v / (1.0 + jnp.exp(-v))
 
@@ -388,8 +388,6 @@
         inputs,
         far=len(inputs),
     )
-    (gate,) = call(gate_kernel, "gate", [field], [], [near_x, near_gate])
-
     h_rounds = swaps("height")
     (column,) = call(
         functools.partial(column_kernel, frames, rows, cols),
@@ -437,6 +435,7 @@
         [own, partner, table, fields[0]],
         2 * frames * x.size,
     )
+    (gate,) = call(gate_kernel, "gate", [field], [], [own, near_x, near_gate])
     other = lax.ppermute(other, "tm", swap)
     end = [shape((frames * cols + 2 * frames, chans), BF16)] * len(h_rounds)
     ends = call(functools.partial(border_kernel, frames, rows, cols), "border", end, [], [mine, own, other])
@@ -447,7 +446,7 @@
             "beside",
             both,
             [],
-            [table] + columns[1:] + [mine],
+            [table] + columns[1:] + [mine, gate],
             LATER,
         )
         other_d = lax.ppermute(other_d, "tm", swap)

time: 15.9 us -> 16 us (level)
  starting transfers between devices: 10 us -> 10.3 us
  waiting for transfers between devices: 1.07 us -> 0.83 us
    ppermute x2, waiting for transfers between devices: 0.2 us -> 0.66 us  [body(): lax.ppermute(e, 'height', pairs)]
    ppermute x2, waiting for transfers between devices: 0.54 us -> 0.16 us  [body(): columns.append(lax.ppermute(column, ('tm', 'height', 'width'), route))]
    ppermute x1, starting transfers between devices: 0.07 us -> 0.43 us  [body(): other_d = lax.ppermute(other_d, 'tm', swap)]
    ppermute x1, waiting for transfers between devices: 0.31 us -> 0.01 us  [body(): other = lax.ppermute(other, 'tm', swap)]
where the time goes in v24:
time: 16 us; the launch traced here: 15.7 us
  starting transfers between devices  10.3 us (64%)
  Pallas kernels  4.46 us (28%)
  waiting for transfers between devices  0.83 us (5%)
    pallas_call x13, Pallas kernels, call(): pl.pallas_call(kernel, out_shape=tuple(outs), in_specs=[HBM] * far + [VME...  4.46 us
    ppermute x2, starting transfers between devices, body(): columns.append(lax.ppermute(column, ('tm', 'height', 'width'), route))  4.22 us
    ppermute x2, starting transfers between devices, body(): lax.ppermute(e, 'height', pairs)  3.07 us
    ppermute x1, starting transfers between devices, body(): rests.append(lax.ppermute(sent[2 * d - 1], 'tm', route))  1.41 us
    ppermute x1, starting transfers between devices, body(): firsts.append(lax.ppermute(sent[2 * d - 2], 'tm', route))  0.69 us
    ppermute x2, waiting for transfers between devices, body(): lax.ppermute(e, 'height', pairs)  0.66 us
    ppermute x1, starting transfers between devices, body(): partner = lax.ppermute(x, 'tm', [(i, i ^ 1) for i in range(n_t)])  0.45 us
    ppermute x1, starting transfers between devices, body(): other_d = lax.ppermute(other_d, 'tm', swap)  0.43 us
  transfers between devices with their start and end apart: 9, of which 3 were waited for; matrix products, arithmetic and copies ran while one was open for 0% of the time, Pallas kernels for 28%

profile of v24, /device:TPU:0, one launch (start us, length us, event | category | flops | bytes accessed | tf_op | source)
XLA Modules:
  0.0 15.7 jit_solution(3381845411341191035)
XLA Ops:
  0.0 0.5 %collective-permute-start = (bf16[256,512]{1,0:T(8,128)(2,1)}, bf16[256,512]{1,0:T(8,128)(2,1)S(1)}, u32[]{:S(2)}, u32[]{:S(2)}) collective-permute-start(bf16[256,512]{1,0:T(8,128)(2,1)} %bitcast.3), channel_id=1, source_target_pairs={{0,8},{8,0},{16,24},{24,16},{1,9},{9,1},{17,25},{25,17},{2,10},{10... | collective-permute-start | bytes 786440 | tf_op jit(solution)/shard_map/ppermute | solution.py:376
  0.5 1.5 %early.1 = (bf16[256,512]{1,0:T(8,128)(2,1)S(1)}, bf16[512,512]{1,0:T(8,128)(2,1)S(1)}, f32[3,3,512]{2,1,0:T(4,128)S(1)}, bf16[512,512]{1,0:T(8,128)(2,1)S(1)}, ...) custom-call(bf16[16,512]{1,0:T(8,128)(2,1)} %refs_0_.1, ...), custom_call_target="tpu_custom_call" | custom-call | bytes 5232640 | tf_op jit(solution)/shard_map/early/pallas_call | solution.py:20
  2.0 0.0 collective-permute-done.partner_ref
  2.0 0.1 column.1
  2.1 2.8 %collective-permute-start.1 = (bf16[64,512]{1,0:T(8,128)(2,1)S(1)}, bf16[64,512]{1,0:T(8,128)(2,1)S(1)}, u32[]{:S(2)}, u32[]{:S(2)}) collective-permute-start(bf16[64,512]{1,0:T(8,128)(2,1)S(1)} %column.1), channel_id=1, source_target_pairs={{0,1},{1,0},{2,3},{3,2},{4,5},{5,4},{6,7},{7,6},{8,12},{9,10},{10,... | collective-permute-start | bytes 196616 | tf_op jit(solution)/shard_map/ppermute | solution.py:421
  4.9 1.4 %collective-permute-start.4 = (bf16[64,512]{1,0:T(8,128)(2,1)S(1)}, bf16[64,512]{1,0:T(8,128)(2,1)S(1)}, u32[]{:S(2)}, u32[]{:S(2)}) collective-permute-start(bf16[64,512]{1,0:T(8,128)(2,1)S(1)} %column.1), channel_id=1, source_target_pairs={{0,17},{1,16},{2,19},{3,18},{4,21},{5,20},{6,23},{7,22},{8,28},{9,... | collective-permute-start | bytes 196616 | tf_op jit(solution)/shard_map/ppermute | solution.py:421
  6.3 0.2 %later.1 = (bf16[64,512]{1,0:T(8,128)(2,1)S(1)}, bf16[192,512]{1,0:T(8,128)(2,1)S(1)}) custom-call(bf16[256,512]{1,0:T(8,128)(2,1)S(1)} %collective-permute-done.partner_ref, f32[24,8,512]{2,1,0:T(8,128)S(1)} %get-tuple-element.24.table_ref, f32[256,512]{1,0:T(8,128)S(1)} %get-tuple-element.38.refs_0_), custom_call_target="tpu_custom_call" | custom-call | flops 1048576 | bytes 1441792 | tf_op jit(solution)/shard_map/later/pallas_call | solution.py:20
  6.5 0.7 %collective-permute-start.6 = (bf16[64,512]{1,0:T(8,128)(2,1)S(1)}, bf16[64,512]{1,0:T(8,128)(2,1)S(1)}, u32[]{:S(2)}, u32[]{:S(2)}) collective-permute-start(bf16[64,512]{1,0:T(8,128)(2,1)S(1)} %get-tuple-element.39), channel_id=1, source_target_pairs={{0,16},{8,24},{16,0},{24,8},{1,17},{9,25},{17,1},{25,9},{2,18},{10... | collective-permute-start | bytes 196616 | tf_op jit(solution)/shard_map/ppermute | solution.py:424
  7.2 1.4 %collective-permute-start.7 = (bf16[192,512]{1,0:T(8,128)(2,1)S(1)}, bf16[192,512]{1,0:T(8,128)(2,1)S(1)}, u32[]{:S(2)}, u32[]{:S(2)}) collective-permute-start(bf16[192,512]{1,0:T(8,128)(2,1)S(1)} %get-tuple-element.40), channel_id=1, source_target_pairs={{0,16},{8,24},{16,0},{24,8},{1,17},{9,25},{17,1},{25,9},{2,18},{10... | collective-permute-start | bytes 589832 | tf_op jit(solution)/shard_map/ppermute | solution.py:425
  8.6 0.0 collective-permute-done.1.refs_0_
  8.6 0.1 side.1
  8.7 0.1 collective-permute-start.2
  8.8 0.4 %gate.1.gate_ref.refs_2_ = f32[256,512]{1,0:T(8,128)S(1)} custom-call(f32[32,512]{1,0:T(8,128)S(1)} %get-tuple-element.26.after_ref.own_ref, bf16[256,512]{1,0:T(8,128)(2,1)S(1)} %get-tuple-element.30.x_ref, bf16[512,512]{1,0:T(8,128)(2,1)S(1)} %get-tuple-element.31.w_ref), custom_call_target="tpu_custom_call" | custom-call | bytes 1376256 | tf_op jit(solution)/shard_map/gate/pallas_call | solution.py:20
  9.1 0.2 %own.1.mine_ref.refs_1_ = f32[256,512]{1,0:T(8,128)S(1)} custom-call(f32[32,512]{1,0:T(8,128)S(1)} %get-tuple-element.26.after_ref.own_ref, bf16[256,512]{1,0:T(8,128)(2,1)S(1)} %collective-permute-done.partner_ref, f32[24,8,512]{2,1,0:T(8,128)S(1)} %get-tuple-element.24.table_ref, f32[256,512]{1,0:T(8,128)S(1)} %get-tuple-element.27.field_ref), custom_call_target="tpu_custom_call" | custom-call | flops 1048576 | bytes 1769472 | tf_op jit(solution)/shard_map/own/pallas_call | solution.py:20
  9.3 0.2 collective-permute-done.4.refs_0_
  9.5 0.1 beside.1
  9.6 0.4 %collective-permute-start.5 = (bf16[32,512]{1,0:T(8,128)(2,1)S(1)}, bf16[32,512]{1,0:T(8,128)(2,1)S(1)}, u32[]{:S(2)}, u32[]{:S(2)}) collective-permute-start(bf16[32,512]{1,0:T(8,128)(2,1)S(1)} %get-tuple-element.37), channel_id=1, source_target_pairs={{0,8},{8,0},{16,24},{24,16},{1,9},{9,1},{17,25},{25,17},{2,10},{10... | collective-permute-start | bytes 98312 | tf_op jit(solution)/shard_map/ppermute | solution.py:452
  10.0 0.0 collective-permute-done.2.other_ref
  10.0 1.6 %collective-permute-start.3 = (bf16[40,512]{1,0:T(8,128)(2,1)S(1)}, bf16[40,512]{1,0:T(8,128)(2,1)S(1)}, u32[]{:S(2)}, u32[]{:S(2)}) collective-permute-start(bf16[40,512]{1,0:T(8,128)(2,1)S(1)} %border.1), channel_id=1, source_target_pairs={{0,4},{4,0},{1,5},{5,1},{2,6},{6,2},{3,7},{7,3},{8,12},{12,8},{9,1... | collective-permute-start | bytes 122888 | tf_op jit(solution)/shard_map/ppermute | solution.py:442
  11.6 0.0 collective-permute-done.6.refs_2_.refs_0_
  11.6 0.0 collective-permute-done.5.refs_1_.other_ref
  11.7 1.5 %collective-permute-start.8 = (bf16[40,512]{1,0:T(8,128)(2,1)S(1)}, bf16[40,512]{1,0:T(8,128)(2,1)S(1)}, u32[]{:S(2)}, u32[]{:S(2)}) collective-permute-start(bf16[40,512]{1,0:T(8,128)(2,1)S(1)} %before.1), channel_id=1, source_target_pairs={{0,4},{4,0},{1,5},{5,1},{2,6},{6,2},{3,7},{7,3},{8,12},{12,8},{9,1... | collective-permute-start | bytes 122888 | tf_op jit(solution)/shard_map/ppermute | solution.py:454
  13.2 0.8 %inner.1 = (bf16[256,512]{1,0:T(8,128)(2,1)S(1)}, f32[256,512]{1,0:T(8,128)S(1)}) custom-call(f32[256,512]{1,0:T(8,128)S(1)} %own.1.mine_ref.refs_1_, f32[32,512]{1,0:T(8,128)S(1)} %get-tuple-element.26.after_ref.own_ref, bf16[32,512]{1,0:T(8,128)(2,1)S(1)} %collective-permute-done.2.other_ref, f32[3,3,512]{2,1,0:T(4,128)S(1)} %get-tuple-element.29.taps_ref, ...), custom_call_target="tpu_custom_call" | custom-call | flops 268435456 | bytes 3000320 | tf_op jit(solution)/shard_map/inner/pallas_call | solution.py:20
  14.0 0.2 %collective-permute-done.3.refs_0_ = bf16[40,512]{1,0:T(8,128)(2,1)S(1)} collective-permute-done((bf16[40,512]{1,0:T(8,128)(2,1)S(1)}, bf16[40,512]{1,0:T(8,128)(2,1)S(1)}, u32[]{:S(2)}, u32[]{:S(2)}) %collective-permute-start.3) | collective-permute-done | bytes 40992 | tf_op jit(solution)/shard_map/ppermute | solution.py:442
  14.1 1.1 %first.1.before_ref = bf16[256,512]{1,0:T(8,128)(2,1)} custom-call(bf16[256,512]{1,0:T(8,128)(2,1)S(1)} %get-tuple-element.34.inner_ref, f32[256,512]{1,0:T(8,128)S(1)} %get-tuple-element.35.totals_ref, f32[3,3,512]{2,1,0:T(4,128)S(1)} %get-tuple-element.29.taps_ref, f32[256,512]{1,0:T(8,128)S(1)} %gate.1.gate_ref.refs_2_, ...), custom_call_target="tpu_custom_call" | custom-call | bytes 2680832 | tf_op jit(solution)/shard_map/first/pallas_call | solution.py:20
  15.2 0.0 collective-permute-done.7.refs_3_
  15.2 0.5 %collective-permute-done.8.refs_1_ = bf16[40,512]{1,0:T(8,128)(2,1)S(1)} collective-permute-done((bf16[40,512]{1,0:T(8,128)(2,1)S(1)}, bf16[40,512]{1,0:T(8,128)(2,1)S(1)}, u32[]{:S(2)}, u32[]{:S(2)}) %collective-permute-start.8) | collective-permute-done | bytes 40992 | tf_op jit(solution)/shard_map/ppermute | solution.py:454
  (4 shorter events, 0.1 us)
Async XLA Ops:
  0.0 2.0 %collective-permute-start = (bf16[256,512]{1,0:T(8,128)(2,1)}, bf16[256,512]{1,0:T(8,128)(2,1)S(1)}, u32[]{:S(2)}, u32[]{:S(2)}) collective-permute-start(bf16[256,512]{1,0:T(8,128)(2,1)} %bitcast.3), channel_id=1, source_target_pairs={{0,8},{8,0},{16,24},{24,16},{1,9},{9,1},{17,25},{25,17},{2,10},{10... | collective-permute-start | bytes 786440 | tf_op jit(solution)/shard_map/ppermute | solution.py:376
  2.1 6.5 %collective-permute-start.1 = (bf16[64,512]{1,0:T(8,128)(2,1)S(1)}, bf16[64,512]{1,0:T(8,128)(2,1)S(1)}, u32[]{:S(2)}, u32[]{:S(2)}) collective-permute-start(bf16[64,512]{1,0:T(8,128)(2,1)S(1)} %column.1), channel_id=1, source_target_pairs={{0,1},{1,0},{2,3},{3,2},{4,5},{5,4},{6,7},{7,6},{8,12},{9,10},{10,... | collective-permute-start | bytes 196616 | tf_op jit(solution)/shard_map/ppermute | solution.py:421
  4.9 4.6 %collective-permute-start.4 = (bf16[64,512]{1,0:T(8,128)(2,1)S(1)}, bf16[64,512]{1,0:T(8,128)(2,1)S(1)}, u32[]{:S(2)}, u32[]{:S(2)}) collective-permute-start(bf16[64,512]{1,0:T(8,128)(2,1)S(1)} %column.1), channel_id=1, source_target_pairs={{0,17},{1,16},{2,19},{3,18},{4,21},{5,20},{6,23},{7,22},{8,28},{9,... | collective-permute-start | bytes 196616 | tf_op jit(solution)/shard_map/ppermute | solution.py:421
  6.5 5.1 %collective-permute-start.6 = (bf16[64,512]{1,0:T(8,128)(2,1)S(1)}, bf16[64,512]{1,0:T(8,128)(2,1)S(1)}, u32[]{:S(2)}, u32[]{:S(2)}) collective-permute-start(bf16[64,512]{1,0:T(8,128)(2,1)S(1)} %get-tuple-element.39), channel_id=1, source_target_pairs={{0,16},{8,24},{16,0},{24,8},{1,17},{9,25},{17,1},{25,9},{2,18},{10... | collective-permute-start | bytes 196616 | tf_op jit(solution)/shard_map/ppermute | solution.py:424
  7.2 8.0 %collective-permute-start.7 = (bf16[192,512]{1,0:T(8,128)(2,1)S(1)}, bf16[192,512]{1,0:T(8,128)(2,1)S(1)}, u32[]{:S(2)}, u32[]{:S(2)}) collective-permute-start(bf16[192,512]{1,0:T(8,128)(2,1)S(1)} %get-tuple-element.40), channel_id=1, source_target_pairs={{0,16},{8,24},{16,0},{24,8},{1,17},{9,25},{17,1},{25,9},{2,18},{10... | collective-permute-start | bytes 589832 | tf_op jit(solution)/shard_map/ppermute | solution.py:425
  8.7 1.3 %collective-permute-start.2 = (bf16[32,512]{1,0:T(8,128)(2,1)S(1)}, bf16[32,512]{1,0:T(8,128)(2,1)S(1)}, u32[]{:S(2)}, u32[]{:S(2)}) collective-permute-start(bf16[32,512]{1,0:T(8,128)(2,1)S(1)} %get-tuple-element.28), channel_id=1, source_target_pairs={{0,8},{8,0},{16,24},{24,16},{1,9},{9,1},{17,25},{25,17},{2,10},{10... | collective-permute-start | bytes 98312 | tf_op jit(solution)/shard_map/ppermute | solution.py:439
  9.6 2.0 %collective-permute-start.5 = (bf16[32,512]{1,0:T(8,128)(2,1)S(1)}, bf16[32,512]{1,0:T(8,128)(2,1)S(1)}, u32[]{:S(2)}, u32[]{:S(2)}) collective-permute-start(bf16[32,512]{1,0:T(8,128)(2,1)S(1)} %get-tuple-element.37), channel_id=1, source_target_pairs={{0,8},{8,0},{16,24},{24,16},{1,9},{9,1},{17,25},{25,17},{2,10},{10... | collective-permute-start | bytes 98312 | tf_op jit(solution)/shard_map/ppermute | solution.py:452
  10.0 4.1 %collective-permute-start.3 = (bf16[40,512]{1,0:T(8,128)(2,1)S(1)}, bf16[40,512]{1,0:T(8,128)(2,1)S(1)}, u32[]{:S(2)}, u32[]{:S(2)}) collective-permute-start(bf16[40,512]{1,0:T(8,128)(2,1)S(1)} %border.1), channel_id=1, source_target_pairs={{0,4},{4,0},{1,5},{5,1},{2,6},{6,2},{3,7},{7,3},{8,12},{12,8},{9,1... | collective-permute-start | bytes 122888 | tf_op jit(solution)/shard_map/ppermute | solution.py:442
  11.7 4.1 %collective-permute-start.8 = (bf16[40,512]{1,0:T(8,128)(2,1)S(1)}, bf16[40,512]{1,0:T(8,128)(2,1)S(1)}, u32[]{:S(2)}, u32[]{:S(2)}) collective-permute-start(bf16[40,512]{1,0:T(8,128)(2,1)S(1)} %before.1), channel_id=1, source_target_pairs={{0,4},{4,0},{1,5},{5,1},{2,6},{6,2},{3,7},{7,3},{8,12},{12,8},{9,1... | collective-permute-start | bytes 122888 | tf_op jit(solution)/shard_map/ppermute | solution.py:454

commit v25 on v22

--- a/solution.py
+++ b/solution.py
@@ -145,7 +145,11 @@
             outs[2 * d - 1][:, span] = jnp.concatenate(tiles[rounds_h + 1 :]).astype(BF16)
 
 
-def own_kernel(frames, rows, cols, after_ref, partner_ref, table_ref, field_ref, mine_ref):
+def rest_kernel(after_ref, rest_ref, out_ref):
+    out_ref[...] = rest_ref[...]
+
+
+def own_kernel(frames, rows, cols, partner_ref, table_ref, field_ref, mine_ref):
     for lane in range(0, mine_ref.shape[1], LANES):
         span = slice(lane, lane + LANES)
         totals = with_partner(frames, rows, cols, 0, field_ref, partner_ref, table_ref, span)
@@ -388,8 +392,6 @@
         inputs,
         far=len(inputs),
     )
-    (gate,) = call(gate_kernel, "gate", [field], [], [near_x, near_gate])
-
     h_rounds = swaps("height")
     (column,) = call(
         functools.partial(column_kernel, frames, rows, cols),
@@ -424,7 +426,7 @@
     for d in range(1, chips):
         route = [(i, (i + 2 * d) % n_t) for i in range(n_t)]
         firsts.append(lax.ppermute(sent[2 * d - 2], "tm", route))
-        rests.append(lax.ppermute(sent[2 * d - 1], "tm", route))
+        rests.append((sent[2 * d - 1], route))
 
     swap = [(i, i ^ 1) for i in range(n_t)]
     both = [shape((lines, chans), F32), shape((lines, chans), BF16)]
@@ -434,10 +436,14 @@
         "own",
         [field],
         [],
-        [own, partner, table, fields[0]],
+        [partner, table, fields[0]],
         2 * frames * x.size,
     )
+    (gate,) = call(gate_kernel, "gate", [field], [], [near_x, near_gate])
     other = lax.ppermute(other, "tm", swap)
+    for d, (rest, route) in enumerate(rests):
+        (rest,) = call(rest_kernel, "rest", [shape(rest.shape, BF16)], [], [own, rest])
+        rests[d] = lax.ppermute(rest, "tm", route)
     end = [shape((frames * cols + 2 * frames, chans), BF16)] * len(h_rounds)
     ends = call(functools.partial(border_kernel, frames, rows, cols), "border", end, [], [mine, own, other])
     ends = [lax.ppermute(e, "height", pairs) for e, pairs in zip(ends, h_rounds)]

time: 15.9 us -> 15.9 us (level)
  the two profiles are of different devices: /device:TPU:0 before, /device:TPU:4 now
where the time goes in v25:
time: 15.9 us; the launch traced here: 15.7 us
  starting transfers between devices  6.85 us (43%)
  Pallas kernels  5.33 us (34%)
  waiting for transfers between devices  3.41 us (21%)
    pallas_call x14, Pallas kernels, call(): pl.pallas_call(kernel, out_shape=tuple(outs), in_specs=[HBM] * far + [VME...  5.33 us
    ppermute x2, starting transfers between devices, body(): lax.ppermute(e, 'height', pairs)  2.72 us
    ppermute x2, waiting for transfers between devices, body(): columns.append(lax.ppermute(column, ('tm', 'height', 'width'), route))  2.33 us
    ppermute x2, starting transfers between devices, body(): columns.append(lax.ppermute(column, ('tm', 'height', 'width'), route))  2.15 us
    ppermute x1, starting transfers between devices, body(): firsts.append(lax.ppermute(sent[2 * d - 2], 'tm', route))  1.47 us
    ppermute x1, waiting for transfers between devices, body(): rests[d] = lax.ppermute(rest, 'tm', route)  0.69 us
    ppermute x1, starting transfers between devices, body(): rests[d] = lax.ppermute(rest, 'tm', route)  0.37 us
  transfers between devices with their start and end apart: 9, of which 6 were waited for; matrix products, arithmetic and copies ran while one was open for 0% of the time, Pallas kernels for 27%

profile of v25, /device:TPU:4, one launch (start us, length us, event | category | flops | bytes accessed | tf_op | source)
XLA Modules:
  0.0 15.7 jit_solution(3076176361088809274)
XLA Ops:
  0.0 0.0 collective-permute-start
  0.0 1.5 %early.1 = (bf16[256,512]{1,0:T(8,128)(2,1)S(1)}, bf16[512,512]{1,0:T(8,128)(2,1)S(1)}, f32[3,3,512]{2,1,0:T(4,128)S(1)}, bf16[512,512]{1,0:T(8,128)(2,1)S(1)}, ...) custom-call(bf16[16,512]{1,0:T(8,128)(2,1)} %refs_0_.1, ...), custom_call_target="tpu_custom_call" | custom-call | bytes 5232640 | tf_op jit(solution)/shard_map/early/pallas_call | solution.py:20
  1.6 0.2 %collective-permute-done.partner_ref = bf16[256,512]{1,0:T(8,128)(2,1)S(1)} collective-permute-done((bf16[256,512]{1,0:T(8,128)(2,1)}, bf16[256,512]{1,0:T(8,128)(2,1)S(1)}, u32[]{:S(2)}, u32[]{:S(2)}) %collective-permute-start) | collective-permute-done | bytes 262176 | tf_op jit(solution)/shard_map/ppermute | solution.py:380
  1.7 0.1 column.1
  1.8 1.6 %collective-permute-start.1 = (bf16[64,512]{1,0:T(8,128)(2,1)S(1)}, bf16[64,512]{1,0:T(8,128)(2,1)S(1)}, u32[]{:S(2)}, u32[]{:S(2)}) collective-permute-start(bf16[64,512]{1,0:T(8,128)(2,1)S(1)} %column.1), channel_id=1, source_target_pairs={{0,1},{1,0},{2,3},{3,2},{4,5},{5,4},{6,7},{7,6},{8,12},{9,10},{10,... | collective-permute-start | bytes 196616 | tf_op jit(solution)/shard_map/ppermute | solution.py:425
  3.5 0.5 %collective-permute-start.4 = (bf16[64,512]{1,0:T(8,128)(2,1)S(1)}, bf16[64,512]{1,0:T(8,128)(2,1)S(1)}, u32[]{:S(2)}, u32[]{:S(2)}) collective-permute-start(bf16[64,512]{1,0:T(8,128)(2,1)S(1)} %column.1), channel_id=1, source_target_pairs={{0,17},{1,16},{2,19},{3,18},{4,21},{5,20},{6,23},{7,22},{8,28},{9,... | collective-permute-start | bytes 196616 | tf_op jit(solution)/shard_map/ppermute | solution.py:425
  4.0 0.2 %later.1 = (bf16[64,512]{1,0:T(8,128)(2,1)S(1)}, bf16[192,512]{1,0:T(8,128)(2,1)S(1)}) custom-call(bf16[256,512]{1,0:T(8,128)(2,1)S(1)} %collective-permute-done.partner_ref, f32[24,8,512]{2,1,0:T(8,128)S(1)} %get-tuple-element.24.table_ref, f32[256,512]{1,0:T(8,128)S(1)} %get-tuple-element.38.refs_0_), custom_call_target="tpu_custom_call" | custom-call | flops 1048576 | bytes 1441792 | tf_op jit(solution)/shard_map/later/pallas_call | solution.py:20
  4.2 1.5 %collective-permute-start.6 = (bf16[64,512]{1,0:T(8,128)(2,1)S(1)}, bf16[64,512]{1,0:T(8,128)(2,1)S(1)}, u32[]{:S(2)}, u32[]{:S(2)}) collective-permute-start(bf16[64,512]{1,0:T(8,128)(2,1)S(1)} %get-tuple-element.39), channel_id=1, source_target_pairs={{0,16},{8,24},{16,0},{24,8},{1,17},{9,25},{17,1},{25,9},{2,18},{10... | collective-permute-start | bytes 196616 | tf_op jit(solution)/shard_map/ppermute | solution.py:428
  5.6 0.2 %own.1.mine_ref.refs_1_ = f32[256,512]{1,0:T(8,128)S(1)} custom-call(bf16[256,512]{1,0:T(8,128)(2,1)S(1)} %collective-permute-done.partner_ref, f32[24,8,512]{2,1,0:T(8,128)S(1)} %get-tuple-element.24.table_ref, f32[256,512]{1,0:T(8,128)S(1)} %get-tuple-element.25.field_ref), custom_call_target="tpu_custom_call" | custom-call | flops 1048576 | bytes 1703936 | tf_op jit(solution)/shard_map/own/pallas_call | solution.py:20
  5.8 0.3 %collective-permute-done.1.refs_0_ = bf16[64,512]{1,0:T(8,128)(2,1)S(1)} collective-permute-done((bf16[64,512]{1,0:T(8,128)(2,1)S(1)}, bf16[64,512]{1,0:T(8,128)(2,1)S(1)}, u32[]{:S(2)}, u32[]{:S(2)}) %collective-permute-start.1) | collective-permute-done | bytes 65568 | tf_op jit(solution)/shard_map/ppermute | solution.py:425
  6.1 0.1 side.1
  6.2 0.1 collective-permute-start.2
  6.3 0.4 %collective-permute-start.7 = (bf16[192,512]{1,0:T(8,128)(2,1)S(1)}, bf16[192,512]{1,0:T(8,128)(2,1)S(1)}, u32[]{:S(2)}, u32[]{:S(2)}) collective-permute-start(bf16[192,512]{1,0:T(8,128)(2,1)S(1)} %rest.1), channel_id=1, source_target_pairs={{0,16},{8,24},{16,0},{24,8},{1,17},{9,25},{17,1},{25,9},{2,18},{10... | collective-permute-start | bytes 589832 | tf_op jit(solution)/shard_map/ppermute | solution.py:446
  6.7 2.0 %collective-permute-done.4.refs_0_ = bf16[64,512]{1,0:T(8,128)(2,1)S(1)} collective-permute-done((bf16[64,512]{1,0:T(8,128)(2,1)S(1)}, bf16[64,512]{1,0:T(8,128)(2,1)S(1)}, u32[]{:S(2)}, u32[]{:S(2)}) %collective-permute-start.4) | collective-permute-done | bytes 65568 | tf_op jit(solution)/shard_map/ppermute | solution.py:425
  8.7 0.1 beside.1
  8.8 0.1 collective-permute-start.5
  8.8 0.0 collective-permute-done.2.other_ref
  8.9 1.6 %collective-permute-start.3 = (bf16[40,512]{1,0:T(8,128)(2,1)S(1)}, bf16[40,512]{1,0:T(8,128)(2,1)S(1)}, u32[]{:S(2)}, u32[]{:S(2)}) collective-permute-start(bf16[40,512]{1,0:T(8,128)(2,1)S(1)} %border.1), channel_id=1, source_target_pairs={{0,4},{4,0},{1,5},{5,1},{2,6},{6,2},{3,7},{7,3},{8,12},{12,8},{9,1... | collective-permute-start | bytes 122888 | tf_op jit(solution)/shard_map/ppermute | solution.py:449
  10.5 0.0 collective-permute-done.6.refs_2_.refs_0_
  10.5 0.0 collective-permute-done.5.refs_1_.other_ref
  10.6 1.1 %collective-permute-start.8 = (bf16[40,512]{1,0:T(8,128)(2,1)S(1)}, bf16[40,512]{1,0:T(8,128)(2,1)S(1)}, u32[]{:S(2)}, u32[]{:S(2)}) collective-permute-start(bf16[40,512]{1,0:T(8,128)(2,1)S(1)} %before.1), channel_id=1, source_target_pairs={{0,4},{4,0},{1,5},{5,1},{2,6},{6,2},{3,7},{7,3},{8,12},{12,8},{9,1... | collective-permute-start | bytes 122888 | tf_op jit(solution)/shard_map/ppermute | solution.py:461
  11.7 0.4 %gate.1.gate_ref = f32[256,512]{1,0:T(8,128)S(1)} custom-call(bf16[256,512]{1,0:T(8,128)(2,1)S(1)} %get-tuple-element.30.x_ref, bf16[512,512]{1,0:T(8,128)(2,1)S(1)} %get-tuple-element.31.w_ref), custom_call_target="tpu_custom_call" | custom-call | bytes 1310720 | tf_op jit(solution)/shard_map/gate/pallas_call | solution.py:20
  12.1 0.8 %inner.1 = (bf16[256,512]{1,0:T(8,128)(2,1)S(1)}, f32[256,512]{1,0:T(8,128)S(1)}) custom-call(f32[256,512]{1,0:T(8,128)S(1)} %own.1.mine_ref.refs_1_, f32[32,512]{1,0:T(8,128)S(1)} %get-tuple-element.27.own_ref.after_ref, bf16[32,512]{1,0:T(8,128)(2,1)S(1)} %collective-permute-done.2.other_ref, f32[3,3,512]{2,1,0:T(4,128)S(1)} %get-tuple-element.29.taps_ref, ...), custom_call_target="tpu_custom_call" | custom-call | flops 268435456 | bytes 3000320 | tf_op jit(solution)/shard_map/inner/pallas_call | solution.py:20
  12.9 0.1 collective-permute-done.3.refs_0_
  13.0 0.7 %collective-permute-done.7.refs_3_ = bf16[192,512]{1,0:T(8,128)(2,1)S(1)} collective-permute-done((bf16[192,512]{1,0:T(8,128)(2,1)S(1)}, bf16[192,512]{1,0:T(8,128)(2,1)S(1)}, u32[]{:S(2)}, u32[]{:S(2)}) %collective-permute-start.7) | collective-permute-done | bytes 196640 | tf_op jit(solution)/shard_map/ppermute | solution.py:446
  13.7 0.9 %block.1 = (bf16[256,512]{1,0:T(8,128)(2,1)S(1)}, f32[256,512]{1,0:T(8,128)S(1)}) custom-call(bf16[256,512]{1,0:T(8,128)(2,1)S(1)} %get-tuple-element.34.inner_ref, f32[256,512]{1,0:T(8,128)S(1)} %get-tuple-element.35.totals_ref, f32[3,3,512]{2,1,0:T(4,128)S(1)} %get-tuple-element.29.taps_ref, ...), custom_call_target="tpu_custom_call", output_to_operand_aliasing={{0}: (0, {}), {1}: (1, {})} | custom-call | bytes 3524608 | tf_op jit(solution)/shard_map/block/pallas_call | solution.py:20
  14.6 0.1 collective-permute-done.8.refs_1_
  14.6 1.1 %last.1 = bf16[256,512]{1,0:T(8,128)(2,1)} custom-call(bf16[256,512]{1,0:T(8,128)(2,1)} %first.1.before_ref, bf16[256,512]{1,0:T(8,128)(2,1)S(1)} %get-tuple-element.41.inner_ref, f32[256,512]{1,0:T(8,128)S(1)} %get-tuple-element.42.totals_ref, f32[3,3,512]{2,1,0:T(4,128)S(1)} %get-tuple-element.29.taps_ref, ...), custom_call_target="tpu_custom_call", output_to_operand_aliasing={{}: (0, {})} | custom-call | bytes 2983936 | tf_op jit(solution)/shard_map/last/pallas_call | solution.py:20
  (4 shorter events, 0.1 us)
Async XLA Ops:
  0.0 1.7 %collective-permute-start = (bf16[256,512]{1,0:T(8,128)(2,1)}, bf16[256,512]{1,0:T(8,128)(2,1)S(1)}, u32[]{:S(2)}, u32[]{:S(2)}) collective-permute-start(bf16[256,512]{1,0:T(8,128)(2,1)} %bitcast.3), channel_id=1, source_target_pairs={{0,8},{8,0},{16,24},{24,16},{1,9},{9,1},{17,25},{25,17},{2,10},{10... | collective-permute-start | bytes 786440 | tf_op jit(solution)/shard_map/ppermute | solution.py:380
  1.8 4.3 %collective-permute-start.1 = (bf16[64,512]{1,0:T(8,128)(2,1)S(1)}, bf16[64,512]{1,0:T(8,128)(2,1)S(1)}, u32[]{:S(2)}, u32[]{:S(2)}) collective-permute-start(bf16[64,512]{1,0:T(8,128)(2,1)S(1)} %column.1), channel_id=1, source_target_pairs={{0,1},{1,0},{2,3},{3,2},{4,5},{5,4},{6,7},{7,6},{8,12},{9,10},{10,... | collective-permute-start | bytes 196616 | tf_op jit(solution)/shard_map/ppermute | solution.py:425
  3.5 5.2 %collective-permute-start.4 = (bf16[64,512]{1,0:T(8,128)(2,1)S(1)}, bf16[64,512]{1,0:T(8,128)(2,1)S(1)}, u32[]{:S(2)}, u32[]{:S(2)}) collective-permute-start(bf16[64,512]{1,0:T(8,128)(2,1)S(1)} %column.1), channel_id=1, source_target_pairs={{0,17},{1,16},{2,19},{3,18},{4,21},{5,20},{6,23},{7,22},{8,28},{9,... | collective-permute-start | bytes 196616 | tf_op jit(solution)/shard_map/ppermute | solution.py:425
  4.2 6.4 %collective-permute-start.6 = (bf16[64,512]{1,0:T(8,128)(2,1)S(1)}, bf16[64,512]{1,0:T(8,128)(2,1)S(1)}, u32[]{:S(2)}, u32[]{:S(2)}) collective-permute-start(bf16[64,512]{1,0:T(8,128)(2,1)S(1)} %get-tuple-element.39), channel_id=1, source_target_pairs={{0,16},{8,24},{16,0},{24,8},{1,17},{9,25},{17,1},{25,9},{2,18},{10... | collective-permute-start | bytes 196616 | tf_op jit(solution)/shard_map/ppermute | solution.py:428
  6.2 2.6 %collective-permute-start.2 = (bf16[32,512]{1,0:T(8,128)(2,1)S(1)}, bf16[32,512]{1,0:T(8,128)(2,1)S(1)}, u32[]{:S(2)}, u32[]{:S(2)}) collective-permute-start(bf16[32,512]{1,0:T(8,128)(2,1)S(1)} %get-tuple-element.28), channel_id=1, source_target_pairs={{0,8},{8,0},{16,24},{24,16},{1,9},{9,1},{17,25},{25,17},{2,10},{10... | collective-permute-start | bytes 98312 | tf_op jit(solution)/shard_map/ppermute | solution.py:443
  6.3 7.4 %collective-permute-start.7 = (bf16[192,512]{1,0:T(8,128)(2,1)S(1)}, bf16[192,512]{1,0:T(8,128)(2,1)S(1)}, u32[]{:S(2)}, u32[]{:S(2)}) collective-permute-start(bf16[192,512]{1,0:T(8,128)(2,1)S(1)} %rest.1), channel_id=1, source_target_pairs={{0,16},{8,24},{16,0},{24,8},{1,17},{9,25},{17,1},{25,9},{2,18},{10... | collective-permute-start | bytes 589832 | tf_op jit(solution)/shard_map/ppermute | solution.py:446
  8.8 1.8 %collective-permute-start.5 = (bf16[32,512]{1,0:T(8,128)(2,1)S(1)}, bf16[32,512]{1,0:T(8,128)(2,1)S(1)}, u32[]{:S(2)}, u32[]{:S(2)}) collective-permute-start(bf16[32,512]{1,0:T(8,128)(2,1)S(1)} %get-tuple-element.37), channel_id=1, source_target_pairs={{0,8},{8,0},{16,24},{24,16},{1,9},{9,1},{17,25},{25,17},{2,10},{10... | collective-permute-start | bytes 98312 | tf_op jit(solution)/shard_map/ppermute | solution.py:459
  8.9 4.1 %collective-permute-start.3 = (bf16[40,512]{1,0:T(8,128)(2,1)S(1)}, bf16[40,512]{1,0:T(8,128)(2,1)S(1)}, u32[]{:S(2)}, u32[]{:S(2)}) collective-permute-start(bf16[40,512]{1,0:T(8,128)(2,1)S(1)} %border.1), channel_id=1, source_target_pairs={{0,4},{4,0},{1,5},{5,1},{2,6},{6,2},{3,7},{7,3},{8,12},{12,8},{9,1... | collective-permute-start | bytes 122888 | tf_op jit(solution)/shard_map/ppermute | solution.py:449
  10.6 4.1 %collective-permute-start.8 = (bf16[40,512]{1,0:T(8,128)(2,1)S(1)}, bf16[40,512]{1,0:T(8,128)(2,1)S(1)}, u32[]{:S(2)}, u32[]{:S(2)}) collective-permute-start(bf16[40,512]{1,0:T(8,128)(2,1)S(1)} %before.1), channel_id=1, source_target_pairs={{0,4},{4,0},{1,5},{5,1},{2,6},{6,2},{3,7},{7,3},{8,12},{12,8},{9,1... | collective-permute-start | bytes 122888 | tf_op jit(solution)/shard_map/ppermute | solution.py:461

commit v26 on v25

--- a/solution.py
+++ b/solution.py
@@ -288,18 +288,17 @@
     sites = rows * cols
     size = frames * cols
 
-    @pl.when(has_earlier())
-    def _():
+    def add(lines_of):
         for lane in range(0, out_ref.shape[1], LANES):
             span = slice(lane, lane + LANES)
             taps = taps_of(taps_ref, span)
             low, high = both_sides(own_ref[:, span], other_ref[:, span].astype(F32))
-            lines = [jnp.zeros((size, LANES), F32)] * rows
+            lines = None
             for d, (first, rest) in enumerate(zip(firsts, rests), 1):
                 more = [first[i * size : (i + 1) * size, span].astype(F32) for i in range(rounds_h + 1)]
                 more += [rest[i * size : (i + 1) * size, span].astype(F32) for i in range(rows - rounds_h - 1)]
-                more = reordered(more, rounds_h, back=True)
-                lines = [line + later(d, other) for line, other in zip(lines, more)]
+                more = lines_of(more)
+                lines = more if d == 1 else [line + later(d, other) for line, other in zip(lines, more)]
             for t in range(frames):
                 at = t * sites
                 lefts = [low[t * rows + r : t * rows + r + 1] for r in range(rows)]
@@ -309,6 +308,13 @@
                 sums_ref[at : at + sites, span] = total
                 mixed[at : at + sites, span] = total.astype(BF16)
         out_ref[...] = projected(mixed[...], gate_ref[...], wv_ref, wo_ref)
+
+    odd = position("height")[0]
+    if rounds_h > 1:
+        pl.when(has_earlier())(lambda: add(lambda more: reordered(more, rounds_h, back=True)))
+    else:
+        pl.when(jnp.logical_and(has_earlier(), odd))(lambda: add(lambda more: more))
+        pl.when(jnp.logical_and(has_earlier(), jnp.logical_not(odd)))(lambda: add(lambda more: more[::-1]))
 
 
 def complete(frames, rows, cols, inner_ref, totals_ref, taps_ref, gate_ref, wv_ref, wo_ref, ends, out_ref, held, done):

time: 15.9 us -> 15.9 us (level)
  no operation moved by 1% of the time
where the time goes in v26:
time: 15.9 us; the launch traced here: 15.7 us
  starting transfers between devices  6.85 us (43%)
  Pallas kernels  5.28 us (33%)
  waiting for transfers between devices  3.45 us (22%)
    pallas_call x14, Pallas kernels, call(): pl.pallas_call(kernel, out_shape=tuple(outs), in_specs=[HBM] * far + [VME...  5.28 us
    ppermute x2, starting transfers between devices, body(): lax.ppermute(e, 'height', pairs)  2.72 us
    ppermute x2, waiting for transfers between devices, body(): columns.append(lax.ppermute(column, ('tm', 'height', 'width'), route))  2.33 us
    ppermute x2, starting transfers between devices, body(): columns.append(lax.ppermute(column, ('tm', 'height', 'width'), route))  2.15 us
    ppermute x1, starting transfers between devices, body(): firsts.append(lax.ppermute(sent[2 * d - 2], 'tm', route))  1.47 us
    ppermute x1, waiting for transfers between devices, body(): rests[d] = lax.ppermute(rest, 'tm', route)  0.69 us
    ppermute x1, starting transfers between devices, body(): rests[d] = lax.ppermute(rest, 'tm', route)  0.37 us
  transfers between devices with their start and end apart: 9, of which 6 were waited for; matrix products, arithmetic and copies ran while one was open for 0% of the time, Pallas kernels for 27%

profile of v26, /device:TPU:4, one launch (start us, length us, event | category | flops | bytes accessed | tf_op | source)
XLA Modules:
  0.0 15.7 jit_solution(14888062851548109626)
XLA Ops:
  0.0 0.0 collective-permute-start
  0.0 1.5 %early.1 = (bf16[256,512]{1,0:T(8,128)(2,1)S(1)}, bf16[512,512]{1,0:T(8,128)(2,1)S(1)}, f32[3,3,512]{2,1,0:T(4,128)S(1)}, bf16[512,512]{1,0:T(8,128)(2,1)S(1)}, ...) custom-call(bf16[16,512]{1,0:T(8,128)(2,1)} %refs_0_.1, ...), custom_call_target="tpu_custom_call" | custom-call | bytes 5232640 | tf_op jit(solution)/shard_map/early/pallas_call | solution.py:20
  1.6 0.2 %collective-permute-done.partner_ref = bf16[256,512]{1,0:T(8,128)(2,1)S(1)} collective-permute-done((bf16[256,512]{1,0:T(8,128)(2,1)}, bf16[256,512]{1,0:T(8,128)(2,1)S(1)}, u32[]{:S(2)}, u32[]{:S(2)}) %collective-permute-start) | collective-permute-done | bytes 262176 | tf_op jit(solution)/shard_map/ppermute | solution.py:386
  1.7 0.1 column.1
  1.8 1.6 %collective-permute-start.1 = (bf16[64,512]{1,0:T(8,128)(2,1)S(1)}, bf16[64,512]{1,0:T(8,128)(2,1)S(1)}, u32[]{:S(2)}, u32[]{:S(2)}) collective-permute-start(bf16[64,512]{1,0:T(8,128)(2,1)S(1)} %column.1), channel_id=1, source_target_pairs={{0,1},{1,0},{2,3},{3,2},{4,5},{5,4},{6,7},{7,6},{8,12},{9,10},{10,... | collective-permute-start | bytes 196616 | tf_op jit(solution)/shard_map/ppermute | solution.py:431
  3.5 0.5 %collective-permute-start.4 = (bf16[64,512]{1,0:T(8,128)(2,1)S(1)}, bf16[64,512]{1,0:T(8,128)(2,1)S(1)}, u32[]{:S(2)}, u32[]{:S(2)}) collective-permute-start(bf16[64,512]{1,0:T(8,128)(2,1)S(1)} %column.1), channel_id=1, source_target_pairs={{0,17},{1,16},{2,19},{3,18},{4,21},{5,20},{6,23},{7,22},{8,28},{9,... | collective-permute-start | bytes 196616 | tf_op jit(solution)/shard_map/ppermute | solution.py:431
  4.0 0.2 %later.1 = (bf16[64,512]{1,0:T(8,128)(2,1)S(1)}, bf16[192,512]{1,0:T(8,128)(2,1)S(1)}) custom-call(bf16[256,512]{1,0:T(8,128)(2,1)S(1)} %collective-permute-done.partner_ref, f32[24,8,512]{2,1,0:T(8,128)S(1)} %get-tuple-element.24.table_ref, f32[256,512]{1,0:T(8,128)S(1)} %get-tuple-element.38.refs_0_), custom_call_target="tpu_custom_call" | custom-call | flops 1048576 | bytes 1441792 | tf_op jit(solution)/shard_map/later/pallas_call | solution.py:20
  4.2 1.5 %collective-permute-start.6 = (bf16[64,512]{1,0:T(8,128)(2,1)S(1)}, bf16[64,512]{1,0:T(8,128)(2,1)S(1)}, u32[]{:S(2)}, u32[]{:S(2)}) collective-permute-start(bf16[64,512]{1,0:T(8,128)(2,1)S(1)} %get-tuple-element.39), channel_id=1, source_target_pairs={{0,16},{8,24},{16,0},{24,8},{1,17},{9,25},{17,1},{25,9},{2,18},{10... | collective-permute-start | bytes 196616 | tf_op jit(solution)/shard_map/ppermute | solution.py:434
  5.6 0.2 %own.1.mine_ref.refs_1_ = f32[256,512]{1,0:T(8,128)S(1)} custom-call(bf16[256,512]{1,0:T(8,128)(2,1)S(1)} %collective-permute-done.partner_ref, f32[24,8,512]{2,1,0:T(8,128)S(1)} %get-tuple-element.24.table_ref, f32[256,512]{1,0:T(8,128)S(1)} %get-tuple-element.25.field_ref), custom_call_target="tpu_custom_call" | custom-call | flops 1048576 | bytes 1703936 | tf_op jit(solution)/shard_map/own/pallas_call | solution.py:20
  5.8 0.3 %collective-permute-done.1.refs_0_ = bf16[64,512]{1,0:T(8,128)(2,1)S(1)} collective-permute-done((bf16[64,512]{1,0:T(8,128)(2,1)S(1)}, bf16[64,512]{1,0:T(8,128)(2,1)S(1)}, u32[]{:S(2)}, u32[]{:S(2)}) %collective-permute-start.1) | collective-permute-done | bytes 65568 | tf_op jit(solution)/shard_map/ppermute | solution.py:431
  6.1 0.1 side.1
  6.2 0.1 collective-permute-start.2
  6.3 0.4 %collective-permute-start.7 = (bf16[192,512]{1,0:T(8,128)(2,1)S(1)}, bf16[192,512]{1,0:T(8,128)(2,1)S(1)}, u32[]{:S(2)}, u32[]{:S(2)}) collective-permute-start(bf16[192,512]{1,0:T(8,128)(2,1)S(1)} %rest.1), channel_id=1, source_target_pairs={{0,16},{8,24},{16,0},{24,8},{1,17},{9,25},{17,1},{25,9},{2,18},{10... | collective-permute-start | bytes 589832 | tf_op jit(solution)/shard_map/ppermute | solution.py:452
  6.7 2.0 %collective-permute-done.4.refs_0_ = bf16[64,512]{1,0:T(8,128)(2,1)S(1)} collective-permute-done((bf16[64,512]{1,0:T(8,128)(2,1)S(1)}, bf16[64,512]{1,0:T(8,128)(2,1)S(1)}, u32[]{:S(2)}, u32[]{:S(2)}) %collective-permute-start.4) | collective-permute-done | bytes 65568 | tf_op jit(solution)/shard_map/ppermute | solution.py:431
  8.7 0.1 beside.1
  8.8 0.1 collective-permute-start.5
  8.8 0.0 collective-permute-done.2.other_ref
  8.9 1.6 %collective-permute-start.3 = (bf16[40,512]{1,0:T(8,128)(2,1)S(1)}, bf16[40,512]{1,0:T(8,128)(2,1)S(1)}, u32[]{:S(2)}, u32[]{:S(2)}) collective-permute-start(bf16[40,512]{1,0:T(8,128)(2,1)S(1)} %border.1), channel_id=1, source_target_pairs={{0,4},{4,0},{1,5},{5,1},{2,6},{6,2},{3,7},{7,3},{8,12},{12,8},{9,1... | collective-permute-start | bytes 122888 | tf_op jit(solution)/shard_map/ppermute | solution.py:455
  10.5 0.0 collective-permute-done.6.refs_2_.refs_0_
  10.5 0.0 collective-permute-done.5.refs_1_.other_ref
  10.6 1.1 %collective-permute-start.8 = (bf16[40,512]{1,0:T(8,128)(2,1)S(1)}, bf16[40,512]{1,0:T(8,128)(2,1)S(1)}, u32[]{:S(2)}, u32[]{:S(2)}) collective-permute-start(bf16[40,512]{1,0:T(8,128)(2,1)S(1)} %before.1), channel_id=1, source_target_pairs={{0,4},{4,0},{1,5},{5,1},{2,6},{6,2},{3,7},{7,3},{8,12},{12,8},{9,1... | collective-permute-start | bytes 122888 | tf_op jit(solution)/shard_map/ppermute | solution.py:467
  11.7 0.4 %gate.1.gate_ref = f32[256,512]{1,0:T(8,128)S(1)} custom-call(bf16[256,512]{1,0:T(8,128)(2,1)S(1)} %get-tuple-element.30.x_ref, bf16[512,512]{1,0:T(8,128)(2,1)S(1)} %get-tuple-element.31.w_ref), custom_call_target="tpu_custom_call" | custom-call | bytes 1310720 | tf_op jit(solution)/shard_map/gate/pallas_call | solution.py:20
  12.1 0.8 %inner.1 = (bf16[256,512]{1,0:T(8,128)(2,1)S(1)}, f32[256,512]{1,0:T(8,128)S(1)}) custom-call(f32[256,512]{1,0:T(8,128)S(1)} %own.1.mine_ref.refs_1_, f32[32,512]{1,0:T(8,128)S(1)} %get-tuple-element.27.own_ref.after_ref, bf16[32,512]{1,0:T(8,128)(2,1)S(1)} %collective-permute-done.2.other_ref, f32[3,3,512]{2,1,0:T(4,128)S(1)} %get-tuple-element.29.taps_ref, ...), custom_call_target="tpu_custom_call" | custom-call | flops 268435456 | bytes 3000320 | tf_op jit(solution)/shard_map/inner/pallas_call | solution.py:20
  12.9 0.1 collective-permute-done.3.refs_0_
  13.0 0.7 %collective-permute-done.7.refs_3_ = bf16[192,512]{1,0:T(8,128)(2,1)S(1)} collective-permute-done((bf16[192,512]{1,0:T(8,128)(2,1)S(1)}, bf16[192,512]{1,0:T(8,128)(2,1)S(1)}, u32[]{:S(2)}, u32[]{:S(2)}) %collective-permute-start.7) | collective-permute-done | bytes 196640 | tf_op jit(solution)/shard_map/ppermute | solution.py:452
  13.7 0.8 %block.1 = (bf16[256,512]{1,0:T(8,128)(2,1)S(1)}, f32[256,512]{1,0:T(8,128)S(1)}) custom-call(bf16[256,512]{1,0:T(8,128)(2,1)S(1)} %get-tuple-element.34.inner_ref, f32[256,512]{1,0:T(8,128)S(1)} %get-tuple-element.35.totals_ref, f32[3,3,512]{2,1,0:T(4,128)S(1)} %get-tuple-element.29.taps_ref, ...), custom_call_target="tpu_custom_call", output_to_operand_aliasing={{0}: (0, {}), {1}: (1, {})} | custom-call | bytes 3524608 | tf_op jit(solution)/shard_map/block/pallas_call | solution.py:20
  14.5 0.1 collective-permute-done.8.refs_1_
  14.6 1.1 %last.1 = bf16[256,512]{1,0:T(8,128)(2,1)} custom-call(bf16[256,512]{1,0:T(8,128)(2,1)} %first.1.before_ref, bf16[256,512]{1,0:T(8,128)(2,1)S(1)} %get-tuple-element.41.inner_ref, f32[256,512]{1,0:T(8,128)S(1)} %get-tuple-element.42.totals_ref, f32[3,3,512]{2,1,0:T(4,128)S(1)} %get-tuple-element.29.taps_ref, ...), custom_call_target="tpu_custom_call", output_to_operand_aliasing={{}: (0, {})} | custom-call | bytes 2983936 | tf_op jit(solution)/shard_map/last/pallas_call | solution.py:20
  (4 shorter events, 0.1 us)
Async XLA Ops:
  0.0 1.7 %collective-permute-start = (bf16[256,512]{1,0:T(8,128)(2,1)}, bf16[256,512]{1,0:T(8,128)(2,1)S(1)}, u32[]{:S(2)}, u32[]{:S(2)}) collective-permute-start(bf16[256,512]{1,0:T(8,128)(2,1)} %bitcast.3), channel_id=1, source_target_pairs={{0,8},{8,0},{16,24},{24,16},{1,9},{9,1},{17,25},{25,17},{2,10},{10... | collective-permute-start | bytes 786440 | tf_op jit(solution)/shard_map/ppermute | solution.py:386
  1.8 4.3 %collective-permute-start.1 = (bf16[64,512]{1,0:T(8,128)(2,1)S(1)}, bf16[64,512]{1,0:T(8,128)(2,1)S(1)}, u32[]{:S(2)}, u32[]{:S(2)}) collective-permute-start(bf16[64,512]{1,0:T(8,128)(2,1)S(1)} %column.1), channel_id=1, source_target_pairs={{0,1},{1,0},{2,3},{3,2},{4,5},{5,4},{6,7},{7,6},{8,12},{9,10},{10,... | collective-permute-start | bytes 196616 | tf_op jit(solution)/shard_map/ppermute | solution.py:431
  3.5 5.2 %collective-permute-start.4 = (bf16[64,512]{1,0:T(8,128)(2,1)S(1)}, bf16[64,512]{1,0:T(8,128)(2,1)S(1)}, u32[]{:S(2)}, u32[]{:S(2)}) collective-permute-start(bf16[64,512]{1,0:T(8,128)(2,1)S(1)} %column.1), channel_id=1, source_target_pairs={{0,17},{1,16},{2,19},{3,18},{4,21},{5,20},{6,23},{7,22},{8,28},{9,... | collective-permute-start | bytes 196616 | tf_op jit(solution)/shard_map/ppermute | solution.py:431
  4.2 6.4 %collective-permute-start.6 = (bf16[64,512]{1,0:T(8,128)(2,1)S(1)}, bf16[64,512]{1,0:T(8,128)(2,1)S(1)}, u32[]{:S(2)}, u32[]{:S(2)}) collective-permute-start(bf16[64,512]{1,0:T(8,128)(2,1)S(1)} %get-tuple-element.39), channel_id=1, source_target_pairs={{0,16},{8,24},{16,0},{24,8},{1,17},{9,25},{17,1},{25,9},{2,18},{10... | collective-permute-start | bytes 196616 | tf_op jit(solution)/shard_map/ppermute | solution.py:434
  6.2 2.6 %collective-permute-start.2 = (bf16[32,512]{1,0:T(8,128)(2,1)S(1)}, bf16[32,512]{1,0:T(8,128)(2,1)S(1)}, u32[]{:S(2)}, u32[]{:S(2)}) collective-permute-start(bf16[32,512]{1,0:T(8,128)(2,1)S(1)} %get-tuple-element.28), channel_id=1, source_target_pairs={{0,8},{8,0},{16,24},{24,16},{1,9},{9,1},{17,25},{25,17},{2,10},{10... | collective-permute-start | bytes 98312 | tf_op jit(solution)/shard_map/ppermute | solution.py:449
  6.3 7.4 %collective-permute-start.7 = (bf16[192,512]{1,0:T(8,128)(2,1)S(1)}, bf16[192,512]{1,0:T(8,128)(2,1)S(1)}, u32[]{:S(2)}, u32[]{:S(2)}) collective-permute-start(bf16[192,512]{1,0:T(8,128)(2,1)S(1)} %rest.1), channel_id=1, source_target_pairs={{0,16},{8,24},{16,0},{24,8},{1,17},{9,25},{17,1},{25,9},{2,18},{10... | collective-permute-start | bytes 589832 | tf_op jit(solution)/shard_map/ppermute | solution.py:452
  8.8 1.8 %collective-permute-start.5 = (bf16[32,512]{1,0:T(8,128)(2,1)S(1)}, bf16[32,512]{1,0:T(8,128)(2,1)S(1)}, u32[]{:S(2)}, u32[]{:S(2)}) collective-permute-start(bf16[32,512]{1,0:T(8,128)(2,1)S(1)} %get-tuple-element.37), channel_id=1, source_target_pairs={{0,8},{8,0},{16,24},{24,16},{1,9},{9,1},{17,25},{25,17},{2,10},{10... | collective-permute-start | bytes 98312 | tf_op jit(solution)/shard_map/ppermute | solution.py:465
  8.9 4.1 %collective-permute-start.3 = (bf16[40,512]{1,0:T(8,128)(2,1)S(1)}, bf16[40,512]{1,0:T(8,128)(2,1)S(1)}, u32[]{:S(2)}, u32[]{:S(2)}) collective-permute-start(bf16[40,512]{1,0:T(8,128)(2,1)S(1)} %border.1), channel_id=1, source_target_pairs={{0,4},{4,0},{1,5},{5,1},{2,6},{6,2},{3,7},{7,3},{8,12},{12,8},{9,1... | collective-permute-start | bytes 122888 | tf_op jit(solution)/shard_map/ppermute | solution.py:455
  10.6 4.1 %collective-permute-start.8 = (bf16[40,512]{1,0:T(8,128)(2,1)S(1)}, bf16[40,512]{1,0:T(8,128)(2,1)S(1)}, u32[]{:S(2)}, u32[]{:S(2)}) collective-permute-start(bf16[40,512]{1,0:T(8,128)(2,1)S(1)} %before.1), channel_id=1, source_target_pairs={{0,4},{4,0},{1,5},{5,1},{2,6},{6,2},{3,7},{7,3},{8,12},{12,8},{9,1... | collective-permute-start | bytes 122888 | tf_op jit(solution)/shard_map/ppermute | solution.py:467

commit v27 on v25

--- a/solution.py
+++ b/solution.py
@@ -51,11 +51,11 @@
 
 
 def on_right():
-    return lax.rem(lax.axis_index("tm") + lax.axis_index("width"), 2) == 0
+    return lax.rem(lax.axis_index("tm") + lax.axis_index("width"), 2) == 1
 
 
 def facing(core, column, columns):
-    to = column + (1 if (core + column) % 2 == 0 else -1)
+    to = column + (1 if (core + column) % 2 == 1 else -1)
     return to if 0 <= to < columns else column
 
 

time: 15.9 us -> 15.9 us (level)
  the two profiles are of different devices: /device:TPU:4 before, /device:TPU:12 now
where the time goes in v27:
time: 15.9 us; the launch traced here: 15.7 us
  starting transfers between devices  7.01 us (44%)
  Pallas kernels  5.32 us (33%)
  waiting for transfers between devices  3.26 us (21%)
    pallas_call x14, Pallas kernels, call(): pl.pallas_call(kernel, out_shape=tuple(outs), in_specs=[HBM] * far + [VME...  5.32 us
    ppermute x2, starting transfers between devices, body(): lax.ppermute(e, 'height', pairs)  2.67 us
    ppermute x2, waiting for transfers between devices, body(): columns.append(lax.ppermute(column, ('tm', 'height', 'width'), route))  2.17 us
    ppermute x2, starting transfers between devices, body(): columns.append(lax.ppermute(column, ('tm', 'height', 'width'), route))  2.15 us
    ppermute x1, starting transfers between devices, body(): firsts.append(lax.ppermute(sent[2 * d - 2], 'tm', route))  1.47 us
    ppermute x1, waiting for transfers between devices, body(): rests[d] = lax.ppermute(rest, 'tm', route)  0.64 us
    ppermute x1, starting transfers between devices, body(): rests[d] = lax.ppermute(rest, 'tm', route)  0.57 us
  transfers between devices with their start and end apart: 9, of which 6 were waited for; matrix products, arithmetic and copies ran while one was open for 0% of the time, Pallas kernels for 27%

profile of v27, /device:TPU:12, one launch (start us, length us, event | category | flops | bytes accessed | tf_op | source)
XLA Modules:
  0.0 15.7 jit_solution(14109659244209938380)
XLA Ops:
  0.0 0.0 collective-permute-start
  0.0 1.5 %early.1 = (bf16[256,512]{1,0:T(8,128)(2,1)S(1)}, bf16[512,512]{1,0:T(8,128)(2,1)S(1)}, f32[3,3,512]{2,1,0:T(4,128)S(1)}, bf16[512,512]{1,0:T(8,128)(2,1)S(1)}, ...) custom-call(bf16[16,512]{1,0:T(8,128)(2,1)} %refs_0_.1, ...), custom_call_target="tpu_custom_call" | custom-call | bytes 5232640 | tf_op jit(solution)/shard_map/early/pallas_call | solution.py:20
  1.6 0.2 %collective-permute-done.partner_ref = bf16[256,512]{1,0:T(8,128)(2,1)S(1)} collective-permute-done((bf16[256,512]{1,0:T(8,128)(2,1)}, bf16[256,512]{1,0:T(8,128)(2,1)S(1)}, u32[]{:S(2)}, u32[]{:S(2)}) %collective-permute-start) | collective-permute-done | bytes 262176 | tf_op jit(solution)/shard_map/ppermute | solution.py:380
  1.7 0.1 column.1
  1.8 1.6 %collective-permute-start.1 = (bf16[64,512]{1,0:T(8,128)(2,1)S(1)}, bf16[64,512]{1,0:T(8,128)(2,1)S(1)}, u32[]{:S(2)}, u32[]{:S(2)}) collective-permute-start(bf16[64,512]{1,0:T(8,128)(2,1)S(1)} %column.1), channel_id=1, source_target_pairs={{0,4},{1,2},{2,1},{3,7},{4,0},{5,6},{6,5},{7,3},{8,9},{9,8},{10,11... | collective-permute-start | bytes 196616 | tf_op jit(solution)/shard_map/ppermute | solution.py:425
  3.5 0.5 %collective-permute-start.4 = (bf16[64,512]{1,0:T(8,128)(2,1)S(1)}, bf16[64,512]{1,0:T(8,128)(2,1)S(1)}, u32[]{:S(2)}, u32[]{:S(2)}) collective-permute-start(bf16[64,512]{1,0:T(8,128)(2,1)S(1)} %column.1), channel_id=1, source_target_pairs={{0,20},{1,18},{2,17},{3,23},{4,16},{5,22},{6,21},{7,19},{8,25},{9,... | collective-permute-start | bytes 196616 | tf_op jit(solution)/shard_map/ppermute | solution.py:425
  4.0 0.2 %later.1 = (bf16[64,512]{1,0:T(8,128)(2,1)S(1)}, bf16[192,512]{1,0:T(8,128)(2,1)S(1)}) custom-call(bf16[256,512]{1,0:T(8,128)(2,1)S(1)} %collective-permute-done.partner_ref, f32[24,8,512]{2,1,0:T(8,128)S(1)} %get-tuple-element.24.table_ref, f32[256,512]{1,0:T(8,128)S(1)} %get-tuple-element.38.refs_0_), custom_call_target="tpu_custom_call" | custom-call | flops 1048576 | bytes 1441792 | tf_op jit(solution)/shard_map/later/pallas_call | solution.py:20
  4.2 1.5 %collective-permute-start.6 = (bf16[64,512]{1,0:T(8,128)(2,1)S(1)}, bf16[64,512]{1,0:T(8,128)(2,1)S(1)}, u32[]{:S(2)}, u32[]{:S(2)}) collective-permute-start(bf16[64,512]{1,0:T(8,128)(2,1)S(1)} %get-tuple-element.39), channel_id=1, source_target_pairs={{0,16},{8,24},{16,0},{24,8},{1,17},{9,25},{17,1},{25,9},{2,18},{10... | collective-permute-start | bytes 196616 | tf_op jit(solution)/shard_map/ppermute | solution.py:428
  5.6 0.2 %own.1.mine_ref.refs_1_ = f32[256,512]{1,0:T(8,128)S(1)} custom-call(bf16[256,512]{1,0:T(8,128)(2,1)S(1)} %collective-permute-done.partner_ref, f32[24,8,512]{2,1,0:T(8,128)S(1)} %get-tuple-element.24.table_ref, f32[256,512]{1,0:T(8,128)S(1)} %get-tuple-element.25.field_ref), custom_call_target="tpu_custom_call" | custom-call | flops 1048576 | bytes 1703936 | tf_op jit(solution)/shard_map/own/pallas_call | solution.py:20
  5.8 0.3 %collective-permute-done.1.refs_0_ = bf16[64,512]{1,0:T(8,128)(2,1)S(1)} collective-permute-done((bf16[64,512]{1,0:T(8,128)(2,1)S(1)}, bf16[64,512]{1,0:T(8,128)(2,1)S(1)}, u32[]{:S(2)}, u32[]{:S(2)}) %collective-permute-start.1) | collective-permute-done | bytes 65568 | tf_op jit(solution)/shard_map/ppermute | solution.py:425
  6.1 0.1 side.1
  6.2 0.1 collective-permute-start.2
  6.3 0.6 %collective-permute-start.7 = (bf16[192,512]{1,0:T(8,128)(2,1)S(1)}, bf16[192,512]{1,0:T(8,128)(2,1)S(1)}, u32[]{:S(2)}, u32[]{:S(2)}) collective-permute-start(bf16[192,512]{1,0:T(8,128)(2,1)S(1)} %rest.1), channel_id=1, source_target_pairs={{0,16},{8,24},{16,0},{24,8},{1,17},{9,25},{17,1},{25,9},{2,18},{10... | collective-permute-start | bytes 589832 | tf_op jit(solution)/shard_map/ppermute | solution.py:446
  6.9 1.8 %collective-permute-done.4.refs_0_ = bf16[64,512]{1,0:T(8,128)(2,1)S(1)} collective-permute-done((bf16[64,512]{1,0:T(8,128)(2,1)S(1)}, bf16[64,512]{1,0:T(8,128)(2,1)S(1)}, u32[]{:S(2)}, u32[]{:S(2)}) %collective-permute-start.4) | collective-permute-done | bytes 65568 | tf_op jit(solution)/shard_map/ppermute | solution.py:425
  8.7 0.1 beside.1
  8.8 0.1 collective-permute-start.5
  8.9 0.0 collective-permute-done.2.other_ref
  9.0 1.6 %collective-permute-start.3 = (bf16[40,512]{1,0:T(8,128)(2,1)S(1)}, bf16[40,512]{1,0:T(8,128)(2,1)S(1)}, u32[]{:S(2)}, u32[]{:S(2)}) collective-permute-start(bf16[40,512]{1,0:T(8,128)(2,1)S(1)} %border.1), channel_id=1, source_target_pairs={{0,4},{4,0},{1,5},{5,1},{2,6},{6,2},{3,7},{7,3},{8,12},{12,8},{9,1... | collective-permute-start | bytes 122888 | tf_op jit(solution)/shard_map/ppermute | solution.py:449
  10.5 0.0 collective-permute-done.6.refs_2_.refs_0_
  10.5 0.0 collective-permute-done.5.refs_1_.other_ref
  10.6 1.1 %collective-permute-start.8 = (bf16[40,512]{1,0:T(8,128)(2,1)S(1)}, bf16[40,512]{1,0:T(8,128)(2,1)S(1)}, u32[]{:S(2)}, u32[]{:S(2)}) collective-permute-start(bf16[40,512]{1,0:T(8,128)(2,1)S(1)} %before.1), channel_id=1, source_target_pairs={{0,4},{4,0},{1,5},{5,1},{2,6},{6,2},{3,7},{7,3},{8,12},{12,8},{9,1... | collective-permute-start | bytes 122888 | tf_op jit(solution)/shard_map/ppermute | solution.py:461
  11.7 0.4 %gate.1.gate_ref = f32[256,512]{1,0:T(8,128)S(1)} custom-call(bf16[256,512]{1,0:T(8,128)(2,1)S(1)} %get-tuple-element.30.x_ref, bf16[512,512]{1,0:T(8,128)(2,1)S(1)} %get-tuple-element.31.w_ref), custom_call_target="tpu_custom_call" | custom-call | bytes 1310720 | tf_op jit(solution)/shard_map/gate/pallas_call | solution.py:20
  12.1 0.8 %inner.1 = (bf16[256,512]{1,0:T(8,128)(2,1)S(1)}, f32[256,512]{1,0:T(8,128)S(1)}) custom-call(f32[256,512]{1,0:T(8,128)S(1)} %own.1.mine_ref.refs_1_, f32[32,512]{1,0:T(8,128)S(1)} %get-tuple-element.27.own_ref.after_ref, bf16[32,512]{1,0:T(8,128)(2,1)S(1)} %collective-permute-done.2.other_ref, f32[3,3,512]{2,1,0:T(4,128)S(1)} %get-tuple-element.29.taps_ref, ...), custom_call_target="tpu_custom_call" | custom-call | flops 268435456 | bytes 3000320 | tf_op jit(solution)/shard_map/inner/pallas_call | solution.py:20
  12.9 0.2 %collective-permute-done.3.refs_0_ = bf16[40,512]{1,0:T(8,128)(2,1)S(1)} collective-permute-done((bf16[40,512]{1,0:T(8,128)(2,1)S(1)}, bf16[40,512]{1,0:T(8,128)(2,1)S(1)}, u32[]{:S(2)}, u32[]{:S(2)}) %collective-permute-start.3) | collective-permute-done | bytes 40992 | tf_op jit(solution)/shard_map/ppermute | solution.py:449
  13.0 0.6 %collective-permute-done.7.refs_3_ = bf16[192,512]{1,0:T(8,128)(2,1)S(1)} collective-permute-done((bf16[192,512]{1,0:T(8,128)(2,1)S(1)}, bf16[192,512]{1,0:T(8,128)(2,1)S(1)}, u32[]{:S(2)}, u32[]{:S(2)}) %collective-permute-start.7) | collective-permute-done | bytes 196640 | tf_op jit(solution)/shard_map/ppermute | solution.py:446
  13.7 0.9 %block.1 = (bf16[256,512]{1,0:T(8,128)(2,1)S(1)}, f32[256,512]{1,0:T(8,128)S(1)}) custom-call(bf16[256,512]{1,0:T(8,128)(2,1)S(1)} %get-tuple-element.34.inner_ref, f32[256,512]{1,0:T(8,128)S(1)} %get-tuple-element.35.totals_ref, f32[3,3,512]{2,1,0:T(4,128)S(1)} %get-tuple-element.29.taps_ref, ...), custom_call_target="tpu_custom_call", output_to_operand_aliasing={{0}: (0, {}), {1}: (1, {})} | custom-call | bytes 3524608 | tf_op jit(solution)/shard_map/block/pallas_call | solution.py:20
  14.6 0.1 collective-permute-done.8.refs_1_
  14.6 1.1 %last.1 = bf16[256,512]{1,0:T(8,128)(2,1)} custom-call(bf16[256,512]{1,0:T(8,128)(2,1)} %first.1.before_ref, bf16[256,512]{1,0:T(8,128)(2,1)S(1)} %get-tuple-element.41.inner_ref, f32[256,512]{1,0:T(8,128)S(1)} %get-tuple-element.42.totals_ref, f32[3,3,512]{2,1,0:T(4,128)S(1)} %get-tuple-element.29.taps_ref, ...), custom_call_target="tpu_custom_call", output_to_operand_aliasing={{}: (0, {})} | custom-call | bytes 2983936 | tf_op jit(solution)/shard_map/last/pallas_call | solution.py:20
  (4 shorter events, 0.1 us)
Async XLA Ops:
  0.0 1.7 %collective-permute-start = (bf16[256,512]{1,0:T(8,128)(2,1)}, bf16[256,512]{1,0:T(8,128)(2,1)S(1)}, u32[]{:S(2)}, u32[]{:S(2)}) collective-permute-start(bf16[256,512]{1,0:T(8,128)(2,1)} %bitcast.3), channel_id=1, source_target_pairs={{0,8},{8,0},{16,24},{24,16},{1,9},{9,1},{17,25},{25,17},{2,10},{10... | collective-permute-start | bytes 786440 | tf_op jit(solution)/shard_map/ppermute | solution.py:380
  1.8 4.3 %collective-permute-start.1 = (bf16[64,512]{1,0:T(8,128)(2,1)S(1)}, bf16[64,512]{1,0:T(8,128)(2,1)S(1)}, u32[]{:S(2)}, u32[]{:S(2)}) collective-permute-start(bf16[64,512]{1,0:T(8,128)(2,1)S(1)} %column.1), channel_id=1, source_target_pairs={{0,4},{1,2},{2,1},{3,7},{4,0},{5,6},{6,5},{7,3},{8,9},{9,8},{10,11... | collective-permute-start | bytes 196616 | tf_op jit(solution)/shard_map/ppermute | solution.py:425
  3.5 5.3 %collective-permute-start.4 = (bf16[64,512]{1,0:T(8,128)(2,1)S(1)}, bf16[64,512]{1,0:T(8,128)(2,1)S(1)}, u32[]{:S(2)}, u32[]{:S(2)}) collective-permute-start(bf16[64,512]{1,0:T(8,128)(2,1)S(1)} %column.1), channel_id=1, source_target_pairs={{0,20},{1,18},{2,17},{3,23},{4,16},{5,22},{6,21},{7,19},{8,25},{9,... | collective-permute-start | bytes 196616 | tf_op jit(solution)/shard_map/ppermute | solution.py:425
  4.2 6.4 %collective-permute-start.6 = (bf16[64,512]{1,0:T(8,128)(2,1)S(1)}, bf16[64,512]{1,0:T(8,128)(2,1)S(1)}, u32[]{:S(2)}, u32[]{:S(2)}) collective-permute-start(bf16[64,512]{1,0:T(8,128)(2,1)S(1)} %get-tuple-element.39), channel_id=1, source_target_pairs={{0,16},{8,24},{16,0},{24,8},{1,17},{9,25},{17,1},{25,9},{2,18},{10... | collective-permute-start | bytes 196616 | tf_op jit(solution)/shard_map/ppermute | solution.py:428
  6.2 2.7 %collective-permute-start.2 = (bf16[32,512]{1,0:T(8,128)(2,1)S(1)}, bf16[32,512]{1,0:T(8,128)(2,1)S(1)}, u32[]{:S(2)}, u32[]{:S(2)}) collective-permute-start(bf16[32,512]{1,0:T(8,128)(2,1)S(1)} %get-tuple-element.28), channel_id=1, source_target_pairs={{0,8},{8,0},{16,24},{24,16},{1,9},{9,1},{17,25},{25,17},{2,10},{10... | collective-permute-start | bytes 98312 | tf_op jit(solution)/shard_map/ppermute | solution.py:443
  6.3 7.4 %collective-permute-start.7 = (bf16[192,512]{1,0:T(8,128)(2,1)S(1)}, bf16[192,512]{1,0:T(8,128)(2,1)S(1)}, u32[]{:S(2)}, u32[]{:S(2)}) collective-permute-start(bf16[192,512]{1,0:T(8,128)(2,1)S(1)} %rest.1), channel_id=1, source_target_pairs={{0,16},{8,24},{16,0},{24,8},{1,17},{9,25},{17,1},{25,9},{2,18},{10... | collective-permute-start | bytes 589832 | tf_op jit(solution)/shard_map/ppermute | solution.py:446
  8.8 1.7 %collective-permute-start.5 = (bf16[32,512]{1,0:T(8,128)(2,1)S(1)}, bf16[32,512]{1,0:T(8,128)(2,1)S(1)}, u32[]{:S(2)}, u32[]{:S(2)}) collective-permute-start(bf16[32,512]{1,0:T(8,128)(2,1)S(1)} %get-tuple-element.37), channel_id=1, source_target_pairs={{0,8},{8,0},{16,24},{24,16},{1,9},{9,1},{17,25},{25,17},{2,10},{10... | collective-permute-start | bytes 98312 | tf_op jit(solution)/shard_map/ppermute | solution.py:459
  9.0 4.1 %collective-permute-start.3 = (bf16[40,512]{1,0:T(8,128)(2,1)S(1)}, bf16[40,512]{1,0:T(8,128)(2,1)S(1)}, u32[]{:S(2)}, u32[]{:S(2)}) collective-permute-start(bf16[40,512]{1,0:T(8,128)(2,1)S(1)} %border.1), channel_id=1, source_target_pairs={{0,4},{4,0},{1,5},{5,1},{2,6},{6,2},{3,7},{7,3},{8,12},{12,8},{9,1... | collective-permute-start | bytes 122888 | tf_op jit(solution)/shard_map/ppermute | solution.py:449
  10.6 4.1 %collective-permute-start.8 = (bf16[40,512]{1,0:T(8,128)(2,1)S(1)}, bf16[40,512]{1,0:T(8,128)(2,1)S(1)}, u32[]{:S(2)}, u32[]{:S(2)}) collective-permute-start(bf16[40,512]{1,0:T(8,128)(2,1)S(1)} %before.1), channel_id=1, source_target_pairs={{0,4},{4,0},{1,5},{5,1},{2,6},{6,2},{3,7},{7,3},{8,12},{12,8},{9,1... | collective-permute-start | bytes 122888 | tf_op jit(solution)/shard_map/ppermute | solution.py:461

commit v28 on v26

--- a/solution.py
+++ b/solution.py
@@ -51,11 +51,11 @@
 
 
 def on_right():
-    return lax.rem(lax.axis_index("tm") + lax.axis_index("width"), 2) == 0
+    return lax.rem(lax.axis_index("tm") + lax.axis_index("width"), 2) == 1
 
 
 def facing(core, column, columns):
-    to = column + (1 if (core + column) % 2 == 0 else -1)
+    to = column + (1 if (core + column) % 2 == 1 else -1)
     return to if 0 <= to < columns else column
 
 

time: 15.9 us -> 15.9 us (level)
  the two profiles are of different devices: /device:TPU:4 before, /device:TPU:12 now
where the time goes in v28:
time: 15.9 us; the launch traced here: 15.7 us
  starting transfers between devices  7.01 us (44%)
  Pallas kernels  5.28 us (33%)
  waiting for transfers between devices  3.3 us (21%)
    pallas_call x14, Pallas kernels, call(): pl.pallas_call(kernel, out_shape=tuple(outs), in_specs=[HBM] * far + [VME...  5.28 us
    ppermute x2, starting transfers between devices, body(): lax.ppermute(e, 'height', pairs)  2.67 us
    ppermute x2, waiting for transfers between devices, body(): columns.append(lax.ppermute(column, ('tm', 'height', 'width'), route))  2.17 us
    ppermute x2, starting transfers between devices, body(): columns.append(lax.ppermute(column, ('tm', 'height', 'width'), route))  2.15 us
    ppermute x1, starting transfers between devices, body(): firsts.append(lax.ppermute(sent[2 * d - 2], 'tm', route))  1.47 us
    ppermute x1, waiting for transfers between devices, body(): rests[d] = lax.ppermute(rest, 'tm', route)  0.64 us
    ppermute x1, starting transfers between devices, body(): rests[d] = lax.ppermute(rest, 'tm', route)  0.57 us
  transfers between devices with their start and end apart: 9, of which 6 were waited for; matrix products, arithmetic and copies ran while one was open for 0% of the time, Pallas kernels for 26%

profile of v28, /device:TPU:12, one launch (start us, length us, event | category | flops | bytes accessed | tf_op | source)
XLA Modules:
  0.0 15.7 jit_solution(2122407375158975760)
XLA Ops:
  0.0 0.0 collective-permute-start
  0.0 1.5 %early.1 = (bf16[256,512]{1,0:T(8,128)(2,1)S(1)}, bf16[512,512]{1,0:T(8,128)(2,1)S(1)}, f32[3,3,512]{2,1,0:T(4,128)S(1)}, bf16[512,512]{1,0:T(8,128)(2,1)S(1)}, ...) custom-call(bf16[16,512]{1,0:T(8,128)(2,1)} %refs_0_.1, ...), custom_call_target="tpu_custom_call" | custom-call | bytes 5232640 | tf_op jit(solution)/shard_map/early/pallas_call | solution.py:20
  1.6 0.2 %collective-permute-done.partner_ref = bf16[256,512]{1,0:T(8,128)(2,1)S(1)} collective-permute-done((bf16[256,512]{1,0:T(8,128)(2,1)}, bf16[256,512]{1,0:T(8,128)(2,1)S(1)}, u32[]{:S(2)}, u32[]{:S(2)}) %collective-permute-start) | collective-permute-done | bytes 262176 | tf_op jit(solution)/shard_map/ppermute | solution.py:386
  1.7 0.1 column.1
  1.8 1.6 %collective-permute-start.1 = (bf16[64,512]{1,0:T(8,128)(2,1)S(1)}, bf16[64,512]{1,0:T(8,128)(2,1)S(1)}, u32[]{:S(2)}, u32[]{:S(2)}) collective-permute-start(bf16[64,512]{1,0:T(8,128)(2,1)S(1)} %column.1), channel_id=1, source_target_pairs={{0,4},{1,2},{2,1},{3,7},{4,0},{5,6},{6,5},{7,3},{8,9},{9,8},{10,11... | collective-permute-start | bytes 196616 | tf_op jit(solution)/shard_map/ppermute | solution.py:431
  3.5 0.5 %collective-permute-start.4 = (bf16[64,512]{1,0:T(8,128)(2,1)S(1)}, bf16[64,512]{1,0:T(8,128)(2,1)S(1)}, u32[]{:S(2)}, u32[]{:S(2)}) collective-permute-start(bf16[64,512]{1,0:T(8,128)(2,1)S(1)} %column.1), channel_id=1, source_target_pairs={{0,20},{1,18},{2,17},{3,23},{4,16},{5,22},{6,21},{7,19},{8,25},{9,... | collective-permute-start | bytes 196616 | tf_op jit(solution)/shard_map/ppermute | solution.py:431
  4.0 0.2 %later.1 = (bf16[64,512]{1,0:T(8,128)(2,1)S(1)}, bf16[192,512]{1,0:T(8,128)(2,1)S(1)}) custom-call(bf16[256,512]{1,0:T(8,128)(2,1)S(1)} %collective-permute-done.partner_ref, f32[24,8,512]{2,1,0:T(8,128)S(1)} %get-tuple-element.24.table_ref, f32[256,512]{1,0:T(8,128)S(1)} %get-tuple-element.38.refs_0_), custom_call_target="tpu_custom_call" | custom-call | flops 1048576 | bytes 1441792 | tf_op jit(solution)/shard_map/later/pallas_call | solution.py:20
  4.2 1.5 %collective-permute-start.6 = (bf16[64,512]{1,0:T(8,128)(2,1)S(1)}, bf16[64,512]{1,0:T(8,128)(2,1)S(1)}, u32[]{:S(2)}, u32[]{:S(2)}) collective-permute-start(bf16[64,512]{1,0:T(8,128)(2,1)S(1)} %get-tuple-element.39), channel_id=1, source_target_pairs={{0,16},{8,24},{16,0},{24,8},{1,17},{9,25},{17,1},{25,9},{2,18},{10... | collective-permute-start | bytes 196616 | tf_op jit(solution)/shard_map/ppermute | solution.py:434
  5.6 0.2 %own.1.mine_ref.refs_1_ = f32[256,512]{1,0:T(8,128)S(1)} custom-call(bf16[256,512]{1,0:T(8,128)(2,1)S(1)} %collective-permute-done.partner_ref, f32[24,8,512]{2,1,0:T(8,128)S(1)} %get-tuple-element.24.table_ref, f32[256,512]{1,0:T(8,128)S(1)} %get-tuple-element.25.field_ref), custom_call_target="tpu_custom_call" | custom-call | flops 1048576 | bytes 1703936 | tf_op jit(solution)/shard_map/own/pallas_call | solution.py:20
  5.8 0.3 %collective-permute-done.1.refs_0_ = bf16[64,512]{1,0:T(8,128)(2,1)S(1)} collective-permute-done((bf16[64,512]{1,0:T(8,128)(2,1)S(1)}, bf16[64,512]{1,0:T(8,128)(2,1)S(1)}, u32[]{:S(2)}, u32[]{:S(2)}) %collective-permute-start.1) | collective-permute-done | bytes 65568 | tf_op jit(solution)/shard_map/ppermute | solution.py:431
  6.1 0.1 side.1
  6.2 0.1 collective-permute-start.2
  6.3 0.6 %collective-permute-start.7 = (bf16[192,512]{1,0:T(8,128)(2,1)S(1)}, bf16[192,512]{1,0:T(8,128)(2,1)S(1)}, u32[]{:S(2)}, u32[]{:S(2)}) collective-permute-start(bf16[192,512]{1,0:T(8,128)(2,1)S(1)} %rest.1), channel_id=1, source_target_pairs={{0,16},{8,24},{16,0},{24,8},{1,17},{9,25},{17,1},{25,9},{2,18},{10... | collective-permute-start | bytes 589832 | tf_op jit(solution)/shard_map/ppermute | solution.py:452
  6.9 1.8 %collective-permute-done.4.refs_0_ = bf16[64,512]{1,0:T(8,128)(2,1)S(1)} collective-permute-done((bf16[64,512]{1,0:T(8,128)(2,1)S(1)}, bf16[64,512]{1,0:T(8,128)(2,1)S(1)}, u32[]{:S(2)}, u32[]{:S(2)}) %collective-permute-start.4) | collective-permute-done | bytes 65568 | tf_op jit(solution)/shard_map/ppermute | solution.py:431
  8.7 0.1 beside.1
  8.8 0.1 collective-permute-start.5
  8.9 0.0 collective-permute-done.2.other_ref
  9.0 1.6 %collective-permute-start.3 = (bf16[40,512]{1,0:T(8,128)(2,1)S(1)}, bf16[40,512]{1,0:T(8,128)(2,1)S(1)}, u32[]{:S(2)}, u32[]{:S(2)}) collective-permute-start(bf16[40,512]{1,0:T(8,128)(2,1)S(1)} %border.1), channel_id=1, source_target_pairs={{0,4},{4,0},{1,5},{5,1},{2,6},{6,2},{3,7},{7,3},{8,12},{12,8},{9,1... | collective-permute-start | bytes 122888 | tf_op jit(solution)/shard_map/ppermute | solution.py:455
  10.5 0.0 collective-permute-done.6.refs_2_.refs_0_
  10.5 0.0 collective-permute-done.5.refs_1_.other_ref
  10.6 1.1 %collective-permute-start.8 = (bf16[40,512]{1,0:T(8,128)(2,1)S(1)}, bf16[40,512]{1,0:T(8,128)(2,1)S(1)}, u32[]{:S(2)}, u32[]{:S(2)}) collective-permute-start(bf16[40,512]{1,0:T(8,128)(2,1)S(1)} %before.1), channel_id=1, source_target_pairs={{0,4},{4,0},{1,5},{5,1},{2,6},{6,2},{3,7},{7,3},{8,12},{12,8},{9,1... | collective-permute-start | bytes 122888 | tf_op jit(solution)/shard_map/ppermute | solution.py:467
  11.7 0.4 %gate.1.gate_ref = f32[256,512]{1,0:T(8,128)S(1)} custom-call(bf16[256,512]{1,0:T(8,128)(2,1)S(1)} %get-tuple-element.30.x_ref, bf16[512,512]{1,0:T(8,128)(2,1)S(1)} %get-tuple-element.31.w_ref), custom_call_target="tpu_custom_call" | custom-call | bytes 1310720 | tf_op jit(solution)/shard_map/gate/pallas_call | solution.py:20
  12.1 0.8 %inner.1 = (bf16[256,512]{1,0:T(8,128)(2,1)S(1)}, f32[256,512]{1,0:T(8,128)S(1)}) custom-call(f32[256,512]{1,0:T(8,128)S(1)} %own.1.mine_ref.refs_1_, f32[32,512]{1,0:T(8,128)S(1)} %get-tuple-element.27.own_ref.after_ref, bf16[32,512]{1,0:T(8,128)(2,1)S(1)} %collective-permute-done.2.other_ref, f32[3,3,512]{2,1,0:T(4,128)S(1)} %get-tuple-element.29.taps_ref, ...), custom_call_target="tpu_custom_call" | custom-call | flops 268435456 | bytes 3000320 | tf_op jit(solution)/shard_map/inner/pallas_call | solution.py:20
  12.9 0.2 %collective-permute-done.3.refs_0_ = bf16[40,512]{1,0:T(8,128)(2,1)S(1)} collective-permute-done((bf16[40,512]{1,0:T(8,128)(2,1)S(1)}, bf16[40,512]{1,0:T(8,128)(2,1)S(1)}, u32[]{:S(2)}, u32[]{:S(2)}) %collective-permute-start.3) | collective-permute-done | bytes 40992 | tf_op jit(solution)/shard_map/ppermute | solution.py:455
  13.0 0.6 %collective-permute-done.7.refs_3_ = bf16[192,512]{1,0:T(8,128)(2,1)S(1)} collective-permute-done((bf16[192,512]{1,0:T(8,128)(2,1)S(1)}, bf16[192,512]{1,0:T(8,128)(2,1)S(1)}, u32[]{:S(2)}, u32[]{:S(2)}) %collective-permute-start.7) | collective-permute-done | bytes 196640 | tf_op jit(solution)/shard_map/ppermute | solution.py:452
  13.7 0.8 %block.1 = (bf16[256,512]{1,0:T(8,128)(2,1)S(1)}, f32[256,512]{1,0:T(8,128)S(1)}) custom-call(bf16[256,512]{1,0:T(8,128)(2,1)S(1)} %get-tuple-element.34.inner_ref, f32[256,512]{1,0:T(8,128)S(1)} %get-tuple-element.35.totals_ref, f32[3,3,512]{2,1,0:T(4,128)S(1)} %get-tuple-element.29.taps_ref, ...), custom_call_target="tpu_custom_call", output_to_operand_aliasing={{0}: (0, {}), {1}: (1, {})} | custom-call | bytes 3524608 | tf_op jit(solution)/shard_map/block/pallas_call | solution.py:20
  14.5 0.1 collective-permute-done.8.refs_1_
  14.6 1.1 %last.1 = bf16[256,512]{1,0:T(8,128)(2,1)} custom-call(bf16[256,512]{1,0:T(8,128)(2,1)} %first.1.before_ref, bf16[256,512]{1,0:T(8,128)(2,1)S(1)} %get-tuple-element.41.inner_ref, f32[256,512]{1,0:T(8,128)S(1)} %get-tuple-element.42.totals_ref, f32[3,3,512]{2,1,0:T(4,128)S(1)} %get-tuple-element.29.taps_ref, ...), custom_call_target="tpu_custom_call", output_to_operand_aliasing={{}: (0, {})} | custom-call | bytes 2983936 | tf_op jit(solution)/shard_map/last/pallas_call | solution.py:20
  (4 shorter events, 0.1 us)
Async XLA Ops:
  0.0 1.7 %collective-permute-start = (bf16[256,512]{1,0:T(8,128)(2,1)}, bf16[256,512]{1,0:T(8,128)(2,1)S(1)}, u32[]{:S(2)}, u32[]{:S(2)}) collective-permute-start(bf16[256,512]{1,0:T(8,128)(2,1)} %bitcast.3), channel_id=1, source_target_pairs={{0,8},{8,0},{16,24},{24,16},{1,9},{9,1},{17,25},{25,17},{2,10},{10... | collective-permute-start | bytes 786440 | tf_op jit(solution)/shard_map/ppermute | solution.py:386
  1.8 4.3 %collective-permute-start.1 = (bf16[64,512]{1,0:T(8,128)(2,1)S(1)}, bf16[64,512]{1,0:T(8,128)(2,1)S(1)}, u32[]{:S(2)}, u32[]{:S(2)}) collective-permute-start(bf16[64,512]{1,0:T(8,128)(2,1)S(1)} %column.1), channel_id=1, source_target_pairs={{0,4},{1,2},{2,1},{3,7},{4,0},{5,6},{6,5},{7,3},{8,9},{9,8},{10,11... | collective-permute-start | bytes 196616 | tf_op jit(solution)/shard_map/ppermute | solution.py:431
  3.5 5.3 %collective-permute-start.4 = (bf16[64,512]{1,0:T(8,128)(2,1)S(1)}, bf16[64,512]{1,0:T(8,128)(2,1)S(1)}, u32[]{:S(2)}, u32[]{:S(2)}) collective-permute-start(bf16[64,512]{1,0:T(8,128)(2,1)S(1)} %column.1), channel_id=1, source_target_pairs={{0,20},{1,18},{2,17},{3,23},{4,16},{5,22},{6,21},{7,19},{8,25},{9,... | collective-permute-start | bytes 196616 | tf_op jit(solution)/shard_map/ppermute | solution.py:431
  4.2 6.4 %collective-permute-start.6 = (bf16[64,512]{1,0:T(8,128)(2,1)S(1)}, bf16[64,512]{1,0:T(8,128)(2,1)S(1)}, u32[]{:S(2)}, u32[]{:S(2)}) collective-permute-start(bf16[64,512]{1,0:T(8,128)(2,1)S(1)} %get-tuple-element.39), channel_id=1, source_target_pairs={{0,16},{8,24},{16,0},{24,8},{1,17},{9,25},{17,1},{25,9},{2,18},{10... | collective-permute-start | bytes 196616 | tf_op jit(solution)/shard_map/ppermute | solution.py:434
  6.2 2.7 %collective-permute-start.2 = (bf16[32,512]{1,0:T(8,128)(2,1)S(1)}, bf16[32,512]{1,0:T(8,128)(2,1)S(1)}, u32[]{:S(2)}, u32[]{:S(2)}) collective-permute-start(bf16[32,512]{1,0:T(8,128)(2,1)S(1)} %get-tuple-element.28), channel_id=1, source_target_pairs={{0,8},{8,0},{16,24},{24,16},{1,9},{9,1},{17,25},{25,17},{2,10},{10... | collective-permute-start | bytes 98312 | tf_op jit(solution)/shard_map/ppermute | solution.py:449
  6.3 7.4 %collective-permute-start.7 = (bf16[192,512]{1,0:T(8,128)(2,1)S(1)}, bf16[192,512]{1,0:T(8,128)(2,1)S(1)}, u32[]{:S(2)}, u32[]{:S(2)}) collective-permute-start(bf16[192,512]{1,0:T(8,128)(2,1)S(1)} %rest.1), channel_id=1, source_target_pairs={{0,16},{8,24},{16,0},{24,8},{1,17},{9,25},{17,1},{25,9},{2,18},{10... | collective-permute-start | bytes 589832 | tf_op jit(solution)/shard_map/ppermute | solution.py:452
  8.8 1.7 %collective-permute-start.5 = (bf16[32,512]{1,0:T(8,128)(2,1)S(1)}, bf16[32,512]{1,0:T(8,128)(2,1)S(1)}, u32[]{:S(2)}, u32[]{:S(2)}) collective-permute-start(bf16[32,512]{1,0:T(8,128)(2,1)S(1)} %get-tuple-element.37), channel_id=1, source_target_pairs={{0,8},{8,0},{16,24},{24,16},{1,9},{9,1},{17,25},{25,17},{2,10},{10... | collective-permute-start | bytes 98312 | tf_op jit(solution)/shard_map/ppermute | solution.py:465
  9.0 4.1 %collective-permute-start.3 = (bf16[40,512]{1,0:T(8,128)(2,1)S(1)}, bf16[40,512]{1,0:T(8,128)(2,1)S(1)}, u32[]{:S(2)}, u32[]{:S(2)}) collective-permute-start(bf16[40,512]{1,0:T(8,128)(2,1)S(1)} %border.1), channel_id=1, source_target_pairs={{0,4},{4,0},{1,5},{5,1},{2,6},{6,2},{3,7},{7,3},{8,12},{12,8},{9,1... | collective-permute-start | bytes 122888 | tf_op jit(solution)/shard_map/ppermute | solution.py:455
  10.6 4.1 %collective-permute-start.8 = (bf16[40,512]{1,0:T(8,128)(2,1)S(1)}, bf16[40,512]{1,0:T(8,128)(2,1)S(1)}, u32[]{:S(2)}, u32[]{:S(2)}) collective-permute-start(bf16[40,512]{1,0:T(8,128)(2,1)S(1)} %before.1), channel_id=1, source_target_pairs={{0,4},{4,0},{1,5},{5,1},{2,6},{6,2},{3,7},{7,3},{8,12},{12,8},{9,1... | collective-permute-start | bytes 122888 | tf_op jit(solution)/shard_map/ppermute | solution.py:467

commit v29 on v25

--- a/solution.py
+++ b/solution.py
@@ -141,8 +141,8 @@
             span = slice(lane, lane + LANES)
             totals = with_partner(frames, rows, cols, d, field, partner_ref, table_ref, span)
             tiles = reordered([jnp.concatenate([t[r] for t in totals]) for r in range(rows)], rounds_h)
-            outs[2 * d - 2][:, span] = jnp.concatenate(tiles[: rounds_h + 1]).astype(BF16)
-            outs[2 * d - 1][:, span] = jnp.concatenate(tiles[rounds_h + 1 :]).astype(BF16)
+            outs[2 * d - 2][:, span] = jnp.concatenate(tiles[: rounds_h + 2]).astype(BF16)
+            outs[2 * d - 1][:, span] = jnp.concatenate(tiles[rounds_h + 2 :]).astype(BF16)
 
 
 def rest_kernel(after_ref, rest_ref, out_ref):
@@ -212,7 +212,7 @@
 
 
 def before_kernel(frames, rows, cols, own_ref, other_ref, *refs):
-    rounds_h = refs[0].shape[0] // (frames * cols) - 1
+    rounds_h = refs[0].shape[0] // (frames * cols) - 2
     firsts, outs = refs[:-rounds_h], refs[-rounds_h:]
     size = frames * cols
     odd, _, _ = position("height")
@@ -296,8 +296,8 @@
             low, high = both_sides(own_ref[:, span], other_ref[:, span].astype(F32))
             lines = [jnp.zeros((size, LANES), F32)] * rows
             for d, (first, rest) in enumerate(zip(firsts, rests), 1):
-                more = [first[i * size : (i + 1) * size, span].astype(F32) for i in range(rounds_h + 1)]
-                more += [rest[i * size : (i + 1) * size, span].astype(F32) for i in range(rows - rounds_h - 1)]
+                more = [first[i * size : (i + 1) * size, span].astype(F32) for i in range(rounds_h + 2)]
+                more += [rest[i * size : (i + 1) * size, span].astype(F32) for i in range(rows - rounds_h - 2)]
                 more = reordered(more, rounds_h, back=True)
                 lines = [line + later(d, other) for line, other in zip(lines, more)]
             for t in range(frames):
@@ -400,7 +400,7 @@
         [pltpu.VMEM((block, LANES), F32)],
         [partner, side],
     )
-    parts = [shape((n * frames * cols, chans), BF16) for n in (len(h_rounds) + 1, rows - len(h_rounds) - 1)]
+    parts = [shape((n * frames * cols, chans), BF16) for n in (len(h_rounds) + 2, rows - len(h_rounds) - 2)]
     sent = call(
         functools.partial(later_kernel, frames, rows, cols, len(h_rounds)),
         "later",

time: 15.9 us -> 16.2 us (1.019)
  the two profiles are of different devices: /device:TPU:4 before, /device:TPU:0 now
where the time goes in v29:
time: 16.2 us; the launch traced here: 16 us
  starting transfers between devices  10.3 us (64%)
  Pallas kernels  4.5 us (28%)
  waiting for transfers between devices  1.1 us (7%)
    pallas_call x14, Pallas kernels, call(): pl.pallas_call(kernel, out_shape=tuple(outs), in_specs=[HBM] * far + [VME...  4.5 us
    ppermute x2, starting transfers between devices, body(): columns.append(lax.ppermute(column, ('tm', 'height', 'width'), route))  4.22 us
    ppermute x2, starting transfers between devices, body(): lax.ppermute(e, 'height', pairs)  2.88 us
    ppermute x1, starting transfers between devices, body(): rests[d] = lax.ppermute(rest, 'tm', route)  1.79 us
    ppermute x1, starting transfers between devices, body(): firsts.append(lax.ppermute(sent[2 * d - 2], 'tm', route))  0.69 us
    ppermute x1, waiting for transfers between devices, body(): firsts.append(lax.ppermute(sent[2 * d - 2], 'tm', route))  0.54 us
    ppermute x1, starting transfers between devices, body(): partner = lax.ppermute(x, 'tm', [(i, i ^ 1) for i in range(n_t)])  0.45 us
    ppermute x2, waiting for transfers between devices, body(): lax.ppermute(e, 'height', pairs)  0.43 us
  transfers between devices with their start and end apart: 9, of which 3 were waited for; matrix products, arithmetic and copies ran while one was open for 0% of the time, Pallas kernels for 28%

profile of v29, /device:TPU:0, one launch (start us, length us, event | category | flops | bytes accessed | tf_op | source)
XLA Modules:
  0.0 16.0 jit_solution(12190999250164640724)
XLA Ops:
  0.0 0.5 %collective-permute-start = (bf16[256,512]{1,0:T(8,128)(2,1)}, bf16[256,512]{1,0:T(8,128)(2,1)S(1)}, u32[]{:S(2)}, u32[]{:S(2)}) collective-permute-start(bf16[256,512]{1,0:T(8,128)(2,1)} %bitcast.3), channel_id=1, source_target_pairs={{0,8},{8,0},{16,24},{24,16},{1,9},{9,1},{17,25},{25,17},{2,10},{10... | collective-permute-start | bytes 786440 | tf_op jit(solution)/shard_map/ppermute | solution.py:380
  0.5 1.5 %early.1 = (bf16[256,512]{1,0:T(8,128)(2,1)S(1)}, bf16[512,512]{1,0:T(8,128)(2,1)S(1)}, f32[3,3,512]{2,1,0:T(4,128)S(1)}, bf16[512,512]{1,0:T(8,128)(2,1)S(1)}, ...) custom-call(bf16[16,512]{1,0:T(8,128)(2,1)} %refs_0_.1, ...), custom_call_target="tpu_custom_call" | custom-call | bytes 5232640 | tf_op jit(solution)/shard_map/early/pallas_call | solution.py:20
  2.0 0.0 collective-permute-done.partner_ref
  2.0 0.1 column.1
  2.1 2.8 %collective-permute-start.1 = (bf16[64,512]{1,0:T(8,128)(2,1)S(1)}, bf16[64,512]{1,0:T(8,128)(2,1)S(1)}, u32[]{:S(2)}, u32[]{:S(2)}) collective-permute-start(bf16[64,512]{1,0:T(8,128)(2,1)S(1)} %column.1), channel_id=1, source_target_pairs={{0,1},{1,0},{2,3},{3,2},{4,5},{5,4},{6,7},{7,6},{8,12},{9,10},{10,... | collective-permute-start | bytes 196616 | tf_op jit(solution)/shard_map/ppermute | solution.py:425
  4.9 1.4 %collective-permute-start.4 = (bf16[64,512]{1,0:T(8,128)(2,1)S(1)}, bf16[64,512]{1,0:T(8,128)(2,1)S(1)}, u32[]{:S(2)}, u32[]{:S(2)}) collective-permute-start(bf16[64,512]{1,0:T(8,128)(2,1)S(1)} %column.1), channel_id=1, source_target_pairs={{0,17},{1,16},{2,19},{3,18},{4,21},{5,20},{6,23},{7,22},{8,28},{9,... | collective-permute-start | bytes 196616 | tf_op jit(solution)/shard_map/ppermute | solution.py:425
  6.3 0.2 %later.1 = (bf16[96,512]{1,0:T(8,128)(2,1)S(1)}, bf16[160,512]{1,0:T(8,128)(2,1)S(1)}) custom-call(bf16[256,512]{1,0:T(8,128)(2,1)S(1)} %collective-permute-done.partner_ref, f32[24,8,512]{2,1,0:T(8,128)S(1)} %get-tuple-element.24.table_ref, f32[256,512]{1,0:T(8,128)S(1)} %get-tuple-element.38.refs_0_), custom_call_target="tpu_custom_call" | custom-call | flops 1048576 | bytes 1441792 | tf_op jit(solution)/shard_map/later/pallas_call | solution.py:20
  6.5 0.7 %collective-permute-start.6 = (bf16[96,512]{1,0:T(8,128)(2,1)S(1)}, bf16[96,512]{1,0:T(8,128)(2,1)S(1)}, u32[]{:S(2)}, u32[]{:S(2)}) collective-permute-start(bf16[96,512]{1,0:T(8,128)(2,1)S(1)} %get-tuple-element.39), channel_id=1, source_target_pairs={{0,16},{8,24},{16,0},{24,8},{1,17},{9,25},{17,1},{25,9},{2,18},{10... | collective-permute-start | bytes 294920 | tf_op jit(solution)/shard_map/ppermute | solution.py:428
  7.2 0.2 %own.1.mine_ref.refs_1_ = f32[256,512]{1,0:T(8,128)S(1)} custom-call(bf16[256,512]{1,0:T(8,128)(2,1)S(1)} %collective-permute-done.partner_ref, f32[24,8,512]{2,1,0:T(8,128)S(1)} %get-tuple-element.24.table_ref, f32[256,512]{1,0:T(8,128)S(1)} %get-tuple-element.25.field_ref), custom_call_target="tpu_custom_call" | custom-call | flops 1048576 | bytes 1703936 | tf_op jit(solution)/shard_map/own/pallas_call | solution.py:20
  7.4 0.0 collective-permute-done.1.refs_0_
  7.4 0.1 side.1
  7.5 0.1 collective-permute-start.2
  7.6 1.8 %collective-permute-start.7 = (bf16[160,512]{1,0:T(8,128)(2,1)S(1)}, bf16[160,512]{1,0:T(8,128)(2,1)S(1)}, u32[]{:S(2)}, u32[]{:S(2)}) collective-permute-start(bf16[160,512]{1,0:T(8,128)(2,1)S(1)} %rest.1), channel_id=1, source_target_pairs={{0,16},{8,24},{16,0},{24,8},{1,17},{9,25},{17,1},{25,9},{2,18},{10... | collective-permute-start | bytes 491528 | tf_op jit(solution)/shard_map/ppermute | solution.py:446
  9.4 0.1 collective-permute-done.4.refs_0_
  9.5 0.1 beside.1
  9.6 0.2 %collective-permute-start.5 = (bf16[32,512]{1,0:T(8,128)(2,1)S(1)}, bf16[32,512]{1,0:T(8,128)(2,1)S(1)}, u32[]{:S(2)}, u32[]{:S(2)}) collective-permute-start(bf16[32,512]{1,0:T(8,128)(2,1)S(1)} %get-tuple-element.37), channel_id=1, source_target_pairs={{0,8},{8,0},{16,24},{24,16},{1,9},{9,1},{17,25},{25,17},{2,10},{10... | collective-permute-start | bytes 98312 | tf_op jit(solution)/shard_map/ppermute | solution.py:459
  9.7 0.0 collective-permute-done.2.other_ref
  9.8 1.6 %collective-permute-start.3 = (bf16[40,512]{1,0:T(8,128)(2,1)S(1)}, bf16[40,512]{1,0:T(8,128)(2,1)S(1)}, u32[]{:S(2)}, u32[]{:S(2)}) collective-permute-start(bf16[40,512]{1,0:T(8,128)(2,1)S(1)} %border.1), channel_id=1, source_target_pairs={{0,4},{4,0},{1,5},{5,1},{2,6},{6,2},{3,7},{7,3},{8,12},{12,8},{9,1... | collective-permute-start | bytes 122888 | tf_op jit(solution)/shard_map/ppermute | solution.py:449
  11.3 0.0 collective-permute-done.5.refs_1_.other_ref
  11.3 0.5 %collective-permute-done.6.refs_2_.refs_0_ = bf16[96,512]{1,0:T(8,128)(2,1)S(1)} collective-permute-done((bf16[96,512]{1,0:T(8,128)(2,1)S(1)}, bf16[96,512]{1,0:T(8,128)(2,1)S(1)}, u32[]{:S(2)}, u32[]{:S(2)}) %collective-permute-start.6) | collective-permute-done | bytes 98336 | tf_op jit(solution)/shard_map/ppermute | solution.py:428
  11.9 1.3 %collective-permute-start.8 = (bf16[40,512]{1,0:T(8,128)(2,1)S(1)}, bf16[40,512]{1,0:T(8,128)(2,1)S(1)}, u32[]{:S(2)}, u32[]{:S(2)}) collective-permute-start(bf16[40,512]{1,0:T(8,128)(2,1)S(1)} %before.1), channel_id=1, source_target_pairs={{0,4},{4,0},{1,5},{5,1},{2,6},{6,2},{3,7},{7,3},{8,12},{12,8},{9,1... | collective-permute-start | bytes 122888 | tf_op jit(solution)/shard_map/ppermute | solution.py:461
  13.2 0.4 %gate.1.gate_ref = f32[256,512]{1,0:T(8,128)S(1)} custom-call(bf16[256,512]{1,0:T(8,128)(2,1)S(1)} %get-tuple-element.30.x_ref, bf16[512,512]{1,0:T(8,128)(2,1)S(1)} %get-tuple-element.31.w_ref), custom_call_target="tpu_custom_call" | custom-call | bytes 1310720 | tf_op jit(solution)/shard_map/gate/pallas_call | solution.py:20
  13.6 0.8 %inner.1 = (bf16[256,512]{1,0:T(8,128)(2,1)S(1)}, f32[256,512]{1,0:T(8,128)S(1)}) custom-call(f32[256,512]{1,0:T(8,128)S(1)} %own.1.mine_ref.refs_1_, f32[32,512]{1,0:T(8,128)S(1)} %get-tuple-element.27.own_ref.after_ref, bf16[32,512]{1,0:T(8,128)(2,1)S(1)} %collective-permute-done.2.other_ref, f32[3,3,512]{2,1,0:T(4,128)S(1)} %get-tuple-element.29.taps_ref, ...), custom_call_target="tpu_custom_call" | custom-call | flops 268435456 | bytes 3000320 | tf_op jit(solution)/shard_map/inner/pallas_call | solution.py:20
  14.4 0.0 collective-permute-done.3.refs_0_
  14.4 1.1 %first.1.before_ref = bf16[256,512]{1,0:T(8,128)(2,1)} custom-call(bf16[256,512]{1,0:T(8,128)(2,1)S(1)} %get-tuple-element.34.inner_ref, f32[256,512]{1,0:T(8,128)S(1)} %get-tuple-element.35.totals_ref, f32[3,3,512]{2,1,0:T(4,128)S(1)} %get-tuple-element.29.taps_ref, f32[256,512]{1,0:T(8,128)S(1)} %gate.1.gate_ref, ...), custom_call_target="tpu_custom_call" | custom-call | bytes 2680832 | tf_op jit(solution)/shard_map/first/pallas_call | solution.py:20
  15.5 0.0 collective-permute-done.7.refs_3_
  15.6 0.4 %collective-permute-done.8.refs_1_ = bf16[40,512]{1,0:T(8,128)(2,1)S(1)} collective-permute-done((bf16[40,512]{1,0:T(8,128)(2,1)S(1)}, bf16[40,512]{1,0:T(8,128)(2,1)S(1)}, u32[]{:S(2)}, u32[]{:S(2)}) %collective-permute-start.8) | collective-permute-done | bytes 40992 | tf_op jit(solution)/shard_map/ppermute | solution.py:461
  (5 shorter events, 0.1 us)
Async XLA Ops:
  0.0 2.0 %collective-permute-start = (bf16[256,512]{1,0:T(8,128)(2,1)}, bf16[256,512]{1,0:T(8,128)(2,1)S(1)}, u32[]{:S(2)}, u32[]{:S(2)}) collective-permute-start(bf16[256,512]{1,0:T(8,128)(2,1)} %bitcast.3), channel_id=1, source_target_pairs={{0,8},{8,0},{16,24},{24,16},{1,9},{9,1},{17,25},{25,17},{2,10},{10... | collective-permute-start | bytes 786440 | tf_op jit(solution)/shard_map/ppermute | solution.py:380
  2.1 5.3 %collective-permute-start.1 = (bf16[64,512]{1,0:T(8,128)(2,1)S(1)}, bf16[64,512]{1,0:T(8,128)(2,1)S(1)}, u32[]{:S(2)}, u32[]{:S(2)}) collective-permute-start(bf16[64,512]{1,0:T(8,128)(2,1)S(1)} %column.1), channel_id=1, source_target_pairs={{0,1},{1,0},{2,3},{3,2},{4,5},{5,4},{6,7},{7,6},{8,12},{9,10},{10,... | collective-permute-start | bytes 196616 | tf_op jit(solution)/shard_map/ppermute | solution.py:425
  4.9 4.6 %collective-permute-start.4 = (bf16[64,512]{1,0:T(8,128)(2,1)S(1)}, bf16[64,512]{1,0:T(8,128)(2,1)S(1)}, u32[]{:S(2)}, u32[]{:S(2)}) collective-permute-start(bf16[64,512]{1,0:T(8,128)(2,1)S(1)} %column.1), channel_id=1, source_target_pairs={{0,17},{1,16},{2,19},{3,18},{4,21},{5,20},{6,23},{7,22},{8,28},{9,... | collective-permute-start | bytes 196616 | tf_op jit(solution)/shard_map/ppermute | solution.py:425
  6.5 5.4 %collective-permute-start.6 = (bf16[96,512]{1,0:T(8,128)(2,1)S(1)}, bf16[96,512]{1,0:T(8,128)(2,1)S(1)}, u32[]{:S(2)}, u32[]{:S(2)}) collective-permute-start(bf16[96,512]{1,0:T(8,128)(2,1)S(1)} %get-tuple-element.39), channel_id=1, source_target_pairs={{0,16},{8,24},{16,0},{24,8},{1,17},{9,25},{17,1},{25,9},{2,18},{10... | collective-permute-start | bytes 294920 | tf_op jit(solution)/shard_map/ppermute | solution.py:428
  7.5 2.3 %collective-permute-start.2 = (bf16[32,512]{1,0:T(8,128)(2,1)S(1)}, bf16[32,512]{1,0:T(8,128)(2,1)S(1)}, u32[]{:S(2)}, u32[]{:S(2)}) collective-permute-start(bf16[32,512]{1,0:T(8,128)(2,1)S(1)} %get-tuple-element.28), channel_id=1, source_target_pairs={{0,8},{8,0},{16,24},{24,16},{1,9},{9,1},{17,25},{25,17},{2,10},{10... | collective-permute-start | bytes 98312 | tf_op jit(solution)/shard_map/ppermute | solution.py:443
  7.6 8.0 %collective-permute-start.7 = (bf16[160,512]{1,0:T(8,128)(2,1)S(1)}, bf16[160,512]{1,0:T(8,128)(2,1)S(1)}, u32[]{:S(2)}, u32[]{:S(2)}) collective-permute-start(bf16[160,512]{1,0:T(8,128)(2,1)S(1)} %rest.1), channel_id=1, source_target_pairs={{0,16},{8,24},{16,0},{24,8},{1,17},{9,25},{17,1},{25,9},{2,18},{10... | collective-permute-start | bytes 491528 | tf_op jit(solution)/shard_map/ppermute | solution.py:446
  9.6 1.8 %collective-permute-start.5 = (bf16[32,512]{1,0:T(8,128)(2,1)S(1)}, bf16[32,512]{1,0:T(8,128)(2,1)S(1)}, u32[]{:S(2)}, u32[]{:S(2)}) collective-permute-start(bf16[32,512]{1,0:T(8,128)(2,1)S(1)} %get-tuple-element.37), channel_id=1, source_target_pairs={{0,8},{8,0},{16,24},{24,16},{1,9},{9,1},{17,25},{25,17},{2,10},{10... | collective-permute-start | bytes 98312 | tf_op jit(solution)/shard_map/ppermute | solution.py:459
  9.8 4.7 %collective-permute-start.3 = (bf16[40,512]{1,0:T(8,128)(2,1)S(1)}, bf16[40,512]{1,0:T(8,128)(2,1)S(1)}, u32[]{:S(2)}, u32[]{:S(2)}) collective-permute-start(bf16[40,512]{1,0:T(8,128)(2,1)S(1)} %border.1), channel_id=1, source_target_pairs={{0,4},{4,0},{1,5},{5,1},{2,6},{6,2},{3,7},{7,3},{8,12},{12,8},{9,1... | collective-permute-start | bytes 122888 | tf_op jit(solution)/shard_map/ppermute | solution.py:449
  11.9 4.1 %collective-permute-start.8 = (bf16[40,512]{1,0:T(8,128)(2,1)S(1)}, bf16[40,512]{1,0:T(8,128)(2,1)S(1)}, u32[]{:S(2)}, u32[]{:S(2)}) collective-permute-start(bf16[40,512]{1,0:T(8,128)(2,1)S(1)} %before.1), channel_id=1, source_target_pairs={{0,4},{4,0},{1,5},{5,1},{2,6},{6,2},{3,7},{7,3},{8,12},{12,8},{9,1... | collective-permute-start | bytes 122888 | tf_op jit(solution)/shard_map/ppermute | solution.py:461
